TPU v7x, 32 devices: a whole 2x2x4 slice. The times are simulated.
32 devices in a mesh: parts: 2 (over y), space: 16 (over z, x, core).
Axes of the slice: x: 2, y: 2, z: 4, core: 2. Of those that a mesh axis runs over, the one named last changes fastest.
Arguments:
- density: float32 [32, 32, 128], P('space', 'parts'), parts along dimension 1, may hold values from 0.14 to 1
- displacement: float32 [16, 3, 32, 32, 128], P('space', None, None, 'parts'), parts along dimension 3, may hold values from -6 to 6
- fixed: int32 [32, 256], P(None, 'parts'), parts along dimension 1, may hold values 0 or 1
- load_index: int32 [32], P('parts'), parts along dimension 0, may hold values from 0 to 65535
- load_force: float32 [32, 3], P('parts'), parts along dimension 0, may hold values from -120 to 120
- radius: int32 [32], P('parts'), parts along dimension 0, may hold values from 1 to 3
Outputs:
- new_density: float32 [32, 32, 128], P('space', 'parts'), parts along dimension 1
- new_displacement: float32 [16, 3, 32, 32, 128], P('space', None, None, 'parts'), parts along dimension 3
There are 2 independent parts, one for each index of `parts`. A program takes and returns all parts, laid end to end along the dimension named above; each array names one. Nothing has to cross between parts.
All inputs are finite; a program needn't handle non-finite values.
Results may differ from a plain program's by a relative error of at most 0.0003.
Values sent between devices are 32-bit elements; how exact they have to be, the bound alone decides.
No kernel may reach another device: no remote copies, remote signals or barrier semaphores. Data moves between devices by JAX's collectives and lax.ppermute only.
A program may use at most 64 MiB of HBM per device.

v0:
```python
import math

import jax
import jax.numpy as jnp
from jax import lax
from jax.sharding import PartitionSpec as P

SWEEPS = 3
SEARCH = 12


floor_modulus = 0.05
relax_factor = 0.6
move_limit = 0.2
density_floor = 0.01
volume_share = 0.5
log_lower = -16.0
log_span = 32.0
window_reach = 2


def from_behind(block, axis, distance):
    devices = range(lax.axis_size(axis))
    route = [(i - distance, i) for i in devices if i - distance in devices]
    return lax.ppermute(block, axis, route)


def extended(x, sides, width):
    for axis, dim in sides:
        size, length = (lax.axis_size(axis), x.shape[dim])
        up = [(i, (i + 1) % size) for i in range(size - 1)]
        down = [(j, i) for i, j in up]
        last = lax.slice_in_dim(x, length - width, length, axis=dim)
        first = lax.slice_in_dim(x, 0, width, axis=dim)
        before = lax.ppermute(last, axis, up)
        after = lax.ppermute(first, axis, down)
        x = jnp.concatenate([before, x, after], axis=dim)
    return x


def from_partner(x, axis, bit):
    return lax.ppermute(x, axis, [(i, i ^ 1 << bit) for i in range(lax.axis_size(axis))])


def window_offsets():
    offsets_list = []
    for across in range(-window_reach, window_reach + 1):
        for upward in range(-window_reach, window_reach + 1):
            for sideways in range(-window_reach, window_reach + 1):
                length = math.sqrt(across * across + upward * upward + sideways * sideways)
                offsets_list.append((across, upward, sideways, length))
    return offsets_list


def layer_weights(radius):
    radial = radius.astype(jnp.float32)
    return jnp.stack(
        [jnp.maximum(radial - length, 0.0) for across, upward, sideways, length in window_offsets()]
    )


def pad_axis(grid_field, along_axis, before, after_cells):
    widths = [(0, 0)] * grid_field.ndim
    widths[along_axis] = (before, after_cells)
    return jnp.pad(grid_field, widths)


def pad_sides(grid_field):
    return jnp.pad(grid_field, ((0, 0), (window_reach, window_reach), (window_reach, window_reach)))


def filter_forward(padded, weights):
    out_rows = padded.shape[0] - 2 * window_reach
    layers = padded.shape[1] - 2 * window_reach
    row_width = padded.shape[2] - 2 * window_reach
    result = jnp.zeros((out_rows, layers, row_width), jnp.float32)
    for offset_index, (across, upward, sideways, length) in enumerate(window_offsets()):
        shifted = padded[
            window_reach + across : window_reach + across + out_rows,
            window_reach + upward : window_reach + upward + layers,
            window_reach + sideways : window_reach + sideways + row_width,
        ]
        result = result + weights[offset_index][None, :, None] * shifted
    return result


def filter_backward(padded, padded_weights):
    out_rows = padded.shape[0] - 2 * window_reach
    layers = padded.shape[1] - 2 * window_reach
    row_width = padded.shape[2] - 2 * window_reach
    result = jnp.zeros((out_rows, layers, row_width), jnp.float32)
    for offset_index, (across, upward, sideways, length) in enumerate(window_offsets()):
        shifted = padded[
            window_reach - across : window_reach - across + out_rows,
            window_reach - upward : window_reach - upward + layers,
            window_reach - sideways : window_reach - sideways + row_width,
        ]
        layer_part = padded_weights[
            offset_index, window_reach - upward : window_reach - upward + layers
        ]
        result = result + layer_part[None, :, None] * shifted
    return result


def stiff_factors(direction):
    return jnp.array(
        [2.0 if component == direction else 1.0 for component in range(3)], jnp.float32
    ).reshape(3, 1, 1, 1)


def relax_slab(padded, displace, face_x, face_z, face_y, force_field, free_cells, diagonal):
    flux_x = stiff_factors(0) * face_x * jnp.diff(padded, axis=1)
    stencil_image = flux_x[:, :-1] - flux_x[:, 1:]
    flux_z = stiff_factors(1) * face_z * jnp.diff(displace, axis=2)
    stencil_image = stencil_image + pad_axis(flux_z, 2, 1, 0) - pad_axis(flux_z, 2, 0, 1)
    flux_y = stiff_factors(2) * face_y * jnp.diff(displace, axis=3)
    stencil_image = stencil_image + pad_axis(flux_y, 3, 1, 0) - pad_axis(flux_y, 3, 0, 1)
    return free_cells * (displace + relax_factor * (force_field - stencil_image) / diagonal)


def slab_energy(grid_field, along_axis, direction, load_cases):
    change = jnp.diff(grid_field, axis=along_axis)
    return jnp.sum(stiff_factors(direction) * change * change, axis=0) / load_cases


def neighbour_planes(displace, load_cases, axis_devices):
    if axis_devices > load_cases:
        below = from_behind(displace[:, -1:], "space", load_cases)
        above = from_behind(displace[:, :1], "space", -load_cases)
    else:
        below = jnp.zeros_like(displace[:, :1])
        above = jnp.zeros_like(displace[:, :1])
    return jnp.concatenate([below, displace, above], axis=1)


def local(density, displacement, fixed, load_index, load_force, radius):
    slab_rows, layers, row_width = density.shape
    load_cases = load_index.shape[0]
    level_count = load_cases.bit_length() - 1
    axis_devices = lax.axis_size("space")
    axis_place = lax.axis_index("space")
    slab_planes = slab_rows * load_cases
    slab_place = axis_place // load_cases
    load_place = axis_place % load_cases
    total_rows = slab_rows * axis_devices
    weights = layer_weights(radius)
    padded_weights = pad_axis(weights, 1, window_reach, window_reach)
    global_rows = (
        jnp.arange(slab_rows + 2 * window_reach, dtype=jnp.int32)
        + axis_place * slab_rows
        - window_reach
    )
    deep_inside = ((global_rows >= 0) & (global_rows < total_rows)).astype(jnp.float32)
    inside_field = deep_inside[:, None, None] * pad_sides(
        jnp.ones((slab_rows + 2 * window_reach, layers, row_width), jnp.float32)
    )
    total_weight = filter_forward(inside_field, weights)
    slab_start = slab_place * slab_planes
    margin_rows = jnp.arange(slab_planes + 2, dtype=jnp.int32) + slab_start - 1
    margin_inside = ((margin_rows >= 0) & (margin_rows < total_rows)).astype(jnp.float32)
    face_valid = margin_inside[1:] * margin_inside[:-1]
    fixed_slab = lax.dynamic_slice_in_dim(fixed, slab_start, slab_planes, 0).astype(jnp.float32)
    bottom_layer = (jnp.arange(layers, dtype=jnp.int32) == 0).astype(jnp.float32)
    free_cells = 1.0 - bottom_layer[None, :, None] * fixed_slab[:, None, :]
    slab_cells = slab_planes * layers * row_width
    cell_index = jnp.arange(slab_cells, dtype=jnp.int32) + slab_place * slab_cells
    load_hot = jnp.arange(load_cases, dtype=jnp.int32) == load_place
    own_index = jnp.sum(jnp.where(load_hot, load_index, 0))
    own_force = jnp.sum(load_hot.astype(jnp.float32)[:, None] * load_force, axis=0)
    load_hits = (cell_index == own_index).astype(jnp.float32)
    force_field = (own_force[:, None] * load_hits[None, :]).reshape(
        3, slab_planes, layers, row_width
    )
    displace = displacement[0] * free_cells
    target = volume_share * total_rows * layers * row_width
    padded = neighbour_planes(displace, load_cases, axis_devices)
    halo_density = extended(density, (("space", 0),), window_reach)
    filtered = filter_forward(pad_sides(halo_density), weights) / total_weight
    whole_field = lax.all_gather(filtered, "space", axis=0, tiled=True)
    margin = lax.dynamic_slice_in_dim(
        pad_axis(whole_field, 0, 1, 1), slab_start, slab_planes + 2, 0
    )
    moduli = floor_modulus + (1.0 - floor_modulus) * margin**3
    face_x = 0.5 * (moduli[1:] + moduli[:-1]) * face_valid[:, None, None]
    inner_moduli = moduli[1:-1]
    face_z = 0.5 * (inner_moduli[:, 1:] + inner_moduli[:, :-1])
    face_y = 0.5 * (inner_moduli[:, :, 1:] + inner_moduli[:, :, :-1])
    sum_x = face_x[:-1] + face_x[1:]
    sum_z = pad_axis(face_z, 1, 1, 0) + pad_axis(face_z, 1, 0, 1)
    sum_y = pad_axis(face_y, 2, 1, 0) + pad_axis(face_y, 2, 0, 1)
    diagonal = stiff_factors(0) * sum_x + stiff_factors(1) * sum_z + stiff_factors(2) * sum_y
    for sweep_index in range(SWEEPS):
        displace = relax_slab(
            padded, displace, face_x, face_z, face_y, force_field, free_cells, diagonal
        )
        padded = neighbour_planes(displace, load_cases, axis_devices)
    energy_x = slab_energy(padded, 1, 0, load_cases) * face_valid[:, None, None]
    energy_z = slab_energy(displace, 2, 1, load_cases)
    energy_y = slab_energy(displace, 3, 2, load_cases)
    sens_term = 0.5 * (
        energy_x[:-1]
        + energy_x[1:]
        + pad_axis(energy_z, 1, 1, 0)
        + pad_axis(energy_z, 1, 0, 1)
        + pad_axis(energy_y, 2, 1, 0)
        + pad_axis(energy_y, 2, 0, 1)
    )
    sensitive = sens_term
    for level in reversed(range(level_count)):
        half_rows = sensitive.shape[0] // 2
        upper_side = load_place // 2**level % 2 == 1
        outgoing = jnp.where(upper_side, sensitive[:half_rows], sensitive[half_rows:])
        keeping = jnp.where(upper_side, sensitive[half_rows:], sensitive[:half_rows])
        sensitive = keeping + from_partner(outgoing, "space", level)
    weighted_share = 3.0 * (1.0 - floor_modulus) * filtered**2 * sensitive / total_weight
    halo_share = extended(weighted_share, (("space", 0),), window_reach)
    root_term = jnp.sqrt(filter_backward(pad_sides(halo_share), padded_weights))
    lowest = jnp.maximum(density - move_limit, density_floor)
    highest = jnp.minimum(density + move_limit, 1.0)
    design_now = density

    def trial_design(log_level):
        return jnp.clip(design_now * root_term * jnp.exp(-0.5 * log_level), lowest, highest)

    start_state = (jnp.asarray(log_lower, jnp.float32), jnp.asarray(log_span, jnp.float32))

    def halve(search_step, search_state):
        lower_end, span_width = search_state
        half_span = span_width * 0.5
        middle = lower_end + half_span
        volume_total = lax.psum(jnp.sum(trial_design(middle)), "space")
        return (jnp.where(volume_total > target, middle, lower_end), half_span)

    lower_end, span_width = lax.fori_loop(0, SEARCH, halve, start_state)
    density = trial_design(lower_end + 0.5 * span_width)
    new_displacement = displace[None]
    return (density, new_displacement)


def solution(mesh):
    in_specs = (
        P("space", "parts", None),
        P("space", None, None, "parts", None),
        P(None, "parts"),
        P("parts"),
        P("parts", None),
        P("parts"),
    )
    out_specs = (P("space", "parts", None), P("space", None, None, "parts", None))
    return jax.shard_map(local, mesh=mesh, in_specs=in_specs, out_specs=out_specs, check_vma=False)
```

profile of v0, /device:TPU:0, one launch (start us, length us, event | category | flops | bytes accessed | tf_op | source)
XLA Modules:
  0.0 452.5 jit_solution(8518269994883493975)
XLA Ops:
  0.6 1.3 collective-permute-start.1
  1.9 3.0 collective-permute-start
  5.1 0.6 copy-done.8
  5.8 0.7 copy-done.9
  6.5 0.6 fusion.520
  7.2 1.2 bitcast_multiply_fusion
  8.6 0.7 fusion.37
  9.3 0.5 fusion.169
  10.1 0.7 copy-done.2
  10.9 0.5 fusion.294
  11.4 23.8 %all_gather.3 = f32[32,16,128]{2,1,0:T(8,128)S(1)} all-gather(f32[2,16,128]{2,1,0:T(8,128)S(1)} %fusion.294), channel_id=1, replica_groups=mesh['parts'=2,'space'=16] {'space'}, dimensions={0}, use_global_device_ids=true | all-gather | bytes 278528 | tf_op jit(solution)/shard_map/all_gather | solution.py:179
  35.7 0.5 copy-done.3
  36.4 0.5 copy-done.5
  36.9 0.3 multiply_multiply_fusion.5
  37.3 0.6 copy-done.4
  38.0 1.0 copy-done.1
  39.0 0.7 fusion.6
  39.9 0.3 multiply_multiply_fusion.4
  40.3 0.7 fusion.10
  41.2 0.3 multiply_multiply_fusion.3
  41.6 0.7 fusion.14
  42.5 0.3 fusion.2
  42.8 0.4 copy-done
  43.8 7.6 %collective-permute-done.2 = f32[16,16,128]{2,1,0:T(8,128)S(1)} collective-permute-done((f32[16,16,128]{2,1,0:T(8,128)S(1)}, f32[16,16,128]{2,1,0:T(8,128)S(1)}, u32[]{:S(2)}, u32[]{:S(2)}) %collective-permute-start.2) | collective-permute-done | bytes 131104 | tf_op jit(solution)/shard_map/ppermute | solution.py:42
  51.6 4.2 collective-permute-done.3
  55.9 3.9 collective-permute-done.4
  59.9 1.2 collective-permute-done.5
  61.1 0.5 multiply_divide_fusion
  61.6 1.3 collective-permute-start.7
  62.9 3.0 collective-permute-start.6
  66.8 0.3 stack.32
  67.1 0.3 fusion.515
  67.4 0.5 fusion.496
  67.9 0.5 fusion.477
  68.5 0.5 fusion.458
  69.0 0.5 fusion.439
  69.5 0.5 fusion.420
  70.1 0.8 fusion.43
  70.9 380.9 %while.14 = (s32[]{:T(128)}, f32[]{:T(128)}, f32[]{:T(128)}, f32[2,16,128]{2,1,0:T(8,128)S(1)}, f32[2,16,128]{2,1,0:T(8,128)S(1)}, /*index=5*/f32[2,16,128]{2,1,...) while((s32[]{:T(128)}, f32[]{:T(128)}, f32[]{:T(128)}, f32[2,16,128]{2,1,0:T(8,128)S(1)}, ...), condition=%wide.region_8.9_spmd, body=%wide.region_5.8_spmd.sunk | while | flops 16391 | bytes 49335 | solution.py:234
  71.0 0.7 minimum_reduce_fusion.2
  71.7 31.6 %psum.10 = f32[]{:T(128)} all-reduce(f32[]{:T(128)} %minimum_reduce_fusion.2), channel_id=1, replica_groups=mesh['parts'=2,'space'=16] {'space'}, use_global_device_ids=true, to_apply=%region_7.7 | all-reduce | flops 1 | bytes 8 | tf_op jit(solution)/shard_map/while/body/eval_jaxpr/psum | solution.py:231
  104.0 0.7 minimum_reduce_fusion.2
  104.7 30.2 %psum.10 = f32[]{:T(128)} all-reduce(f32[]{:T(128)} %minimum_reduce_fusion.2), channel_id=1, replica_groups=mesh['parts'=2,'space'=16] {'space'}, use_global_device_ids=true, to_apply=%region_7.7 | all-reduce | flops 1 | bytes 8 | tf_op jit(solution)/shard_map/while/body/eval_jaxpr/psum | solution.py:231
  135.6 0.7 minimum_reduce_fusion.2
  136.3 30.2 %psum.10 = f32[]{:T(128)} all-reduce(f32[]{:T(128)} %minimum_reduce_fusion.2), channel_id=1, replica_groups=mesh['parts'=2,'space'=16] {'space'}, use_global_device_ids=true, to_apply=%region_7.7 | all-reduce | flops 1 | bytes 8 | tf_op jit(solution)/shard_map/while/body/eval_jaxpr/psum | solution.py:231
  167.3 0.7 minimum_reduce_fusion.2
  167.9 30.2 %psum.10 = f32[]{:T(128)} all-reduce(f32[]{:T(128)} %minimum_reduce_fusion.2), channel_id=1, replica_groups=mesh['parts'=2,'space'=16] {'space'}, use_global_device_ids=true, to_apply=%region_7.7 | all-reduce | flops 1 | bytes 8 | tf_op jit(solution)/shard_map/while/body/eval_jaxpr/psum | solution.py:231
  198.9 0.7 minimum_reduce_fusion.2
  199.6 30.2 %psum.10 = f32[]{:T(128)} all-reduce(f32[]{:T(128)} %minimum_reduce_fusion.2), channel_id=1, replica_groups=mesh['parts'=2,'space'=16] {'space'}, use_global_device_ids=true, to_apply=%region_7.7 | all-reduce | flops 1 | bytes 8 | tf_op jit(solution)/shard_map/while/body/eval_jaxpr/psum | solution.py:231
  230.5 0.7 minimum_reduce_fusion.2
  231.2 30.2 %psum.10 = f32[]{:T(128)} all-reduce(f32[]{:T(128)} %minimum_reduce_fusion.2), channel_id=1, replica_groups=mesh['parts'=2,'space'=16] {'space'}, use_global_device_ids=true, to_apply=%region_7.7 | all-reduce | flops 1 | bytes 8 | tf_op jit(solution)/shard_map/while/body/eval_jaxpr/psum | solution.py:231
  262.1 0.7 minimum_reduce_fusion.2
  262.8 30.2 %psum.10 = f32[]{:T(128)} all-reduce(f32[]{:T(128)} %minimum_reduce_fusion.2), channel_id=1, replica_groups=mesh['parts'=2,'space'=16] {'space'}, use_global_device_ids=true, to_apply=%region_7.7 | all-reduce | flops 1 | bytes 8 | tf_op jit(solution)/shard_map/while/body/eval_jaxpr/psum | solution.py:231
  293.8 0.7 minimum_reduce_fusion.2
  294.4 30.2 %psum.10 = f32[]{:T(128)} all-reduce(f32[]{:T(128)} %minimum_reduce_fusion.2), channel_id=1, replica_groups=mesh['parts'=2,'space'=16] {'space'}, use_global_device_ids=true, to_apply=%region_7.7 | all-reduce | flops 1 | bytes 8 | tf_op jit(solution)/shard_map/while/body/eval_jaxpr/psum | solution.py:231
  325.4 0.7 minimum_reduce_fusion.2
  326.1 30.2 %psum.10 = f32[]{:T(128)} all-reduce(f32[]{:T(128)} %minimum_reduce_fusion.2), channel_id=1, replica_groups=mesh['parts'=2,'space'=16] {'space'}, use_global_device_ids=true, to_apply=%region_7.7 | all-reduce | flops 1 | bytes 8 | tf_op jit(solution)/shard_map/while/body/eval_jaxpr/psum | solution.py:231
  357.0 0.7 minimum_reduce_fusion.2
  357.7 30.2 %psum.10 = f32[]{:T(128)} all-reduce(f32[]{:T(128)} %minimum_reduce_fusion.2), channel_id=1, replica_groups=mesh['parts'=2,'space'=16] {'space'}, use_global_device_ids=true, to_apply=%region_7.7 | all-reduce | flops 1 | bytes 8 | tf_op jit(solution)/shard_map/while/body/eval_jaxpr/psum | solution.py:231
  388.6 0.7 minimum_reduce_fusion.2
  389.3 30.2 %psum.10 = f32[]{:T(128)} all-reduce(f32[]{:T(128)} %minimum_reduce_fusion.2), channel_id=1, replica_groups=mesh['parts'=2,'space'=16] {'space'}, use_global_device_ids=true, to_apply=%region_7.7 | all-reduce | flops 1 | bytes 8 | tf_op jit(solution)/shard_map/while/body/eval_jaxpr/psum | solution.py:231
  420.3 0.7 minimum_reduce_fusion.2
  421.0 30.2 %psum.10 = f32[]{:T(128)} all-reduce(f32[]{:T(128)} %minimum_reduce_fusion.2), channel_id=1, replica_groups=mesh['parts'=2,'space'=16] {'space'}, use_global_device_ids=true, to_apply=%region_7.7 | all-reduce | flops 1 | bytes 8 | tf_op jit(solution)/shard_map/while/body/eval_jaxpr/psum | solution.py:231
  451.9 0.6 maximum_minimum_fusion
  (70 shorter events, 4.2 us)
Async XLA Ops:
  0.6 4.4 copy-start.6
  0.6 9.5 %collective-permute-start.1 = (f32[2,16,128]{2,1,0:T(8,128)}, f32[2,16,128]{2,1,0:T(8,128)S(1)}, u32[]{:S(2)}, u32[]{:S(2)}) collective-permute-start(f32[2,16,128]{2,1,0:T(8,128)} %param.23), channel_id=1, source_target_pairs={{1,0},{2,1},{3,2},{4,3},{5,4},{6,5},{7,6},{8,7},{9,8},{10,9},{11,1... | collective-permute-start | bytes 49160 | tf_op jit(solution)/shard_map/ppermute | solution.py:36
  1.9 8.2 %collective-permute-start = (f32[2,16,128]{2,1,0:T(8,128)}, f32[2,16,128]{2,1,0:T(8,128)S(1)}, u32[]{:S(2)}, u32[]{:S(2)}) collective-permute-start(f32[2,16,128]{2,1,0:T(8,128)} %param.23), channel_id=1, source_target_pairs={{0,1},{1,2},{2,3},{3,4},{4,5},{5,6},{6,7},{7,8},{8,9},{9,10},{10,1... | collective-permute-start | bytes 49160 | tf_op jit(solution)/shard_map/ppermute | solution.py:35
  5.0 0.7 copy-start.8
  5.8 0.7 copy-start.9
  9.3 0.7 copy-start.7
  10.1 0.7 copy-start.2
  35.6 0.7 copy-start.3
  36.2 0.7 copy-start.5
  37.2 0.7 copy-start.4
  37.9 1.1 copy-start.1
  42.3 0.9 copy-start
  43.7 7.7 %collective-permute-start.2 = (f32[16,16,128]{2,1,0:T(8,128)S(1)}, f32[16,16,128]{2,1,0:T(8,128)S(1)}, u32[]{:S(2)}, u32[]{:S(2)}) collective-permute-start(f32[16,16,128]{2,1,0:T(8,128)S(1)} %slice_select_fusion), channel_id=1, source_target_pairs={{0,8},{1,9},{2,10},{3,11},{4,12},{5,13},{6,14},{7,15},{8,0},{9,1},... | collective-permute-start | bytes 393224 | tf_op jit(solution)/shard_map/ppermute | solution.py:42
  51.5 4.3 collective-permute-start.3
  55.9 4.0 collective-permute-start.4
  59.9 1.2 collective-permute-start.5
  61.6 8.4 %collective-permute-start.7 = (f32[2,16,128]{2,1,0:T(8,128)S(1)}, f32[2,16,128]{2,1,0:T(8,128)S(1)}, u32[]{:S(2)}, u32[]{:S(2)}) collective-permute-start(f32[2,16,128]{2,1,0:T(8,128)S(1)} %multiply_divide_fusion), channel_id=1, source_target_pairs={{1,0},{2,1},{3,2},{4,3},{5,4},{6,5},{7,6},{8,7},{9,8},{10,9},{11,1... | collective-permute-start | bytes 49160 | tf_op jit(solution)/shard_map/ppermute | solution.py:36
  62.9 7.1 %collective-permute-start.6 = (f32[2,16,128]{2,1,0:T(8,128)S(1)}, f32[2,16,128]{2,1,0:T(8,128)S(1)}, u32[]{:S(2)}, u32[]{:S(2)}) collective-permute-start(f32[2,16,128]{2,1,0:T(8,128)S(1)} %multiply_divide_fusion), channel_id=1, source_target_pairs={{0,1},{1,2},{2,3},{3,4},{4,5},{5,6},{6,7},{7,8},{8,9},{9,10},{10,1... | collective-permute-start | bytes 49160 | tf_op jit(solution)/shard_map/ppermute | solution.py:35
where the time goes:
time: 453 us
  blocking collectives  387 us (85%)
  other arithmetic  19.6 us (4%)
  waiting for transfers between devices  16.9 us (4%)
  local copies, waits for them, and re-layouts  9.21 us (2%)
  loops' own time  9.14 us (2%)
  starting transfers between devices  8.93 us (2%)
    psum x12, blocking collectives, halve(): volume_total = lax.psum(jnp.sum(trial_design(middle)), 'space')  364 us
    all_gather x1, blocking collectives, local(): whole_field = lax.all_gather(filtered, 'space', axis=0, tiled=True)  23.8 us
    ppermute x4, waiting for transfers between devices, from_partner(): lax.ppermute(x, axis, [(i, i ^ 1 << bit) for i in range(lax.axis_size(axi...  16.9 us
    another operation x1, loops' own time, local(): lower_end, span_width = lax.fori_loop(0, SEARCH, halve, start_state)  9.14 us
  transfers between devices with their start and end apart: 8, of which 4 were waited for; matrix products, arithmetic and copies ran while one was open for 2% of the time, Pallas kernels for 0%

commit v1 on v0

--- a/solution.py
+++ b/solution.py
@@ -3,6 +3,8 @@
 import jax
 import jax.numpy as jnp
 from jax import lax
+from jax.experimental import pallas as pl
+from jax.experimental.pallas import tpu as pltpu
 from jax.sharding import PartitionSpec as P
 
 SWEEPS = 3
@@ -17,6 +19,405 @@
 log_lower = -16.0
 log_span = 32.0
 window_reach = 2
+
+PLANE_SQUARES = (0, 1, 2, 4, 5, 8)
+ALL_SQUARES = (0, 1, 2, 3, 4, 5, 6, 8, 9, 12)
+
+
+def spot_iota(shape, dim):
+    return lax.broadcasted_iota(jnp.int32, shape, dim)
+
+
+def layer_radius(radius_ref, layers, row_width):
+    z = spot_iota((layers, row_width), 0)
+    result = jnp.zeros((layers, row_width), jnp.int32)
+    for layer in range(layers):
+        result = jnp.where(z == layer, radius_ref[layer], result)
+    return result.astype(jnp.float32)
+
+
+def class_weights(radius_ref, weight_ref):
+    layers, row_width = weight_ref.shape[1:]
+    radial = layer_radius(radius_ref, layers, row_width)
+    for place, square in enumerate(ALL_SQUARES):
+        weight_ref[place] = jnp.maximum(radial - math.sqrt(square), 0.0)
+
+
+def shift_sum(field, dim, distance):
+    size = field.shape[dim]
+    spot = spot_iota(field.shape, dim)
+    ahead = jnp.where(spot < size - distance, pltpu.roll(field, size - distance, dim), 0.0)
+    behind = jnp.where(spot >= distance, pltpu.roll(field, distance, dim), 0.0)
+    return ahead + behind
+
+
+def plane_sums(plane):
+    beside = shift_sum(plane, 1, 1)
+    further = shift_sum(plane, 1, 2)
+    return {
+        0: plane,
+        1: beside + shift_sum(plane, 0, 1),
+        2: shift_sum(beside, 0, 1),
+        4: further + shift_sum(plane, 0, 2),
+        5: shift_sum(further, 0, 1) + shift_sum(beside, 0, 2),
+        8: shift_sum(further, 0, 2),
+    }
+
+
+def weigh(sums, weight_ref, square):
+    result = None
+    for inner in PLANE_SQUARES:
+        term = weight_ref[ALL_SQUARES.index(inner + square)] * sums[inner]
+        result = term if result is None else result + term
+    return result
+
+
+def forward_planes(plane, weight_ref):
+    sums = plane_sums(plane)
+    return [weigh(sums, weight_ref, square) for square in (0, 1, 4)]
+
+
+def backward_planes(plane, weight_ref):
+    beside = shift_sum(plane, 1, 1)
+    further = shift_sum(plane, 1, 2)
+    results = []
+    for square in (0, 1, 4):
+
+        def weight(more):
+            return weight_ref[ALL_SQUARES.index(square + more)]
+
+        level = weight(0) * plane + weight(1) * beside + weight(4) * further
+        near = weight(1) * plane + weight(2) * beside + weight(5) * further
+        far = weight(4) * plane + weight(5) * beside + weight(8) * further
+        results.append(level + shift_sum(near, 0, 1) + shift_sum(far, 0, 2))
+    return results
+
+
+def edge_class(x, planes):
+    return jnp.minimum(x, 2) + jnp.maximum(x - (planes - 3), 0)
+
+
+def zero_edges(ref):
+    planes = ref.shape[0]
+    for place in (0, 1, planes - 2, planes - 1):
+        ref[place] = jnp.zeros(ref.shape[1:], ref.dtype)
+
+
+def sweep_kernel(
+    radius_ref,
+    index_ref,
+    force_ref,
+    density_ref,
+    fixed_ref,
+    start_ref,
+    disp_ref,
+    sens_ref,
+    coef_ref,
+    weight_ref,
+    total_ref,
+    near_ref,
+    side_ref,
+    far_ref,
+    modulus_ref,
+    across_ref,
+    up_ref,
+    down_ref,
+    right_ref,
+    left_ref,
+    rate_ref,
+    keep_ref,
+    first_ref,
+    second_ref,
+):
+    planes, layers, row_width = density_ref.shape
+    load_cases = index_ref.shape[0]
+    load_place = lax.axis_index("space")
+    shape = (layers, row_width)
+    z = spot_iota(shape, 0)
+    y = spot_iota(shape, 1)
+    zero = jnp.zeros(shape, jnp.float32)
+
+    class_weights(radius_ref, weight_ref)
+    for ref in (side_ref, far_ref):
+        zero_edges(ref)
+
+    ones = forward_planes(jnp.ones(shape, jnp.float32), weight_ref)
+    for place, (lower, upper) in enumerate(((0, 2), (1, 2), (2, 2), (2, 1), (2, 0))):
+        total_ref[place] = (
+            ones[0] + min(lower, 1) * ones[1] + min(upper, 1) * ones[1]
+            + (lower // 2) * ones[2] + (upper // 2) * ones[2]
+        )
+
+    def filter_plane(x, carry):
+        near, side, far = forward_planes(density_ref[x], weight_ref)
+        near_ref[x + 2] = near
+        side_ref[x + 2] = side
+        far_ref[x + 2] = far
+        return carry
+
+    lax.fori_loop(0, planes, filter_plane, 0, unroll=2)
+
+    def modulus_plane(x, carry):
+        total = total_ref[edge_class(x, planes)]
+        filtered = (
+            near_ref[x + 2]
+            + side_ref[x + 1]
+            + side_ref[x + 3]
+            + far_ref[x]
+            + far_ref[x + 4]
+        ) / total
+        modulus = floor_modulus + (1.0 - floor_modulus) * (filtered * filtered * filtered)
+        modulus_ref[x] = modulus
+        coef_ref[x] = 3.0 * (1.0 - floor_modulus) * (filtered * filtered) / total
+        return carry
+
+    lax.fori_loop(0, planes, modulus_plane, 0, unroll=2)
+
+    across_ref[0] = zero
+    across_ref[planes] = zero
+    first_ref[:, 0] = jnp.zeros((3,) + shape, jnp.float32)
+    second_ref[:, 0] = jnp.zeros((3,) + shape, jnp.float32)
+    first_ref[:, planes + 1] = jnp.zeros((3,) + shape, jnp.float32)
+    second_ref[:, planes + 1] = jnp.zeros((3,) + shape, jnp.float32)
+
+    def face_plane(x, carry):
+        modulus = modulus_ref[x]
+        later = modulus_ref[jnp.minimum(x + 1, planes - 1)]
+        ahead = jnp.where(x + 1 < planes, 0.5 * (modulus + later), 0.0)
+        across_ref[x + 1] = ahead
+        up = jnp.where(z < layers - 1, 0.5 * (modulus + pltpu.roll(modulus, layers - 1, 0)), 0.0)
+        down = pltpu.roll(up, 1, 0)
+        right = jnp.where(
+            y < row_width - 1, 0.5 * (modulus + pltpu.roll(modulus, row_width - 1, 1)), 0.0
+        )
+        left = pltpu.roll(right, 1, 1)
+        up_ref[x] = up
+        down_ref[x] = down
+        right_ref[x] = right
+        left_ref[x] = left
+        free = jnp.where(z == 0, 1.0 - fixed_ref[pl.ds(x, 1), :].astype(jnp.float32), 1.0)
+        keep_ref[x] = (1.0 - relax_factor) * free
+        sums = (carry + ahead, up + down, left + right)
+        every = sums[0] + sums[1] + sums[2]
+        push = relax_factor * free
+        for part in range(3):
+            rate_ref[part, x] = push / (every + sums[part])
+            first_ref[part, x + 1] = start_ref[part, x] * free
+        return ahead
+
+    lax.fori_loop(0, planes, face_plane, zero, unroll=2)
+
+    own_index = index_ref[load_place]
+    own_x = own_index // (layers * row_width)
+    own_z = own_index // row_width % layers
+    own_y = own_index % row_width
+    hit = (z == own_z) & (y == own_y)
+
+    def sweep(source, target, lead):
+        def sweep_plane(x, carry):
+            before, after = across_ref[x], across_ref[x + 1]
+            up, down, right, left = up_ref[x], down_ref[x], right_ref[x], left_ref[x]
+            keep = keep_ref[x]
+            for part in range(3):
+                here = source[part, x + 1]
+                pulls = [
+                    before * source[part, x] + after * source[part, x + 2],
+                    up * pltpu.roll(here, layers - 1, 0) + down * pltpu.roll(here, 1, 0),
+                    right * pltpu.roll(here, row_width - 1, 1) + left * pltpu.roll(here, 1, 1),
+                ]
+                pull = pulls[0] + pulls[1] + pulls[2] + pulls[part]
+                target[part, x + lead] = keep * here + rate_ref[part, x] * pull
+            return carry
+
+        lax.fori_loop(0, planes, sweep_plane, 0, unroll=2)
+        for part in range(3):
+            push = rate_ref[part, own_x] * force_ref[load_place, part]
+            target[part, own_x + lead] += jnp.where(hit, push, 0.0)
+
+    stages = [first_ref, second_ref]
+    for turn in range(SWEEPS - 1):
+        sweep(stages[turn % 2], stages[(turn + 1) % 2], 1)
+    sweep(stages[(SWEEPS - 1) % 2], disp_ref, 0)
+
+    def energy_plane(x, carry):
+        later = jnp.minimum(x + 1, planes - 1)
+        ahead, upward, right = zero, zero, zero
+        for part in range(3):
+            here = disp_ref[part, x]
+            step = disp_ref[part, later] - here
+            climb = pltpu.roll(here, layers - 1, 0) - here
+            slide = pltpu.roll(here, row_width - 1, 1) - here
+            ahead = ahead + (2.0 if part == 0 else 1.0) * (step * step)
+            upward = upward + (2.0 if part == 1 else 1.0) * (climb * climb)
+            right = right + (2.0 if part == 2 else 1.0) * (slide * slide)
+        upward = jnp.where(z < layers - 1, upward, 0.0)
+        right = jnp.where(y < row_width - 1, right, 0.0)
+        total = carry + ahead + upward + pltpu.roll(upward, 1, 0) + right + pltpu.roll(right, 1, 1)
+        sens_ref[x] = (0.5 / load_cases) * total
+        return ahead
+
+    lax.fori_loop(0, planes, energy_plane, zero, unroll=2)
+
+
+def design_kernel(
+    radius_ref,
+    sens_ref,
+    coef_ref,
+    density_ref,
+    new_ref,
+    weight_ref,
+    near_ref,
+    side_ref,
+    far_ref,
+    pull_ref,
+    low_ref,
+    high_ref,
+):
+    planes, layers, row_width = density_ref.shape
+    own_planes = new_ref.shape[0]
+    place = lax.axis_index("space")
+    shape = (layers, row_width)
+    zero = jnp.zeros(shape, jnp.float32)
+    class_weights(radius_ref, weight_ref)
+    for ref in (side_ref, far_ref):
+        zero_edges(ref)
+
+    def filter_plane(x, carry):
+        near, side, far = backward_planes(sens_ref[x] * coef_ref[x], weight_ref)
+        near_ref[x + 2] = near
+        side_ref[x + 2] = side
+        far_ref[x + 2] = far
+        return carry
+
+    lax.fori_loop(0, planes, filter_plane, 0, unroll=2)
+
+    def root_plane(x, carry):
+        root = jnp.sqrt(
+            near_ref[x + 2] + side_ref[x + 1] + side_ref[x + 3] + far_ref[x] + far_ref[x + 4]
+        )
+        density = density_ref[x]
+        pull_ref[x] = density * root
+        low_ref[x] = jnp.maximum(density - move_limit, density_floor)
+        high_ref[x] = jnp.minimum(density + move_limit, 1.0)
+        return carry
+
+    lax.fori_loop(0, planes, root_plane, 0, unroll=2)
+
+    target = volume_share * planes * layers * row_width
+
+    def trial(x, factor):
+        return jnp.minimum(jnp.maximum(pull_ref[x] * factor, low_ref[x]), high_ref[x])
+
+    def halve(step, state):
+        lower, span = state
+        half = span * 0.5
+        middle = lower + half
+        factor = jnp.exp(-0.5 * middle)
+        total = lax.fori_loop(
+            0, planes, lambda x, acc: acc + trial(x, factor), zero, unroll=8
+        )
+        volume = jnp.sum(jnp.sum(total, axis=0, keepdims=True), axis=1, keepdims=True)
+        return jnp.where(volume > target, middle, lower), half
+
+    start = (jnp.full((1, 1), log_lower, jnp.float32), jnp.full((1, 1), log_span, jnp.float32))
+    lower, span = lax.fori_loop(0, SEARCH, halve, start)
+    factor = jnp.exp(-0.5 * (lower + 0.5 * span))
+    for own in range(own_planes):
+        new_ref[own] = trial(place * own_planes + own, factor)
+
+
+def in_vmem():
+    return pl.BlockSpec(memory_space=pltpu.VMEM)
+
+
+def in_smem():
+    return pl.BlockSpec(memory_space=pltpu.SMEM)
+
+
+KERNEL_VMEM = 24 * 2**20
+
+
+def sweep_call(radius, load_index, load_force, density, fixed, displacement):
+    planes, layers, row_width = density.shape
+    grid_field = (planes, layers, row_width)
+
+    def scratch(*lead):
+        return pltpu.VMEM(lead + (layers, row_width), jnp.float32)
+
+    return pl.pallas_call(
+        sweep_kernel,
+        out_shape=[
+            jax.ShapeDtypeStruct((3,) + grid_field, jnp.float32),
+            jax.ShapeDtypeStruct(grid_field, jnp.float32),
+            jax.ShapeDtypeStruct(grid_field, jnp.float32),
+        ],
+        in_specs=[in_smem()] * 3 + [in_vmem()] * 3,
+        out_specs=[in_vmem()] * 3,
+        scratch_shapes=[
+            scratch(len(ALL_SQUARES)),
+            scratch(2 * window_reach + 1),
+            scratch(planes + 4),
+            scratch(planes + 4),
+            scratch(planes + 4),
+            scratch(planes),
+            scratch(planes + 1),
+            scratch(planes),
+            scratch(planes),
+            scratch(planes),
+            scratch(planes),
+            scratch(3, planes),
+            scratch(planes),
+            scratch(3, planes + 2),
+            scratch(3, planes + 2),
+        ],
+        compiler_params=pltpu.CompilerParams(vmem_limit_bytes=KERNEL_VMEM),
+        name="sweeps",
+    )(radius, load_index, load_force, density, fixed, displacement)
+
+
+def design_call(radius, sens, coef, density, own_planes):
+    planes, layers, row_width = density.shape
+
+    def scratch(*lead):
+        return pltpu.VMEM(lead + (layers, row_width), jnp.float32)
+
+    return pl.pallas_call(
+        design_kernel,
+        out_shape=jax.ShapeDtypeStruct((own_planes, layers, row_width), jnp.float32),
+        in_specs=[in_smem()] + [in_vmem()] * 3,
+        out_specs=in_vmem(),
+        scratch_shapes=[
+            scratch(len(ALL_SQUARES)),
+            scratch(planes + 4),
+            scratch(planes + 4),
+            scratch(planes + 4),
+            scratch(planes),
+            scratch(planes),
+            scratch(planes),
+        ],
+        compiler_params=pltpu.CompilerParams(vmem_limit_bytes=KERNEL_VMEM),
+        name="design",
+    )(radius, sens, coef, density)
+
+
+def gathered(block):
+    return lax.all_gather(block, "space", axis=0, tiled=True)
+
+
+def scattered_sum(field):
+    devices = lax.axis_size("space")
+    pieces = field.reshape((devices, field.shape[0] // devices) + field.shape[1:])
+    return jnp.sum(lax.all_to_all(pieces, "space", 0, 0), axis=0)
+
+
+def one_slab(density, displacement, fixed, load_index, load_force, radius):
+    whole = gathered(density)
+    new_displacement, sens, coef = sweep_call(
+        radius, load_index, load_force, whole, fixed, displacement[0]
+    )
+    sens = gathered(scattered_sum(sens))
+    new_density = design_call(radius, sens, coef, whole, density.shape[0])
+    return new_density, new_displacement[None]
 
 
 def from_behind(block, axis, distance):
@@ -133,7 +534,7 @@
     return jnp.concatenate([below, displace, above], axis=1)
 
 
-def local(density, displacement, fixed, load_index, load_force, radius):
+def many_slabs(density, displacement, fixed, load_index, load_force, radius):
     slab_rows, layers, row_width = density.shape
     load_cases = load_index.shape[0]
     level_count = load_cases.bit_length() - 1
@@ -247,4 +648,10 @@
         P("parts"),
     )
     out_specs = (P("space", "parts", None), P("space", None, None, "parts", None))
+
+    def local(density, displacement, fixed, load_index, load_force, radius):
+        alone = lax.axis_size("space") == load_index.shape[0]
+        run = one_slab if alone else many_slabs
+        return run(density, displacement, fixed, load_index, load_force, radius)
+
     return jax.shard_map(local, mesh=mesh, in_specs=in_specs, out_specs=out_specs, check_vma=False)

time: 453 us -> 78.1 us (0.17)
  blocking collectives: 387 us -> 56.2 us
  other arithmetic: 19.6 us -> 0.02 us
  Pallas kernels: 0 us -> 18.5 us
  waiting for transfers between devices: 16.9 us -> 0 us
  loops' own time: 9.14 us -> 0 us
  starting transfers between devices: 8.93 us -> 0 us
  local copies, waits for them, and re-layouts: 9.21 us -> 2.56 us
    psum x12 -> x0, blocking collectives: 364 us -> none  [halve(): volume_total = lax.psum(jnp.sum(trial_design(middle)), 'space')]
    all_gather x1 -> x2, blocking collectives: 23.8 us -> 43.5 us  [gathered(): return lax.all_gather(block, 'space', axis=0, tiled=True)]
    pallas_call x0 -> x2, Pallas kernels: none -> 18.5 us  [the longest x1 13.4 us: sweep_call(): pl.pallas_call(sweep_kernel, out_shape=[jax.ShapeDtypeStruct((3,) + grid_...]
    ppermute x8 -> x0, waiting for transfers between devices: 16.9 us -> none  [the longest x4 16.9 us: from_partner(): lax.ppermute(x, axis, [(i, i ^ 1 << bit) for i in range(lax.axis_size(axi...]
    all_to_all x0 -> x1, blocking collectives: none -> 12.6 us  [scattered_sum(): return jnp.sum(lax.all_to_all(pieces, 'space', 0, 0), axis=0)]
    reduce_sum x17 -> x1, other arithmetic: 9.58 us -> 0.02 us  [scattered_sum(): return jnp.sum(lax.all_to_all(pieces, 'space', 0, 0), axis=0)]
    another operation x1 -> x0, loops' own time: 9.14 us -> none  [local(): lower_end, span_width = lax.fori_loop(0, SEARCH, halve, start_state)]
    ppermute x8 -> x0, starting transfers between devices: 8.93 us -> none  [the longest x2 6.07 us: extended(): before = lax.ppermute(last, axis, up)]
  transfers between devices with their start and end apart: 8 -> 0, of which waited for: 4 -> 0; matrix products, arithmetic and copies ran while one was open for 2% -> 0% of each run, Pallas kernels for 0% -> 0%
where the time goes in v1:
time: 78.1 us; the launch traced here: 77.8 us
  blocking collectives  56.2 us (72%)
  Pallas kernels  18.5 us (24%)
  local copies, waits for them, and re-layouts  2.56 us (3%)
    all_gather x2, blocking collectives, gathered(): return lax.all_gather(block, 'space', axis=0, tiled=True)  43.5 us
    pallas_call x1, Pallas kernels, sweep_call(): pl.pallas_call(sweep_kernel, out_shape=[jax.ShapeDtypeStruct((3,) + grid_...  13.4 us
    all_to_all x1, blocking collectives, scattered_sum(): return jnp.sum(lax.all_to_all(pieces, 'space', 0, 0), axis=0)  12.6 us
    pallas_call x1, Pallas kernels, design_call(): pl.pallas_call(design_kernel, out_shape=jax.ShapeDtypeStruct((own_planes,...  5.07 us
    unnamed x9, local copies, waits for them, and re-layouts  2.56 us

profile of v1, /device:TPU:0, one launch (start us, length us, event | category | flops | bytes accessed | tf_op | source)
XLA Modules:
  0.0 77.8 jit_solution(1900160061992244090)
XLA Ops:
  0.6 0.8 copy.9.force_ref
  1.4 0.0 copy-start.1
  1.4 24.1 %all_gather.6.density_ref = f32[32,16,128]{2,1,0:T(8,128)S(1)} all-gather(f32[2,16,128]{2,1,0:T(8,128)} %param.6), channel_id=1, replica_groups=mesh['parts'=2,'space'=16] {'space'}, dimensions={0}, use_global_device_ids=true | all-gather | bytes 278528 | tf_op jit(solution)/shard_map/all_gather | solution.py:404
  25.5 0.0 copy-start.2
  25.5 0.0 copy-start.3
  25.5 0.0 copy-done.1
  25.5 0.6 copy-done.2
  26.2 0.0 copy-done.3
  26.2 0.0 copy-start
  26.2 1.1 %copy-done = f32[1,3,32,16,128]{4,3,2,1,0:T(8,128)S(1)} copy-done((f32[1,3,32,16,128]{4,3,2,1,0:T(8,128)S(1)}, f32[1,3,32,16,128]{4,3,2,1,0:T(8,128)}, u32[]{:S(2)}) %copy-start) | copy-done | bytes 786456
  27.3 13.4 %sweeps.1 = (f32[3,32,16,128]{3,2,1,0:T(8,128)}, f32[32,16,128]{2,1,0:T(8,128)S(1)}, f32[32,16,128]{2,1,0:T(8,128)S(1)}) custom-call(s32[16]{0:T(128)S(1)} %copy-done.2, s32[16]{0:T(128)S(1)} %copy-done.3, f32[16,3]{1,0:T(8,128)S(1)} %copy.9.force_ref, f32[32,16,128]{2,1,0:T(8,128)S(1)} %all_gather.6.density_ref, s32[32,128]{1,0:T(8,128)S(1)} %copy-done.1, ...), custom_call_target="tpu_custom_call" | custom-call | tf_op jit(solution)/shard_map/sweeps/pallas_call | solution.py:347
  40.7 12.6 %all_to_all.5 = f32[16,2,16,128]{3,2,1,0:T(8,128)S(1)} all-to-all(f32[16,2,16,128]{3,2,1,0:T(8,128)S(1)} %bitcast.4), channel_id=1, replica_groups=mesh['parts'=2,'space'=16] {'space'}, dimensions={0} | all-to-all | bytes 524288 | tf_op jit(solution)/shard_map/all_to_all | solution.py:410
  53.4 19.4 %all_gather.7.sens_ref = f32[32,16,128]{2,1,0:T(8,128)S(1)} all-gather(f32[2,16,128]{2,1,0:T(8,128)S(1)} %reduce_sum.9), channel_id=1, replica_groups=mesh['parts'=2,'space'=16] {'space'}, dimensions={0}, use_global_device_ids=true | all-gather | bytes 278528 | tf_op jit(solution)/shard_map/all_gather | solution.py:404
  72.8 5.1 %design.1 = f32[2,16,128]{2,1,0:T(8,128)} custom-call(s32[16]{0:T(128)S(1)} %copy-done.2, f32[32,16,128]{2,1,0:T(8,128)S(1)} %all_gather.7.sens_ref, f32[32,16,128]{2,1,0:T(8,128)S(1)} %get-tuple-element.6.coef_ref, f32[32,16,128]{2,1,0:T(8,128)S(1)} %all_gather.6.density_ref), custom_call_target="tpu_custom_call" | custom-call | tf_op jit(solution)/shard_map/design/pallas_call | solution.py:384
  (1 shorter events, 0.0 us)
Async XLA Ops:
  1.4 24.1 %copy-start.1 = (s32[32,128]{1,0:T(8,128)S(1)}, s32[32,128]{1,0:T(8,128)}, u32[]{:S(2)}) copy-start(s32[32,128]{1,0:T(8,128)} %fixed_ref.1) | copy-start | bytes 49156
  25.5 0.7 copy-start.2
  25.5 0.7 copy-start.3
  26.2 1.1 %copy-start = (f32[1,3,32,16,128]{4,3,2,1,0:T(8,128)S(1)}, f32[1,3,32,16,128]{4,3,2,1,0:T(8,128)}, u32[]{:S(2)}) copy-start(f32[1,3,32,16,128]{4,3,2,1,0:T(8,128)} %param.7) | copy-start | bytes 2359300

commit v2 on v1

--- a/solution.py
+++ b/solution.py
@@ -401,7 +401,10 @@
 
 
 def gathered(block):
-    return lax.all_gather(block, "space", axis=0, tiled=True)
+    devices = lax.axis_size("space")
+    copies = jnp.broadcast_to(block[None], (devices,) + block.shape)
+    blocks = lax.all_to_all(copies, "space", 0, 0)
+    return blocks.reshape((devices * block.shape[0],) + block.shape[1:])
 
 
 def scattered_sum(field):

time: 78.1 us -> 65 us (0.83)
  blocking collectives: 56.2 us -> 25.6 us
  waiting for transfers between devices: 0 us -> 9.95 us
  starting transfers between devices: 0 us -> 7.49 us
    all_gather x2 -> x0, blocking collectives: 43.5 us -> none  [gathered(): return lax.all_gather(block, 'space', axis=0, tiled=True)]
    all_to_all x0 -> x1, blocking collectives: none -> 12.8 us  [gathered(): blocks = lax.all_to_all(copies, 'space', 0, 0)]
    all_to_all x0 -> x1, waiting for transfers between devices: none -> 9.95 us  [gathered(): blocks = lax.all_to_all(copies, 'space', 0, 0)]
    all_to_all x0 -> x1, starting transfers between devices: none -> 7.49 us  [gathered(): blocks = lax.all_to_all(copies, 'space', 0, 0)]
    unnamed x9 -> x11, local copies, waits for them, and re-layouts: 2.56 us -> 0.76 us
    broadcast_in_dim x0 -> x2, local copies, waits for them, and re-layouts: none -> 1.54 us  [gathered(): copies = jnp.broadcast_to(block[None], (devices,) + block.shape)]
  transfers between devices with their start and end apart: 0 -> 1, of which waited for: 0 -> 1; matrix products, arithmetic and copies ran while one was open for 0% -> 0% of each run, Pallas kernels for 0% -> 0%
where the time goes in v2:
time: 65 us; the launch traced here: 64.5 us
  blocking collectives  25.6 us (39%)
  Pallas kernels  18.5 us (28%)
  waiting for transfers between devices  9.95 us (15%)
  starting transfers between devices  7.49 us (12%)
  local copies, waits for them, and re-layouts  2.3 us (4%)
  between operations  0.68 us (1%)
    pallas_call x1, Pallas kernels, sweep_call(): pl.pallas_call(sweep_kernel, out_shape=[jax.ShapeDtypeStruct((3,) + grid_...  13.4 us
    all_to_all x1, blocking collectives, gathered(): blocks = lax.all_to_all(copies, 'space', 0, 0)  12.8 us
    all_to_all x1, blocking collectives, scattered_sum(): return jnp.sum(lax.all_to_all(pieces, 'space', 0, 0), axis=0)  12.8 us
    all_to_all x1, waiting for transfers between devices, gathered(): blocks = lax.all_to_all(copies, 'space', 0, 0)  9.95 us
    all_to_all x1, starting transfers between devices, gathered(): blocks = lax.all_to_all(copies, 'space', 0, 0)  7.49 us
    pallas_call x1, Pallas kernels, design_call(): pl.pallas_call(design_kernel, out_shape=jax.ShapeDtypeStruct((own_planes,...  5.07 us
    broadcast_in_dim x2, local copies, waits for them, and re-layouts, gathered(): copies = jnp.broadcast_to(block[None], (devices,) + block.shape)  1.54 us
  transfers between devices with their start and end apart: 1, of which 1 were waited for; matrix products, arithmetic and copies ran while one was open for 0% of the time, Pallas kernels for 0%

profile of v2, /device:TPU:0, one launch (start us, length us, event | category | flops | bytes accessed | tf_op | source)
XLA Modules:
  0.0 64.5 jit_solution(6705712917387333296)
XLA Ops:
  0.6 0.0 copy-start.4
  0.6 0.0 copy-start
  0.6 1.5 %broadcast_in_dim.6 = f32[16,2,16,128]{3,2,1,0:T(8,128)} broadcast(f32[2,16,128]{2,1,0:T(8,128)} %param.6), dimensions={1,2,3} | broadcast | bytes 278528 | tf_op jit(solution)/shard_map/broadcast_in_dim | solution.py:405
  2.2 0.0 copy-start.1
  2.2 7.5 %all-to-all-start = ((f32[16,2,16,128]{3,2,1,0:T(8,128)}), f32[16,2,16,128]{3,2,1,0:T(8,128)S(1)}, u32[]{:S(2)}, u32[]{:S(2)}) async-start(f32[16,2,16,128]{3,2,1,0:T(8,128)} %broadcast_in_dim.6), calls=%async_computation | async-start | bytes 524288 | tf_op jit(solution)/shard_map/all_to_all | solution.py:406
  9.7 0.0 copy-done.4
  9.7 0.1 copy.8.force_ref
  9.8 10.0 %all-to-all-done = f32[16,2,16,128]{3,2,1,0:T(8,128)S(1)} async-done(((f32[16,2,16,128]{3,2,1,0:T(8,128)}), f32[16,2,16,128]{3,2,1,0:T(8,128)S(1)}, u32[]{:S(2)}, u32[]{:S(2)}) %all-to-all-start) | async-done | bytes 262176 | tf_op jit(solution)/shard_map/all_to_all | solution.py:406
  19.7 0.0 copy-start.2
  19.7 0.0 copy-start.3
  19.7 0.0 copy-done
  19.7 0.0 copy-done.1
  19.7 0.6 copy-done.2
  20.4 0.0 copy-done.3
  20.4 13.4 %sweeps.1 = (f32[3,32,16,128]{3,2,1,0:T(8,128)}, f32[32,16,128]{2,1,0:T(8,128)S(1)}, f32[32,16,128]{2,1,0:T(8,128)S(1)}) custom-call(s32[16]{0:T(128)S(1)} %copy-done.2, s32[16]{0:T(128)S(1)} %copy-done.3, f32[16,3]{1,0:T(8,128)S(1)} %copy.8.force_ref, f32[32,16,128]{2,1,0:T(8,128)S(1)} %bitcast.5, s32[32,128]{1,0:T(8,128)S(1)} %copy-done.1, ...), custom_call_target="tpu_custom_call" | custom-call | tf_op jit(solution)/shard_map/sweeps/pallas_call | solution.py:347
  33.8 12.8 %all_to_all.15 = f32[16,2,16,128]{3,2,1,0:T(8,128)S(1)} all-to-all(f32[16,2,16,128]{3,2,1,0:T(8,128)S(1)} %bitcast.9), channel_id=1, replica_groups=mesh['parts'=2,'space'=16] {'space'}, dimensions={0} | all-to-all | bytes 524288 | tf_op jit(solution)/shard_map/all_to_all | solution.py:413
  46.6 12.8 %all_to_all.16 = f32[16,2,16,128]{3,2,1,0:T(8,128)S(1)} all-to-all(f32[16,2,16,128]{3,2,1,0:T(8,128)S(1)} %broadcast_in_dim.7), channel_id=1, replica_groups=mesh['parts'=2,'space'=16] {'space'}, dimensions={0} | all-to-all | bytes 524288 | tf_op jit(solution)/shard_map/all_to_all | solution.py:406
  59.5 5.1 %design.1 = f32[2,16,128]{2,1,0:T(8,128)} custom-call(s32[16]{0:T(128)S(1)} %copy-done.2, f32[32,16,128]{2,1,0:T(8,128)S(1)} %bitcast.7, f32[32,16,128]{2,1,0:T(8,128)S(1)} %get-tuple-element.6.coef_ref, f32[32,16,128]{2,1,0:T(8,128)S(1)} %bitcast.6), custom_call_target="tpu_custom_call" | custom-call | tf_op jit(solution)/shard_map/design/pallas_call | solution.py:384
  (2 shorter events, 0.0 us)
Async XLA Ops:
  0.6 9.0 %copy-start.4 = (f32[16,3]{0,1:T(4,128)S(1)}, f32[16,3]{0,1:T(4,128)}, u32[]{:S(2)}) copy-start(f32[16,3]{0,1:T(4,128)} %param.10) | copy-start | bytes 580
  0.6 19.1 %copy-start = (f32[1,3,32,16,128]{4,3,2,1,0:T(8,128)S(1)}, f32[1,3,32,16,128]{4,3,2,1,0:T(8,128)}, u32[]{:S(2)}) copy-start(f32[1,3,32,16,128]{4,3,2,1,0:T(8,128)} %param.7) | copy-start | bytes 2359300
  2.2 17.6 %copy-start.1 = (s32[32,128]{1,0:T(8,128)S(1)}, s32[32,128]{1,0:T(8,128)}, u32[]{:S(2)}) copy-start(s32[32,128]{1,0:T(8,128)} %fixed_ref.1) | copy-start | bytes 49156
  2.2 17.5 %all-to-all-start = ((f32[16,2,16,128]{3,2,1,0:T(8,128)}), f32[16,2,16,128]{3,2,1,0:T(8,128)S(1)}, u32[]{:S(2)}, u32[]{:S(2)}) async-start(f32[16,2,16,128]{3,2,1,0:T(8,128)} %broadcast_in_dim.6), calls=%async_computation | async-start | bytes 524288 | tf_op jit(solution)/shard_map/all_to_all | solution.py:406
  19.7 0.7 %copy-start.2 = (s32[16]{0:T(128)S(1)}, s32[16]{0:T(128)}, u32[]{:S(2)}) copy-start(s32[16]{0:T(128)} %radius_ref.3) | copy-start | bytes 196
  19.7 0.7 %copy-start.3 = (s32[16]{0:T(128)S(1)}, s32[16]{0:T(128)}, u32[]{:S(2)}) copy-start(s32[16]{0:T(128)} %index_ref.1) | copy-start | bytes 196

commit v3 on v2

--- a/solution.py
+++ b/solution.py
@@ -155,7 +155,7 @@
         far_ref[x + 2] = far
         return carry
 
-    lax.fori_loop(0, planes, filter_plane, 0, unroll=2)
+    lax.fori_loop(0, planes, filter_plane, 0, unroll=8)
 
     def modulus_plane(x, carry):
         total = total_ref[edge_class(x, planes)]
@@ -171,7 +171,7 @@
         coef_ref[x] = 3.0 * (1.0 - floor_modulus) * (filtered * filtered) / total
         return carry
 
-    lax.fori_loop(0, planes, modulus_plane, 0, unroll=2)
+    lax.fori_loop(0, planes, modulus_plane, 0, unroll=8)
 
     across_ref[0] = zero
     across_ref[planes] = zero
@@ -205,7 +205,7 @@
             first_ref[part, x + 1] = start_ref[part, x] * free
         return ahead
 
-    lax.fori_loop(0, planes, face_plane, zero, unroll=2)
+    lax.fori_loop(0, planes, face_plane, zero, unroll=8)
 
     own_index = index_ref[load_place]
     own_x = own_index // (layers * row_width)
@@ -229,7 +229,7 @@
                 target[part, x + lead] = keep * here + rate_ref[part, x] * pull
             return carry
 
-        lax.fori_loop(0, planes, sweep_plane, 0, unroll=2)
+        lax.fori_loop(0, planes, sweep_plane, 0, unroll=8)
         for part in range(3):
             push = rate_ref[part, own_x] * force_ref[load_place, part]
             target[part, own_x + lead] += jnp.where(hit, push, 0.0)
@@ -256,7 +256,7 @@
         sens_ref[x] = (0.5 / load_cases) * total
         return ahead
 
-    lax.fori_loop(0, planes, energy_plane, zero, unroll=2)
+    lax.fori_loop(0, planes, energy_plane, zero, unroll=8)
 
 
 def design_kernel(
@@ -289,7 +289,7 @@
         far_ref[x + 2] = far
         return carry
 
-    lax.fori_loop(0, planes, filter_plane, 0, unroll=2)
+    lax.fori_loop(0, planes, filter_plane, 0, unroll=8)
 
     def root_plane(x, carry):
         root = jnp.sqrt(
@@ -301,7 +301,7 @@
         high_ref[x] = jnp.minimum(density + move_limit, 1.0)
         return carry
 
-    lax.fori_loop(0, planes, root_plane, 0, unroll=2)
+    lax.fori_loop(0, planes, root_plane, 0, unroll=8)
 
     target = volume_share * planes * layers * row_width
 

time: 65 us -> 56.9 us (0.88)
  Pallas kernels: 18.5 us -> 10.4 us
    pallas_call x1, Pallas kernels: 13.4 us -> 6.31 us  [sweep_call(): pl.pallas_call(sweep_kernel, out_shape=[jax.ShapeDtypeStruct((3,) + grid_...]
    pallas_call x1, Pallas kernels: 5.07 us -> 4.07 us  [design_call(): pl.pallas_call(design_kernel, out_shape=jax.ShapeDtypeStruct((own_planes,...]
where the time goes in v3:
time: 56.9 us; the launch traced here: 56.5 us
  blocking collectives  25.6 us (45%)
  Pallas kernels  10.4 us (18%)
  waiting for transfers between devices  9.95 us (17%)
  starting transfers between devices  7.49 us (13%)
  local copies, waits for them, and re-layouts  2.3 us (4%)
  between operations  0.68 us (1%)
    all_to_all x1, blocking collectives, gathered(): blocks = lax.all_to_all(copies, 'space', 0, 0)  12.8 us
    all_to_all x1, blocking collectives, scattered_sum(): return jnp.sum(lax.all_to_all(pieces, 'space', 0, 0), axis=0)  12.8 us
    all_to_all x1, waiting for transfers between devices, gathered(): blocks = lax.all_to_all(copies, 'space', 0, 0)  9.95 us
    all_to_all x1, starting transfers between devices, gathered(): blocks = lax.all_to_all(copies, 'space', 0, 0)  7.49 us
    pallas_call x1, Pallas kernels, sweep_call(): pl.pallas_call(sweep_kernel, out_shape=[jax.ShapeDtypeStruct((3,) + grid_...  6.31 us
    pallas_call x1, Pallas kernels, design_call(): pl.pallas_call(design_kernel, out_shape=jax.ShapeDtypeStruct((own_planes,...  4.07 us
    broadcast_in_dim x2, local copies, waits for them, and re-layouts, gathered(): copies = jnp.broadcast_to(block[None], (devices,) + block.shape)  1.54 us
  transfers between devices with their start and end apart: 1, of which 1 were waited for; matrix products, arithmetic and copies ran while one was open for 0% of the time, Pallas kernels for 0%

profile of v3, /device:TPU:0, one launch (start us, length us, event | category | flops | bytes accessed | tf_op | source)
XLA Modules:
  0.0 56.5 jit_solution(10563715384112994651)
XLA Ops:
  0.6 0.0 copy-start.4
  0.6 0.0 copy-start
  0.6 1.5 %broadcast_in_dim.6 = f32[16,2,16,128]{3,2,1,0:T(8,128)} broadcast(f32[2,16,128]{2,1,0:T(8,128)} %param.6), dimensions={1,2,3} | broadcast | bytes 278528 | tf_op jit(solution)/shard_map/broadcast_in_dim | solution.py:405
  2.2 0.0 copy-start.1
  2.2 7.5 %all-to-all-start = ((f32[16,2,16,128]{3,2,1,0:T(8,128)}), f32[16,2,16,128]{3,2,1,0:T(8,128)S(1)}, u32[]{:S(2)}, u32[]{:S(2)}) async-start(f32[16,2,16,128]{3,2,1,0:T(8,128)} %broadcast_in_dim.6), calls=%async_computation | async-start | bytes 524288 | tf_op jit(solution)/shard_map/all_to_all | solution.py:406
  9.7 0.0 copy-done.4
  9.7 0.1 copy.8.force_ref
  9.8 10.0 %all-to-all-done = f32[16,2,16,128]{3,2,1,0:T(8,128)S(1)} async-done(((f32[16,2,16,128]{3,2,1,0:T(8,128)}), f32[16,2,16,128]{3,2,1,0:T(8,128)S(1)}, u32[]{:S(2)}, u32[]{:S(2)}) %all-to-all-start) | async-done | bytes 262176 | tf_op jit(solution)/shard_map/all_to_all | solution.py:406
  19.7 0.0 copy-start.2
  19.7 0.0 copy-start.3
  19.7 0.0 copy-done
  19.7 0.0 copy-done.1
  19.7 0.6 %copy-done.2 = s32[16]{0:T(128)S(1)} copy-done((s32[16]{0:T(128)S(1)}, s32[16]{0:T(128)}, u32[]{:S(2)}) %copy-start.2) | copy-done | bytes 88
  20.4 0.0 copy-done.3
  20.4 6.3 %sweeps.1 = (f32[3,32,16,128]{3,2,1,0:T(8,128)}, f32[32,16,128]{2,1,0:T(8,128)S(1)}, f32[32,16,128]{2,1,0:T(8,128)S(1)}) custom-call(s32[16]{0:T(128)S(1)} %copy-done.2, s32[16]{0:T(128)S(1)} %copy-done.3, f32[16,3]{1,0:T(8,128)S(1)} %copy.8.force_ref, f32[32,16,128]{2,1,0:T(8,128)S(1)} %bitcast.5, s32[32,128]{1,0:T(8,128)S(1)} %copy-done.1, ...), custom_call_target="tpu_custom_call" | custom-call | tf_op jit(solution)/shard_map/sweeps/pallas_call | solution.py:347
  26.7 12.8 %all_to_all.15 = f32[16,2,16,128]{3,2,1,0:T(8,128)S(1)} all-to-all(f32[16,2,16,128]{3,2,1,0:T(8,128)S(1)} %bitcast.9), channel_id=1, replica_groups=mesh['parts'=2,'space'=16] {'space'}, dimensions={0} | all-to-all | bytes 524288 | tf_op jit(solution)/shard_map/all_to_all | solution.py:413
  39.6 12.8 %all_to_all.16 = f32[16,2,16,128]{3,2,1,0:T(8,128)S(1)} all-to-all(f32[16,2,16,128]{3,2,1,0:T(8,128)S(1)} %broadcast_in_dim.7), channel_id=1, replica_groups=mesh['parts'=2,'space'=16] {'space'}, dimensions={0} | all-to-all | bytes 524288 | tf_op jit(solution)/shard_map/all_to_all | solution.py:406
  52.4 4.1 %design.1 = f32[2,16,128]{2,1,0:T(8,128)} custom-call(s32[16]{0:T(128)S(1)} %copy-done.2, f32[32,16,128]{2,1,0:T(8,128)S(1)} %bitcast.7, f32[32,16,128]{2,1,0:T(8,128)S(1)} %get-tuple-element.6.coef_ref, f32[32,16,128]{2,1,0:T(8,128)S(1)} %bitcast.6), custom_call_target="tpu_custom_call" | custom-call | tf_op jit(solution)/shard_map/design/pallas_call | solution.py:384
  (2 shorter events, 0.0 us)
Async XLA Ops:
  0.6 9.0 %copy-start.4 = (f32[16,3]{0,1:T(4,128)S(1)}, f32[16,3]{0,1:T(4,128)}, u32[]{:S(2)}) copy-start(f32[16,3]{0,1:T(4,128)} %param.10) | copy-start | bytes 580
  0.6 19.1 %copy-start = (f32[1,3,32,16,128]{4,3,2,1,0:T(8,128)S(1)}, f32[1,3,32,16,128]{4,3,2,1,0:T(8,128)}, u32[]{:S(2)}) copy-start(f32[1,3,32,16,128]{4,3,2,1,0:T(8,128)} %param.7) | copy-start | bytes 2359300
  2.2 17.6 %copy-start.1 = (s32[32,128]{1,0:T(8,128)S(1)}, s32[32,128]{1,0:T(8,128)}, u32[]{:S(2)}) copy-start(s32[32,128]{1,0:T(8,128)} %fixed_ref.1) | copy-start | bytes 49156
  2.2 17.5 %all-to-all-start = ((f32[16,2,16,128]{3,2,1,0:T(8,128)}), f32[16,2,16,128]{3,2,1,0:T(8,128)S(1)}, u32[]{:S(2)}, u32[]{:S(2)}) async-start(f32[16,2,16,128]{3,2,1,0:T(8,128)} %broadcast_in_dim.6), calls=%async_computation | async-start | bytes 524288 | tf_op jit(solution)/shard_map/all_to_all | solution.py:406
  19.7 0.7 %copy-start.2 = (s32[16]{0:T(128)S(1)}, s32[16]{0:T(128)}, u32[]{:S(2)}) copy-start(s32[16]{0:T(128)} %radius_ref.3) | copy-start | bytes 196
  19.7 0.7 %copy-start.3 = (s32[16]{0:T(128)S(1)}, s32[16]{0:T(128)}, u32[]{:S(2)}) copy-start(s32[16]{0:T(128)} %index_ref.1) | copy-start | bytes 196

commit v4 on v3

--- a/solution.py
+++ b/solution.py
@@ -91,6 +91,19 @@
         far = weight(4) * plane + weight(5) * beside + weight(8) * further
         results.append(level + shift_sum(near, 0, 1) + shift_sum(far, 0, 2))
     return results
+
+
+def reverse_bits(value, count):
+    result = 0
+    for bit in range(count):
+        result = result + ((value >> bit) & 1) * (1 << (count - 1 - bit))
+    return result
+
+
+def partner_spot(x, own_planes, devices):
+    mine = lax.axis_index("space")
+    order = reverse_bits((x // own_planes) ^ mine, devices.bit_length() - 1)
+    return order, x % own_planes
 
 
 def edge_class(x, planes):
@@ -129,7 +142,8 @@
     first_ref,
     second_ref,
 ):
-    planes, layers, row_width = density_ref.shape
+    devices, own_planes, layers, row_width = density_ref.shape
+    planes = devices * own_planes
     load_cases = index_ref.shape[0]
     load_place = lax.axis_index("space")
     shape = (layers, row_width)
@@ -149,7 +163,9 @@
         )
 
     def filter_plane(x, carry):
-        near, side, far = forward_planes(density_ref[x], weight_ref)
+        near, side, far = forward_planes(
+            density_ref[partner_spot(x, own_planes, devices)], weight_ref
+        )
         near_ref[x + 2] = near
         side_ref[x + 2] = side
         far_ref[x + 2] = far
@@ -253,7 +269,7 @@
         upward = jnp.where(z < layers - 1, upward, 0.0)
         right = jnp.where(y < row_width - 1, right, 0.0)
         total = carry + ahead + upward + pltpu.roll(upward, 1, 0) + right + pltpu.roll(right, 1, 1)
-        sens_ref[x] = (0.5 / load_cases) * total
+        sens_ref[partner_spot(x, own_planes, devices)] = (0.5 / load_cases) * total
         return ahead
 
     lax.fori_loop(0, planes, energy_plane, zero, unroll=8)
@@ -273,8 +289,8 @@
     low_ref,
     high_ref,
 ):
-    planes, layers, row_width = density_ref.shape
-    own_planes = new_ref.shape[0]
+    devices, own_planes, layers, row_width = density_ref.shape
+    planes = devices * own_planes
     place = lax.axis_index("space")
     shape = (layers, row_width)
     zero = jnp.zeros(shape, jnp.float32)
@@ -283,7 +299,9 @@
         zero_edges(ref)
 
     def filter_plane(x, carry):
-        near, side, far = backward_planes(sens_ref[x] * coef_ref[x], weight_ref)
+        near, side, far = backward_planes(
+            sens_ref[partner_spot(x, own_planes, devices)] * coef_ref[x], weight_ref
+        )
         near_ref[x + 2] = near
         side_ref[x + 2] = side
         far_ref[x + 2] = far
@@ -295,7 +313,7 @@
         root = jnp.sqrt(
             near_ref[x + 2] + side_ref[x + 1] + side_ref[x + 3] + far_ref[x] + far_ref[x + 4]
         )
-        density = density_ref[x]
+        density = density_ref[partner_spot(x, own_planes, devices)]
         pull_ref[x] = density * root
         low_ref[x] = jnp.maximum(density - move_limit, density_floor)
         high_ref[x] = jnp.minimum(density + move_limit, 1.0)
@@ -338,7 +356,8 @@
 
 
 def sweep_call(radius, load_index, load_force, density, fixed, displacement):
-    planes, layers, row_width = density.shape
+    devices, own_planes, layers, row_width = density.shape
+    planes = devices * own_planes
     grid_field = (planes, layers, row_width)
 
     def scratch(*lead):
@@ -348,7 +367,7 @@
         sweep_kernel,
         out_shape=[
             jax.ShapeDtypeStruct((3,) + grid_field, jnp.float32),
-            jax.ShapeDtypeStruct(grid_field, jnp.float32),
+            jax.ShapeDtypeStruct(density.shape, jnp.float32),
             jax.ShapeDtypeStruct(grid_field, jnp.float32),
         ],
         in_specs=[in_smem()] * 3 + [in_vmem()] * 3,
@@ -375,8 +394,9 @@
     )(radius, load_index, load_force, density, fixed, displacement)
 
 
-def design_call(radius, sens, coef, density, own_planes):
-    planes, layers, row_width = density.shape
+def design_call(radius, sens, coef, density):
+    devices, own_planes, layers, row_width = density.shape
+    planes = devices * own_planes
 
     def scratch(*lead):
         return pltpu.VMEM(lead + (layers, row_width), jnp.float32)
@@ -400,17 +420,27 @@
     )(radius, sens, coef, density)
 
 
+def swapped(block, bit):
+    devices = lax.axis_size("space")
+    return lax.ppermute(block, "space", [(i, i ^ 1 << bit) for i in range(devices)])
+
+
+def partner_bits(devices):
+    return devices.bit_length() - 1
+
+
 def gathered(block):
-    devices = lax.axis_size("space")
-    copies = jnp.broadcast_to(block[None], (devices,) + block.shape)
-    blocks = lax.all_to_all(copies, "space", 0, 0)
-    return blocks.reshape((devices * block.shape[0],) + block.shape[1:])
-
-
-def scattered_sum(field):
-    devices = lax.axis_size("space")
-    pieces = field.reshape((devices, field.shape[0] // devices) + field.shape[1:])
-    return jnp.sum(lax.all_to_all(pieces, "space", 0, 0), axis=0)
+    pieces = block[None]
+    for bit in reversed(range(partner_bits(lax.axis_size("space")))):
+        pieces = jnp.concatenate([pieces, swapped(pieces, bit)])
+    return pieces
+
+
+def scattered_sum(pieces):
+    for bit in range(partner_bits(lax.axis_size("space"))):
+        half = pieces.shape[0] // 2
+        pieces = pieces[:half] + swapped(pieces[half:], bit)
+    return pieces[0]
 
 
 def one_slab(density, displacement, fixed, load_index, load_force, radius):
@@ -419,7 +449,7 @@
         radius, load_index, load_force, whole, fixed, displacement[0]
     )
     sens = gathered(scattered_sum(sens))
-    new_density = design_call(radius, sens, coef, whole, density.shape[0])
+    new_density = design_call(radius, sens, coef, whole)
     return new_density, new_displacement[None]
 
 

time: 56.9 us -> 57.6 us (1.012)
  blocking collectives: 25.6 us -> 0 us
  starting transfers between devices: 7.49 us -> 21.7 us
  waiting for transfers between devices: 9.95 us -> 21.7 us
  local copies, waits for them, and re-layouts: 2.3 us -> 1.49 us
  other arithmetic: 0.02 us -> 0.79 us
    all_to_all x2 -> x0, blocking collectives: 25.6 us -> none  [the longest x1 12.8 us: gathered(): blocks = lax.all_to_all(copies, 'space', 0, 0)]
    ppermute x0 -> x12, starting transfers between devices: none -> 21.7 us  [swapped(): lax.ppermute(block, 'space', [(i, i ^ 1 << bit) for i in range(devices)])]
    ppermute x0 -> x12, waiting for transfers between devices: none -> 21.7 us  [swapped(): lax.ppermute(block, 'space', [(i, i ^ 1 << bit) for i in range(devices)])]
    all_to_all x1 -> x0, waiting for transfers between devices: 9.95 us -> none  [gathered(): blocks = lax.all_to_all(copies, 'space', 0, 0)]
    all_to_all x1 -> x0, starting transfers between devices: 7.49 us -> none  [gathered(): blocks = lax.all_to_all(copies, 'space', 0, 0)]
    broadcast_in_dim x2 -> x0, local copies, waits for them, and re-layouts: 1.54 us -> none  [gathered(): copies = jnp.broadcast_to(block[None], (devices,) + block.shape)]
    concatenate x0 -> x6, other arithmetic: none -> 0.75 us  [gathered(): pieces = jnp.concatenate([pieces, swapped(pieces, bit)])]
    unnamed x11 -> x18, local copies, waits for them, and re-layouts: 0.76 us -> 1.44 us
  transfers between devices with their start and end apart: 1 -> 12, of which waited for: 1 -> 12; matrix products, arithmetic and copies ran while one was open for 0% -> 1% of each run, Pallas kernels for 0% -> 0%
where the time goes in v4:
time: 57.6 us; the launch traced here: 57.4 us
  starting transfers between devices  21.7 us (38%)
  waiting for transfers between devices  21.7 us (38%)
  Pallas kernels  10.9 us (19%)
  local copies, waits for them, and re-layouts  1.49 us (3%)
  other arithmetic  0.79 us (1%)
  between operations  0.79 us (1%)
    ppermute x12, starting transfers between devices, swapped(): lax.ppermute(block, 'space', [(i, i ^ 1 << bit) for i in range(devices)])  21.7 us
    ppermute x12, waiting for transfers between devices, swapped(): lax.ppermute(block, 'space', [(i, i ^ 1 << bit) for i in range(devices)])  21.7 us
    pallas_call x1, Pallas kernels, sweep_call(): pl.pallas_call(sweep_kernel, out_shape=[jax.ShapeDtypeStruct((3,) + grid_...  6.54 us
    pallas_call x1, Pallas kernels, design_call(): pl.pallas_call(design_kernel, out_shape=jax.ShapeDtypeStruct((own_planes,...  4.34 us
    unnamed x18, local copies, waits for them, and re-layouts  1.44 us
  transfers between devices with their start and end apart: 12, of which 12 were waited for; matrix products, arithmetic and copies ran while one was open for 1% of the time, Pallas kernels for 0%

profile of v4, /device:TPU:0, one launch (start us, length us, event | category | flops | bytes accessed | tf_op | source)
XLA Modules:
  0.0 57.4 jit_solution(7650290690172695308)
XLA Ops:
  0.6 0.0 copy-start.4
  0.6 0.0 copy-start
  0.6 4.1 %collective-permute-start = (f32[1,2,16,128]{3,2,1,0:T(8,128)}, f32[1,2,16,128]{3,2,1,0:T(8,128)S(1)}, u32[]{:S(2)}, u32[]{:S(2)}) collective-permute-start(f32[1,2,16,128]{3,2,1,0:T(8,128)} %bitcast.5), channel_id=1, source_target_pairs={{0,8},{1,9},{2,10},{3,11},{4,12},{5,13},{6,14},{7,15},{8,0},{9,1},... | collective-permute-start | bytes 49160 | tf_op jit(solution)/shard_map/ppermute | solution.py:425
  4.8 1.9 %collective-permute-done = f32[1,2,16,128]{3,2,1,0:T(8,128)S(1)} collective-permute-done((f32[1,2,16,128]{3,2,1,0:T(8,128)}, f32[1,2,16,128]{3,2,1,0:T(8,128)S(1)}, u32[]{:S(2)}, u32[]{:S(2)}) %collective-permute-start) | collective-permute-done | bytes 16416 | tf_op jit(solution)/shard_map/ppermute | solution.py:425
  6.7 0.7 %pad_maximum_fusion.4 = f32[2,2,16,128]{3,2,1,0:T(8,128)S(1)} fusion(f32[1,2,16,128]{3,2,1,0:T(8,128)S(1)} %collective-permute-done, f32[1,2,16,128]{3,2,1,0:T(8,128)} %bitcast.6), kind=kLoop, calls=%fused_computation.7 | loop fusion | flops 8192 | bytes 65536 | tf_op jit(solution)/shard_map/concatenate | solution.py:435
  7.4 1.9 %collective-permute-start.1 = (f32[2,2,16,128]{3,2,1,0:T(8,128)S(1)}, f32[2,2,16,128]{3,2,1,0:T(8,128)S(1)}, u32[]{:S(2)}, u32[]{:S(2)}) collective-permute-start(f32[2,2,16,128]{3,2,1,0:T(8,128)S(1)} %pad_maximum_fusion.4), channel_id=1, source_target_pairs={{0,4},{1,5},{2,6},{3,7},{4,0},{5,1},{6,2},{7,3},{8,12},{9,13},{10,... | collective-permute-start | bytes 98312 | tf_op jit(solution)/shard_map/ppermute | solution.py:425
  9.3 0.0 copy-done.4
  9.3 0.8 %copy.8.force_ref = f32[16,3]{1,0:T(8,128)S(1)} copy(f32[16,3]{0,1:T(4,128)} %param.10) | data formatting | bytes 384 | tf_op args[4]
  10.1 1.2 %collective-permute-done.1 = f32[2,2,16,128]{3,2,1,0:T(8,128)S(1)} collective-permute-done((f32[2,2,16,128]{3,2,1,0:T(8,128)S(1)}, f32[2,2,16,128]{3,2,1,0:T(8,128)S(1)}, u32[]{:S(2)}, u32[]{:S(2)}) %collective-permute-start.1) | collective-permute-done | bytes 32800 | tf_op jit(solution)/shard_map/ppermute | solution.py:425
  11.3 1.9 %collective-permute-start.2 = (f32[4,2,16,128]{3,2,1,0:T(8,128)S(1)}, f32[4,2,16,128]{3,2,1,0:T(8,128)S(1)}, u32[]{:S(2)}, u32[]{:S(2)}) collective-permute-start(f32[4,2,16,128]{3,2,1,0:T(8,128)S(1)} %pad_maximum_fusion.2), channel_id=1, source_target_pairs={{0,2},{1,3},{2,0},{3,1},{4,6},{5,7},{6,4},{7,5},{8,10},{9,11},{10,... | collective-permute-start | bytes 196616 | tf_op jit(solution)/shard_map/ppermute | solution.py:425
  13.2 2.4 %collective-permute-done.2 = f32[4,2,16,128]{3,2,1,0:T(8,128)S(1)} collective-permute-done((f32[4,2,16,128]{3,2,1,0:T(8,128)S(1)}, f32[4,2,16,128]{3,2,1,0:T(8,128)S(1)}, u32[]{:S(2)}, u32[]{:S(2)}) %collective-permute-start.2) | collective-permute-done | bytes 65568 | tf_op jit(solution)/shard_map/ppermute | solution.py:425
  15.6 0.1 collective-permute-start.3
  15.7 0.0 copy-start.1
  15.7 1.3 %collective-permute-done.3 = f32[8,2,16,128]{3,2,1,0:T(8,128)S(1)} collective-permute-done((f32[8,2,16,128]{3,2,1,0:T(8,128)S(1)}, f32[8,2,16,128]{3,2,1,0:T(8,128)S(1)}, u32[]{:S(2)}, u32[]{:S(2)}) %collective-permute-start.3) | collective-permute-done | bytes 131104 | tf_op jit(solution)/shard_map/ppermute | solution.py:425
  17.0 0.0 copy-start.2
  17.0 0.0 copy-start.3
  17.1 0.0 copy-done
  17.1 0.0 copy-done.1
  17.1 0.6 %copy-done.2 = s32[16]{0:T(128)S(1)} copy-done((s32[16]{0:T(128)S(1)}, s32[16]{0:T(128)}, u32[]{:S(2)}) %copy-start.2) | copy-done | bytes 88
  17.7 0.0 copy-done.3
  17.7 6.5 %sweeps.1 = (f32[3,32,16,128]{3,2,1,0:T(8,128)}, f32[16,2,16,128]{3,2,1,0:T(8,128)S(1)}, f32[32,16,128]{2,1,0:T(8,128)S(1)}) custom-call(s32[16]{0:T(128)S(1)} %copy-done.2, s32[16]{0:T(128)S(1)} %copy-done.3, f32[16,3]{1,0:T(8,128)S(1)} %copy.8.force_ref, f32[16,2,16,128]{3,2,1,0:T(8,128)S(1)} %constant_dynamic-update-slice_fusion.density_ref, ...), custom_call_target="tpu_custom_call" | custom-call | tf_op jit(solution)/shard_map/sweeps/pallas_call | solution.py:366
  24.3 0.2 collective-permute-start.4
  24.5 1.2 %collective-permute-done.4 = f32[8,2,16,128]{3,2,1,0:T(8,128)S(1)} collective-permute-done((f32[8,2,16,128]{3,2,1,0:T(8,128)S(1)}, f32[8,2,16,128]{3,2,1,0:T(8,128)S(1)}, u32[]{:S(2)}, u32[]{:S(2)}) %collective-permute-start.4) | collective-permute-done | bytes 131104 | tf_op jit(solution)/shard_map/ppermute | solution.py:425
  25.7 1.9 %collective-permute-start.5 = (f32[4,2,16,128]{3,2,1,0:T(8,128)S(1)}, f32[4,2,16,128]{3,2,1,0:T(8,128)S(1)}, u32[]{:S(2)}, u32[]{:S(2)}) collective-permute-start(f32[4,2,16,128]{3,2,1,0:T(8,128)S(1)} %slice.33), channel_id=1, source_target_pairs={{0,2},{1,3},{2,0},{3,1},{4,6},{5,7},{6,4},{7,5},{8,10},{9,11},{10,... | collective-permute-start | bytes 196616 | tf_op jit(solution)/shard_map/ppermute | solution.py:425
  27.7 2.4 %collective-permute-done.5 = f32[4,2,16,128]{3,2,1,0:T(8,128)S(1)} collective-permute-done((f32[4,2,16,128]{3,2,1,0:T(8,128)S(1)}, f32[4,2,16,128]{3,2,1,0:T(8,128)S(1)}, u32[]{:S(2)}, u32[]{:S(2)}) %collective-permute-start.5) | collective-permute-done | bytes 65568 | tf_op jit(solution)/shard_map/ppermute | solution.py:425
  30.1 1.9 %collective-permute-start.6 = (f32[2,2,16,128]{3,2,1,0:T(8,128)S(1)}, f32[2,2,16,128]{3,2,1,0:T(8,128)S(1)}, u32[]{:S(2)}, u32[]{:S(2)}) collective-permute-start(f32[2,2,16,128]{3,2,1,0:T(8,128)S(1)} %slice.35), channel_id=1, source_target_pairs={{0,4},{1,5},{2,6},{3,7},{4,0},{5,1},{6,2},{7,3},{8,12},{9,13},{10,... | collective-permute-start | bytes 98312 | tf_op jit(solution)/shard_map/ppermute | solution.py:425
  32.0 2.0 %collective-permute-done.6 = f32[2,2,16,128]{3,2,1,0:T(8,128)S(1)} collective-permute-done((f32[2,2,16,128]{3,2,1,0:T(8,128)S(1)}, f32[2,2,16,128]{3,2,1,0:T(8,128)S(1)}, u32[]{:S(2)}, u32[]{:S(2)}) %collective-permute-start.6) | collective-permute-done | bytes 32800 | tf_op jit(solution)/shard_map/ppermute | solution.py:425
  34.1 3.0 %collective-permute-start.7 = (f32[1,2,16,128]{3,2,1,0:T(8,128)S(1)}, f32[1,2,16,128]{3,2,1,0:T(8,128)S(1)}, u32[]{:S(2)}, u32[]{:S(2)}) collective-permute-start(f32[1,2,16,128]{3,2,1,0:T(8,128)S(1)} %slice.37), channel_id=1, source_target_pairs={{0,8},{1,9},{2,10},{3,11},{4,12},{5,13},{6,14},{7,15},{8,0},{9,1},... | collective-permute-start | bytes 49160 | tf_op jit(solution)/shard_map/ppermute | solution.py:425
  37.0 1.7 %collective-permute-done.7 = f32[1,2,16,128]{3,2,1,0:T(8,128)S(1)} collective-permute-done((f32[1,2,16,128]{3,2,1,0:T(8,128)S(1)}, f32[1,2,16,128]{3,2,1,0:T(8,128)S(1)}, u32[]{:S(2)}, u32[]{:S(2)}) %collective-permute-start.7) | collective-permute-done | bytes 16416 | tf_op jit(solution)/shard_map/ppermute | solution.py:425
  38.8 2.9 %collective-permute-start.8 = (f32[1,2,16,128]{3,2,1,0:T(8,128)S(1)}, f32[1,2,16,128]{3,2,1,0:T(8,128)S(1)}, u32[]{:S(2)}, u32[]{:S(2)}) collective-permute-start(f32[1,2,16,128]{3,2,1,0:T(8,128)S(1)} %get-tuple-element.9), channel_id=1, source_target_pairs={{0,8},{1,9},{2,10},{3,11},{4,12},{5,13},{6,14},{7,15},{8,0},{9,1},... | collective-permute-start | bytes 49160 | tf_op jit(solution)/shard_map/ppermute | solution.py:425
  41.7 1.7 %collective-permute-done.8 = f32[1,2,16,128]{3,2,1,0:T(8,128)S(1)} collective-permute-done((f32[1,2,16,128]{3,2,1,0:T(8,128)S(1)}, f32[1,2,16,128]{3,2,1,0:T(8,128)S(1)}, u32[]{:S(2)}, u32[]{:S(2)}) %collective-permute-start.8) | collective-permute-done | bytes 16416 | tf_op jit(solution)/shard_map/ppermute | solution.py:425
  43.4 1.9 %collective-permute-start.9 = (f32[2,2,16,128]{3,2,1,0:T(8,128)S(1)}, f32[2,2,16,128]{3,2,1,0:T(8,128)S(1)}, u32[]{:S(2)}, u32[]{:S(2)}) collective-permute-start(f32[2,2,16,128]{3,2,1,0:T(8,128)S(1)} %pad_maximum_fusion.5), channel_id=1, source_target_pairs={{0,4},{1,5},{2,6},{3,7},{4,0},{5,1},{6,2},{7,3},{8,12},{9,13},{10,... | collective-permute-start | bytes 98312 | tf_op jit(solution)/shard_map/ppermute | solution.py:425
  45.3 2.0 %collective-permute-done.9 = f32[2,2,16,128]{3,2,1,0:T(8,128)S(1)} collective-permute-done((f32[2,2,16,128]{3,2,1,0:T(8,128)S(1)}, f32[2,2,16,128]{3,2,1,0:T(8,128)S(1)}, u32[]{:S(2)}, u32[]{:S(2)}) %collective-permute-start.9) | collective-permute-done | bytes 32800 | tf_op jit(solution)/shard_map/ppermute | solution.py:425
  47.4 1.9 %collective-permute-start.10 = (f32[4,2,16,128]{3,2,1,0:T(8,128)S(1)}, f32[4,2,16,128]{3,2,1,0:T(8,128)S(1)}, u32[]{:S(2)}, u32[]{:S(2)}) collective-permute-start(f32[4,2,16,128]{3,2,1,0:T(8,128)S(1)} %pad_maximum_fusion.3), channel_id=1, source_target_pairs={{0,2},{1,3},{2,0},{3,1},{4,6},{5,7},{6,4},{7,5},{8,10},{9,11},{10,... | collective-permute-start | bytes 196616 | tf_op jit(solution)/shard_map/ppermute | solution.py:425
  49.2 2.4 %collective-permute-done.10 = f32[4,2,16,128]{3,2,1,0:T(8,128)S(1)} collective-permute-done((f32[4,2,16,128]{3,2,1,0:T(8,128)S(1)}, f32[4,2,16,128]{3,2,1,0:T(8,128)S(1)}, u32[]{:S(2)}, u32[]{:S(2)}) %collective-permute-start.10) | collective-permute-done | bytes 65568 | tf_op jit(solution)/shard_map/ppermute | solution.py:425
  51.6 0.1 collective-permute-start.11
  51.7 1.3 %collective-permute-done.11 = f32[8,2,16,128]{3,2,1,0:T(8,128)S(1)} collective-permute-done((f32[8,2,16,128]{3,2,1,0:T(8,128)S(1)}, f32[8,2,16,128]{3,2,1,0:T(8,128)S(1)}, u32[]{:S(2)}, u32[]{:S(2)}) %collective-permute-start.11) | collective-permute-done | bytes 131104 | tf_op jit(solution)/shard_map/ppermute | solution.py:425
  53.1 4.3 %design.1 = f32[2,16,128]{2,1,0:T(8,128)} custom-call(s32[16]{0:T(128)S(1)} %copy-done.2, f32[16,2,16,128]{3,2,1,0:T(8,128)S(1)} %constant_dynamic-update-slice_fusion.5.sens_ref, f32[32,16,128]{2,1,0:T(8,128)S(1)} %get-tuple-element.6.coef_ref, f32[16,2,16,128]{3,2,1,0:T(8,128)S(1)} %constant_dynamic-update-slice_fusion.density_ref), custom_call_target="tpu_custom_call" | custom-call | tf_op jit(solution)/shard_map/design/pallas_call | solution.py:404
  (22 shorter events, 0.2 us)
Async XLA Ops:
  0.6 8.7 %copy-start.4 = (f32[2,16,128]{2,1,0:T(8,128)S(1)}, f32[2,16,128]{2,1,0:T(8,128)}, u32[]{:S(2)}) copy-start(f32[2,16,128]{2,1,0:T(8,128)} %param.6) | copy-start | bytes 49156
  0.6 16.4 %copy-start = (f32[1,3,32,16,128]{4,3,2,1,0:T(8,128)S(1)}, f32[1,3,32,16,128]{4,3,2,1,0:T(8,128)}, u32[]{:S(2)}) copy-start(f32[1,3,32,16,128]{4,3,2,1,0:T(8,128)} %param.7) | copy-start | bytes 2359300
  0.6 6.0 %collective-permute-start = (f32[1,2,16,128]{3,2,1,0:T(8,128)}, f32[1,2,16,128]{3,2,1,0:T(8,128)S(1)}, u32[]{:S(2)}, u32[]{:S(2)}) collective-permute-start(f32[1,2,16,128]{3,2,1,0:T(8,128)} %bitcast.5), channel_id=1, source_target_pairs={{0,8},{1,9},{2,10},{3,11},{4,12},{5,13},{6,14},{7,15},{8,0},{9,1},... | collective-permute-start | bytes 49160 | tf_op jit(solution)/shard_map/ppermute | solution.py:425
  7.4 3.9 %collective-permute-start.1 = (f32[2,2,16,128]{3,2,1,0:T(8,128)S(1)}, f32[2,2,16,128]{3,2,1,0:T(8,128)S(1)}, u32[]{:S(2)}, u32[]{:S(2)}) collective-permute-start(f32[2,2,16,128]{3,2,1,0:T(8,128)S(1)} %pad_maximum_fusion.4), channel_id=1, source_target_pairs={{0,4},{1,5},{2,6},{3,7},{4,0},{5,1},{6,2},{7,3},{8,12},{9,13},{10,... | collective-permute-start | bytes 98312 | tf_op jit(solution)/shard_map/ppermute | solution.py:425
  11.3 4.3 %collective-permute-start.2 = (f32[4,2,16,128]{3,2,1,0:T(8,128)S(1)}, f32[4,2,16,128]{3,2,1,0:T(8,128)S(1)}, u32[]{:S(2)}, u32[]{:S(2)}) collective-permute-start(f32[4,2,16,128]{3,2,1,0:T(8,128)S(1)} %pad_maximum_fusion.2), channel_id=1, source_target_pairs={{0,2},{1,3},{2,0},{3,1},{4,6},{5,7},{6,4},{7,5},{8,10},{9,11},{10,... | collective-permute-start | bytes 196616 | tf_op jit(solution)/shard_map/ppermute | solution.py:425
  15.6 1.4 %collective-permute-start.3 = (f32[8,2,16,128]{3,2,1,0:T(8,128)S(1)}, f32[8,2,16,128]{3,2,1,0:T(8,128)S(1)}, u32[]{:S(2)}, u32[]{:S(2)}) collective-permute-start(f32[8,2,16,128]{3,2,1,0:T(8,128)S(1)} %pad_maximum_fusion), channel_id=1, source_target_pairs={{0,1},{1,0},{2,3},{3,2},{4,5},{5,4},{6,7},{7,6},{8,9},{9,8},{10,11... | collective-permute-start | bytes 393224 | tf_op jit(solution)/shard_map/ppermute | solution.py:425
  15.7 1.4 %copy-start.1 = (s32[32,128]{1,0:T(8,128)S(1)}, s32[32,128]{1,0:T(8,128)}, u32[]{:S(2)}) copy-start(s32[32,128]{1,0:T(8,128)} %fixed_ref.1) | copy-start | bytes 49156
  17.0 0.7 %copy-start.2 = (s32[16]{0:T(128)S(1)}, s32[16]{0:T(128)}, u32[]{:S(2)}) copy-start(s32[16]{0:T(128)} %radius_ref.3) | copy-start | bytes 196
  17.0 0.7 %copy-start.3 = (s32[16]{0:T(128)S(1)}, s32[16]{0:T(128)}, u32[]{:S(2)}) copy-start(s32[16]{0:T(128)} %index_ref.1) | copy-start | bytes 196
  24.3 1.4 %collective-permute-start.4 = (f32[8,2,16,128]{3,2,1,0:T(8,128)S(1)}, f32[8,2,16,128]{3,2,1,0:T(8,128)S(1)}, u32[]{:S(2)}, u32[]{:S(2)}) collective-permute-start(f32[8,2,16,128]{3,2,1,0:T(8,128)S(1)} %slice.25), channel_id=1, source_target_pairs={{0,1},{1,0},{2,3},{3,2},{4,5},{5,4},{6,7},{7,6},{8,9},{9,8},{10,11... | collective-permute-start | bytes 393224 | tf_op jit(solution)/shard_map/ppermute | solution.py:425
  25.7 4.4 %collective-permute-start.5 = (f32[4,2,16,128]{3,2,1,0:T(8,128)S(1)}, f32[4,2,16,128]{3,2,1,0:T(8,128)S(1)}, u32[]{:S(2)}, u32[]{:S(2)}) collective-permute-start(f32[4,2,16,128]{3,2,1,0:T(8,128)S(1)} %slice.33), channel_id=1, source_target_pairs={{0,2},{1,3},{2,0},{3,1},{4,6},{5,7},{6,4},{7,5},{8,10},{9,11},{10,... | collective-permute-start | bytes 196616 | tf_op jit(solution)/shard_map/ppermute | solution.py:425
  30.1 4.0 %collective-permute-start.6 = (f32[2,2,16,128]{3,2,1,0:T(8,128)S(1)}, f32[2,2,16,128]{3,2,1,0:T(8,128)S(1)}, u32[]{:S(2)}, u32[]{:S(2)}) collective-permute-start(f32[2,2,16,128]{3,2,1,0:T(8,128)S(1)} %slice.35), channel_id=1, source_target_pairs={{0,4},{1,5},{2,6},{3,7},{4,0},{5,1},{6,2},{7,3},{8,12},{9,13},{10,... | collective-permute-start | bytes 98312 | tf_op jit(solution)/shard_map/ppermute | solution.py:425
  34.1 4.7 %collective-permute-start.7 = (f32[1,2,16,128]{3,2,1,0:T(8,128)S(1)}, f32[1,2,16,128]{3,2,1,0:T(8,128)S(1)}, u32[]{:S(2)}, u32[]{:S(2)}) collective-permute-start(f32[1,2,16,128]{3,2,1,0:T(8,128)S(1)} %slice.37), channel_id=1, source_target_pairs={{0,8},{1,9},{2,10},{3,11},{4,12},{5,13},{6,14},{7,15},{8,0},{9,1},... | collective-permute-start | bytes 49160 | tf_op jit(solution)/shard_map/ppermute | solution.py:425
  38.8 4.6 %collective-permute-start.8 = (f32[1,2,16,128]{3,2,1,0:T(8,128)S(1)}, f32[1,2,16,128]{3,2,1,0:T(8,128)S(1)}, u32[]{:S(2)}, u32[]{:S(2)}) collective-permute-start(f32[1,2,16,128]{3,2,1,0:T(8,128)S(1)} %get-tuple-element.9), channel_id=1, source_target_pairs={{0,8},{1,9},{2,10},{3,11},{4,12},{5,13},{6,14},{7,15},{8,0},{9,1},... | collective-permute-start | bytes 49160 | tf_op jit(solution)/shard_map/ppermute | solution.py:425
  43.4 3.9 %collective-permute-start.9 = (f32[2,2,16,128]{3,2,1,0:T(8,128)S(1)}, f32[2,2,16,128]{3,2,1,0:T(8,128)S(1)}, u32[]{:S(2)}, u32[]{:S(2)}) collective-permute-start(f32[2,2,16,128]{3,2,1,0:T(8,128)S(1)} %pad_maximum_fusion.5), channel_id=1, source_target_pairs={{0,4},{1,5},{2,6},{3,7},{4,0},{5,1},{6,2},{7,3},{8,12},{9,13},{10,... | collective-permute-start | bytes 98312 | tf_op jit(solution)/shard_map/ppermute | solution.py:425
  47.4 4.3 %collective-permute-start.10 = (f32[4,2,16,128]{3,2,1,0:T(8,128)S(1)}, f32[4,2,16,128]{3,2,1,0:T(8,128)S(1)}, u32[]{:S(2)}, u32[]{:S(2)}) collective-permute-start(f32[4,2,16,128]{3,2,1,0:T(8,128)S(1)} %pad_maximum_fusion.3), channel_id=1, source_target_pairs={{0,2},{1,3},{2,0},{3,1},{4,6},{5,7},{6,4},{7,5},{8,10},{9,11},{10,... | collective-permute-start | bytes 196616 | tf_op jit(solution)/shard_map/ppermute | solution.py:425
  51.6 1.4 %collective-permute-start.11 = (f32[8,2,16,128]{3,2,1,0:T(8,128)S(1)}, f32[8,2,16,128]{3,2,1,0:T(8,128)S(1)}, u32[]{:S(2)}, u32[]{:S(2)}) collective-permute-start(f32[8,2,16,128]{3,2,1,0:T(8,128)S(1)} %pad_maximum_fusion.1), channel_id=1, source_target_pairs={{0,1},{1,0},{2,3},{3,2},{4,5},{5,4},{6,7},{7,6},{8,9},{9,8},{10,11... | collective-permute-start | bytes 393224 | tf_op jit(solution)/shard_map/ppermute | solution.py:425

commit v5 on v3

--- a/solution.py
+++ b/solution.py
@@ -91,6 +91,12 @@
         far = weight(4) * plane + weight(5) * beside + weight(8) * further
         results.append(level + shift_sum(near, 0, 1) + shift_sum(far, 0, 2))
     return results
+
+
+def pair_spot(x, own_planes):
+    device = x // own_planes
+    core = (device ^ lax.axis_index("space")) & 1
+    return core, device >> 1, x % own_planes
 
 
 def edge_class(x, planes):
@@ -129,7 +135,8 @@
     first_ref,
     second_ref,
 ):
-    planes, layers, row_width = density_ref.shape
+    cores, chips, own_planes, layers, row_width = density_ref.shape
+    planes = cores * chips * own_planes
     load_cases = index_ref.shape[0]
     load_place = lax.axis_index("space")
     shape = (layers, row_width)
@@ -149,7 +156,9 @@
         )
 
     def filter_plane(x, carry):
-        near, side, far = forward_planes(density_ref[x], weight_ref)
+        near, side, far = forward_planes(
+            density_ref[pair_spot(x, own_planes)], weight_ref
+        )
         near_ref[x + 2] = near
         side_ref[x + 2] = side
         far_ref[x + 2] = far
@@ -253,7 +262,7 @@
         upward = jnp.where(z < layers - 1, upward, 0.0)
         right = jnp.where(y < row_width - 1, right, 0.0)
         total = carry + ahead + upward + pltpu.roll(upward, 1, 0) + right + pltpu.roll(right, 1, 1)
-        sens_ref[x] = (0.5 / load_cases) * total
+        sens_ref[pair_spot(x, own_planes)] = (0.5 / load_cases) * total
         return ahead
 
     lax.fori_loop(0, planes, energy_plane, zero, unroll=8)
@@ -273,8 +282,8 @@
     low_ref,
     high_ref,
 ):
-    planes, layers, row_width = density_ref.shape
-    own_planes = new_ref.shape[0]
+    cores, chips, own_planes, layers, row_width = density_ref.shape
+    planes = cores * chips * own_planes
     place = lax.axis_index("space")
     shape = (layers, row_width)
     zero = jnp.zeros(shape, jnp.float32)
@@ -283,7 +292,9 @@
         zero_edges(ref)
 
     def filter_plane(x, carry):
-        near, side, far = backward_planes(sens_ref[x] * coef_ref[x], weight_ref)
+        near, side, far = backward_planes(
+            sens_ref[pair_spot(x, own_planes)] * coef_ref[x], weight_ref
+        )
         near_ref[x + 2] = near
         side_ref[x + 2] = side
         far_ref[x + 2] = far
@@ -295,7 +306,7 @@
         root = jnp.sqrt(
             near_ref[x + 2] + side_ref[x + 1] + side_ref[x + 3] + far_ref[x] + far_ref[x + 4]
         )
-        density = density_ref[x]
+        density = density_ref[pair_spot(x, own_planes)]
         pull_ref[x] = density * root
         low_ref[x] = jnp.maximum(density - move_limit, density_floor)
         high_ref[x] = jnp.minimum(density + move_limit, 1.0)
@@ -338,7 +349,8 @@
 
 
 def sweep_call(radius, load_index, load_force, density, fixed, displacement):
-    planes, layers, row_width = density.shape
+    cores, chips, own_planes, layers, row_width = density.shape
+    planes = cores * chips * own_planes
     grid_field = (planes, layers, row_width)
 
     def scratch(*lead):
@@ -348,7 +360,7 @@
         sweep_kernel,
         out_shape=[
             jax.ShapeDtypeStruct((3,) + grid_field, jnp.float32),
-            jax.ShapeDtypeStruct(grid_field, jnp.float32),
+            jax.ShapeDtypeStruct(density.shape, jnp.float32),
             jax.ShapeDtypeStruct(grid_field, jnp.float32),
         ],
         in_specs=[in_smem()] * 3 + [in_vmem()] * 3,
@@ -375,8 +387,9 @@
     )(radius, load_index, load_force, density, fixed, displacement)
 
 
-def design_call(radius, sens, coef, density, own_planes):
-    planes, layers, row_width = density.shape
+def design_call(radius, sens, coef, density):
+    cores, chips, own_planes, layers, row_width = density.shape
+    planes = cores * chips * own_planes
 
     def scratch(*lead):
         return pltpu.VMEM(lead + (layers, row_width), jnp.float32)
@@ -400,17 +413,25 @@
     )(radius, sens, coef, density)
 
 
+def other_core(block):
+    devices = lax.axis_size("space")
+    return lax.ppermute(block, "space", [(i, i ^ 1) for i in range(devices)])
+
+
+def between_chips(pieces):
+    devices = lax.axis_size("space")
+    groups = [list(range(core, devices, 2)) for core in range(2)]
+    return lax.all_to_all(pieces, "space", 0, 0, axis_index_groups=groups)
+
+
 def gathered(block):
-    devices = lax.axis_size("space")
-    copies = jnp.broadcast_to(block[None], (devices,) + block.shape)
-    blocks = lax.all_to_all(copies, "space", 0, 0)
-    return blocks.reshape((devices * block.shape[0],) + block.shape[1:])
-
-
-def scattered_sum(field):
-    devices = lax.axis_size("space")
-    pieces = field.reshape((devices, field.shape[0] // devices) + field.shape[1:])
-    return jnp.sum(lax.all_to_all(pieces, "space", 0, 0), axis=0)
+    chips = lax.axis_size("space") // 2
+    same = between_chips(jnp.broadcast_to(block[None], (chips,) + block.shape))
+    return jnp.stack([same, other_core(same)])
+
+
+def scattered_sum(pieces):
+    return jnp.sum(between_chips(pieces[0] + other_core(pieces[1])), axis=0)
 
 
 def one_slab(density, displacement, fixed, load_index, load_force, radius):
@@ -419,7 +440,7 @@
         radius, load_index, load_force, whole, fixed, displacement[0]
     )
     sens = gathered(scattered_sum(sens))
-    new_density = design_call(radius, sens, coef, whole, density.shape[0])
+    new_density = design_call(radius, sens, coef, whole)
     return new_density, new_displacement[None]
 
 

time: 56.9 us -> 51.7 us (0.909)
  blocking collectives: 25.6 us -> 34.2 us
  starting transfers between devices: 7.49 us -> 0.22 us
  waiting for transfers between devices: 9.95 us -> 3.13 us
    all_to_all x1 -> x0, waiting for transfers between devices: 9.95 us -> none  [gathered(): blocks = lax.all_to_all(copies, 'space', 0, 0)]
    all_to_all x2 -> x3, blocking collectives: 25.6 us -> 34.2 us  [between_chips(): return lax.all_to_all(pieces, 'space', 0, 0, axis_index_groups=groups)]
    all_to_all x1 -> x0, starting transfers between devices: 7.49 us -> none  [gathered(): blocks = lax.all_to_all(copies, 'space', 0, 0)]
    ppermute x0 -> x3, waiting for transfers between devices: none -> 3.13 us  [other_core(): return lax.ppermute(block, 'space', [(i, i ^ 1) for i in range(devices)])]
    broadcast_in_dim x2, local copies, waits for them, and re-layouts: 1.54 us -> 0.81 us  [gathered(): same = between_chips(jnp.broadcast_to(block[None], (chips,) + block.shape))]
    unnamed x11 -> x9, local copies, waits for them, and re-layouts: 0.76 us -> 1.44 us
  transfers between devices with their start and end apart: 1 -> 3, of which waited for: 1 -> 3; matrix products, arithmetic and copies ran while one was open for 0% -> 1% of each run, Pallas kernels for 0% -> 0%
where the time goes in v5:
time: 51.7 us; the launch traced here: 51.3 us
  blocking collectives  34.2 us (66%)
  Pallas kernels  10.7 us (21%)
  waiting for transfers between devices  3.13 us (6%)
  local copies, waits for them, and re-layouts  2.26 us (4%)
  between operations  0.69 us (1%)
    all_to_all x3, blocking collectives, between_chips(): return lax.all_to_all(pieces, 'space', 0, 0, axis_index_groups=groups)  34.2 us
    pallas_call x1, Pallas kernels, sweep_call(): pl.pallas_call(sweep_kernel, out_shape=[jax.ShapeDtypeStruct((3,) + grid_...  6.5 us
    pallas_call x1, Pallas kernels, design_call(): pl.pallas_call(design_kernel, out_shape=jax.ShapeDtypeStruct((own_planes,...  4.19 us
    ppermute x3, waiting for transfers between devices, other_core(): return lax.ppermute(block, 'space', [(i, i ^ 1) for i in range(devices)])  3.13 us
    unnamed x9, local copies, waits for them, and re-layouts  1.44 us
  transfers between devices with their start and end apart: 3, of which 3 were waited for; matrix products, arithmetic and copies ran while one was open for 1% of the time, Pallas kernels for 0%

profile of v5, /device:TPU:0, one launch (start us, length us, event | category | flops | bytes accessed | tf_op | source)
XLA Modules:
  0.0 51.3 jit_solution(16273117108486763794)
XLA Ops:
  0.6 0.0 copy-start
  0.6 0.8 %broadcast_in_dim.6 = f32[8,2,16,128]{3,2,1,0:T(8,128)S(1)} broadcast(f32[2,16,128]{2,1,0:T(8,128)} %param.6), dimensions={1,2,3} | broadcast | bytes 147456 | tf_op jit(solution)/shard_map/broadcast_in_dim | solution.py:429
  1.4 14.4 %all_to_all.15 = f32[8,2,16,128]{3,2,1,0:T(8,128)S(1)} all-to-all(f32[8,2,16,128]{3,2,1,0:T(8,128)S(1)} %broadcast_in_dim.6), channel_id=1, replica_groups={{0,2,4,6,8,10,12,14},{1,3,5,7,9,11,13,15},{16,18,20,22,24,26,28,30},{17..., dimensions={0} | all-to-all | bytes 262144 | tf_op jit(solution)/shard_map/all_to_all | solution.py:424
  15.8 0.0 collective-permute-start
  15.8 0.8 %copy.8.force_ref = f32[16,3]{1,0:T(8,128)S(1)} copy(f32[16,3]{0,1:T(4,128)} %param.10) | data formatting | bytes 384 | tf_op args[4]
  16.6 0.6 %collective-permute-done = f32[8,2,16,128]{3,2,1,0:T(8,128)S(1)} collective-permute-done((f32[8,2,16,128]{3,2,1,0:T(8,128)S(1)}, f32[8,2,16,128]{3,2,1,0:T(8,128)S(1)}, u32[]{:S(2)}, u32[]{:S(2)}) %collective-permute-start) | collective-permute-done | bytes 131104 | tf_op jit(solution)/shard_map/ppermute | solution.py:418
  17.2 0.0 copy-start.1
  17.2 0.0 copy-start.2
  17.2 0.0 copy-start.3
  17.2 0.0 copy-done
  17.2 0.7 %copy-done.1 = s32[32,128]{1,0:T(8,128)S(1)} copy-done((s32[32,128]{1,0:T(8,128)S(1)}, s32[32,128]{1,0:T(8,128)}, u32[]{:S(2)}) %copy-start.1) | copy-done | bytes 16408
  17.9 0.0 copy-done.2
  17.9 0.0 copy-done.3
  17.9 6.5 %sweeps.1 = (f32[3,32,16,128]{3,2,1,0:T(8,128)}, f32[2,8,2,16,128]{4,3,2,1,0:T(8,128)S(1)}, f32[32,16,128]{2,1,0:T(8,128)S(1)}) custom-call(s32[16]{0:T(128)S(1)} %copy-done.2, s32[16]{0:T(128)S(1)} %copy-done.3, f32[16,3]{1,0:T(8,128)S(1)} %copy.8.force_ref, f32[2,8,2,16,128]{4,3,2,1,0:T(8,128)S(1)} %pad_maximum_fusion.density_ref, ...), custom_call_target="tpu_custom_call" | custom-call | tf_op jit(solution)/shard_map/sweeps/pallas_call | solution.py:359
  24.4 0.2 collective-permute-start.1
  24.6 1.2 %collective-permute-done.1 = f32[8,2,16,128]{3,2,1,0:T(8,128)S(1)} collective-permute-done((f32[8,2,16,128]{3,2,1,0:T(8,128)S(1)}, f32[8,2,16,128]{3,2,1,0:T(8,128)S(1)}, u32[]{:S(2)}, u32[]{:S(2)}) %collective-permute-start.1) | collective-permute-done | bytes 131104 | tf_op jit(solution)/shard_map/ppermute | solution.py:418
  25.9 10.0 %all_to_all.16 = f32[8,2,16,128]{3,2,1,0:T(8,128)S(1)} all-to-all(f32[8,2,16,128]{3,2,1,0:T(8,128)S(1)} %bitcast_add_fusion), channel_id=1, replica_groups={{0,2,4,6,8,10,12,14},{1,3,5,7,9,11,13,15},{16,18,20,22,24,26,28,30},{17..., dimensions={0} | all-to-all | bytes 262144 | tf_op jit(solution)/shard_map/all_to_all | solution.py:424
  35.9 9.8 %all_to_all.17 = f32[8,2,16,128]{3,2,1,0:T(8,128)S(1)} all-to-all(f32[8,2,16,128]{3,2,1,0:T(8,128)S(1)} %broadcast_in_dim.7), channel_id=1, replica_groups={{0,2,4,6,8,10,12,14},{1,3,5,7,9,11,13,15},{16,18,20,22,24,26,28,30},{17..., dimensions={0} | all-to-all | bytes 262144 | tf_op jit(solution)/shard_map/all_to_all | solution.py:424
  45.7 0.0 collective-permute-start.2
  45.7 1.3 %collective-permute-done.2 = f32[8,2,16,128]{3,2,1,0:T(8,128)S(1)} collective-permute-done((f32[8,2,16,128]{3,2,1,0:T(8,128)S(1)}, f32[8,2,16,128]{3,2,1,0:T(8,128)S(1)}, u32[]{:S(2)}, u32[]{:S(2)}) %collective-permute-start.2) | collective-permute-done | bytes 131104 | tf_op jit(solution)/shard_map/ppermute | solution.py:418
  47.1 4.2 %design.1 = f32[2,16,128]{2,1,0:T(8,128)} custom-call(s32[16]{0:T(128)S(1)} %copy-done.2, f32[2,8,2,16,128]{4,3,2,1,0:T(8,128)S(1)} %pad_maximum_fusion.1.sens_ref, f32[32,16,128]{2,1,0:T(8,128)S(1)} %get-tuple-element.6.coef_ref, f32[2,8,2,16,128]{4,3,2,1,0:T(8,128)S(1)} %pad_maximum_fusion.density_ref), custom_call_target="tpu_custom_call" | custom-call | tf_op jit(solution)/shard_map/design/pallas_call | solution.py:397
  (6 shorter events, 0.1 us)
Async XLA Ops:
  0.6 16.6 %copy-start = (f32[1,3,32,16,128]{4,3,2,1,0:T(8,128)S(1)}, f32[1,3,32,16,128]{4,3,2,1,0:T(8,128)}, u32[]{:S(2)}) copy-start(f32[1,3,32,16,128]{4,3,2,1,0:T(8,128)} %param.7) | copy-start | bytes 2359300
  15.8 1.3 %collective-permute-start = (f32[8,2,16,128]{3,2,1,0:T(8,128)S(1)}, f32[8,2,16,128]{3,2,1,0:T(8,128)S(1)}, u32[]{:S(2)}, u32[]{:S(2)}) collective-permute-start(f32[8,2,16,128]{3,2,1,0:T(8,128)S(1)} %all_to_all.15), channel_id=1, source_target_pairs={{0,1},{1,0},{2,3},{3,2},{4,5},{5,4},{6,7},{7,6},{8,9},{9,8},{10,11... | collective-permute-start | bytes 393224 | tf_op jit(solution)/shard_map/ppermute | solution.py:418
  17.2 0.7 %copy-start.1 = (s32[32,128]{1,0:T(8,128)S(1)}, s32[32,128]{1,0:T(8,128)}, u32[]{:S(2)}) copy-start(s32[32,128]{1,0:T(8,128)} %fixed_ref.1) | copy-start | bytes 49156
  17.2 0.7 %copy-start.2 = (s32[16]{0:T(128)S(1)}, s32[16]{0:T(128)}, u32[]{:S(2)}) copy-start(s32[16]{0:T(128)} %radius_ref.3) | copy-start | bytes 196
  17.2 0.7 %copy-start.3 = (s32[16]{0:T(128)S(1)}, s32[16]{0:T(128)}, u32[]{:S(2)}) copy-start(s32[16]{0:T(128)} %index_ref.1) | copy-start | bytes 196
  24.4 1.4 %collective-permute-start.1 = (f32[8,2,16,128]{3,2,1,0:T(8,128)S(1)}, f32[8,2,16,128]{3,2,1,0:T(8,128)S(1)}, u32[]{:S(2)}, u32[]{:S(2)}) collective-permute-start(f32[8,2,16,128]{3,2,1,0:T(8,128)S(1)} %slice_bitcast_fusion), channel_id=1, source_target_pairs={{0,1},{1,0},{2,3},{3,2},{4,5},{5,4},{6,7},{7,6},{8,9},{9,8},{10,11... | collective-permute-start | bytes 393224 | tf_op jit(solution)/shard_map/ppermute | solution.py:418
  45.7 1.3 %collective-permute-start.2 = (f32[8,2,16,128]{3,2,1,0:T(8,128)S(1)}, f32[8,2,16,128]{3,2,1,0:T(8,128)S(1)}, u32[]{:S(2)}, u32[]{:S(2)}) collective-permute-start(f32[8,2,16,128]{3,2,1,0:T(8,128)S(1)} %all_to_all.17), channel_id=1, source_target_pairs={{0,1},{1,0},{2,3},{3,2},{4,5},{5,4},{6,7},{7,6},{8,9},{9,8},{10,11... | collective-permute-start | bytes 393224 | tf_op jit(solution)/shard_map/ppermute | solution.py:418

commit v6 on v5

--- a/solution.py
+++ b/solution.py
@@ -109,18 +109,65 @@
         ref[place] = jnp.zeros(ref.shape[1:], ref.dtype)
 
 
-def sweep_kernel(
+def prepare_kernel(
     radius_ref,
     index_ref,
     force_ref,
-    density_ref,
     fixed_ref,
     start_ref,
+    weight_ref,
+    total_ref,
+    first_ref,
+    push_ref,
+    load_ref,
+    spot_ref,
+):
+    planes, layers, row_width = start_ref.shape[1:]
+    load_place = lax.axis_index("space")
+    shape = (layers, row_width)
+    z = spot_iota(shape, 0)
+    y = spot_iota(shape, 1)
+
+    class_weights(radius_ref, weight_ref)
+    ones = forward_planes(jnp.ones(shape, jnp.float32), weight_ref)
+    for place, (lower, upper) in enumerate(((0, 2), (1, 2), (2, 2), (2, 1), (2, 0))):
+        total_ref[place] = (
+            ones[0] + min(lower, 1) * ones[1] + min(upper, 1) * ones[1]
+            + (lower // 2) * ones[2] + (upper // 2) * ones[2]
+        )
+
+    def free_plane(x, carry):
+        free = jnp.where(z == 0, 1.0 - fixed_ref[pl.ds(x, 1), :].astype(jnp.float32), 1.0)
+        push_ref[x] = relax_factor * free
+        for part in range(3):
+            first_ref[part, x + 1] = start_ref[part, x] * free
+        return carry
+
+    lax.fori_loop(0, planes, free_plane, 0, unroll=8)
+    for part in range(3):
+        first_ref[part, 0] = jnp.zeros(shape, jnp.float32)
+        first_ref[part, planes + 1] = jnp.zeros(shape, jnp.float32)
+
+    own_index = index_ref[load_place]
+    own_z = own_index // row_width % layers
+    own_y = own_index % row_width
+    hit = (z == own_z) & (y == own_y)
+    for part in range(3):
+        load_ref[part] = jnp.where(hit, force_ref[part, load_place], 0.0)
+    spot_ref[0] = own_index // (layers * row_width)
+
+
+def sweep_kernel(
+    spot_ref,
+    load_ref,
+    weight_ref,
+    total_ref,
+    push_ref,
+    density_ref,
+    first_ref,
     disp_ref,
     sens_ref,
     coef_ref,
-    weight_ref,
-    total_ref,
     near_ref,
     side_ref,
     far_ref,
@@ -131,29 +178,19 @@
     right_ref,
     left_ref,
     rate_ref,
-    keep_ref,
-    first_ref,
     second_ref,
+    third_ref,
 ):
     cores, chips, own_planes, layers, row_width = density_ref.shape
     planes = cores * chips * own_planes
-    load_cases = index_ref.shape[0]
-    load_place = lax.axis_index("space")
+    load_cases = lax.axis_size("space")
     shape = (layers, row_width)
     z = spot_iota(shape, 0)
     y = spot_iota(shape, 1)
     zero = jnp.zeros(shape, jnp.float32)
 
-    class_weights(radius_ref, weight_ref)
     for ref in (side_ref, far_ref):
         zero_edges(ref)
-
-    ones = forward_planes(jnp.ones(shape, jnp.float32), weight_ref)
-    for place, (lower, upper) in enumerate(((0, 2), (1, 2), (2, 2), (2, 1), (2, 0))):
-        total_ref[place] = (
-            ones[0] + min(lower, 1) * ones[1] + min(upper, 1) * ones[1]
-            + (lower // 2) * ones[2] + (upper // 2) * ones[2]
-        )
 
     def filter_plane(x, carry):
         near, side, far = forward_planes(
@@ -184,10 +221,10 @@
 
     across_ref[0] = zero
     across_ref[planes] = zero
-    first_ref[:, 0] = jnp.zeros((3,) + shape, jnp.float32)
-    second_ref[:, 0] = jnp.zeros((3,) + shape, jnp.float32)
-    first_ref[:, planes + 1] = jnp.zeros((3,) + shape, jnp.float32)
-    second_ref[:, planes + 1] = jnp.zeros((3,) + shape, jnp.float32)
+    for ref in (second_ref, third_ref):
+        for part in range(3):
+            ref[part, 0] = zero
+            ref[part, planes + 1] = zero
 
     def face_plane(x, carry):
         modulus = modulus_ref[x]
@@ -204,29 +241,21 @@
         down_ref[x] = down
         right_ref[x] = right
         left_ref[x] = left
-        free = jnp.where(z == 0, 1.0 - fixed_ref[pl.ds(x, 1), :].astype(jnp.float32), 1.0)
-        keep_ref[x] = (1.0 - relax_factor) * free
         sums = (carry + ahead, up + down, left + right)
         every = sums[0] + sums[1] + sums[2]
-        push = relax_factor * free
+        push = push_ref[x]
         for part in range(3):
             rate_ref[part, x] = push / (every + sums[part])
-            first_ref[part, x + 1] = start_ref[part, x] * free
         return ahead
 
     lax.fori_loop(0, planes, face_plane, zero, unroll=8)
 
-    own_index = index_ref[load_place]
-    own_x = own_index // (layers * row_width)
-    own_z = own_index // row_width % layers
-    own_y = own_index % row_width
-    hit = (z == own_z) & (y == own_y)
+    own_x = spot_ref[0]
 
     def sweep(source, target, lead):
         def sweep_plane(x, carry):
             before, after = across_ref[x], across_ref[x + 1]
             up, down, right, left = up_ref[x], down_ref[x], right_ref[x], left_ref[x]
-            keep = keep_ref[x]
             for part in range(3):
                 here = source[part, x + 1]
                 pulls = [
@@ -235,18 +264,19 @@
                     right * pltpu.roll(here, row_width - 1, 1) + left * pltpu.roll(here, 1, 1),
                 ]
                 pull = pulls[0] + pulls[1] + pulls[2] + pulls[part]
-                target[part, x + lead] = keep * here + rate_ref[part, x] * pull
+                target[part, x + lead] = (1.0 - relax_factor) * here + rate_ref[part, x] * pull
             return carry
 
         lax.fori_loop(0, planes, sweep_plane, 0, unroll=8)
         for part in range(3):
-            push = rate_ref[part, own_x] * force_ref[load_place, part]
-            target[part, own_x + lead] += jnp.where(hit, push, 0.0)
-
-    stages = [first_ref, second_ref]
+            target[part, own_x + lead] += rate_ref[part, own_x] * load_ref[part]
+
+    source = first_ref
     for turn in range(SWEEPS - 1):
-        sweep(stages[turn % 2], stages[(turn + 1) % 2], 1)
-    sweep(stages[(SWEEPS - 1) % 2], disp_ref, 0)
+        target = (second_ref, third_ref)[turn % 2]
+        sweep(source, target, 1)
+        source = target
+    sweep(source, disp_ref, 0)
 
     def energy_plane(x, carry):
         later = jnp.minimum(x + 1, planes - 1)
@@ -269,12 +299,11 @@
 
 
 def design_kernel(
-    radius_ref,
+    weight_ref,
     sens_ref,
     coef_ref,
     density_ref,
     new_ref,
-    weight_ref,
     near_ref,
     side_ref,
     far_ref,
@@ -287,7 +316,6 @@
     place = lax.axis_index("space")
     shape = (layers, row_width)
     zero = jnp.zeros(shape, jnp.float32)
-    class_weights(radius_ref, weight_ref)
     for ref in (side_ref, far_ref):
         zero_edges(ref)
 
@@ -348,10 +376,37 @@
 KERNEL_VMEM = 24 * 2**20
 
 
-def sweep_call(radius, load_index, load_force, density, fixed, displacement):
+def floats(*shape):
+    return jax.ShapeDtypeStruct(shape, jnp.float32)
+
+
+def prepare_call(radius, load_index, load_force, fixed, displacement):
+    planes, layers, row_width = displacement.shape[1:]
+    return pl.pallas_call(
+        prepare_kernel,
+        out_shape=[
+            floats(len(ALL_SQUARES), layers, row_width),
+            floats(2 * window_reach + 1, layers, row_width),
+            floats(3, planes + 2, layers, row_width),
+            floats(planes, layers, row_width),
+            floats(3, layers, row_width),
+            jax.ShapeDtypeStruct((1,), jnp.int32),
+        ],
+        in_specs=[in_smem()] * 3 + [in_vmem()] * 2,
+        out_specs=[in_vmem()] * 5 + [in_smem()],
+        compiler_params=pltpu.CompilerParams(vmem_limit_bytes=KERNEL_VMEM),
+        cost_estimate=pl.CostEstimate(
+            flops=4 * displacement.size,
+            bytes_accessed=8 * displacement.size,
+            transcendentals=0,
+        ),
+        name="prepare",
+    )(radius, load_index, load_force, fixed, displacement)
+
+
+def sweep_call(spot, load, weights, totals, push, density, first):
     cores, chips, own_planes, layers, row_width = density.shape
     planes = cores * chips * own_planes
-    grid_field = (planes, layers, row_width)
 
     def scratch(*lead):
         return pltpu.VMEM(lead + (layers, row_width), jnp.float32)
@@ -359,15 +414,13 @@
     return pl.pallas_call(
         sweep_kernel,
         out_shape=[
-            jax.ShapeDtypeStruct((3,) + grid_field, jnp.float32),
-            jax.ShapeDtypeStruct(density.shape, jnp.float32),
-            jax.ShapeDtypeStruct(grid_field, jnp.float32),
+            floats(3, planes, layers, row_width),
+            floats(*density.shape),
+            floats(planes, layers, row_width),
         ],
-        in_specs=[in_smem()] * 3 + [in_vmem()] * 3,
+        in_specs=[in_smem()] + [in_vmem()] * 6,
         out_specs=[in_vmem()] * 3,
         scratch_shapes=[
-            scratch(len(ALL_SQUARES)),
-            scratch(2 * window_reach + 1),
             scratch(planes + 4),
             scratch(planes + 4),
             scratch(planes + 4),
@@ -378,16 +431,15 @@
             scratch(planes),
             scratch(planes),
             scratch(3, planes),
-            scratch(planes),
             scratch(3, planes + 2),
             scratch(3, planes + 2),
         ],
         compiler_params=pltpu.CompilerParams(vmem_limit_bytes=KERNEL_VMEM),
         name="sweeps",
-    )(radius, load_index, load_force, density, fixed, displacement)
-
-
-def design_call(radius, sens, coef, density):
+    )(spot, load, weights, totals, push, density, first)
+
+
+def design_call(weights, sens, coef, density):
     cores, chips, own_planes, layers, row_width = density.shape
     planes = cores * chips * own_planes
 
@@ -397,10 +449,9 @@
     return pl.pallas_call(
         design_kernel,
         out_shape=jax.ShapeDtypeStruct((own_planes, layers, row_width), jnp.float32),
-        in_specs=[in_smem()] + [in_vmem()] * 3,
+        in_specs=[in_vmem()] * 4,
         out_specs=in_vmem(),
         scratch_shapes=[
-            scratch(len(ALL_SQUARES)),
             scratch(planes + 4),
             scratch(planes + 4),
             scratch(planes + 4),
@@ -410,7 +461,7 @@
         ],
         compiler_params=pltpu.CompilerParams(vmem_limit_bytes=KERNEL_VMEM),
         name="design",
-    )(radius, sens, coef, density)
+    )(weights, sens, coef, density)
 
 
 def other_core(block):
@@ -424,10 +475,11 @@
     return lax.all_to_all(pieces, "space", 0, 0, axis_index_groups=groups)
 
 
-def gathered(block):
+def gathered(block, beside=()):
     chips = lax.axis_size("space") // 2
     same = between_chips(jnp.broadcast_to(block[None], (chips,) + block.shape))
-    return jnp.stack([same, other_core(same)])
+    same, beside = lax.optimization_barrier((same, beside))
+    return jnp.stack([same, other_core(same)]), beside
 
 
 def scattered_sum(pieces):
@@ -435,12 +487,12 @@
 
 
 def one_slab(density, displacement, fixed, load_index, load_force, radius):
-    whole = gathered(density)
-    new_displacement, sens, coef = sweep_call(
-        radius, load_index, load_force, whole, fixed, displacement[0]
-    )
-    sens = gathered(scattered_sum(sens))
-    new_density = design_call(radius, sens, coef, whole)
+    prepared = prepare_call(radius, load_index, load_force.T, fixed, displacement[0])
+    whole, prepared = gathered(density, prepared)
+    weights, totals, first, push, load, spot = prepared
+    new_displacement, sens, coef = sweep_call(spot, load, weights, totals, push, whole, first)
+    sens, _ = gathered(scattered_sum(sens))
+    new_density = design_call(weights, sens, coef, whole)
     return new_density, new_displacement[None]
 
 

time: 51.7 us -> 51.3 us (level)
  blocking collectives: 34.2 us -> 19.8 us
  starting transfers between devices: 0.22 us -> 7.61 us
  waiting for transfers between devices: 3.13 us -> 8.13 us
  local copies, waits for them, and re-layouts: 2.26 us -> 3.2 us
  Pallas kernels: 10.7 us -> 11.3 us
    all_to_all x3 -> x2, blocking collectives: 34.2 us -> 19.8 us  [between_chips(): return lax.all_to_all(pieces, 'space', 0, 0, axis_index_groups=groups)]
    all_to_all x0 -> x1, starting transfers between devices: none -> 7.38 us  [between_chips(): return lax.all_to_all(pieces, 'space', 0, 0, axis_index_groups=groups)]
    all_to_all x0 -> x1, waiting for transfers between devices: none -> 4.24 us  [between_chips(): return lax.all_to_all(pieces, 'space', 0, 0, axis_index_groups=groups)]
    pallas_call x1 -> x2, Pallas kernels: 6.5 us -> 7.69 us  [the longest x1 6.42 us: sweep_call(): pl.pallas_call(sweep_kernel, out_shape=[floats(3, planes, layers, row_wid...]
    ppermute x3, waiting for transfers between devices: 3.13 us -> 3.89 us  [other_core(): return lax.ppermute(block, 'space', [(i, i ^ 1) for i in range(devices)])]
    broadcast_in_dim x2, local copies, waits for them, and re-layouts: 0.81 us -> 1.39 us  [gathered(): same = between_chips(jnp.broadcast_to(block[None], (chips,) + block.shape))]
    pallas_call x1, Pallas kernels: 4.19 us -> 3.64 us  [design_call(): pl.pallas_call(design_kernel, out_shape=jax.ShapeDtypeStruct((own_planes,...]
    unnamed x9 -> x10, local copies, waits for them, and re-layouts: 1.44 us -> 1.79 us
  transfers between devices with their start and end apart: 3 -> 4, of which waited for: 3 -> 4; matrix products, arithmetic and copies ran while one was open for 1% -> 0% of each run, Pallas kernels for 0% -> 2%
where the time goes in v6:
time: 51.3 us; the launch traced here: 50.8 us
  blocking collectives  19.8 us (39%)
  Pallas kernels  11.3 us (22%)
  waiting for transfers between devices  8.13 us (16%)
  starting transfers between devices  7.61 us (15%)
  local copies, waits for them, and re-layouts  3.2 us (6%)
  between operations  0.7 us (1%)
    all_to_all x2, blocking collectives, between_chips(): return lax.all_to_all(pieces, 'space', 0, 0, axis_index_groups=groups)  19.8 us
    all_to_all x1, starting transfers between devices, between_chips(): return lax.all_to_all(pieces, 'space', 0, 0, axis_index_groups=groups)  7.38 us
    pallas_call x1, Pallas kernels, sweep_call(): pl.pallas_call(sweep_kernel, out_shape=[floats(3, planes, layers, row_wid...  6.42 us
    all_to_all x1, waiting for transfers between devices, between_chips(): return lax.all_to_all(pieces, 'space', 0, 0, axis_index_groups=groups)  4.24 us
    ppermute x3, waiting for transfers between devices, other_core(): return lax.ppermute(block, 'space', [(i, i ^ 1) for i in range(devices)])  3.89 us
    pallas_call x1, Pallas kernels, design_call(): pl.pallas_call(design_kernel, out_shape=jax.ShapeDtypeStruct((own_planes,...  3.64 us
    unnamed x10, local copies, waits for them, and re-layouts  1.79 us
    broadcast_in_dim x2, local copies, waits for them, and re-layouts, gathered(): same = between_chips(jnp.broadcast_to(block[None], (chips,) + block.shape))  1.39 us
  transfers between devices with their start and end apart: 4, of which 4 were waited for; matrix products, arithmetic and copies ran while one was open for 0% of the time, Pallas kernels for 2%

profile of v6, /device:TPU:0, one launch (start us, length us, event | category | flops | bytes accessed | tf_op | source)
XLA Modules:
  0.0 50.8 jit_solution(17679070873909840626)
XLA Ops:
  0.6 1.4 %broadcast_in_dim.6 = f32[8,2,16,128]{3,2,1,0:T(8,128)} broadcast(f32[2,16,128]{2,1,0:T(8,128)} %param.6), dimensions={1,2,3} | broadcast | bytes 147456 | tf_op jit(solution)/shard_map/broadcast_in_dim | solution.py:480
  2.0 0.0 copy-start.1
  2.0 7.4 %all-to-all-start = ((f32[8,2,16,128]{3,2,1,0:T(8,128)}), f32[8,2,16,128]{3,2,1,0:T(8,128)S(1)}, u32[]{:S(2)}, u32[]{:S(2)}) async-start(f32[8,2,16,128]{3,2,1,0:T(8,128)} %broadcast_in_dim.6), calls=%async_computation | async-start | bytes 262144 | tf_op jit(solution)/shard_map/all_to_all | solution.py:475
  9.4 0.0 copy-start.2
  9.4 0.0 copy-start.3
  9.4 0.0 copy-start.4
  9.4 0.0 copy-done.1
  9.4 0.6 %copy-done.2 = f32[16,3]{0,1:T(4,128)S(1)} copy-done((f32[16,3]{0,1:T(4,128)S(1)}, f32[16,3]{0,1:T(4,128)}, u32[]{:S(2)}) %copy-start.2) | copy-done | bytes 216
  10.1 0.0 copy-done.3
  10.1 0.0 copy-done.4
  10.1 0.0 copy-start
  10.1 1.1 %copy-done = f32[1,3,32,16,128]{4,3,2,1,0:T(8,128)S(1)} copy-done((f32[1,3,32,16,128]{4,3,2,1,0:T(8,128)S(1)}, f32[1,3,32,16,128]{4,3,2,1,0:T(8,128)}, u32[]{:S(2)}) %copy-start) | copy-done | bytes 786456
  11.2 1.3 %prepare.1 = (f32[10,16,128]{2,1,0:T(8,128)S(1)}, f32[5,16,128]{2,1,0:T(8,128)S(1)}, f32[3,34,16,128]{3,2,1,0:T(8,128)S(1)}, f32[32,16,128]{2,1,0:T(8,128)S(1)}, f32[3,16,128]{2,1,0:T(8,128)S(1)}, /*index=5*/s32[1]{0:T(128)}) custom-call(s32[16]{0:T(128)S(1)} %copy-done.3, s32[16]{0:T(128)S(1)} %copy-done.4, f32[3,16]{1,0:T(4,128)S(1)} %bitcast.12, ...), custom_call_target="tpu_custom_call" | custom-call | flops 786432 | bytes 1572864 | tf_op jit(solution)/shard_map/prepare/pallas_call | solution.py:385
  12.5 4.2 %all-to-all-done = f32[8,2,16,128]{3,2,1,0:T(8,128)S(1)} async-done(((f32[8,2,16,128]{3,2,1,0:T(8,128)}), f32[8,2,16,128]{3,2,1,0:T(8,128)S(1)}, u32[]{:S(2)}, u32[]{:S(2)}) %all-to-all-start) | async-done | bytes 131104 | tf_op jit(solution)/shard_map/all_to_all | solution.py:475
  16.7 0.0 collective-permute-start
  16.7 1.3 %collective-permute-done = f32[8,2,16,128]{3,2,1,0:T(8,128)S(1)} collective-permute-done((f32[8,2,16,128]{3,2,1,0:T(8,128)S(1)}, f32[8,2,16,128]{3,2,1,0:T(8,128)S(1)}, u32[]{:S(2)}, u32[]{:S(2)}) %collective-permute-start) | collective-permute-done | bytes 131104 | tf_op jit(solution)/shard_map/ppermute | solution.py:469
  18.1 6.4 %sweeps.1 = (f32[3,32,16,128]{3,2,1,0:T(8,128)}, f32[2,8,2,16,128]{4,3,2,1,0:T(8,128)S(1)}, f32[32,16,128]{2,1,0:T(8,128)S(1)}) custom-call(s32[1]{0:T(128)} %get-tuple-element.25.spot_ref, f32[3,16,128]{2,1,0:T(8,128)S(1)} %get-tuple-element.26.load_ref, f32[10,16,128]{2,1,0:T(8,128)S(1)} %get-tuple-element.24.weight_ref, ...), custom_call_target="tpu_custom_call" | custom-call | tf_op jit(solution)/shard_map/sweeps/pallas_call | solution.py:414
  24.5 0.2 collective-permute-start.1
  24.8 1.2 %collective-permute-done.1 = f32[8,2,16,128]{3,2,1,0:T(8,128)S(1)} collective-permute-done((f32[8,2,16,128]{3,2,1,0:T(8,128)S(1)}, f32[8,2,16,128]{3,2,1,0:T(8,128)S(1)}, u32[]{:S(2)}, u32[]{:S(2)}) %collective-permute-start.1) | collective-permute-done | bytes 131104 | tf_op jit(solution)/shard_map/ppermute | solution.py:469
  26.0 10.0 %all_to_all.15 = f32[8,2,16,128]{3,2,1,0:T(8,128)S(1)} all-to-all(f32[8,2,16,128]{3,2,1,0:T(8,128)S(1)} %bitcast_add_fusion), channel_id=1, replica_groups={{0,2,4,6,8,10,12,14},{1,3,5,7,9,11,13,15},{16,18,20,22,24,26,28,30},{17..., dimensions={0} | all-to-all | bytes 262144 | tf_op jit(solution)/shard_map/all_to_all | solution.py:475
  36.0 9.8 %all_to_all.16 = f32[8,2,16,128]{3,2,1,0:T(8,128)S(1)} all-to-all(f32[8,2,16,128]{3,2,1,0:T(8,128)S(1)} %broadcast_in_dim.7), channel_id=1, replica_groups={{0,2,4,6,8,10,12,14},{1,3,5,7,9,11,13,15},{16,18,20,22,24,26,28,30},{17..., dimensions={0} | all-to-all | bytes 262144 | tf_op jit(solution)/shard_map/all_to_all | solution.py:475
  45.8 0.0 collective-permute-start.2
  45.8 1.3 %collective-permute-done.2 = f32[8,2,16,128]{3,2,1,0:T(8,128)S(1)} collective-permute-done((f32[8,2,16,128]{3,2,1,0:T(8,128)S(1)}, f32[8,2,16,128]{3,2,1,0:T(8,128)S(1)}, u32[]{:S(2)}, u32[]{:S(2)}) %collective-permute-start.2) | collective-permute-done | bytes 131104 | tf_op jit(solution)/shard_map/ppermute | solution.py:469
  47.2 3.6 %design.1 = f32[2,16,128]{2,1,0:T(8,128)} custom-call(f32[10,16,128]{2,1,0:T(8,128)S(1)} %get-tuple-element.24.weight_ref, f32[2,8,2,16,128]{4,3,2,1,0:T(8,128)S(1)} %pad_maximum_fusion.1.sens_ref, f32[32,16,128]{2,1,0:T(8,128)S(1)} %get-tuple-element.32.coef_ref, f32[2,8,2,16,128]{4,3,2,1,0:T(8,128)S(1)} %pad_maximum_fusion.density_ref), custom_call_target="tpu_custom_call" | custom-call | tf_op jit(solution)/shard_map/design/pallas_call | solution.py:449
  (6 shorter events, 0.1 us)
Async XLA Ops:
  2.0 7.4 %copy-start.1 = (s32[32,128]{1,0:T(8,128)S(1)}, s32[32,128]{1,0:T(8,128)}, u32[]{:S(2)}) copy-start(s32[32,128]{1,0:T(8,128)} %fixed_ref.1) | copy-start | bytes 49156
  2.0 14.7 %all-to-all-start = ((f32[8,2,16,128]{3,2,1,0:T(8,128)}), f32[8,2,16,128]{3,2,1,0:T(8,128)S(1)}, u32[]{:S(2)}, u32[]{:S(2)}) async-start(f32[8,2,16,128]{3,2,1,0:T(8,128)} %broadcast_in_dim.6), calls=%async_computation | async-start | bytes 262144 | tf_op jit(solution)/shard_map/all_to_all | solution.py:475
  9.4 0.7 %copy-start.2 = (f32[16,3]{0,1:T(4,128)S(1)}, f32[16,3]{0,1:T(4,128)}, u32[]{:S(2)}) copy-start(f32[16,3]{0,1:T(4,128)} %param.10) | copy-start | bytes 580
  9.4 0.7 %copy-start.3 = (s32[16]{0:T(128)S(1)}, s32[16]{0:T(128)}, u32[]{:S(2)}) copy-start(s32[16]{0:T(128)} %radius_ref.1) | copy-start | bytes 196
  9.4 0.7 %copy-start.4 = (s32[16]{0:T(128)S(1)}, s32[16]{0:T(128)}, u32[]{:S(2)}) copy-start(s32[16]{0:T(128)} %index_ref.1) | copy-start | bytes 196
  10.1 1.1 %copy-start = (f32[1,3,32,16,128]{4,3,2,1,0:T(8,128)S(1)}, f32[1,3,32,16,128]{4,3,2,1,0:T(8,128)}, u32[]{:S(2)}) copy-start(f32[1,3,32,16,128]{4,3,2,1,0:T(8,128)} %param.7) | copy-start | bytes 2359300
  16.7 1.3 %collective-permute-start = (f32[8,2,16,128]{3,2,1,0:T(8,128)S(1)}, f32[8,2,16,128]{3,2,1,0:T(8,128)S(1)}, u32[]{:S(2)}, u32[]{:S(2)}) collective-permute-start(f32[8,2,16,128]{3,2,1,0:T(8,128)S(1)} %all-to-all-done), channel_id=1, source_target_pairs={{0,1},{1,0},{2,3},{3,2},{4,5},{5,4},{6,7},{7,6},{8,9},{9,8},{10,11... | collective-permute-start | bytes 393224 | tf_op jit(solution)/shard_map/ppermute | solution.py:469
  24.5 1.4 %collective-permute-start.1 = (f32[8,2,16,128]{3,2,1,0:T(8,128)S(1)}, f32[8,2,16,128]{3,2,1,0:T(8,128)S(1)}, u32[]{:S(2)}, u32[]{:S(2)}) collective-permute-start(f32[8,2,16,128]{3,2,1,0:T(8,128)S(1)} %slice_bitcast_fusion), channel_id=1, source_target_pairs={{0,1},{1,0},{2,3},{3,2},{4,5},{5,4},{6,7},{7,6},{8,9},{9,8},{10,11... | collective-permute-start | bytes 393224 | tf_op jit(solution)/shard_map/ppermute | solution.py:469
  45.8 1.3 %collective-permute-start.2 = (f32[8,2,16,128]{3,2,1,0:T(8,128)S(1)}, f32[8,2,16,128]{3,2,1,0:T(8,128)S(1)}, u32[]{:S(2)}, u32[]{:S(2)}) collective-permute-start(f32[8,2,16,128]{3,2,1,0:T(8,128)S(1)} %all_to_all.16), channel_id=1, source_target_pairs={{0,1},{1,0},{2,3},{3,2},{4,5},{5,4},{6,7},{7,6},{8,9},{9,8},{10,11... | collective-permute-start | bytes 393224 | tf_op jit(solution)/shard_map/ppermute | solution.py:469

commit v7 on v6

--- a/solution.py
+++ b/solution.py
@@ -469,15 +469,17 @@
     return lax.ppermute(block, "space", [(i, i ^ 1) for i in range(devices)])
 
 
+def same_core_groups():
+    devices = lax.axis_size("space")
+    return [list(range(core, devices, 2)) for core in range(2)]
+
+
 def between_chips(pieces):
-    devices = lax.axis_size("space")
-    groups = [list(range(core, devices, 2)) for core in range(2)]
-    return lax.all_to_all(pieces, "space", 0, 0, axis_index_groups=groups)
+    return lax.all_to_all(pieces, "space", 0, 0, axis_index_groups=same_core_groups())
 
 
 def gathered(block, beside=()):
-    chips = lax.axis_size("space") // 2
-    same = between_chips(jnp.broadcast_to(block[None], (chips,) + block.shape))
+    same = lax.all_gather(block, "space", axis_index_groups=same_core_groups())
     same, beside = lax.optimization_barrier((same, beside))
     return jnp.stack([same, other_core(same)]), beside
 

time: 51.3 us -> 94 us (1.83)
  blocking collectives: 19.8 us -> 75.7 us
  starting transfers between devices: 7.61 us -> 0.28 us
  waiting for transfers between devices: 8.13 us -> 3.88 us
  local copies, waits for them, and re-layouts: 3.2 us -> 1.82 us
    all_gather x0 -> x2, blocking collectives: none -> 63.1 us  [gathered(): same = lax.all_gather(block, 'space', axis_index_groups=same_core_groups())]
    all_to_all x1 -> x0, starting transfers between devices: 7.38 us -> none  [between_chips(): return lax.all_to_all(pieces, 'space', 0, 0, axis_index_groups=groups)]
    all_to_all x2 -> x1, blocking collectives: 19.8 us -> 12.6 us  [between_chips(): lax.all_to_all(pieces, 'space', 0, 0, axis_index_groups=same_core_groups())]
    all_to_all x1 -> x0, waiting for transfers between devices: 4.24 us -> none  [between_chips(): return lax.all_to_all(pieces, 'space', 0, 0, axis_index_groups=groups)]
    broadcast_in_dim x2 -> x0, local copies, waits for them, and re-layouts: 1.39 us -> none  [gathered(): same = between_chips(jnp.broadcast_to(block[None], (chips,) + block.shape))]
  transfers between devices with their start and end apart: 4 -> 3, of which waited for: 4 -> 3; matrix products, arithmetic and copies ran while one was open for 0% -> 0% of each run, Pallas kernels for 2% -> 0%
where the time goes in v7:
time: 94 us; the launch traced here: 93.7 us
  blocking collectives  75.7 us (81%)
  Pallas kernels  11.3 us (12%)
  waiting for transfers between devices  3.88 us (4%)
  local copies, waits for them, and re-layouts  1.82 us (2%)
    all_gather x2, blocking collectives, gathered(): same = lax.all_gather(block, 'space', axis_index_groups=same_core_groups())  63.1 us
    all_to_all x1, blocking collectives, between_chips(): lax.all_to_all(pieces, 'space', 0, 0, axis_index_groups=same_core_groups())  12.6 us
    pallas_call x1, Pallas kernels, sweep_call(): pl.pallas_call(sweep_kernel, out_shape=[floats(3, planes, layers, row_wid...  6.43 us
    ppermute x3, waiting for transfers between devices, other_core(): return lax.ppermute(block, 'space', [(i, i ^ 1) for i in range(devices)])  3.88 us
    pallas_call x1, Pallas kernels, design_call(): pl.pallas_call(design_kernel, out_shape=jax.ShapeDtypeStruct((own_planes,...  3.64 us
  transfers between devices with their start and end apart: 3, of which 3 were waited for; matrix products, arithmetic and copies ran while one was open for 0% of the time, Pallas kernels for 0%

profile of v7, /device:TPU:0, one launch (start us, length us, event | category | flops | bytes accessed | tf_op | source)
XLA Modules:
  0.0 93.7 jit_solution(6047547409360375321)
XLA Ops:
  0.6 0.0 copy-start.1
  0.6 32.5 %all-gather = f32[16,16,128]{2,1,0:T(8,128)S(1)} all-gather(f32[2,16,128]{2,1,0:T(8,128)} %param.6), channel_id=2, replica_groups={{0,2,4,6,8,10,12,14},{1,3,5,7,9,11,13,15},{16,18,20,22,24,26,28,30},{17..., dimensions={0}, use_global_device_ids=true | all-gather | bytes 147456 | tf_op jit(solution)/shard_map/all_gather | solution.py:482
  33.2 0.0 copy-start.2
  33.2 0.0 copy-start.3
  33.2 0.0 copy-start.4
  33.2 0.0 copy-done.1
  33.2 0.7 copy-done.2
  33.8 0.0 copy-done.3
  33.8 0.0 copy-done.4
  33.8 0.0 copy-start
  33.8 1.1 %copy-done = f32[1,3,32,16,128]{4,3,2,1,0:T(8,128)S(1)} copy-done((f32[1,3,32,16,128]{4,3,2,1,0:T(8,128)S(1)}, f32[1,3,32,16,128]{4,3,2,1,0:T(8,128)}, u32[]{:S(2)}) %copy-start) | copy-done | bytes 786456
  35.0 1.3 %prepare.1 = (f32[10,16,128]{2,1,0:T(8,128)S(1)}, f32[5,16,128]{2,1,0:T(8,128)S(1)}, f32[3,34,16,128]{3,2,1,0:T(8,128)S(1)}, f32[32,16,128]{2,1,0:T(8,128)S(1)}, f32[3,16,128]{2,1,0:T(8,128)S(1)}, /*index=5*/s32[1]{0:T(128)}) custom-call(s32[16]{0:T(128)S(1)} %copy-done.3, s32[16]{0:T(128)S(1)} %copy-done.4, f32[3,16]{1,0:T(4,128)S(1)} %bitcast.14, ...), custom_call_target="tpu_custom_call" | custom-call | flops 786432 | bytes 1572864 | tf_op jit(solution)/shard_map/prepare/pallas_call | solution.py:385
  36.3 0.1 collective-permute-start
  36.3 1.3 %collective-permute-done = f32[8,2,16,128]{3,2,1,0:T(8,128)S(1)} collective-permute-done((f32[8,2,16,128]{3,2,1,0:T(8,128)S(1)}, f32[8,2,16,128]{3,2,1,0:T(8,128)S(1)}, u32[]{:S(2)}, u32[]{:S(2)}) %collective-permute-start) | collective-permute-done | bytes 131104 | tf_op jit(solution)/shard_map/ppermute | solution.py:469
  37.7 6.4 %sweeps.1 = (f32[3,32,16,128]{3,2,1,0:T(8,128)}, f32[2,8,2,16,128]{4,3,2,1,0:T(8,128)S(1)}, f32[32,16,128]{2,1,0:T(8,128)S(1)}) custom-call(s32[1]{0:T(128)} %get-tuple-element.25.spot_ref, f32[3,16,128]{2,1,0:T(8,128)S(1)} %get-tuple-element.26.load_ref, f32[10,16,128]{2,1,0:T(8,128)S(1)} %get-tuple-element.24.weight_ref, ...), custom_call_target="tpu_custom_call" | custom-call | tf_op jit(solution)/shard_map/sweeps/pallas_call | solution.py:414
  44.1 0.2 collective-permute-start.1
  44.3 1.2 %collective-permute-done.1 = f32[8,2,16,128]{3,2,1,0:T(8,128)S(1)} collective-permute-done((f32[8,2,16,128]{3,2,1,0:T(8,128)S(1)}, f32[8,2,16,128]{3,2,1,0:T(8,128)S(1)}, u32[]{:S(2)}, u32[]{:S(2)}) %collective-permute-start.1) | collective-permute-done | bytes 131104 | tf_op jit(solution)/shard_map/ppermute | solution.py:469
  45.6 12.6 %all_to_all.5 = f32[8,2,16,128]{3,2,1,0:T(8,128)S(1)} all-to-all(f32[8,2,16,128]{3,2,1,0:T(8,128)S(1)} %bitcast_add_fusion), channel_id=1, replica_groups={{0,2,4,6,8,10,12,14},{1,3,5,7,9,11,13,15},{16,18,20,22,24,26,28,30},{17..., dimensions={0} | all-to-all | bytes 262144 | tf_op jit(solution)/shard_map/all_to_all | solution.py:478
  58.2 30.6 %all-gather.1 = f32[16,16,128]{2,1,0:T(8,128)S(1)} all-gather(f32[2,16,128]{2,1,0:T(8,128)S(1)} %reduce_sum.9), channel_id=3, replica_groups={{0,2,4,6,8,10,12,14},{1,3,5,7,9,11,13,15},{16,18,20,22,24,26,28,30},{17..., dimensions={0}, use_global_device_ids=true | all-gather | bytes 147456 | tf_op jit(solution)/shard_map/all_gather | solution.py:482
  88.7 0.0 collective-permute-start.2
  88.7 1.3 %collective-permute-done.2 = f32[8,2,16,128]{3,2,1,0:T(8,128)S(1)} collective-permute-done((f32[8,2,16,128]{3,2,1,0:T(8,128)S(1)}, f32[8,2,16,128]{3,2,1,0:T(8,128)S(1)}, u32[]{:S(2)}, u32[]{:S(2)}) %collective-permute-start.2) | collective-permute-done | bytes 131104 | tf_op jit(solution)/shard_map/ppermute | solution.py:469
  90.1 3.6 %design.1 = f32[2,16,128]{2,1,0:T(8,128)} custom-call(f32[10,16,128]{2,1,0:T(8,128)S(1)} %get-tuple-element.24.weight_ref, f32[2,8,2,16,128]{4,3,2,1,0:T(8,128)S(1)} %pad_maximum_fusion.1.sens_ref, f32[32,16,128]{2,1,0:T(8,128)S(1)} %get-tuple-element.32.coef_ref, f32[2,8,2,16,128]{4,3,2,1,0:T(8,128)S(1)} %pad_maximum_fusion.density_ref), custom_call_target="tpu_custom_call" | custom-call | tf_op jit(solution)/shard_map/design/pallas_call | solution.py:449
  (5 shorter events, 0.1 us)
Async XLA Ops:
  0.6 32.5 %copy-start.1 = (s32[32,128]{1,0:T(8,128)S(1)}, s32[32,128]{1,0:T(8,128)}, u32[]{:S(2)}) copy-start(s32[32,128]{1,0:T(8,128)} %fixed_ref.1) | copy-start | bytes 49156
  33.2 0.7 copy-start.2
  33.2 0.7 copy-start.3
  33.2 0.7 copy-start.4
  33.8 1.1 %copy-start = (f32[1,3,32,16,128]{4,3,2,1,0:T(8,128)S(1)}, f32[1,3,32,16,128]{4,3,2,1,0:T(8,128)}, u32[]{:S(2)}) copy-start(f32[1,3,32,16,128]{4,3,2,1,0:T(8,128)} %param.7) | copy-start | bytes 2359300
  36.3 1.4 %collective-permute-start = (f32[8,2,16,128]{3,2,1,0:T(8,128)S(1)}, f32[8,2,16,128]{3,2,1,0:T(8,128)S(1)}, u32[]{:S(2)}, u32[]{:S(2)}) collective-permute-start(f32[8,2,16,128]{3,2,1,0:T(8,128)S(1)} %bitcast.15), channel_id=1, source_target_pairs={{0,1},{1,0},{2,3},{3,2},{4,5},{5,4},{6,7},{7,6},{8,9},{9,8},{10,11... | collective-permute-start | bytes 393224 | tf_op jit(solution)/shard_map/ppermute | solution.py:469
  44.1 1.4 %collective-permute-start.1 = (f32[8,2,16,128]{3,2,1,0:T(8,128)S(1)}, f32[8,2,16,128]{3,2,1,0:T(8,128)S(1)}, u32[]{:S(2)}, u32[]{:S(2)}) collective-permute-start(f32[8,2,16,128]{3,2,1,0:T(8,128)S(1)} %slice_bitcast_fusion), channel_id=1, source_target_pairs={{0,1},{1,0},{2,3},{3,2},{4,5},{5,4},{6,7},{7,6},{8,9},{9,8},{10,11... | collective-permute-start | bytes 393224 | tf_op jit(solution)/shard_map/ppermute | solution.py:469
  88.7 1.3 %collective-permute-start.2 = (f32[8,2,16,128]{3,2,1,0:T(8,128)S(1)}, f32[8,2,16,128]{3,2,1,0:T(8,128)S(1)}, u32[]{:S(2)}, u32[]{:S(2)}) collective-permute-start(f32[8,2,16,128]{3,2,1,0:T(8,128)S(1)} %bitcast.17), channel_id=1, source_target_pairs={{0,1},{1,0},{2,3},{3,2},{4,5},{5,4},{6,7},{7,6},{8,9},{9,8},{10,11... | collective-permute-start | bytes 393224 | tf_op jit(solution)/shard_map/ppermute | solution.py:469

commit v8 on v6

--- a/solution.py
+++ b/solution.py
@@ -93,6 +93,19 @@
     return results
 
 
+def reverse_bits(value, count):
+    result = 0
+    for bit in range(count):
+        result = result + ((value >> bit) & 1) * (1 << (count - 1 - bit))
+    return result
+
+
+def partner_spot(x, own_planes):
+    devices = lax.axis_size("space")
+    order = reverse_bits((x // own_planes) ^ lax.axis_index("space"), devices.bit_length() - 1)
+    return order, x % own_planes
+
+
 def pair_spot(x, own_planes):
     device = x // own_planes
     core = (device ^ lax.axis_index("space")) & 1
@@ -114,20 +127,22 @@
     index_ref,
     force_ref,
     fixed_ref,
-    start_ref,
+    density_ref,
+    own_ref,
     weight_ref,
     total_ref,
-    first_ref,
-    push_ref,
+    free_ref,
     load_ref,
     spot_ref,
 ):
-    planes, layers, row_width = start_ref.shape[1:]
+    planes, row_width = fixed_ref.shape
+    layers = density_ref.shape[1]
     load_place = lax.axis_index("space")
     shape = (layers, row_width)
     z = spot_iota(shape, 0)
     y = spot_iota(shape, 1)
 
+    own_ref[0] = density_ref[...]
     class_weights(radius_ref, weight_ref)
     ones = forward_planes(jnp.ones(shape, jnp.float32), weight_ref)
     for place, (lower, upper) in enumerate(((0, 2), (1, 2), (2, 2), (2, 1), (2, 0))):
@@ -137,16 +152,12 @@
         )
 
     def free_plane(x, carry):
-        free = jnp.where(z == 0, 1.0 - fixed_ref[pl.ds(x, 1), :].astype(jnp.float32), 1.0)
-        push_ref[x] = relax_factor * free
-        for part in range(3):
-            first_ref[part, x + 1] = start_ref[part, x] * free
+        free_ref[x] = jnp.where(
+            z == 0, 1.0 - fixed_ref[pl.ds(x, 1), :].astype(jnp.float32), 1.0
+        )
         return carry
 
     lax.fori_loop(0, planes, free_plane, 0, unroll=8)
-    for part in range(3):
-        first_ref[part, 0] = jnp.zeros(shape, jnp.float32)
-        first_ref[part, planes + 1] = jnp.zeros(shape, jnp.float32)
 
     own_index = index_ref[load_place]
     own_z = own_index // row_width % layers
@@ -162,9 +173,9 @@
     load_ref,
     weight_ref,
     total_ref,
-    push_ref,
+    free_ref,
     density_ref,
-    first_ref,
+    start_ref,
     disp_ref,
     sens_ref,
     coef_ref,
@@ -178,11 +189,11 @@
     right_ref,
     left_ref,
     rate_ref,
+    first_ref,
     second_ref,
-    third_ref,
 ):
-    cores, chips, own_planes, layers, row_width = density_ref.shape
-    planes = cores * chips * own_planes
+    planes, layers, row_width = coef_ref.shape
+    own_planes = density_ref.shape[1]
     load_cases = lax.axis_size("space")
     shape = (layers, row_width)
     z = spot_iota(shape, 0)
@@ -193,9 +204,7 @@
         zero_edges(ref)
 
     def filter_plane(x, carry):
-        near, side, far = forward_planes(
-            density_ref[pair_spot(x, own_planes)], weight_ref
-        )
+        near, side, far = forward_planes(density_ref[partner_spot(x, own_planes)], weight_ref)
         near_ref[x + 2] = near
         side_ref[x + 2] = side
         far_ref[x + 2] = far
@@ -221,7 +230,7 @@
 
     across_ref[0] = zero
     across_ref[planes] = zero
-    for ref in (second_ref, third_ref):
+    for ref in (first_ref, second_ref):
         for part in range(3):
             ref[part, 0] = zero
             ref[part, planes + 1] = zero
@@ -243,9 +252,11 @@
         left_ref[x] = left
         sums = (carry + ahead, up + down, left + right)
         every = sums[0] + sums[1] + sums[2]
-        push = push_ref[x]
+        free = free_ref[x]
+        push = relax_factor * free
         for part in range(3):
             rate_ref[part, x] = push / (every + sums[part])
+            first_ref[part, x + 1] = start_ref[part, x] * free
         return ahead
 
     lax.fori_loop(0, planes, face_plane, zero, unroll=8)
@@ -271,12 +282,10 @@
         for part in range(3):
             target[part, own_x + lead] += rate_ref[part, own_x] * load_ref[part]
 
-    source = first_ref
+    stages = (first_ref, second_ref)
     for turn in range(SWEEPS - 1):
-        target = (second_ref, third_ref)[turn % 2]
-        sweep(source, target, 1)
-        source = target
-    sweep(source, disp_ref, 0)
+        sweep(stages[turn % 2], stages[(turn + 1) % 2], 1)
+    sweep(stages[(SWEEPS - 1) % 2], disp_ref, 0)
 
     def energy_plane(x, carry):
         later = jnp.minimum(x + 1, planes - 1)
@@ -311,8 +320,8 @@
     low_ref,
     high_ref,
 ):
-    cores, chips, own_planes, layers, row_width = density_ref.shape
-    planes = cores * chips * own_planes
+    planes, layers, row_width = coef_ref.shape
+    own_planes = density_ref.shape[1]
     place = lax.axis_index("space")
     shape = (layers, row_width)
     zero = jnp.zeros(shape, jnp.float32)
@@ -334,7 +343,7 @@
         root = jnp.sqrt(
             near_ref[x + 2] + side_ref[x + 1] + side_ref[x + 3] + far_ref[x] + far_ref[x + 4]
         )
-        density = density_ref[pair_spot(x, own_planes)]
+        density = density_ref[partner_spot(x, own_planes)]
         pull_ref[x] = density * root
         low_ref[x] = jnp.maximum(density - move_limit, density_floor)
         high_ref[x] = jnp.minimum(density + move_limit, 1.0)
@@ -380,14 +389,15 @@
     return jax.ShapeDtypeStruct(shape, jnp.float32)
 
 
-def prepare_call(radius, load_index, load_force, fixed, displacement):
-    planes, layers, row_width = displacement.shape[1:]
+def prepare_call(radius, load_index, load_force, fixed, density):
+    layers, row_width = density.shape[1:]
+    planes = fixed.shape[0]
     return pl.pallas_call(
         prepare_kernel,
         out_shape=[
+            floats(1, *density.shape),
             floats(len(ALL_SQUARES), layers, row_width),
             floats(2 * window_reach + 1, layers, row_width),
-            floats(3, planes + 2, layers, row_width),
             floats(planes, layers, row_width),
             floats(3, layers, row_width),
             jax.ShapeDtypeStruct((1,), jnp.int32),
@@ -396,17 +406,17 @@
         out_specs=[in_vmem()] * 5 + [in_smem()],
         compiler_params=pltpu.CompilerParams(vmem_limit_bytes=KERNEL_VMEM),
         cost_estimate=pl.CostEstimate(
-            flops=4 * displacement.size,
-            bytes_accessed=8 * displacement.size,
+            flops=40 * planes * layers * row_width,
+            bytes_accessed=8 * planes * layers * row_width,
             transcendentals=0,
         ),
         name="prepare",
-    )(radius, load_index, load_force, fixed, displacement)
-
-
-def sweep_call(spot, load, weights, totals, push, density, first):
-    cores, chips, own_planes, layers, row_width = density.shape
-    planes = cores * chips * own_planes
+    )(radius, load_index, load_force, fixed, density)
+
+
+def sweep_call(spot, load, weights, totals, free, density, displacement):
+    devices, own_planes, layers, row_width = density.shape
+    planes = devices * own_planes
 
     def scratch(*lead):
         return pltpu.VMEM(lead + (layers, row_width), jnp.float32)
@@ -415,7 +425,7 @@
         sweep_kernel,
         out_shape=[
             floats(3, planes, layers, row_width),
-            floats(*density.shape),
+            floats(2, devices // 2, own_planes, layers, row_width),
             floats(planes, layers, row_width),
         ],
         in_specs=[in_smem()] + [in_vmem()] * 6,
@@ -436,12 +446,12 @@
         ],
         compiler_params=pltpu.CompilerParams(vmem_limit_bytes=KERNEL_VMEM),
         name="sweeps",
-    )(spot, load, weights, totals, push, density, first)
+    )(spot, load, weights, totals, free, density, displacement)
 
 
 def design_call(weights, sens, coef, density):
-    cores, chips, own_planes, layers, row_width = density.shape
-    planes = cores * chips * own_planes
+    devices, own_planes, layers, row_width = density.shape
+    planes = devices * own_planes
 
     def scratch(*lead):
         return pltpu.VMEM(lead + (layers, row_width), jnp.float32)
@@ -475,11 +485,25 @@
     return lax.all_to_all(pieces, "space", 0, 0, axis_index_groups=groups)
 
 
-def gathered(block, beside=()):
+def gathered(block):
     chips = lax.axis_size("space") // 2
     same = between_chips(jnp.broadcast_to(block[None], (chips,) + block.shape))
-    same, beside = lax.optimization_barrier((same, beside))
-    return jnp.stack([same, other_core(same)]), beside
+    return jnp.stack([same, other_core(same)])
+
+
+def partner_gathered(block, prepare):
+    devices = lax.axis_size("space")
+
+    def swapped(pieces, bit):
+        return lax.ppermute(pieces, "space", [(i, i ^ 1 << bit) for i in range(devices)])
+
+    first, *bits = reversed(range(devices.bit_length() - 1))
+    other = swapped(block[None], first)
+    other, (own, *prepared) = lax.optimization_barrier((other, prepare()))
+    pieces = jnp.concatenate([own, other])
+    for bit in bits:
+        pieces = jnp.concatenate([pieces, swapped(pieces, bit)])
+    return pieces, prepared
 
 
 def scattered_sum(pieces):
@@ -487,11 +511,14 @@
 
 
 def one_slab(density, displacement, fixed, load_index, load_force, radius):
-    prepared = prepare_call(radius, load_index, load_force.T, fixed, displacement[0])
-    whole, prepared = gathered(density, prepared)
-    weights, totals, first, push, load, spot = prepared
-    new_displacement, sens, coef = sweep_call(spot, load, weights, totals, push, whole, first)
-    sens, _ = gathered(scattered_sum(sens))
+    whole, prepared = partner_gathered(
+        density, lambda: prepare_call(radius, load_index, load_force.T, fixed, density)
+    )
+    weights, totals, free, load, spot = prepared
+    new_displacement, sens, coef = sweep_call(
+        spot, load, weights, totals, free, whole, displacement[0]
+    )
+    sens = gathered(scattered_sum(sens))
     new_density = design_call(weights, sens, coef, whole)
     return new_density, new_displacement[None]
 

time: 51.3 us -> 53.3 us (1.039)
  blocking collectives: 19.8 us -> 20.7 us
  waiting for transfers between devices: 8.13 us -> 8.95 us
    all_to_all x1 -> x0, starting transfers between devices: 7.38 us -> none  [between_chips(): return lax.all_to_all(pieces, 'space', 0, 0, axis_index_groups=groups)]
    ppermute x0 -> x4, starting transfers between devices: none -> 7.31 us  [swapped(): lax.ppermute(pieces, 'space', [(i, i ^ 1 << bit) for i in range(devices)])]
    ppermute x0 -> x4, waiting for transfers between devices: none -> 6.42 us  [swapped(): lax.ppermute(pieces, 'space', [(i, i ^ 1 << bit) for i in range(devices)])]
    all_to_all x1 -> x0, waiting for transfers between devices: 4.24 us -> none  [between_chips(): return lax.all_to_all(pieces, 'space', 0, 0, axis_index_groups=groups)]
    unnamed x10 -> x16, local copies, waits for them, and re-layouts: 1.79 us -> 3.45 us
    broadcast_in_dim x2 -> x1, local copies, waits for them, and re-layouts: 1.39 us -> 0.01 us  [gathered(): same = between_chips(jnp.broadcast_to(block[None], (chips,) + block.shape))]
    ppermute x3 -> x2, waiting for transfers between devices: 3.89 us -> 2.54 us  [other_core(): return lax.ppermute(block, 'space', [(i, i ^ 1) for i in range(devices)])]
    all_to_all x2, blocking collectives: 19.8 us -> 20.7 us  [between_chips(): return lax.all_to_all(pieces, 'space', 0, 0, axis_index_groups=groups)]
  transfers between devices with their start and end apart: 4 -> 6, of which waited for: 4 -> 5; matrix products, arithmetic and copies ran while one was open for 0% -> 0% of each run, Pallas kernels for 2% -> 2%
where the time goes in v8:
time: 53.3 us; the launch traced here: 52.9 us
  blocking collectives  20.7 us (39%)
  Pallas kernels  11.4 us (21%)
  waiting for transfers between devices  8.95 us (17%)
  starting transfers between devices  7.53 us (14%)
  local copies, waits for them, and re-layouts  3.48 us (7%)
  between operations  0.73 us (1%)
    all_to_all x2, blocking collectives, between_chips(): return lax.all_to_all(pieces, 'space', 0, 0, axis_index_groups=groups)  20.7 us
    ppermute x4, starting transfers between devices, swapped(): lax.ppermute(pieces, 'space', [(i, i ^ 1 << bit) for i in range(devices)])  7.31 us
    pallas_call x1, Pallas kernels, sweep_call(): pl.pallas_call(sweep_kernel, out_shape=[floats(3, planes, layers, row_wid...  6.42 us
    ppermute x4, waiting for transfers between devices, swapped(): lax.ppermute(pieces, 'space', [(i, i ^ 1 << bit) for i in range(devices)])  6.42 us
    pallas_call x1, Pallas kernels, design_call(): pl.pallas_call(design_kernel, out_shape=jax.ShapeDtypeStruct((own_planes,...  3.72 us
    unnamed x16, local copies, waits for them, and re-layouts  3.45 us
    ppermute x2, waiting for transfers between devices, other_core(): return lax.ppermute(block, 'space', [(i, i ^ 1) for i in range(devices)])  2.54 us
    pallas_call x1, Pallas kernels, prepare_call(): pl.pallas_call(prepare_kernel, out_shape=[floats(1, *density.shape), floa...  1.22 us
  transfers between devices with their start and end apart: 6, of which 5 were waited for; matrix products, arithmetic and copies ran while one was open for 0% of the time, Pallas kernels for 2%

profile of v8, /device:TPU:0, one launch (start us, length us, event | category | flops | bytes accessed | tf_op | source)
XLA Modules:
  0.0 52.9 jit_solution(6747409370526982212)
XLA Ops:
  0.6 0.0 copy-start
  0.6 4.1 %collective-permute-start = (f32[1,2,16,128]{3,2,1,0:T(8,128)}, f32[1,2,16,128]{3,2,1,0:T(8,128)S(1)}, u32[]{:S(2)}, u32[]{:S(2)}) collective-permute-start(f32[1,2,16,128]{3,2,1,0:T(8,128)} %bitcast.11), channel_id=1, source_target_pairs={{0,8},{1,9},{2,10},{3,11},{4,12},{5,13},{6,14},{7,15},{8,0},{9,1},... | collective-permute-start | bytes 49160 | tf_op jit(solution)/shard_map/ppermute | solution.py:498
  4.7 0.0 copy-start.1
  4.7 0.7 %copy-done.1 = s32[32,128]{1,0:T(8,128)S(1)} copy-done((s32[32,128]{1,0:T(8,128)S(1)}, s32[32,128]{1,0:T(8,128)}, u32[]{:S(2)}) %copy-start.1) | copy-done | bytes 16408
  5.5 0.0 copy-start.2
  5.5 0.7 %copy-done.2 = f32[2,16,128]{2,1,0:T(8,128)S(1)} copy-done((f32[2,16,128]{2,1,0:T(8,128)S(1)}, f32[2,16,128]{2,1,0:T(8,128)}, u32[]{:S(2)}) %copy-start.2) | copy-done | bytes 16408
  6.2 0.0 copy-start.3
  6.2 0.7 %copy-done.3 = f32[16,3]{0,1:T(4,128)S(1)} copy-done((f32[16,3]{0,1:T(4,128)S(1)}, f32[16,3]{0,1:T(4,128)}, u32[]{:S(2)}) %copy-start.3) | copy-done | bytes 216
  6.9 0.0 copy-start.4
  6.9 0.7 %copy-done.4 = s32[16]{0:T(128)S(1)} copy-done((s32[16]{0:T(128)S(1)}, s32[16]{0:T(128)}, u32[]{:S(2)}) %copy-start.4) | copy-done | bytes 88
  7.5 0.0 copy-start.5
  7.5 0.7 %copy-done.5 = s32[16]{0:T(128)S(1)} copy-done((s32[16]{0:T(128)S(1)}, s32[16]{0:T(128)}, u32[]{:S(2)}) %copy-start.5) | copy-done | bytes 88
  8.2 1.2 %prepare.1 = (f32[1,2,16,128]{3,2,1,0:T(8,128)S(1)}, f32[10,16,128]{2,1,0:T(8,128)S(1)}, f32[5,16,128]{2,1,0:T(8,128)S(1)}, f32[32,16,128]{2,1,0:T(8,128)S(1)}, f32[3,16,128]{2,1,0:T(8,128)S(1)}, /*index=5*/s32[1]{0:T(128)}) custom-call(s32[16]{0:T(128)S(1)} %copy-done.4, s32[16]{0:T(128)S(1)} %copy-done.5, f32[3,16]{1,0:T(4,128)S(1)} %bitcast.12, ...), custom_call_target="tpu_custom_call" | custom-call | flops 2621440 | bytes 524288 | tf_op jit(solution)/shard_map/prepare/pallas_call | solution.py:395
  9.4 0.0 collective-permute-done
  9.4 1.6 %collective-permute-start.1 = (f32[2,2,16,128]{3,2,1,0:T(8,128)S(1)}, f32[2,2,16,128]{3,2,1,0:T(8,128)S(1)}, u32[]{:S(2)}, u32[]{:S(2)}) collective-permute-start(f32[2,2,16,128]{3,2,1,0:T(8,128)S(1)} %pad_maximum_fusion.3), channel_id=1, source_target_pairs={{0,4},{1,5},{2,6},{3,7},{4,0},{5,1},{6,2},{7,3},{8,12},{9,13},{10,... | collective-permute-start | bytes 98312 | tf_op jit(solution)/shard_map/ppermute | solution.py:498
  11.1 2.3 %collective-permute-done.1 = f32[2,2,16,128]{3,2,1,0:T(8,128)S(1)} collective-permute-done((f32[2,2,16,128]{3,2,1,0:T(8,128)S(1)}, f32[2,2,16,128]{3,2,1,0:T(8,128)S(1)}, u32[]{:S(2)}, u32[]{:S(2)}) %collective-permute-start.1) | collective-permute-done | bytes 32800 | tf_op jit(solution)/shard_map/ppermute | solution.py:498
  13.4 1.5 %collective-permute-start.2 = (f32[4,2,16,128]{3,2,1,0:T(8,128)S(1)}, f32[4,2,16,128]{3,2,1,0:T(8,128)S(1)}, u32[]{:S(2)}, u32[]{:S(2)}) collective-permute-start(f32[4,2,16,128]{3,2,1,0:T(8,128)S(1)} %pad_maximum_fusion.2), channel_id=1, source_target_pairs={{0,2},{1,3},{2,0},{3,1},{4,6},{5,7},{6,4},{7,5},{8,10},{9,11},{10,... | collective-permute-start | bytes 196616 | tf_op jit(solution)/shard_map/ppermute | solution.py:498
  14.9 2.8 %collective-permute-done.2 = f32[4,2,16,128]{3,2,1,0:T(8,128)S(1)} collective-permute-done((f32[4,2,16,128]{3,2,1,0:T(8,128)S(1)}, f32[4,2,16,128]{3,2,1,0:T(8,128)S(1)}, u32[]{:S(2)}, u32[]{:S(2)}) %collective-permute-start.2) | collective-permute-done | bytes 65568 | tf_op jit(solution)/shard_map/ppermute | solution.py:498
  17.7 0.1 collective-permute-start.3
  17.8 1.3 %collective-permute-done.3 = f32[8,2,16,128]{3,2,1,0:T(8,128)S(1)} collective-permute-done((f32[8,2,16,128]{3,2,1,0:T(8,128)S(1)}, f32[8,2,16,128]{3,2,1,0:T(8,128)S(1)}, u32[]{:S(2)}, u32[]{:S(2)}) %collective-permute-start.3) | collective-permute-done | bytes 131104 | tf_op jit(solution)/shard_map/ppermute | solution.py:498
  19.1 0.0 copy-done
  19.1 6.4 %sweeps.1 = (f32[3,32,16,128]{3,2,1,0:T(8,128)}, f32[2,8,2,16,128]{4,3,2,1,0:T(8,128)S(1)}, f32[32,16,128]{2,1,0:T(8,128)S(1)}) custom-call(s32[1]{0:T(128)} %get-tuple-element.25.spot_ref, f32[3,16,128]{2,1,0:T(8,128)S(1)} %get-tuple-element.26.load_ref, f32[10,16,128]{2,1,0:T(8,128)S(1)} %get-tuple-element.24.weight_ref, ...), custom_call_target="tpu_custom_call" | custom-call | tf_op jit(solution)/shard_map/sweeps/pallas_call | solution.py:424
  25.6 0.2 collective-permute-start.4
  25.8 1.2 %collective-permute-done.4 = f32[8,2,16,128]{3,2,1,0:T(8,128)S(1)} collective-permute-done((f32[8,2,16,128]{3,2,1,0:T(8,128)S(1)}, f32[8,2,16,128]{3,2,1,0:T(8,128)S(1)}, u32[]{:S(2)}, u32[]{:S(2)}) %collective-permute-start.4) | collective-permute-done | bytes 131104 | tf_op jit(solution)/shard_map/ppermute | solution.py:479
  27.0 10.9 %all_to_all.10 = f32[8,2,16,128]{3,2,1,0:T(8,128)S(1)} all-to-all(f32[8,2,16,128]{3,2,1,0:T(8,128)S(1)} %bitcast_add_fusion), channel_id=1, replica_groups={{0,2,4,6,8,10,12,14},{1,3,5,7,9,11,13,15},{16,18,20,22,24,26,28,30},{17..., dimensions={0} | all-to-all | bytes 262144 | tf_op jit(solution)/shard_map/all_to_all | solution.py:485
  38.0 9.8 %all_to_all.11 = f32[8,2,16,128]{3,2,1,0:T(8,128)S(1)} all-to-all(f32[8,2,16,128]{3,2,1,0:T(8,128)S(1)} %broadcast_in_dim.13), channel_id=1, replica_groups={{0,2,4,6,8,10,12,14},{1,3,5,7,9,11,13,15},{16,18,20,22,24,26,28,30},{17..., dimensions={0} | all-to-all | bytes 262144 | tf_op jit(solution)/shard_map/all_to_all | solution.py:485
  47.8 0.0 collective-permute-start.5
  47.8 1.3 %collective-permute-done.5 = f32[8,2,16,128]{3,2,1,0:T(8,128)S(1)} collective-permute-done((f32[8,2,16,128]{3,2,1,0:T(8,128)S(1)}, f32[8,2,16,128]{3,2,1,0:T(8,128)S(1)}, u32[]{:S(2)}, u32[]{:S(2)}) %collective-permute-start.5) | collective-permute-done | bytes 131104 | tf_op jit(solution)/shard_map/ppermute | solution.py:479
  49.1 3.7 %design.1 = f32[2,16,128]{2,1,0:T(8,128)} custom-call(f32[10,16,128]{2,1,0:T(8,128)S(1)} %get-tuple-element.24.weight_ref, f32[2,8,2,16,128]{4,3,2,1,0:T(8,128)S(1)} %pad_maximum_fusion.sens_ref, f32[32,16,128]{2,1,0:T(8,128)S(1)} %get-tuple-element.32.coef_ref, f32[16,2,16,128]{3,2,1,0:T(8,128)S(1)} %constant_dynamic-update-slice_fusion.density_ref), custom_call_target="tpu_custom_call" | custom-call | tf_op jit(solution)/shard_map/design/pallas_call | solution.py:459
  (13 shorter events, 0.1 us)
Async XLA Ops:
  0.6 18.5 %copy-start = (f32[1,3,32,16,128]{4,3,2,1,0:T(8,128)S(1)}, f32[1,3,32,16,128]{4,3,2,1,0:T(8,128)}, u32[]{:S(2)}) copy-start(f32[1,3,32,16,128]{4,3,2,1,0:T(8,128)} %param.7) | copy-start | bytes 2359300
  0.6 8.8 %collective-permute-start = (f32[1,2,16,128]{3,2,1,0:T(8,128)}, f32[1,2,16,128]{3,2,1,0:T(8,128)S(1)}, u32[]{:S(2)}, u32[]{:S(2)}) collective-permute-start(f32[1,2,16,128]{3,2,1,0:T(8,128)} %bitcast.11), channel_id=1, source_target_pairs={{0,8},{1,9},{2,10},{3,11},{4,12},{5,13},{6,14},{7,15},{8,0},{9,1},... | collective-permute-start | bytes 49160 | tf_op jit(solution)/shard_map/ppermute | solution.py:498
  4.7 0.7 %copy-start.1 = (s32[32,128]{1,0:T(8,128)S(1)}, s32[32,128]{1,0:T(8,128)}, u32[]{:S(2)}) copy-start(s32[32,128]{1,0:T(8,128)} %fixed_ref.1) | copy-start | bytes 49156
  5.5 0.7 %copy-start.2 = (f32[2,16,128]{2,1,0:T(8,128)S(1)}, f32[2,16,128]{2,1,0:T(8,128)}, u32[]{:S(2)}) copy-start(f32[2,16,128]{2,1,0:T(8,128)} %density_ref.1) | copy-start | bytes 49156
  6.2 0.7 %copy-start.3 = (f32[16,3]{0,1:T(4,128)S(1)}, f32[16,3]{0,1:T(4,128)}, u32[]{:S(2)}) copy-start(f32[16,3]{0,1:T(4,128)} %param.10) | copy-start | bytes 580
  6.9 0.7 %copy-start.4 = (s32[16]{0:T(128)S(1)}, s32[16]{0:T(128)}, u32[]{:S(2)}) copy-start(s32[16]{0:T(128)} %radius_ref.1) | copy-start | bytes 196
  7.5 0.7 %copy-start.5 = (s32[16]{0:T(128)S(1)}, s32[16]{0:T(128)}, u32[]{:S(2)}) copy-start(s32[16]{0:T(128)} %index_ref.1) | copy-start | bytes 196
  9.4 4.0 %collective-permute-start.1 = (f32[2,2,16,128]{3,2,1,0:T(8,128)S(1)}, f32[2,2,16,128]{3,2,1,0:T(8,128)S(1)}, u32[]{:S(2)}, u32[]{:S(2)}) collective-permute-start(f32[2,2,16,128]{3,2,1,0:T(8,128)S(1)} %pad_maximum_fusion.3), channel_id=1, source_target_pairs={{0,4},{1,5},{2,6},{3,7},{4,0},{5,1},{6,2},{7,3},{8,12},{9,13},{10,... | collective-permute-start | bytes 98312 | tf_op jit(solution)/shard_map/ppermute | solution.py:498
  13.4 4.3 %collective-permute-start.2 = (f32[4,2,16,128]{3,2,1,0:T(8,128)S(1)}, f32[4,2,16,128]{3,2,1,0:T(8,128)S(1)}, u32[]{:S(2)}, u32[]{:S(2)}) collective-permute-start(f32[4,2,16,128]{3,2,1,0:T(8,128)S(1)} %pad_maximum_fusion.2), channel_id=1, source_target_pairs={{0,2},{1,3},{2,0},{3,1},{4,6},{5,7},{6,4},{7,5},{8,10},{9,11},{10,... | collective-permute-start | bytes 196616 | tf_op jit(solution)/shard_map/ppermute | solution.py:498
  17.7 1.4 %collective-permute-start.3 = (f32[8,2,16,128]{3,2,1,0:T(8,128)S(1)}, f32[8,2,16,128]{3,2,1,0:T(8,128)S(1)}, u32[]{:S(2)}, u32[]{:S(2)}) collective-permute-start(f32[8,2,16,128]{3,2,1,0:T(8,128)S(1)} %pad_maximum_fusion.1), channel_id=1, source_target_pairs={{0,1},{1,0},{2,3},{3,2},{4,5},{5,4},{6,7},{7,6},{8,9},{9,8},{10,11... | collective-permute-start | bytes 393224 | tf_op jit(solution)/shard_map/ppermute | solution.py:498
  25.6 1.4 %collective-permute-start.4 = (f32[8,2,16,128]{3,2,1,0:T(8,128)S(1)}, f32[8,2,16,128]{3,2,1,0:T(8,128)S(1)}, u32[]{:S(2)}, u32[]{:S(2)}) collective-permute-start(f32[8,2,16,128]{3,2,1,0:T(8,128)S(1)} %slice_bitcast_fusion), channel_id=1, source_target_pairs={{0,1},{1,0},{2,3},{3,2},{4,5},{5,4},{6,7},{7,6},{8,9},{9,8},{10,11... | collective-permute-start | bytes 393224 | tf_op jit(solution)/shard_map/ppermute | solution.py:479
  47.8 1.3 %collective-permute-start.5 = (f32[8,2,16,128]{3,2,1,0:T(8,128)S(1)}, f32[8,2,16,128]{3,2,1,0:T(8,128)S(1)}, u32[]{:S(2)}, u32[]{:S(2)}) collective-permute-start(f32[8,2,16,128]{3,2,1,0:T(8,128)S(1)} %all_to_all.11), channel_id=1, source_target_pairs={{0,1},{1,0},{2,3},{3,2},{4,5},{5,4},{6,7},{7,6},{8,9},{9,8},{10,11... | collective-permute-start | bytes 393224 | tf_op jit(solution)/shard_map/ppermute | solution.py:479

commit v9 on v8

--- a/solution.py
+++ b/solution.py
@@ -123,26 +123,46 @@
 
 
 def prepare_kernel(
-    radius_ref,
-    index_ref,
-    force_ref,
-    fixed_ref,
-    density_ref,
+    radius_hbm,
+    index_hbm,
+    force_hbm,
+    fixed_hbm,
+    density_hbm,
     own_ref,
     weight_ref,
     total_ref,
     free_ref,
     load_ref,
     spot_ref,
+    radius_ref,
+    index_ref,
+    force_ref,
+    fixed_ref,
+    arrived,
 ):
+    copies = [
+        pltpu.make_async_copy(source, target, arrived.at[place])
+        for place, (source, target) in enumerate(
+            (
+                (radius_hbm, radius_ref),
+                (index_hbm, index_ref),
+                (force_hbm, force_ref),
+                (fixed_hbm, fixed_ref),
+                (density_hbm, own_ref.at[0]),
+            )
+        )
+    ]
+    for copy in copies:
+        copy.start()
+    for copy in copies:
+        copy.wait()
     planes, row_width = fixed_ref.shape
-    layers = density_ref.shape[1]
+    layers = own_ref.shape[2]
     load_place = lax.axis_index("space")
     shape = (layers, row_width)
     z = spot_iota(shape, 0)
     y = spot_iota(shape, 1)
 
-    own_ref[0] = density_ref[...]
     class_weights(radius_ref, weight_ref)
     ones = forward_planes(jnp.ones(shape, jnp.float32), weight_ref)
     for place, (lower, upper) in enumerate(((0, 2), (1, 2), (2, 2), (2, 1), (2, 0))):
@@ -402,8 +422,15 @@
             floats(3, layers, row_width),
             jax.ShapeDtypeStruct((1,), jnp.int32),
         ],
-        in_specs=[in_smem()] * 3 + [in_vmem()] * 2,
+        in_specs=[pl.BlockSpec(memory_space=pltpu.HBM)] * 5,
         out_specs=[in_vmem()] * 5 + [in_smem()],
+        scratch_shapes=[
+            pltpu.SMEM(radius.shape, radius.dtype),
+            pltpu.SMEM(load_index.shape, load_index.dtype),
+            pltpu.SMEM(load_force.shape, load_force.dtype),
+            pltpu.VMEM(fixed.shape, fixed.dtype),
+            pltpu.SemaphoreType.DMA((5,)),
+        ],
         compiler_params=pltpu.CompilerParams(vmem_limit_bytes=KERNEL_VMEM),
         cost_estimate=pl.CostEstimate(
             flops=40 * planes * layers * row_width,
@@ -411,7 +438,12 @@
             transcendentals=0,
         ),
         name="prepare",
-    )(radius, load_index, load_force, fixed, density)
+    )(
+        *(
+            pltpu.with_memory_space_constraint(array, pltpu.HBM)
+            for array in (radius, load_index, load_force, fixed, density)
+        )
+    )
 
 
 def sweep_call(spot, load, weights, totals, free, density, displacement):

time: 53.3 us -> 52.8 us (level)
  local copies, waits for them, and re-layouts: 3.48 us -> 0.05 us
  blocking collectives: 20.7 us -> 23.2 us
  starting transfers between devices: 7.53 us -> 8.18 us
    unnamed x16 -> x6, local copies, waits for them, and re-layouts: 3.45 us -> 0.02 us
    all_to_all x2, blocking collectives: 20.7 us -> 23.2 us  [between_chips(): return lax.all_to_all(pieces, 'space', 0, 0, axis_index_groups=groups)]
    ppermute x4, starting transfers between devices: 7.31 us -> 7.95 us  [swapped(): lax.ppermute(pieces, 'space', [(i, i ^ 1 << bit) for i in range(devices)])]
  transfers between devices with their start and end apart: 6 -> 6, of which waited for: 5 -> 6; matrix products, arithmetic and copies ran while one was open for 0% -> 0% of each run, Pallas kernels for 2% -> 3%
where the time goes in v9:
time: 52.8 us; the launch traced here: 52.5 us
  blocking collectives  23.2 us (44%)
  Pallas kernels  11.6 us (22%)
  waiting for transfers between devices  8.71 us (16%)
  starting transfers between devices  8.18 us (15%)
  between operations  0.71 us (1%)
    all_to_all x2, blocking collectives, between_chips(): return lax.all_to_all(pieces, 'space', 0, 0, axis_index_groups=groups)  23.2 us
    ppermute x4, starting transfers between devices, swapped(): lax.ppermute(pieces, 'space', [(i, i ^ 1 << bit) for i in range(devices)])  7.95 us
    pallas_call x1, Pallas kernels, sweep_call(): pl.pallas_call(sweep_kernel, out_shape=[floats(3, planes, layers, row_wid...  6.42 us
    ppermute x4, waiting for transfers between devices, swapped(): lax.ppermute(pieces, 'space', [(i, i ^ 1 << bit) for i in range(devices)])  6.18 us
    pallas_call x1, Pallas kernels, design_call(): pl.pallas_call(design_kernel, out_shape=jax.ShapeDtypeStruct((own_planes,...  3.72 us
    ppermute x2, waiting for transfers between devices, other_core(): return lax.ppermute(block, 'space', [(i, i ^ 1) for i in range(devices)])  2.54 us
    pallas_call x1, Pallas kernels, prepare_call(): pl.pallas_call(prepare_kernel, out_shape=[floats(1, *density.shape), floa...  1.44 us
  transfers between devices with their start and end apart: 6, of which 6 were waited for; matrix products, arithmetic and copies ran while one was open for 0% of the time, Pallas kernels for 3%

profile of v9, /device:TPU:0, one launch (start us, length us, event | category | flops | bytes accessed | tf_op | source)
XLA Modules:
  0.0 52.5 jit_solution(3077831394561944357)
XLA Ops:
  0.6 0.0 copy-start
  0.6 4.1 %collective-permute-start = (f32[1,2,16,128]{3,2,1,0:T(8,128)}, f32[1,2,16,128]{3,2,1,0:T(8,128)S(1)}, u32[]{:S(2)}, u32[]{:S(2)}) collective-permute-start(f32[1,2,16,128]{3,2,1,0:T(8,128)} %bitcast.13), channel_id=1, source_target_pairs={{0,8},{1,9},{2,10},{3,11},{4,12},{5,13},{6,14},{7,15},{8,0},{9,1},... | collective-permute-start | bytes 49160 | tf_op jit(solution)/shard_map/ppermute | solution.py:530
  4.7 1.4 %prepare.1 = (f32[1,2,16,128]{3,2,1,0:T(8,128)S(1)}, f32[10,16,128]{2,1,0:T(8,128)S(1)}, f32[5,16,128]{2,1,0:T(8,128)S(1)}, f32[32,16,128]{2,1,0:T(8,128)S(1)}, f32[3,16,128]{2,1,0:T(8,128)S(1)}, /*index=5*/s32[1]{0:T(128)}) custom-call(s32[16]{0:T(128)} %radius_hbm.1, s32[16]{0:T(128)} %index_hbm.1, f32[3,16]{1,0:T(4,128)} %bitcast.14, ...), custom_call_target="tpu_custom_call" | custom-call | flops 2621440 | bytes 524288 | tf_op jit(solution)/shard_map/prepare/pallas_call | solution.py:415
  6.2 0.5 collective-permute-done
  6.7 1.9 %collective-permute-start.1 = (f32[2,2,16,128]{3,2,1,0:T(8,128)S(1)}, f32[2,2,16,128]{3,2,1,0:T(8,128)S(1)}, u32[]{:S(2)}, u32[]{:S(2)}) collective-permute-start(f32[2,2,16,128]{3,2,1,0:T(8,128)S(1)} %pad_maximum_fusion.3), channel_id=1, source_target_pairs={{0,4},{1,5},{2,6},{3,7},{4,0},{5,1},{6,2},{7,3},{8,12},{9,13},{10,... | collective-permute-start | bytes 98312 | tf_op jit(solution)/shard_map/ppermute | solution.py:530
  8.6 2.0 %collective-permute-done.1 = f32[2,2,16,128]{3,2,1,0:T(8,128)S(1)} collective-permute-done((f32[2,2,16,128]{3,2,1,0:T(8,128)S(1)}, f32[2,2,16,128]{3,2,1,0:T(8,128)S(1)}, u32[]{:S(2)}, u32[]{:S(2)}) %collective-permute-start.1) | collective-permute-done | bytes 32800 | tf_op jit(solution)/shard_map/ppermute | solution.py:530
  10.6 1.9 %collective-permute-start.2 = (f32[4,2,16,128]{3,2,1,0:T(8,128)S(1)}, f32[4,2,16,128]{3,2,1,0:T(8,128)S(1)}, u32[]{:S(2)}, u32[]{:S(2)}) collective-permute-start(f32[4,2,16,128]{3,2,1,0:T(8,128)S(1)} %pad_maximum_fusion.2), channel_id=1, source_target_pairs={{0,2},{1,3},{2,0},{3,1},{4,6},{5,7},{6,4},{7,5},{8,10},{9,11},{10,... | collective-permute-start | bytes 196616 | tf_op jit(solution)/shard_map/ppermute | solution.py:530
  12.5 2.4 %collective-permute-done.2 = f32[4,2,16,128]{3,2,1,0:T(8,128)S(1)} collective-permute-done((f32[4,2,16,128]{3,2,1,0:T(8,128)S(1)}, f32[4,2,16,128]{3,2,1,0:T(8,128)S(1)}, u32[]{:S(2)}, u32[]{:S(2)}) %collective-permute-start.2) | collective-permute-done | bytes 65568 | tf_op jit(solution)/shard_map/ppermute | solution.py:530
  14.9 0.1 collective-permute-start.3
  15.0 1.3 %collective-permute-done.3 = f32[8,2,16,128]{3,2,1,0:T(8,128)S(1)} collective-permute-done((f32[8,2,16,128]{3,2,1,0:T(8,128)S(1)}, f32[8,2,16,128]{3,2,1,0:T(8,128)S(1)}, u32[]{:S(2)}, u32[]{:S(2)}) %collective-permute-start.3) | collective-permute-done | bytes 131104 | tf_op jit(solution)/shard_map/ppermute | solution.py:530
  16.3 0.0 copy-done
  16.3 6.4 %sweeps.1 = (f32[3,32,16,128]{3,2,1,0:T(8,128)}, f32[2,8,2,16,128]{4,3,2,1,0:T(8,128)S(1)}, f32[32,16,128]{2,1,0:T(8,128)S(1)}) custom-call(s32[1]{0:T(128)} %get-tuple-element.25.spot_ref, f32[3,16,128]{2,1,0:T(8,128)S(1)} %get-tuple-element.26.load_ref, f32[10,16,128]{2,1,0:T(8,128)S(1)} %get-tuple-element.24.weight_ref, ...), custom_call_target="tpu_custom_call" | custom-call | tf_op jit(solution)/shard_map/sweeps/pallas_call | solution.py:456
  22.7 0.2 collective-permute-start.4
  23.0 1.2 %collective-permute-done.4 = f32[8,2,16,128]{3,2,1,0:T(8,128)S(1)} collective-permute-done((f32[8,2,16,128]{3,2,1,0:T(8,128)S(1)}, f32[8,2,16,128]{3,2,1,0:T(8,128)S(1)}, u32[]{:S(2)}, u32[]{:S(2)}) %collective-permute-start.4) | collective-permute-done | bytes 131104 | tf_op jit(solution)/shard_map/ppermute | solution.py:511
  24.2 13.3 %all_to_all.10 = f32[8,2,16,128]{3,2,1,0:T(8,128)S(1)} all-to-all(f32[8,2,16,128]{3,2,1,0:T(8,128)S(1)} %bitcast_add_fusion), channel_id=1, replica_groups={{0,2,4,6,8,10,12,14},{1,3,5,7,9,11,13,15},{16,18,20,22,24,26,28,30},{17..., dimensions={0} | all-to-all | bytes 262144 | tf_op jit(solution)/shard_map/all_to_all | solution.py:517
  37.6 9.8 %all_to_all.11 = f32[8,2,16,128]{3,2,1,0:T(8,128)S(1)} all-to-all(f32[8,2,16,128]{3,2,1,0:T(8,128)S(1)} %broadcast_in_dim.13), channel_id=1, replica_groups={{0,2,4,6,8,10,12,14},{1,3,5,7,9,11,13,15},{16,18,20,22,24,26,28,30},{17..., dimensions={0} | all-to-all | bytes 262144 | tf_op jit(solution)/shard_map/all_to_all | solution.py:517
  47.4 0.0 collective-permute-start.5
  47.4 1.3 %collective-permute-done.5 = f32[8,2,16,128]{3,2,1,0:T(8,128)S(1)} collective-permute-done((f32[8,2,16,128]{3,2,1,0:T(8,128)S(1)}, f32[8,2,16,128]{3,2,1,0:T(8,128)S(1)}, u32[]{:S(2)}, u32[]{:S(2)}) %collective-permute-start.5) | collective-permute-done | bytes 131104 | tf_op jit(solution)/shard_map/ppermute | solution.py:511
  48.7 3.7 %design.1 = f32[2,16,128]{2,1,0:T(8,128)} custom-call(f32[10,16,128]{2,1,0:T(8,128)S(1)} %get-tuple-element.24.weight_ref, f32[2,8,2,16,128]{4,3,2,1,0:T(8,128)S(1)} %pad_maximum_fusion.sens_ref, f32[32,16,128]{2,1,0:T(8,128)S(1)} %get-tuple-element.32.coef_ref, f32[16,2,16,128]{3,2,1,0:T(8,128)S(1)} %constant_dynamic-update-slice_fusion.density_ref), custom_call_target="tpu_custom_call" | custom-call | tf_op jit(solution)/shard_map/design/pallas_call | solution.py:491
  (13 shorter events, 0.1 us)
Async XLA Ops:
  0.6 15.7 %copy-start = (f32[1,3,32,16,128]{4,3,2,1,0:T(8,128)S(1)}, f32[1,3,32,16,128]{4,3,2,1,0:T(8,128)}, u32[]{:S(2)}) copy-start(f32[1,3,32,16,128]{4,3,2,1,0:T(8,128)} %param.7) | copy-start | bytes 2359300
  0.6 6.0 %collective-permute-start = (f32[1,2,16,128]{3,2,1,0:T(8,128)}, f32[1,2,16,128]{3,2,1,0:T(8,128)S(1)}, u32[]{:S(2)}, u32[]{:S(2)}) collective-permute-start(f32[1,2,16,128]{3,2,1,0:T(8,128)} %bitcast.13), channel_id=1, source_target_pairs={{0,8},{1,9},{2,10},{3,11},{4,12},{5,13},{6,14},{7,15},{8,0},{9,1},... | collective-permute-start | bytes 49160 | tf_op jit(solution)/shard_map/ppermute | solution.py:530
  6.7 3.9 %collective-permute-start.1 = (f32[2,2,16,128]{3,2,1,0:T(8,128)S(1)}, f32[2,2,16,128]{3,2,1,0:T(8,128)S(1)}, u32[]{:S(2)}, u32[]{:S(2)}) collective-permute-start(f32[2,2,16,128]{3,2,1,0:T(8,128)S(1)} %pad_maximum_fusion.3), channel_id=1, source_target_pairs={{0,4},{1,5},{2,6},{3,7},{4,0},{5,1},{6,2},{7,3},{8,12},{9,13},{10,... | collective-permute-start | bytes 98312 | tf_op jit(solution)/shard_map/ppermute | solution.py:530
  10.6 4.3 %collective-permute-start.2 = (f32[4,2,16,128]{3,2,1,0:T(8,128)S(1)}, f32[4,2,16,128]{3,2,1,0:T(8,128)S(1)}, u32[]{:S(2)}, u32[]{:S(2)}) collective-permute-start(f32[4,2,16,128]{3,2,1,0:T(8,128)S(1)} %pad_maximum_fusion.2), channel_id=1, source_target_pairs={{0,2},{1,3},{2,0},{3,1},{4,6},{5,7},{6,4},{7,5},{8,10},{9,11},{10,... | collective-permute-start | bytes 196616 | tf_op jit(solution)/shard_map/ppermute | solution.py:530
  14.9 1.4 %collective-permute-start.3 = (f32[8,2,16,128]{3,2,1,0:T(8,128)S(1)}, f32[8,2,16,128]{3,2,1,0:T(8,128)S(1)}, u32[]{:S(2)}, u32[]{:S(2)}) collective-permute-start(f32[8,2,16,128]{3,2,1,0:T(8,128)S(1)} %pad_maximum_fusion.1), channel_id=1, source_target_pairs={{0,1},{1,0},{2,3},{3,2},{4,5},{5,4},{6,7},{7,6},{8,9},{9,8},{10,11... | collective-permute-start | bytes 393224 | tf_op jit(solution)/shard_map/ppermute | solution.py:530
  22.7 1.4 %collective-permute-start.4 = (f32[8,2,16,128]{3,2,1,0:T(8,128)S(1)}, f32[8,2,16,128]{3,2,1,0:T(8,128)S(1)}, u32[]{:S(2)}, u32[]{:S(2)}) collective-permute-start(f32[8,2,16,128]{3,2,1,0:T(8,128)S(1)} %slice_bitcast_fusion), channel_id=1, source_target_pairs={{0,1},{1,0},{2,3},{3,2},{4,5},{5,4},{6,7},{7,6},{8,9},{9,8},{10,11... | collective-permute-start | bytes 393224 | tf_op jit(solution)/shard_map/ppermute | solution.py:511
  47.4 1.3 %collective-permute-start.5 = (f32[8,2,16,128]{3,2,1,0:T(8,128)S(1)}, f32[8,2,16,128]{3,2,1,0:T(8,128)S(1)}, u32[]{:S(2)}, u32[]{:S(2)}) collective-permute-start(f32[8,2,16,128]{3,2,1,0:T(8,128)S(1)} %all_to_all.11), channel_id=1, source_target_pairs={{0,1},{1,0},{2,3},{3,2},{4,5},{5,4},{6,7},{7,6},{8,9},{9,8},{10,11... | collective-permute-start | bytes 393224 | tf_op jit(solution)/shard_map/ppermute | solution.py:511

commit v10 on v9

--- a/solution.py
+++ b/solution.py
@@ -93,19 +93,6 @@
     return results
 
 
-def reverse_bits(value, count):
-    result = 0
-    for bit in range(count):
-        result = result + ((value >> bit) & 1) * (1 << (count - 1 - bit))
-    return result
-
-
-def partner_spot(x, own_planes):
-    devices = lax.axis_size("space")
-    order = reverse_bits((x // own_planes) ^ lax.axis_index("space"), devices.bit_length() - 1)
-    return order, x % own_planes
-
-
 def pair_spot(x, own_planes):
     device = x // own_planes
     core = (device ^ lax.axis_index("space")) & 1
@@ -127,8 +114,6 @@
     index_hbm,
     force_hbm,
     fixed_hbm,
-    density_hbm,
-    own_ref,
     weight_ref,
     total_ref,
     free_ref,
@@ -148,7 +133,6 @@
                 (index_hbm, index_ref),
                 (force_hbm, force_ref),
                 (fixed_hbm, fixed_ref),
-                (density_hbm, own_ref.at[0]),
             )
         )
     ]
@@ -156,8 +140,7 @@
         copy.start()
     for copy in copies:
         copy.wait()
-    planes, row_width = fixed_ref.shape
-    layers = own_ref.shape[2]
+    planes, layers, row_width = free_ref.shape
     load_place = lax.axis_index("space")
     shape = (layers, row_width)
     z = spot_iota(shape, 0)
@@ -213,7 +196,7 @@
     second_ref,
 ):
     planes, layers, row_width = coef_ref.shape
-    own_planes = density_ref.shape[1]
+    own_planes = density_ref.shape[2]
     load_cases = lax.axis_size("space")
     shape = (layers, row_width)
     z = spot_iota(shape, 0)
@@ -224,7 +207,7 @@
         zero_edges(ref)
 
     def filter_plane(x, carry):
-        near, side, far = forward_planes(density_ref[partner_spot(x, own_planes)], weight_ref)
+        near, side, far = forward_planes(density_ref[pair_spot(x, own_planes)], weight_ref)
         near_ref[x + 2] = near
         side_ref[x + 2] = side
         far_ref[x + 2] = far
@@ -341,7 +324,7 @@
     high_ref,
 ):
     planes, layers, row_width = coef_ref.shape
-    own_planes = density_ref.shape[1]
+    own_planes = density_ref.shape[2]
     place = lax.axis_index("space")
     shape = (layers, row_width)
     zero = jnp.zeros(shape, jnp.float32)
@@ -363,7 +346,7 @@
         root = jnp.sqrt(
             near_ref[x + 2] + side_ref[x + 1] + side_ref[x + 3] + far_ref[x] + far_ref[x + 4]
         )
-        density = density_ref[partner_spot(x, own_planes)]
+        density = density_ref[pair_spot(x, own_planes)]
         pull_ref[x] = density * root
         low_ref[x] = jnp.maximum(density - move_limit, density_floor)
         high_ref[x] = jnp.minimum(density + move_limit, 1.0)
@@ -409,27 +392,26 @@
     return jax.ShapeDtypeStruct(shape, jnp.float32)
 
 
-def prepare_call(radius, load_index, load_force, fixed, density):
-    layers, row_width = density.shape[1:]
-    planes = fixed.shape[0]
+def prepare_call(radius, load_index, load_force, fixed):
+    planes, row_width = fixed.shape
+    layers = radius.shape[0]
     return pl.pallas_call(
         prepare_kernel,
         out_shape=[
-            floats(1, *density.shape),
             floats(len(ALL_SQUARES), layers, row_width),
             floats(2 * window_reach + 1, layers, row_width),
             floats(planes, layers, row_width),
             floats(3, layers, row_width),
             jax.ShapeDtypeStruct((1,), jnp.int32),
         ],
-        in_specs=[pl.BlockSpec(memory_space=pltpu.HBM)] * 5,
-        out_specs=[in_vmem()] * 5 + [in_smem()],
+        in_specs=[pl.BlockSpec(memory_space=pltpu.HBM)] * 4,
+        out_specs=[in_vmem()] * 4 + [in_smem()],
         scratch_shapes=[
             pltpu.SMEM(radius.shape, radius.dtype),
             pltpu.SMEM(load_index.shape, load_index.dtype),
             pltpu.SMEM(load_force.shape, load_force.dtype),
             pltpu.VMEM(fixed.shape, fixed.dtype),
-            pltpu.SemaphoreType.DMA((5,)),
+            pltpu.SemaphoreType.DMA((4,)),
         ],
         compiler_params=pltpu.CompilerParams(vmem_limit_bytes=KERNEL_VMEM),
         cost_estimate=pl.CostEstimate(
@@ -441,14 +423,14 @@
     )(
         *(
             pltpu.with_memory_space_constraint(array, pltpu.HBM)
-            for array in (radius, load_index, load_force, fixed, density)
+            for array in (radius, load_index, load_force, fixed)
         )
     )
 
 
 def sweep_call(spot, load, weights, totals, free, density, displacement):
-    devices, own_planes, layers, row_width = density.shape
-    planes = devices * own_planes
+    cores, chips, own_planes, layers, row_width = density.shape
+    planes = cores * chips * own_planes
 
     def scratch(*lead):
         return pltpu.VMEM(lead + (layers, row_width), jnp.float32)
@@ -457,7 +439,7 @@
         sweep_kernel,
         out_shape=[
             floats(3, planes, layers, row_width),
-            floats(2, devices // 2, own_planes, layers, row_width),
+            floats(*density.shape),
             floats(planes, layers, row_width),
         ],
         in_specs=[in_smem()] + [in_vmem()] * 6,
@@ -482,8 +464,8 @@
 
 
 def design_call(weights, sens, coef, density):
-    devices, own_planes, layers, row_width = density.shape
-    planes = devices * own_planes
+    cores, chips, own_planes, layers, row_width = density.shape
+    planes = cores * chips * own_planes
 
     def scratch(*lead):
         return pltpu.VMEM(lead + (layers, row_width), jnp.float32)
@@ -517,25 +499,13 @@
     return lax.all_to_all(pieces, "space", 0, 0, axis_index_groups=groups)
 
 
-def gathered(block):
+def chip_gathered(block):
     chips = lax.axis_size("space") // 2
-    same = between_chips(jnp.broadcast_to(block[None], (chips,) + block.shape))
-    return jnp.stack([same, other_core(same)])
-
-
-def partner_gathered(block, prepare):
-    devices = lax.axis_size("space")
-
-    def swapped(pieces, bit):
-        return lax.ppermute(pieces, "space", [(i, i ^ 1 << bit) for i in range(devices)])
-
-    first, *bits = reversed(range(devices.bit_length() - 1))
-    other = swapped(block[None], first)
-    other, (own, *prepared) = lax.optimization_barrier((other, prepare()))
-    pieces = jnp.concatenate([own, other])
-    for bit in bits:
-        pieces = jnp.concatenate([pieces, swapped(pieces, bit)])
-    return pieces, prepared
+    return between_chips(jnp.broadcast_to(block[None], (chips,) + block.shape))
+
+
+def with_other_core(blocks):
+    return jnp.stack([blocks, other_core(blocks)])
 
 
 def scattered_sum(pieces):
@@ -543,14 +513,15 @@
 
 
 def one_slab(density, displacement, fixed, load_index, load_force, radius):
-    whole, prepared = partner_gathered(
-        density, lambda: prepare_call(radius, load_index, load_force.T, fixed, density)
-    )
-    weights, totals, free, load, spot = prepared
+    same_core, small = lax.optimization_barrier(
+        (chip_gathered(density), (radius, load_index, load_force.T, fixed))
+    )
+    whole = with_other_core(same_core)
+    weights, totals, free, load, spot = prepare_call(*small)
     new_displacement, sens, coef = sweep_call(
         spot, load, weights, totals, free, whole, displacement[0]
     )
-    sens = gathered(scattered_sum(sens))
+    sens = with_other_core(chip_gathered(scattered_sum(sens)))
     new_density = design_call(weights, sens, coef, whole)
     return new_density, new_displacement[None]
 

time: 52.8 us -> 50.8 us (0.962)
  blocking collectives: 23.2 us -> 34.4 us
  starting transfers between devices: 8.18 us -> 0.58 us
  waiting for transfers between devices: 8.71 us -> 2.33 us
  local copies, waits for them, and re-layouts: 0.05 us -> 0.82 us
    all_to_all x2 -> x3, blocking collectives: 23.2 us -> 34.4 us  [between_chips(): return lax.all_to_all(pieces, 'space', 0, 0, axis_index_groups=groups)]
    ppermute x4 -> x0, starting transfers between devices: 7.95 us -> none  [swapped(): lax.ppermute(pieces, 'space', [(i, i ^ 1 << bit) for i in range(devices)])]
    ppermute x4 -> x0, waiting for transfers between devices: 6.18 us -> none  [swapped(): lax.ppermute(pieces, 'space', [(i, i ^ 1 << bit) for i in range(devices)])]
    broadcast_in_dim x1 -> x2, local copies, waits for them, and re-layouts: 0.01 us -> 0.81 us  [chip_gathered(): return between_chips(jnp.broadcast_to(block[None], (chips,) + block.shape))]
    ppermute x2 -> x3, waiting for transfers between devices: 2.54 us -> 2.33 us  [other_core(): return lax.ppermute(block, 'space', [(i, i ^ 1) for i in range(devices)])]
  transfers between devices with their start and end apart: 6 -> 3, of which waited for: 6 -> 2; matrix products, arithmetic and copies ran while one was open for 0% -> 0% of each run, Pallas kernels for 3% -> 3%
where the time goes in v10:
time: 50.8 us; the launch traced here: 50.4 us
  blocking collectives  34.4 us (68%)
  Pallas kernels  11.4 us (22%)
  waiting for transfers between devices  2.33 us (5%)
  local copies, waits for them, and re-layouts  0.82 us (2%)
  between operations  0.69 us (1%)
  starting transfers between devices  0.58 us (1%)
    all_to_all x3, blocking collectives, between_chips(): return lax.all_to_all(pieces, 'space', 0, 0, axis_index_groups=groups)  34.4 us
    pallas_call x1, Pallas kernels, sweep_call(): pl.pallas_call(sweep_kernel, out_shape=[floats(3, planes, layers, row_wid...  6.4 us
    pallas_call x1, Pallas kernels, design_call(): pl.pallas_call(design_kernel, out_shape=jax.ShapeDtypeStruct((own_planes,...  3.64 us
    ppermute x3, waiting for transfers between devices, other_core(): return lax.ppermute(block, 'space', [(i, i ^ 1) for i in range(devices)])  2.33 us
    pallas_call x1, Pallas kernels, prepare_call(): pl.pallas_call(prepare_kernel, out_shape=[floats(len(ALL_SQUARES), layers...  1.4 us
  transfers between devices with their start and end apart: 3, of which 2 were waited for; matrix products, arithmetic and copies ran while one was open for 0% of the time, Pallas kernels for 3%

profile of v10, /device:TPU:0, one launch (start us, length us, event | category | flops | bytes accessed | tf_op | source)
XLA Modules:
  0.0 50.4 jit_solution(7299744361631519544)
XLA Ops:
  0.6 0.0 copy-start
  0.6 0.8 %broadcast_in_dim.6 = f32[8,2,16,128]{3,2,1,0:T(8,128)S(1)} broadcast(f32[2,16,128]{2,1,0:T(8,128)} %param.6), dimensions={1,2,3} | broadcast | bytes 147456 | tf_op jit(solution)/shard_map/broadcast_in_dim | solution.py:504
  1.4 14.4 %all_to_all.15 = f32[8,2,16,128]{3,2,1,0:T(8,128)S(1)} all-to-all(f32[8,2,16,128]{3,2,1,0:T(8,128)S(1)} %broadcast_in_dim.6), channel_id=1, replica_groups={{0,2,4,6,8,10,12,14},{1,3,5,7,9,11,13,15},{16,18,20,22,24,26,28,30},{17..., dimensions={0} | all-to-all | bytes 262144 | tf_op jit(solution)/shard_map/all_to_all | solution.py:499
  15.8 0.0 collective-permute-start
  15.8 1.4 %prepare.1 = (f32[10,16,128]{2,1,0:T(8,128)S(1)}, f32[5,16,128]{2,1,0:T(8,128)S(1)}, f32[32,16,128]{2,1,0:T(8,128)S(1)}, f32[3,16,128]{2,1,0:T(8,128)S(1)}, s32[1]{0:T(128)}) custom-call(s32[16]{0:T(128)} %radius_hbm, s32[16]{0:T(128)} %index_hbm, f32[3,16]{1,0:T(4,128)} %bitcast.16, s32[32,128]{1,0:T(8,128)} %fixed_hbm), custom_call_target="tpu_custom_call" | custom-call | flops 2621440 | bytes 524288 | tf_op jit(solution)/shard_map/prepare/pallas_call | solution.py:398
  17.2 0.0 collective-permute-done
  17.3 0.0 copy-done
  17.3 6.4 %sweeps.1 = (f32[3,32,16,128]{3,2,1,0:T(8,128)}, f32[2,8,2,16,128]{4,3,2,1,0:T(8,128)S(1)}, f32[32,16,128]{2,1,0:T(8,128)S(1)}) custom-call(s32[1]{0:T(128)} %get-tuple-element.20.spot_ref, f32[3,16,128]{2,1,0:T(8,128)S(1)} %get-tuple-element.21.load_ref, f32[10,16,128]{2,1,0:T(8,128)S(1)} %get-tuple-element.19.weight_ref, ...), custom_call_target="tpu_custom_call" | custom-call | tf_op jit(solution)/shard_map/sweeps/pallas_call | solution.py:438
  23.7 0.6 %collective-permute-start.1 = (f32[8,2,16,128]{3,2,1,0:T(8,128)S(1)}, f32[8,2,16,128]{3,2,1,0:T(8,128)S(1)}, u32[]{:S(2)}, u32[]{:S(2)}) collective-permute-start(f32[8,2,16,128]{3,2,1,0:T(8,128)S(1)} %slice_bitcast_fusion), channel_id=1, source_target_pairs={{0,1},{1,0},{2,3},{3,2},{4,5},{5,4},{6,7},{7,6},{8,9},{9,8},{10,11... | collective-permute-start | bytes 393224 | tf_op jit(solution)/shard_map/ppermute | solution.py:493
  24.3 1.0 %collective-permute-done.1 = f32[8,2,16,128]{3,2,1,0:T(8,128)S(1)} collective-permute-done((f32[8,2,16,128]{3,2,1,0:T(8,128)S(1)}, f32[8,2,16,128]{3,2,1,0:T(8,128)S(1)}, u32[]{:S(2)}, u32[]{:S(2)}) %collective-permute-start.1) | collective-permute-done | bytes 131104 | tf_op jit(solution)/shard_map/ppermute | solution.py:493
  25.3 10.2 %all_to_all.16 = f32[8,2,16,128]{3,2,1,0:T(8,128)S(1)} all-to-all(f32[8,2,16,128]{3,2,1,0:T(8,128)S(1)} %bitcast_add_fusion), channel_id=1, replica_groups={{0,2,4,6,8,10,12,14},{1,3,5,7,9,11,13,15},{16,18,20,22,24,26,28,30},{17..., dimensions={0} | all-to-all | bytes 262144 | tf_op jit(solution)/shard_map/all_to_all | solution.py:499
  35.5 9.8 %all_to_all.17 = f32[8,2,16,128]{3,2,1,0:T(8,128)S(1)} all-to-all(f32[8,2,16,128]{3,2,1,0:T(8,128)S(1)} %broadcast_in_dim.7), channel_id=1, replica_groups={{0,2,4,6,8,10,12,14},{1,3,5,7,9,11,13,15},{16,18,20,22,24,26,28,30},{17..., dimensions={0} | all-to-all | bytes 262144 | tf_op jit(solution)/shard_map/all_to_all | solution.py:499
  45.3 0.0 collective-permute-start.2
  45.4 1.3 %collective-permute-done.2 = f32[8,2,16,128]{3,2,1,0:T(8,128)S(1)} collective-permute-done((f32[8,2,16,128]{3,2,1,0:T(8,128)S(1)}, f32[8,2,16,128]{3,2,1,0:T(8,128)S(1)}, u32[]{:S(2)}, u32[]{:S(2)}) %collective-permute-start.2) | collective-permute-done | bytes 131104 | tf_op jit(solution)/shard_map/ppermute | solution.py:493
  46.7 3.6 %design.1 = f32[2,16,128]{2,1,0:T(8,128)} custom-call(f32[10,16,128]{2,1,0:T(8,128)S(1)} %get-tuple-element.19.weight_ref, f32[2,8,2,16,128]{4,3,2,1,0:T(8,128)S(1)} %pad_maximum_fusion.1.sens_ref, f32[32,16,128]{2,1,0:T(8,128)S(1)} %get-tuple-element.26.coef_ref, f32[2,8,2,16,128]{4,3,2,1,0:T(8,128)S(1)} %pad_maximum_fusion.density_ref), custom_call_target="tpu_custom_call" | custom-call | tf_op jit(solution)/shard_map/design/pallas_call | solution.py:473
  (6 shorter events, 0.1 us)
Async XLA Ops:
  0.6 16.7 %copy-start = (f32[1,3,32,16,128]{4,3,2,1,0:T(8,128)S(1)}, f32[1,3,32,16,128]{4,3,2,1,0:T(8,128)}, u32[]{:S(2)}) copy-start(f32[1,3,32,16,128]{4,3,2,1,0:T(8,128)} %param.7) | copy-start | bytes 2359300
  15.8 1.4 %collective-permute-start = (f32[8,2,16,128]{3,2,1,0:T(8,128)S(1)}, f32[8,2,16,128]{3,2,1,0:T(8,128)S(1)}, u32[]{:S(2)}, u32[]{:S(2)}) collective-permute-start(f32[8,2,16,128]{3,2,1,0:T(8,128)S(1)} %all_to_all.15), channel_id=1, source_target_pairs={{0,1},{1,0},{2,3},{3,2},{4,5},{5,4},{6,7},{7,6},{8,9},{9,8},{10,11... | collective-permute-start | bytes 393224 | tf_op jit(solution)/shard_map/ppermute | solution.py:493
  23.7 1.6 %collective-permute-start.1 = (f32[8,2,16,128]{3,2,1,0:T(8,128)S(1)}, f32[8,2,16,128]{3,2,1,0:T(8,128)S(1)}, u32[]{:S(2)}, u32[]{:S(2)}) collective-permute-start(f32[8,2,16,128]{3,2,1,0:T(8,128)S(1)} %slice_bitcast_fusion), channel_id=1, source_target_pairs={{0,1},{1,0},{2,3},{3,2},{4,5},{5,4},{6,7},{7,6},{8,9},{9,8},{10,11... | collective-permute-start | bytes 393224 | tf_op jit(solution)/shard_map/ppermute | solution.py:493
  45.3 1.3 %collective-permute-start.2 = (f32[8,2,16,128]{3,2,1,0:T(8,128)S(1)}, f32[8,2,16,128]{3,2,1,0:T(8,128)S(1)}, u32[]{:S(2)}, u32[]{:S(2)}) collective-permute-start(f32[8,2,16,128]{3,2,1,0:T(8,128)S(1)} %all_to_all.17), channel_id=1, source_target_pairs={{0,1},{1,0},{2,3},{3,2},{4,5},{5,4},{6,7},{7,6},{8,9},{9,8},{10,11... | collective-permute-start | bytes 393224 | tf_op jit(solution)/shard_map/ppermute | solution.py:493

commit v11 on v10

--- a/solution.py
+++ b/solution.py
@@ -160,7 +160,7 @@
         )
         return carry
 
-    lax.fori_loop(0, planes, free_plane, 0, unroll=8)
+    lax.fori_loop(0, planes, free_plane, 0, unroll=16)
 
     own_index = index_ref[load_place]
     own_z = own_index // row_width % layers
@@ -213,7 +213,7 @@
         far_ref[x + 2] = far
         return carry
 
-    lax.fori_loop(0, planes, filter_plane, 0, unroll=8)
+    lax.fori_loop(0, planes, filter_plane, 0, unroll=16)
 
     def modulus_plane(x, carry):
         total = total_ref[edge_class(x, planes)]
@@ -229,7 +229,7 @@
         coef_ref[x] = 3.0 * (1.0 - floor_modulus) * (filtered * filtered) / total
         return carry
 
-    lax.fori_loop(0, planes, modulus_plane, 0, unroll=8)
+    lax.fori_loop(0, planes, modulus_plane, 0, unroll=16)
 
     across_ref[0] = zero
     across_ref[planes] = zero
@@ -262,7 +262,7 @@
             first_ref[part, x + 1] = start_ref[part, x] * free
         return ahead
 
-    lax.fori_loop(0, planes, face_plane, zero, unroll=8)
+    lax.fori_loop(0, planes, face_plane, zero, unroll=16)
 
     own_x = spot_ref[0]
 
@@ -281,7 +281,7 @@
                 target[part, x + lead] = (1.0 - relax_factor) * here + rate_ref[part, x] * pull
             return carry
 
-        lax.fori_loop(0, planes, sweep_plane, 0, unroll=8)
+        lax.fori_loop(0, planes, sweep_plane, 0, unroll=16)
         for part in range(3):
             target[part, own_x + lead] += rate_ref[part, own_x] * load_ref[part]
 
@@ -307,7 +307,7 @@
         sens_ref[pair_spot(x, own_planes)] = (0.5 / load_cases) * total
         return ahead
 
-    lax.fori_loop(0, planes, energy_plane, zero, unroll=8)
+    lax.fori_loop(0, planes, energy_plane, zero, unroll=16)
 
 
 def design_kernel(
@@ -340,7 +340,7 @@
         far_ref[x + 2] = far
         return carry
 
-    lax.fori_loop(0, planes, filter_plane, 0, unroll=8)
+    lax.fori_loop(0, planes, filter_plane, 0, unroll=16)
 
     def root_plane(x, carry):
         root = jnp.sqrt(
@@ -352,7 +352,7 @@
         high_ref[x] = jnp.minimum(density + move_limit, 1.0)
         return carry
 
-    lax.fori_loop(0, planes, root_plane, 0, unroll=8)
+    lax.fori_loop(0, planes, root_plane, 0, unroll=16)
 
     target = volume_share * planes * layers * row_width
 

time: 50.8 us -> 49.7 us (0.978)
  Pallas kernels: 11.4 us -> 10.4 us
    pallas_call x1, Pallas kernels: 6.4 us -> 5.49 us  [sweep_call(): pl.pallas_call(sweep_kernel, out_shape=[floats(3, planes, layers, row_wid...]
where the time goes in v11:
time: 49.7 us; the launch traced here: 49.3 us
  blocking collectives  34.4 us (69%)
  Pallas kernels  10.4 us (21%)
  waiting for transfers between devices  2.33 us (5%)
  local copies, waits for them, and re-layouts  0.82 us (2%)
  between operations  0.69 us (1%)
  starting transfers between devices  0.58 us (1%)
    all_to_all x3, blocking collectives, between_chips(): return lax.all_to_all(pieces, 'space', 0, 0, axis_index_groups=groups)  34.4 us
    pallas_call x1, Pallas kernels, sweep_call(): pl.pallas_call(sweep_kernel, out_shape=[floats(3, planes, layers, row_wid...  5.49 us
    pallas_call x1, Pallas kernels, design_call(): pl.pallas_call(design_kernel, out_shape=jax.ShapeDtypeStruct((own_planes,...  3.49 us
    ppermute x3, waiting for transfers between devices, other_core(): return lax.ppermute(block, 'space', [(i, i ^ 1) for i in range(devices)])  2.33 us
    pallas_call x1, Pallas kernels, prepare_call(): pl.pallas_call(prepare_kernel, out_shape=[floats(len(ALL_SQUARES), layers...  1.4 us
  transfers between devices with their start and end apart: 3, of which 2 were waited for; matrix products, arithmetic and copies ran while one was open for 0% of the time, Pallas kernels for 3%

profile of v11, /device:TPU:0, one launch (start us, length us, event | category | flops | bytes accessed | tf_op | source)
XLA Modules:
  0.0 49.3 jit_solution(699404343704822924)
XLA Ops:
  0.6 0.0 copy-start
  0.6 0.8 %broadcast_in_dim.6 = f32[8,2,16,128]{3,2,1,0:T(8,128)S(1)} broadcast(f32[2,16,128]{2,1,0:T(8,128)} %param.6), dimensions={1,2,3} | broadcast | bytes 147456 | tf_op jit(solution)/shard_map/broadcast_in_dim | solution.py:504
  1.4 14.4 %all_to_all.15 = f32[8,2,16,128]{3,2,1,0:T(8,128)S(1)} all-to-all(f32[8,2,16,128]{3,2,1,0:T(8,128)S(1)} %broadcast_in_dim.6), channel_id=1, replica_groups={{0,2,4,6,8,10,12,14},{1,3,5,7,9,11,13,15},{16,18,20,22,24,26,28,30},{17..., dimensions={0} | all-to-all | bytes 262144 | tf_op jit(solution)/shard_map/all_to_all | solution.py:499
  15.8 0.0 collective-permute-start
  15.8 1.4 %prepare.1 = (f32[10,16,128]{2,1,0:T(8,128)S(1)}, f32[5,16,128]{2,1,0:T(8,128)S(1)}, f32[32,16,128]{2,1,0:T(8,128)S(1)}, f32[3,16,128]{2,1,0:T(8,128)S(1)}, s32[1]{0:T(128)}) custom-call(s32[16]{0:T(128)} %radius_hbm, s32[16]{0:T(128)} %index_hbm, f32[3,16]{1,0:T(4,128)} %bitcast.16, s32[32,128]{1,0:T(8,128)} %fixed_hbm), custom_call_target="tpu_custom_call" | custom-call | flops 2621440 | bytes 524288 | tf_op jit(solution)/shard_map/prepare/pallas_call | solution.py:398
  17.2 0.0 collective-permute-done
  17.3 0.0 copy-done
  17.3 5.5 %sweeps.1 = (f32[3,32,16,128]{3,2,1,0:T(8,128)}, f32[2,8,2,16,128]{4,3,2,1,0:T(8,128)S(1)}, f32[32,16,128]{2,1,0:T(8,128)S(1)}) custom-call(s32[1]{0:T(128)} %get-tuple-element.20.spot_ref, f32[3,16,128]{2,1,0:T(8,128)S(1)} %get-tuple-element.21.load_ref, f32[10,16,128]{2,1,0:T(8,128)S(1)} %get-tuple-element.19.weight_ref, ...), custom_call_target="tpu_custom_call" | custom-call | tf_op jit(solution)/shard_map/sweeps/pallas_call | solution.py:438
  22.8 0.6 %collective-permute-start.1 = (f32[8,2,16,128]{3,2,1,0:T(8,128)S(1)}, f32[8,2,16,128]{3,2,1,0:T(8,128)S(1)}, u32[]{:S(2)}, u32[]{:S(2)}) collective-permute-start(f32[8,2,16,128]{3,2,1,0:T(8,128)S(1)} %slice_bitcast_fusion), channel_id=1, source_target_pairs={{0,1},{1,0},{2,3},{3,2},{4,5},{5,4},{6,7},{7,6},{8,9},{9,8},{10,11... | collective-permute-start | bytes 393224 | tf_op jit(solution)/shard_map/ppermute | solution.py:493
  23.4 1.0 %collective-permute-done.1 = f32[8,2,16,128]{3,2,1,0:T(8,128)S(1)} collective-permute-done((f32[8,2,16,128]{3,2,1,0:T(8,128)S(1)}, f32[8,2,16,128]{3,2,1,0:T(8,128)S(1)}, u32[]{:S(2)}, u32[]{:S(2)}) %collective-permute-start.1) | collective-permute-done | bytes 131104 | tf_op jit(solution)/shard_map/ppermute | solution.py:493
  24.4 10.2 %all_to_all.16 = f32[8,2,16,128]{3,2,1,0:T(8,128)S(1)} all-to-all(f32[8,2,16,128]{3,2,1,0:T(8,128)S(1)} %bitcast_add_fusion), channel_id=1, replica_groups={{0,2,4,6,8,10,12,14},{1,3,5,7,9,11,13,15},{16,18,20,22,24,26,28,30},{17..., dimensions={0} | all-to-all | bytes 262144 | tf_op jit(solution)/shard_map/all_to_all | solution.py:499
  34.6 9.8 %all_to_all.17 = f32[8,2,16,128]{3,2,1,0:T(8,128)S(1)} all-to-all(f32[8,2,16,128]{3,2,1,0:T(8,128)S(1)} %broadcast_in_dim.7), channel_id=1, replica_groups={{0,2,4,6,8,10,12,14},{1,3,5,7,9,11,13,15},{16,18,20,22,24,26,28,30},{17..., dimensions={0} | all-to-all | bytes 262144 | tf_op jit(solution)/shard_map/all_to_all | solution.py:499
  44.4 0.0 collective-permute-start.2
  44.4 1.3 %collective-permute-done.2 = f32[8,2,16,128]{3,2,1,0:T(8,128)S(1)} collective-permute-done((f32[8,2,16,128]{3,2,1,0:T(8,128)S(1)}, f32[8,2,16,128]{3,2,1,0:T(8,128)S(1)}, u32[]{:S(2)}, u32[]{:S(2)}) %collective-permute-start.2) | collective-permute-done | bytes 131104 | tf_op jit(solution)/shard_map/ppermute | solution.py:493
  45.8 3.5 %design.1 = f32[2,16,128]{2,1,0:T(8,128)} custom-call(f32[10,16,128]{2,1,0:T(8,128)S(1)} %get-tuple-element.19.weight_ref, f32[2,8,2,16,128]{4,3,2,1,0:T(8,128)S(1)} %pad_maximum_fusion.1.sens_ref, f32[32,16,128]{2,1,0:T(8,128)S(1)} %get-tuple-element.26.coef_ref, f32[2,8,2,16,128]{4,3,2,1,0:T(8,128)S(1)} %pad_maximum_fusion.density_ref), custom_call_target="tpu_custom_call" | custom-call | tf_op jit(solution)/shard_map/design/pallas_call | solution.py:473
  (6 shorter events, 0.1 us)
Async XLA Ops:
  0.6 16.7 %copy-start = (f32[1,3,32,16,128]{4,3,2,1,0:T(8,128)S(1)}, f32[1,3,32,16,128]{4,3,2,1,0:T(8,128)}, u32[]{:S(2)}) copy-start(f32[1,3,32,16,128]{4,3,2,1,0:T(8,128)} %param.7) | copy-start | bytes 2359300
  15.8 1.4 %collective-permute-start = (f32[8,2,16,128]{3,2,1,0:T(8,128)S(1)}, f32[8,2,16,128]{3,2,1,0:T(8,128)S(1)}, u32[]{:S(2)}, u32[]{:S(2)}) collective-permute-start(f32[8,2,16,128]{3,2,1,0:T(8,128)S(1)} %all_to_all.15), channel_id=1, source_target_pairs={{0,1},{1,0},{2,3},{3,2},{4,5},{5,4},{6,7},{7,6},{8,9},{9,8},{10,11... | collective-permute-start | bytes 393224 | tf_op jit(solution)/shard_map/ppermute | solution.py:493
  22.8 1.6 %collective-permute-start.1 = (f32[8,2,16,128]{3,2,1,0:T(8,128)S(1)}, f32[8,2,16,128]{3,2,1,0:T(8,128)S(1)}, u32[]{:S(2)}, u32[]{:S(2)}) collective-permute-start(f32[8,2,16,128]{3,2,1,0:T(8,128)S(1)} %slice_bitcast_fusion), channel_id=1, source_target_pairs={{0,1},{1,0},{2,3},{3,2},{4,5},{5,4},{6,7},{7,6},{8,9},{9,8},{10,11... | collective-permute-start | bytes 393224 | tf_op jit(solution)/shard_map/ppermute | solution.py:493
  44.4 1.3 %collective-permute-start.2 = (f32[8,2,16,128]{3,2,1,0:T(8,128)S(1)}, f32[8,2,16,128]{3,2,1,0:T(8,128)S(1)}, u32[]{:S(2)}, u32[]{:S(2)}) collective-permute-start(f32[8,2,16,128]{3,2,1,0:T(8,128)S(1)} %all_to_all.17), channel_id=1, source_target_pairs={{0,1},{1,0},{2,3},{3,2},{4,5},{5,4},{6,7},{7,6},{8,9},{9,8},{10,11... | collective-permute-start | bytes 393224 | tf_op jit(solution)/shard_map/ppermute | solution.py:493

commit v12 on v11

--- a/solution.py
+++ b/solution.py
@@ -115,7 +115,7 @@
     force_hbm,
     fixed_hbm,
     weight_ref,
-    total_ref,
+    inverse_ref,
     free_ref,
     load_ref,
     spot_ref,
@@ -149,7 +149,7 @@
     class_weights(radius_ref, weight_ref)
     ones = forward_planes(jnp.ones(shape, jnp.float32), weight_ref)
     for place, (lower, upper) in enumerate(((0, 2), (1, 2), (2, 2), (2, 1), (2, 0))):
-        total_ref[place] = (
+        inverse_ref[place] = 1.0 / (
             ones[0] + min(lower, 1) * ones[1] + min(upper, 1) * ones[1]
             + (lower // 2) * ones[2] + (upper // 2) * ones[2]
         )
@@ -175,11 +175,11 @@
     spot_ref,
     load_ref,
     weight_ref,
-    total_ref,
+    inverse_ref,
     free_ref,
     density_ref,
     start_ref,
-    disp_ref,
+    disp_hbm,
     sens_ref,
     coef_ref,
     near_ref,
@@ -194,6 +194,8 @@
     rate_ref,
     first_ref,
     second_ref,
+    disp_ref,
+    stored,
 ):
     planes, layers, row_width = coef_ref.shape
     own_planes = density_ref.shape[2]
@@ -216,17 +218,17 @@
     lax.fori_loop(0, planes, filter_plane, 0, unroll=16)
 
     def modulus_plane(x, carry):
-        total = total_ref[edge_class(x, planes)]
+        inverse = inverse_ref[edge_class(x, planes)]
         filtered = (
             near_ref[x + 2]
             + side_ref[x + 1]
             + side_ref[x + 3]
             + far_ref[x]
             + far_ref[x + 4]
-        ) / total
+        ) * inverse
         modulus = floor_modulus + (1.0 - floor_modulus) * (filtered * filtered * filtered)
         modulus_ref[x] = modulus
-        coef_ref[x] = 3.0 * (1.0 - floor_modulus) * (filtered * filtered) / total
+        coef_ref[x] = 3.0 * (1.0 - floor_modulus) * (filtered * filtered) * inverse
         return carry
 
     lax.fori_loop(0, planes, modulus_plane, 0, unroll=16)
@@ -257,8 +259,14 @@
         every = sums[0] + sums[1] + sums[2]
         free = free_ref[x]
         push = relax_factor * free
+        diagonal = [every + part_sum for part_sum in sums]
+        pair = diagonal[0] * diagonal[1]
+        push = push / (pair * diagonal[2])
+        side = push * diagonal[2]
+        rate_ref[0, x] = side * diagonal[1]
+        rate_ref[1, x] = side * diagonal[0]
+        rate_ref[2, x] = push * pair
         for part in range(3):
-            rate_ref[part, x] = push / (every + sums[part])
             first_ref[part, x + 1] = start_ref[part, x] * free
         return ahead
 
@@ -289,6 +297,8 @@
     for turn in range(SWEEPS - 1):
         sweep(stages[turn % 2], stages[(turn + 1) % 2], 1)
     sweep(stages[(SWEEPS - 1) % 2], disp_ref, 0)
+    store = pltpu.make_async_copy(disp_ref, disp_hbm, stored)
+    store.start()
 
     def energy_plane(x, carry):
         later = jnp.minimum(x + 1, planes - 1)
@@ -308,6 +318,7 @@
         return ahead
 
     lax.fori_loop(0, planes, energy_plane, zero, unroll=16)
+    store.wait()
 
 
 def design_kernel(
@@ -428,7 +439,7 @@
     )
 
 
-def sweep_call(spot, load, weights, totals, free, density, displacement):
+def sweep_call(spot, load, weights, inverses, free, density, displacement):
     cores, chips, own_planes, layers, row_width = density.shape
     planes = cores * chips * own_planes
 
@@ -443,7 +454,7 @@
             floats(planes, layers, row_width),
         ],
         in_specs=[in_smem()] + [in_vmem()] * 6,
-        out_specs=[in_vmem()] * 3,
+        out_specs=[pl.BlockSpec(memory_space=pltpu.HBM), in_vmem(), in_vmem()],
         scratch_shapes=[
             scratch(planes + 4),
             scratch(planes + 4),
@@ -457,10 +468,12 @@
             scratch(3, planes),
             scratch(3, planes + 2),
             scratch(3, planes + 2),
+            scratch(3, planes),
+            pltpu.SemaphoreType.DMA(()),
         ],
         compiler_params=pltpu.CompilerParams(vmem_limit_bytes=KERNEL_VMEM),
         name="sweeps",
-    )(spot, load, weights, totals, free, density, displacement)
+    )(spot, load, weights, inverses, free, density, displacement)
 
 
 def design_call(weights, sens, coef, density):
@@ -517,9 +530,9 @@
         (chip_gathered(density), (radius, load_index, load_force.T, fixed))
     )
     whole = with_other_core(same_core)
-    weights, totals, free, load, spot = prepare_call(*small)
+    weights, inverses, free, load, spot = prepare_call(*small)
     new_displacement, sens, coef = sweep_call(
-        spot, load, weights, totals, free, whole, displacement[0]
+        spot, load, weights, inverses, free, whole, displacement[0]
     )
     sens = with_other_core(chip_gathered(scattered_sum(sens)))
     new_density = design_call(weights, sens, coef, whole)

time: 49.7 us -> 49.2 us (0.990)
  Pallas kernels: 10.4 us -> 9.81 us
    pallas_call x1, Pallas kernels: 5.49 us -> 4.92 us  [sweep_call(): pl.pallas_call(sweep_kernel, out_shape=[floats(3, planes, layers, row_wid...]
where the time goes in v12:
time: 49.2 us; the launch traced here: 48.8 us
  blocking collectives  34.4 us (70%)
  Pallas kernels  9.81 us (20%)
  waiting for transfers between devices  2.33 us (5%)
  local copies, waits for them, and re-layouts  0.83 us (2%)
  between operations  0.71 us (1%)
  starting transfers between devices  0.59 us (1%)
    all_to_all x3, blocking collectives, between_chips(): return lax.all_to_all(pieces, 'space', 0, 0, axis_index_groups=groups)  34.4 us
    pallas_call x1, Pallas kernels, sweep_call(): pl.pallas_call(sweep_kernel, out_shape=[floats(3, planes, layers, row_wid...  4.92 us
    pallas_call x1, Pallas kernels, design_call(): pl.pallas_call(design_kernel, out_shape=jax.ShapeDtypeStruct((own_planes,...  3.49 us
    ppermute x3, waiting for transfers between devices, other_core(): return lax.ppermute(block, 'space', [(i, i ^ 1) for i in range(devices)])  2.33 us
    pallas_call x1, Pallas kernels, prepare_call(): pl.pallas_call(prepare_kernel, out_shape=[floats(len(ALL_SQUARES), layers...  1.4 us
  transfers between devices with their start and end apart: 3, of which 2 were waited for; matrix products, arithmetic and copies ran while one was open for 0% of the time, Pallas kernels for 3%

profile of v12, /device:TPU:0, one launch (start us, length us, event | category | flops | bytes accessed | tf_op | source)
XLA Modules:
  0.0 48.8 jit_solution(4548464868562435749)
XLA Ops:
  0.6 0.0 copy-start
  0.6 0.8 %broadcast_in_dim.6 = f32[8,2,16,128]{3,2,1,0:T(8,128)S(1)} broadcast(f32[2,16,128]{2,1,0:T(8,128)} %param.6), dimensions={1,2,3} | broadcast | bytes 147456 | tf_op jit(solution)/shard_map/broadcast_in_dim | solution.py:517
  1.4 14.4 %all_to_all.15 = f32[8,2,16,128]{3,2,1,0:T(8,128)S(1)} all-to-all(f32[8,2,16,128]{3,2,1,0:T(8,128)S(1)} %broadcast_in_dim.6), channel_id=1, replica_groups={{0,2,4,6,8,10,12,14},{1,3,5,7,9,11,13,15},{16,18,20,22,24,26,28,30},{17..., dimensions={0} | all-to-all | bytes 262144 | tf_op jit(solution)/shard_map/all_to_all | solution.py:512
  15.8 0.0 collective-permute-start
  15.8 1.4 %prepare.1 = (f32[10,16,128]{2,1,0:T(8,128)S(1)}, f32[5,16,128]{2,1,0:T(8,128)S(1)}, f32[32,16,128]{2,1,0:T(8,128)S(1)}, f32[3,16,128]{2,1,0:T(8,128)S(1)}, s32[1]{0:T(128)}) custom-call(s32[16]{0:T(128)} %radius_hbm, s32[16]{0:T(128)} %index_hbm, f32[3,16]{1,0:T(4,128)} %bitcast.16, s32[32,128]{1,0:T(8,128)} %fixed_hbm), custom_call_target="tpu_custom_call" | custom-call | flops 2621440 | bytes 524288 | tf_op jit(solution)/shard_map/prepare/pallas_call | solution.py:409
  17.3 0.0 collective-permute-done
  17.3 0.0 copy-done
  17.3 4.9 %sweeps.1 = (f32[3,32,16,128]{3,2,1,0:T(8,128)}, f32[2,8,2,16,128]{4,3,2,1,0:T(8,128)S(1)}, f32[32,16,128]{2,1,0:T(8,128)S(1)}) custom-call(s32[1]{0:T(128)} %get-tuple-element.20.spot_ref, f32[3,16,128]{2,1,0:T(8,128)S(1)} %get-tuple-element.21.load_ref, f32[10,16,128]{2,1,0:T(8,128)S(1)} %get-tuple-element.19.weight_ref, ...), custom_call_target="tpu_custom_call" | custom-call | tf_op jit(solution)/shard_map/sweeps/pallas_call | solution.py:449
  22.2 0.6 %collective-permute-start.1 = (f32[8,2,16,128]{3,2,1,0:T(8,128)S(1)}, f32[8,2,16,128]{3,2,1,0:T(8,128)S(1)}, u32[]{:S(2)}, u32[]{:S(2)}) collective-permute-start(f32[8,2,16,128]{3,2,1,0:T(8,128)S(1)} %slice_bitcast_fusion), channel_id=1, source_target_pairs={{0,1},{1,0},{2,3},{3,2},{4,5},{5,4},{6,7},{7,6},{8,9},{9,8},{10,11... | collective-permute-start | bytes 393224 | tf_op jit(solution)/shard_map/ppermute | solution.py:506
  22.8 1.0 %collective-permute-done.1 = f32[8,2,16,128]{3,2,1,0:T(8,128)S(1)} collective-permute-done((f32[8,2,16,128]{3,2,1,0:T(8,128)S(1)}, f32[8,2,16,128]{3,2,1,0:T(8,128)S(1)}, u32[]{:S(2)}, u32[]{:S(2)}) %collective-permute-start.1) | collective-permute-done | bytes 131104 | tf_op jit(solution)/shard_map/ppermute | solution.py:506
  23.8 10.2 %all_to_all.16 = f32[8,2,16,128]{3,2,1,0:T(8,128)S(1)} all-to-all(f32[8,2,16,128]{3,2,1,0:T(8,128)S(1)} %bitcast_add_fusion), channel_id=1, replica_groups={{0,2,4,6,8,10,12,14},{1,3,5,7,9,11,13,15},{16,18,20,22,24,26,28,30},{17..., dimensions={0} | all-to-all | bytes 262144 | tf_op jit(solution)/shard_map/all_to_all | solution.py:512
  34.0 9.8 %all_to_all.17 = f32[8,2,16,128]{3,2,1,0:T(8,128)S(1)} all-to-all(f32[8,2,16,128]{3,2,1,0:T(8,128)S(1)} %broadcast_in_dim.7), channel_id=1, replica_groups={{0,2,4,6,8,10,12,14},{1,3,5,7,9,11,13,15},{16,18,20,22,24,26,28,30},{17..., dimensions={0} | all-to-all | bytes 262144 | tf_op jit(solution)/shard_map/all_to_all | solution.py:512
  43.9 0.0 collective-permute-start.2
  43.9 1.3 %collective-permute-done.2 = f32[8,2,16,128]{3,2,1,0:T(8,128)S(1)} collective-permute-done((f32[8,2,16,128]{3,2,1,0:T(8,128)S(1)}, f32[8,2,16,128]{3,2,1,0:T(8,128)S(1)}, u32[]{:S(2)}, u32[]{:S(2)}) %collective-permute-start.2) | collective-permute-done | bytes 131104 | tf_op jit(solution)/shard_map/ppermute | solution.py:506
  45.3 3.5 %design.1 = f32[2,16,128]{2,1,0:T(8,128)} custom-call(f32[10,16,128]{2,1,0:T(8,128)S(1)} %get-tuple-element.19.weight_ref, f32[2,8,2,16,128]{4,3,2,1,0:T(8,128)S(1)} %pad_maximum_fusion.1.sens_ref, f32[32,16,128]{2,1,0:T(8,128)S(1)} %get-tuple-element.26.coef_ref, f32[2,8,2,16,128]{4,3,2,1,0:T(8,128)S(1)} %pad_maximum_fusion.density_ref), custom_call_target="tpu_custom_call" | custom-call | tf_op jit(solution)/shard_map/design/pallas_call | solution.py:486
  (6 shorter events, 0.1 us)
Async XLA Ops:
  0.6 16.7 %copy-start = (f32[1,3,32,16,128]{4,3,2,1,0:T(8,128)S(1)}, f32[1,3,32,16,128]{4,3,2,1,0:T(8,128)}, u32[]{:S(2)}) copy-start(f32[1,3,32,16,128]{4,3,2,1,0:T(8,128)} %param.7) | copy-start | bytes 2359300
  15.8 1.4 %collective-permute-start = (f32[8,2,16,128]{3,2,1,0:T(8,128)S(1)}, f32[8,2,16,128]{3,2,1,0:T(8,128)S(1)}, u32[]{:S(2)}, u32[]{:S(2)}) collective-permute-start(f32[8,2,16,128]{3,2,1,0:T(8,128)S(1)} %all_to_all.15), channel_id=1, source_target_pairs={{0,1},{1,0},{2,3},{3,2},{4,5},{5,4},{6,7},{7,6},{8,9},{9,8},{10,11... | collective-permute-start | bytes 393224 | tf_op jit(solution)/shard_map/ppermute | solution.py:506
  22.2 1.6 %collective-permute-start.1 = (f32[8,2,16,128]{3,2,1,0:T(8,128)S(1)}, f32[8,2,16,128]{3,2,1,0:T(8,128)S(1)}, u32[]{:S(2)}, u32[]{:S(2)}) collective-permute-start(f32[8,2,16,128]{3,2,1,0:T(8,128)S(1)} %slice_bitcast_fusion), channel_id=1, source_target_pairs={{0,1},{1,0},{2,3},{3,2},{4,5},{5,4},{6,7},{7,6},{8,9},{9,8},{10,11... | collective-permute-start | bytes 393224 | tf_op jit(solution)/shard_map/ppermute | solution.py:506
  43.9 1.3 %collective-permute-start.2 = (f32[8,2,16,128]{3,2,1,0:T(8,128)S(1)}, f32[8,2,16,128]{3,2,1,0:T(8,128)S(1)}, u32[]{:S(2)}, u32[]{:S(2)}) collective-permute-start(f32[8,2,16,128]{3,2,1,0:T(8,128)S(1)} %all_to_all.17), channel_id=1, source_target_pairs={{0,1},{1,0},{2,3},{3,2},{4,5},{5,4},{6,7},{7,6},{8,9},{9,8},{10,11... | collective-permute-start | bytes 393224 | tf_op jit(solution)/shard_map/ppermute | solution.py:506

commit v13 on v12

--- a/solution.py
+++ b/solution.py
@@ -95,8 +95,8 @@
 
 def pair_spot(x, own_planes):
     device = x // own_planes
-    core = (device ^ lax.axis_index("space")) & 1
-    return core, device >> 1, x % own_planes
+    apart = device ^ lax.axis_index("space")
+    return (apart ^ apart >> 1) & 1, device >> 1, x % own_planes
 
 
 def edge_class(x, planes):
@@ -506,10 +506,13 @@
     return lax.ppermute(block, "space", [(i, i ^ 1) for i in range(devices)])
 
 
+def chip_groups():
+    chips = lax.axis_size("space") // 2
+    return [[2 * chip + (chip ^ group) % 2 for chip in range(chips)] for group in range(2)]
+
+
 def between_chips(pieces):
-    devices = lax.axis_size("space")
-    groups = [list(range(core, devices, 2)) for core in range(2)]
-    return lax.all_to_all(pieces, "space", 0, 0, axis_index_groups=groups)
+    return lax.all_to_all(pieces, "space", 0, 0, axis_index_groups=chip_groups())
 
 
 def chip_gathered(block):
@@ -526,10 +529,10 @@
 
 
 def one_slab(density, displacement, fixed, load_index, load_force, radius):
-    same_core, small = lax.optimization_barrier(
+    same_group, small = lax.optimization_barrier(
         (chip_gathered(density), (radius, load_index, load_force.T, fixed))
     )
-    whole = with_other_core(same_core)
+    whole = with_other_core(same_group)
     weights, inverses, free, load, spot = prepare_call(*small)
     new_displacement, sens, coef = sweep_call(
         spot, load, weights, inverses, free, whole, displacement[0]

time: 49.2 us -> 48.9 us (level)
  blocking collectives: 34.4 us -> 33.4 us
  starting transfers between devices: 0.59 us -> 1.31 us
    all_to_all x3, blocking collectives: 34.4 us -> 33.4 us  [between_chips(): lax.all_to_all(pieces, 'space', 0, 0, axis_index_groups=chip_groups())]
    ppermute x3, starting transfers between devices: 0.59 us -> 1.31 us  [other_core(): return lax.ppermute(block, 'space', [(i, i ^ 1) for i in range(devices)])]
where the time goes in v13:
time: 48.9 us; the launch traced here: 48.4 us
  blocking collectives  33.4 us (68%)
  Pallas kernels  9.84 us (20%)
  waiting for transfers between devices  2.32 us (5%)
  starting transfers between devices  1.31 us (3%)
  local copies, waits for them, and re-layouts  0.83 us (2%)
  between operations  0.71 us (1%)
    all_to_all x3, blocking collectives, between_chips(): lax.all_to_all(pieces, 'space', 0, 0, axis_index_groups=chip_groups())  33.4 us
    pallas_call x1, Pallas kernels, sweep_call(): pl.pallas_call(sweep_kernel, out_shape=[floats(3, planes, layers, row_wid...  4.92 us
    pallas_call x1, Pallas kernels, design_call(): pl.pallas_call(design_kernel, out_shape=jax.ShapeDtypeStruct((own_planes,...  3.52 us
    ppermute x3, waiting for transfers between devices, other_core(): return lax.ppermute(block, 'space', [(i, i ^ 1) for i in range(devices)])  2.32 us
    pallas_call x1, Pallas kernels, prepare_call(): pl.pallas_call(prepare_kernel, out_shape=[floats(len(ALL_SQUARES), layers...  1.4 us
    ppermute x3, starting transfers between devices, other_core(): return lax.ppermute(block, 'space', [(i, i ^ 1) for i in range(devices)])  1.31 us
  transfers between devices with their start and end apart: 3, of which 2 were waited for; matrix products, arithmetic and copies ran while one was open for 0% of the time, Pallas kernels for 3%

profile of v13, /device:TPU:0, one launch (start us, length us, event | category | flops | bytes accessed | tf_op | source)
XLA Modules:
  0.0 48.4 jit_solution(8220430338458676743)
XLA Ops:
  0.6 0.0 copy-start
  0.6 0.8 %broadcast_in_dim.6 = f32[8,2,16,128]{3,2,1,0:T(8,128)S(1)} broadcast(f32[2,16,128]{2,1,0:T(8,128)} %param.6), dimensions={1,2,3} | broadcast | bytes 147456 | tf_op jit(solution)/shard_map/broadcast_in_dim | solution.py:520
  1.4 13.5 %all_to_all.15 = f32[8,2,16,128]{3,2,1,0:T(8,128)S(1)} all-to-all(f32[8,2,16,128]{3,2,1,0:T(8,128)S(1)} %broadcast_in_dim.6), channel_id=1, replica_groups={{0,3,4,7,8,11,12,15},{1,2,5,6,9,10,13,14},{16,19,20,23,24,27,28,31},{17..., dimensions={0} | all-to-all | bytes 262144 | tf_op jit(solution)/shard_map/all_to_all | solution.py:515
  14.9 0.7 %collective-permute-start = (f32[8,2,16,128]{3,2,1,0:T(8,128)S(1)}, f32[8,2,16,128]{3,2,1,0:T(8,128)S(1)}, u32[]{:S(2)}, u32[]{:S(2)}) collective-permute-start(f32[8,2,16,128]{3,2,1,0:T(8,128)S(1)} %all_to_all.15), channel_id=1, source_target_pairs={{0,1},{1,0},{2,3},{3,2},{4,5},{5,4},{6,7},{7,6},{8,9},{9,8},{10,11... | collective-permute-start | bytes 393224 | tf_op jit(solution)/shard_map/ppermute | solution.py:506
  15.6 1.4 %prepare.1 = (f32[10,16,128]{2,1,0:T(8,128)S(1)}, f32[5,16,128]{2,1,0:T(8,128)S(1)}, f32[32,16,128]{2,1,0:T(8,128)S(1)}, f32[3,16,128]{2,1,0:T(8,128)S(1)}, s32[1]{0:T(128)}) custom-call(s32[16]{0:T(128)} %radius_hbm, s32[16]{0:T(128)} %index_hbm, f32[3,16]{1,0:T(4,128)} %bitcast.16, s32[32,128]{1,0:T(8,128)} %fixed_hbm), custom_call_target="tpu_custom_call" | custom-call | flops 2621440 | bytes 524288 | tf_op jit(solution)/shard_map/prepare/pallas_call | solution.py:409
  17.0 0.0 collective-permute-done
  17.0 0.0 copy-done
  17.0 4.9 %sweeps.1 = (f32[3,32,16,128]{3,2,1,0:T(8,128)}, f32[2,8,2,16,128]{4,3,2,1,0:T(8,128)S(1)}, f32[32,16,128]{2,1,0:T(8,128)S(1)}) custom-call(s32[1]{0:T(128)} %get-tuple-element.20.spot_ref, f32[3,16,128]{2,1,0:T(8,128)S(1)} %get-tuple-element.21.load_ref, f32[10,16,128]{2,1,0:T(8,128)S(1)} %get-tuple-element.19.weight_ref, ...), custom_call_target="tpu_custom_call" | custom-call | tf_op jit(solution)/shard_map/sweeps/pallas_call | solution.py:449
  22.0 0.1 collective-permute-start.1
  22.1 1.3 %collective-permute-done.1 = f32[8,2,16,128]{3,2,1,0:T(8,128)S(1)} collective-permute-done((f32[8,2,16,128]{3,2,1,0:T(8,128)S(1)}, f32[8,2,16,128]{3,2,1,0:T(8,128)S(1)}, u32[]{:S(2)}, u32[]{:S(2)}) %collective-permute-start.1) | collective-permute-done | bytes 131104 | tf_op jit(solution)/shard_map/ppermute | solution.py:506
  23.4 10.1 %all_to_all.16 = f32[8,2,16,128]{3,2,1,0:T(8,128)S(1)} all-to-all(f32[8,2,16,128]{3,2,1,0:T(8,128)S(1)} %bitcast_add_fusion), channel_id=1, replica_groups={{0,3,4,7,8,11,12,15},{1,2,5,6,9,10,13,14},{16,19,20,23,24,27,28,31},{17..., dimensions={0} | all-to-all | bytes 262144 | tf_op jit(solution)/shard_map/all_to_all | solution.py:515
  33.6 9.8 %all_to_all.17 = f32[8,2,16,128]{3,2,1,0:T(8,128)S(1)} all-to-all(f32[8,2,16,128]{3,2,1,0:T(8,128)S(1)} %broadcast_in_dim.7), channel_id=1, replica_groups={{0,3,4,7,8,11,12,15},{1,2,5,6,9,10,13,14},{16,19,20,23,24,27,28,31},{17..., dimensions={0} | all-to-all | bytes 262144 | tf_op jit(solution)/shard_map/all_to_all | solution.py:515
  43.4 0.6 %collective-permute-start.2 = (f32[8,2,16,128]{3,2,1,0:T(8,128)S(1)}, f32[8,2,16,128]{3,2,1,0:T(8,128)S(1)}, u32[]{:S(2)}, u32[]{:S(2)}) collective-permute-start(f32[8,2,16,128]{3,2,1,0:T(8,128)S(1)} %all_to_all.17), channel_id=1, source_target_pairs={{0,1},{1,0},{2,3},{3,2},{4,5},{5,4},{6,7},{7,6},{8,9},{9,8},{10,11... | collective-permute-start | bytes 393224 | tf_op jit(solution)/shard_map/ppermute | solution.py:506
  43.9 1.0 %collective-permute-done.2 = f32[8,2,16,128]{3,2,1,0:T(8,128)S(1)} collective-permute-done((f32[8,2,16,128]{3,2,1,0:T(8,128)S(1)}, f32[8,2,16,128]{3,2,1,0:T(8,128)S(1)}, u32[]{:S(2)}, u32[]{:S(2)}) %collective-permute-start.2) | collective-permute-done | bytes 131104 | tf_op jit(solution)/shard_map/ppermute | solution.py:506
  44.9 3.5 %design.1 = f32[2,16,128]{2,1,0:T(8,128)} custom-call(f32[10,16,128]{2,1,0:T(8,128)S(1)} %get-tuple-element.19.weight_ref, f32[2,8,2,16,128]{4,3,2,1,0:T(8,128)S(1)} %pad_maximum_fusion.1.sens_ref, f32[32,16,128]{2,1,0:T(8,128)S(1)} %get-tuple-element.26.coef_ref, f32[2,8,2,16,128]{4,3,2,1,0:T(8,128)S(1)} %pad_maximum_fusion.density_ref), custom_call_target="tpu_custom_call" | custom-call | tf_op jit(solution)/shard_map/design/pallas_call | solution.py:486
  (6 shorter events, 0.1 us)
Async XLA Ops:
  0.6 16.4 %copy-start = (f32[1,3,32,16,128]{4,3,2,1,0:T(8,128)S(1)}, f32[1,3,32,16,128]{4,3,2,1,0:T(8,128)}, u32[]{:S(2)}) copy-start(f32[1,3,32,16,128]{4,3,2,1,0:T(8,128)} %param.7) | copy-start | bytes 2359300
  14.9 2.1 %collective-permute-start = (f32[8,2,16,128]{3,2,1,0:T(8,128)S(1)}, f32[8,2,16,128]{3,2,1,0:T(8,128)S(1)}, u32[]{:S(2)}, u32[]{:S(2)}) collective-permute-start(f32[8,2,16,128]{3,2,1,0:T(8,128)S(1)} %all_to_all.15), channel_id=1, source_target_pairs={{0,1},{1,0},{2,3},{3,2},{4,5},{5,4},{6,7},{7,6},{8,9},{9,8},{10,11... | collective-permute-start | bytes 393224 | tf_op jit(solution)/shard_map/ppermute | solution.py:506
  22.0 1.4 %collective-permute-start.1 = (f32[8,2,16,128]{3,2,1,0:T(8,128)S(1)}, f32[8,2,16,128]{3,2,1,0:T(8,128)S(1)}, u32[]{:S(2)}, u32[]{:S(2)}) collective-permute-start(f32[8,2,16,128]{3,2,1,0:T(8,128)S(1)} %slice_bitcast_fusion), channel_id=1, source_target_pairs={{0,1},{1,0},{2,3},{3,2},{4,5},{5,4},{6,7},{7,6},{8,9},{9,8},{10,11... | collective-permute-start | bytes 393224 | tf_op jit(solution)/shard_map/ppermute | solution.py:506
  43.4 1.5 %collective-permute-start.2 = (f32[8,2,16,128]{3,2,1,0:T(8,128)S(1)}, f32[8,2,16,128]{3,2,1,0:T(8,128)S(1)}, u32[]{:S(2)}, u32[]{:S(2)}) collective-permute-start(f32[8,2,16,128]{3,2,1,0:T(8,128)S(1)} %all_to_all.17), channel_id=1, source_target_pairs={{0,1},{1,0},{2,3},{3,2},{4,5},{5,4},{6,7},{7,6},{8,9},{9,8},{10,11... | collective-permute-start | bytes 393224 | tf_op jit(solution)/shard_map/ppermute | solution.py:506

commit v14 on v13

--- a/solution.py
+++ b/solution.py
@@ -77,20 +77,19 @@
     return [weigh(sums, weight_ref, square) for square in (0, 1, 4)]
 
 
-def backward_planes(plane, weight_ref):
-    beside = shift_sum(plane, 1, 1)
-    further = shift_sum(plane, 1, 2)
-    results = []
-    for square in (0, 1, 4):
-
-        def weight(more):
-            return weight_ref[ALL_SQUARES.index(square + more)]
-
-        level = weight(0) * plane + weight(1) * beside + weight(4) * further
-        near = weight(1) * plane + weight(2) * beside + weight(5) * further
-        far = weight(4) * plane + weight(5) * beside + weight(8) * further
-        results.append(level + shift_sum(near, 0, 1) + shift_sum(far, 0, 2))
-    return results
+def rows(x, layers, shift=0):
+    return pl.ds(x * layers + shift, layers)
+
+
+GAP = 8
+
+
+def gapped(x, layers, shift=0):
+    return pl.ds(GAP + x * (layers + GAP) + shift, layers)
+
+
+def gap(x, layers):
+    return pl.ds(x * (layers + GAP), GAP)
 
 
 def pair_spot(x, own_planes):
@@ -182,13 +181,15 @@
     disp_hbm,
     sens_ref,
     coef_ref,
+    plane_ref,
+    beside_ref,
+    further_ref,
     near_ref,
     side_ref,
     far_ref,
     modulus_ref,
     across_ref,
     up_ref,
-    down_ref,
     right_ref,
     left_ref,
     rate_ref,
@@ -204,15 +205,40 @@
     z = spot_iota(shape, 0)
     y = spot_iota(shape, 1)
     zero = jnp.zeros(shape, jnp.float32)
+    zero_gap = jnp.zeros((GAP, row_width), jnp.float32)
 
     for ref in (side_ref, far_ref):
         zero_edges(ref)
+    for ref in (plane_ref, beside_ref, further_ref):
+        ref[gap(planes, layers)] = zero_gap
+
+    def spread_plane(x, carry):
+        plane = density_ref[pair_spot(x, own_planes)]
+        fields = (plane, shift_sum(plane, 1, 1), shift_sum(plane, 1, 2))
+        for ref, field in zip((plane_ref, beside_ref, further_ref), fields):
+            ref[gap(x, layers)] = zero_gap
+            ref[gapped(x, layers)] = field
+        return carry
+
+    lax.fori_loop(0, planes, spread_plane, 0, unroll=16)
 
     def filter_plane(x, carry):
-        near, side, far = forward_planes(density_ref[pair_spot(x, own_planes)], weight_ref)
-        near_ref[x + 2] = near
-        side_ref[x + 2] = side
-        far_ref[x + 2] = far
+        def around(ref, distance):
+            return ref[gapped(x, layers, distance)] + ref[gapped(x, layers, -distance)]
+
+        beside = beside_ref[gapped(x, layers)]
+        further = further_ref[gapped(x, layers)]
+        sums = {
+            0: plane_ref[gapped(x, layers)],
+            1: beside + around(plane_ref, 1),
+            2: around(beside_ref, 1),
+            4: further + around(plane_ref, 2),
+            5: around(further_ref, 1) + around(beside_ref, 2),
+            8: around(further_ref, 2),
+        }
+        near_ref[x + 2] = weigh(sums, weight_ref, 0)
+        side_ref[x + 2] = weigh(sums, weight_ref, 1)
+        far_ref[x + 2] = weigh(sums, weight_ref, 4)
         return carry
 
     lax.fori_loop(0, planes, filter_plane, 0, unroll=16)
@@ -227,37 +253,39 @@
             + far_ref[x + 4]
         ) * inverse
         modulus = floor_modulus + (1.0 - floor_modulus) * (filtered * filtered * filtered)
-        modulus_ref[x] = modulus
+        modulus_ref[rows(x, layers)] = modulus
         coef_ref[x] = 3.0 * (1.0 - floor_modulus) * (filtered * filtered) * inverse
         return carry
 
     lax.fori_loop(0, planes, modulus_plane, 0, unroll=16)
 
+    modulus_ref[rows(planes, layers)] = zero
     across_ref[0] = zero
     across_ref[planes] = zero
+    up_ref[rows(0, layers)] = zero
     for ref in (first_ref, second_ref):
         for part in range(3):
-            ref[part, 0] = zero
-            ref[part, planes + 1] = zero
+            ref[part, rows(0, layers)] = zero
+            ref[part, rows(planes + 1, layers)] = zero
 
     def face_plane(x, carry):
-        modulus = modulus_ref[x]
-        later = modulus_ref[jnp.minimum(x + 1, planes - 1)]
+        before = carry
+        modulus = modulus_ref[rows(x, layers)]
+        later = modulus_ref[rows(x + 1, layers)]
         ahead = jnp.where(x + 1 < planes, 0.5 * (modulus + later), 0.0)
         across_ref[x + 1] = ahead
-        up = jnp.where(z < layers - 1, 0.5 * (modulus + pltpu.roll(modulus, layers - 1, 0)), 0.0)
-        down = pltpu.roll(up, 1, 0)
+        above = modulus_ref[rows(x, layers, 1)]
+        up = jnp.where(z < layers - 1, 0.5 * (modulus + above), 0.0)
         right = jnp.where(
             y < row_width - 1, 0.5 * (modulus + pltpu.roll(modulus, row_width - 1, 1)), 0.0
         )
         left = pltpu.roll(right, 1, 1)
-        up_ref[x] = up
-        down_ref[x] = down
+        up_ref[rows(x + 1, layers)] = up
         right_ref[x] = right
         left_ref[x] = left
-        sums = (carry + ahead, up + down, left + right)
+        free = free_ref[x]
+        sums = (before + ahead, up + pltpu.roll(up, 1, 0), left + right)
         every = sums[0] + sums[1] + sums[2]
-        free = free_ref[x]
         push = relax_factor * free
         diagonal = [every + part_sum for part_sum in sums]
         pair = diagonal[0] * diagonal[1]
@@ -267,7 +295,7 @@
         rate_ref[1, x] = side * diagonal[0]
         rate_ref[2, x] = push * pair
         for part in range(3):
-            first_ref[part, x + 1] = start_ref[part, x] * free
+            first_ref[part, rows(x + 1, layers)] = start_ref[part, x] * free
         return ahead
 
     lax.fori_loop(0, planes, face_plane, zero, unroll=16)
@@ -277,36 +305,43 @@
     def sweep(source, target, lead):
         def sweep_plane(x, carry):
             before, after = across_ref[x], across_ref[x + 1]
-            up, down, right, left = up_ref[x], down_ref[x], right_ref[x], left_ref[x]
+            up, down = up_ref[rows(x + 1, layers)], up_ref[rows(x + 1, layers, -1)]
+            right, left = right_ref[x], left_ref[x]
             for part in range(3):
-                here = source[part, x + 1]
+                here = source[part, rows(x + 1, layers)]
                 pulls = [
-                    before * source[part, x] + after * source[part, x + 2],
-                    up * pltpu.roll(here, layers - 1, 0) + down * pltpu.roll(here, 1, 0),
+                    before * source[part, rows(x, layers)]
+                    + after * source[part, rows(x + 2, layers)],
+                    up * source[part, rows(x + 1, layers, 1)]
+                    + down * source[part, rows(x + 1, layers, -1)],
                     right * pltpu.roll(here, row_width - 1, 1) + left * pltpu.roll(here, 1, 1),
                 ]
                 pull = pulls[0] + pulls[1] + pulls[2] + pulls[part]
-                target[part, x + lead] = (1.0 - relax_factor) * here + rate_ref[part, x] * pull
+                target[part, rows(x + lead, layers)] = (
+                    1.0 - relax_factor
+                ) * here + rate_ref[part, x] * pull
             return carry
 
         lax.fori_loop(0, planes, sweep_plane, 0, unroll=16)
         for part in range(3):
-            target[part, own_x + lead] += rate_ref[part, own_x] * load_ref[part]
+            target[part, rows(own_x + lead, layers)] += rate_ref[part, own_x] * load_ref[part]
 
     stages = (first_ref, second_ref)
     for turn in range(SWEEPS - 1):
         sweep(stages[turn % 2], stages[(turn + 1) % 2], 1)
     sweep(stages[(SWEEPS - 1) % 2], disp_ref, 0)
-    store = pltpu.make_async_copy(disp_ref, disp_hbm, stored)
+    store = pltpu.make_async_copy(
+        disp_ref.at[:, pl.ds(0, planes * layers)], disp_hbm, stored
+    )
     store.start()
 
     def energy_plane(x, carry):
         later = jnp.minimum(x + 1, planes - 1)
         ahead, upward, right = zero, zero, zero
         for part in range(3):
-            here = disp_ref[part, x]
-            step = disp_ref[part, later] - here
-            climb = pltpu.roll(here, layers - 1, 0) - here
+            here = disp_ref[part, rows(x, layers)]
+            step = disp_ref[part, rows(later, layers)] - here
+            climb = disp_ref[part, rows(x, layers, 1)] - here
             slide = pltpu.roll(here, row_width - 1, 1) - here
             ahead = ahead + (2.0 if part == 0 else 1.0) * (step * step)
             upward = upward + (2.0 if part == 1 else 1.0) * (climb * climb)
@@ -327,8 +362,11 @@
     coef_ref,
     density_ref,
     new_ref,
+    plane_ref,
+    beside_ref,
+    further_ref,
+    level_ref,
     near_ref,
-    side_ref,
     far_ref,
     pull_ref,
     low_ref,
@@ -339,23 +377,48 @@
     place = lax.axis_index("space")
     shape = (layers, row_width)
     zero = jnp.zeros(shape, jnp.float32)
-    for ref in (side_ref, far_ref):
+    zero_gap = jnp.zeros((GAP, row_width), jnp.float32)
+    for ref in (plane_ref, beside_ref, further_ref):
         zero_edges(ref)
+    for ref in (near_ref, far_ref):
+        ref[gap(planes, layers)] = zero_gap
+
+    def spread_plane(x, carry):
+        plane = sens_ref[pair_spot(x, own_planes)] * coef_ref[x]
+        plane_ref[x + 2] = plane
+        beside_ref[x + 2] = shift_sum(plane, 1, 1)
+        further_ref[x + 2] = shift_sum(plane, 1, 2)
+        return carry
+
+    lax.fori_loop(0, planes, spread_plane, 0, unroll=16)
 
     def filter_plane(x, carry):
-        near, side, far = backward_planes(
-            sens_ref[pair_spot(x, own_planes)] * coef_ref[x], weight_ref
-        )
-        near_ref[x + 2] = near
-        side_ref[x + 2] = side
-        far_ref[x + 2] = far
+        def around(ref, distance):
+            return ref[x + 2 + distance] + ref[x + 2 - distance]
+
+        sums = {
+            0: plane_ref[x + 2],
+            1: beside_ref[x + 2] + around(plane_ref, 1),
+            2: around(beside_ref, 1),
+            4: further_ref[x + 2] + around(plane_ref, 2),
+            5: around(further_ref, 1) + around(beside_ref, 2),
+            8: around(further_ref, 2),
+        }
+        level_ref[x] = weigh(sums, weight_ref, 0)
+        for ref, square in ((near_ref, 1), (far_ref, 4)):
+            ref[gap(x, layers)] = zero_gap
+            ref[gapped(x, layers)] = weigh(sums, weight_ref, square)
         return carry
 
     lax.fori_loop(0, planes, filter_plane, 0, unroll=16)
 
     def root_plane(x, carry):
         root = jnp.sqrt(
-            near_ref[x + 2] + side_ref[x + 1] + side_ref[x + 3] + far_ref[x] + far_ref[x + 4]
+            level_ref[x]
+            + near_ref[gapped(x, layers, 1)]
+            + near_ref[gapped(x, layers, -1)]
+            + far_ref[gapped(x, layers, 2)]
+            + far_ref[gapped(x, layers, -2)]
         )
         density = density_ref[pair_spot(x, own_planes)]
         pull_ref[x] = density * root
@@ -376,7 +439,7 @@
         middle = lower + half
         factor = jnp.exp(-0.5 * middle)
         total = lax.fori_loop(
-            0, planes, lambda x, acc: acc + trial(x, factor), zero, unroll=8
+            0, planes, lambda x, acc: acc + trial(x, factor), zero, unroll=16
         )
         volume = jnp.sum(jnp.sum(total, axis=0, keepdims=True), axis=1, keepdims=True)
         return jnp.where(volume > target, middle, lower), half
@@ -444,31 +507,33 @@
     planes = cores * chips * own_planes
 
     def scratch(*lead):
-        return pltpu.VMEM(lead + (layers, row_width), jnp.float32)
+        return pltpu.VMEM(lead + (row_width,), jnp.float32)
 
     return pl.pallas_call(
         sweep_kernel,
         out_shape=[
-            floats(3, planes, layers, row_width),
+            floats(3, planes * layers, row_width),
             floats(*density.shape),
             floats(planes, layers, row_width),
         ],
         in_specs=[in_smem()] + [in_vmem()] * 6,
         out_specs=[pl.BlockSpec(memory_space=pltpu.HBM), in_vmem(), in_vmem()],
         scratch_shapes=[
-            scratch(planes + 4),
-            scratch(planes + 4),
-            scratch(planes + 4),
-            scratch(planes),
-            scratch(planes + 1),
-            scratch(planes),
-            scratch(planes),
-            scratch(planes),
-            scratch(planes),
-            scratch(3, planes),
-            scratch(3, planes + 2),
-            scratch(3, planes + 2),
-            scratch(3, planes),
+            scratch(planes * (layers + GAP) + GAP),
+            scratch(planes * (layers + GAP) + GAP),
+            scratch(planes * (layers + GAP) + GAP),
+            scratch(planes + 4, layers),
+            scratch(planes + 4, layers),
+            scratch(planes + 4, layers),
+            scratch((planes + 1) * layers),
+            scratch(planes + 1, layers),
+            scratch((planes + 1) * layers),
+            scratch(planes, layers),
+            scratch(planes, layers),
+            scratch(3, planes, layers),
+            scratch(3, (planes + 2) * layers),
+            scratch(3, (planes + 2) * layers),
+            scratch(3, (planes + 1) * layers),
             pltpu.SemaphoreType.DMA(()),
         ],
         compiler_params=pltpu.CompilerParams(vmem_limit_bytes=KERNEL_VMEM),
@@ -481,20 +546,23 @@
     planes = cores * chips * own_planes
 
     def scratch(*lead):
-        return pltpu.VMEM(lead + (layers, row_width), jnp.float32)
+        return pltpu.VMEM(lead + (row_width,), jnp.float32)
 
     return pl.pallas_call(
         design_kernel,
-        out_shape=jax.ShapeDtypeStruct((own_planes, layers, row_width), jnp.float32),
+        out_shape=floats(own_planes, layers, row_width),
         in_specs=[in_vmem()] * 4,
         out_specs=in_vmem(),
         scratch_shapes=[
-            scratch(planes + 4),
-            scratch(planes + 4),
-            scratch(planes + 4),
-            scratch(planes),
-            scratch(planes),
-            scratch(planes),
+            scratch(planes + 4, layers),
+            scratch(planes + 4, layers),
+            scratch(planes + 4, layers),
+            scratch(planes, layers),
+            scratch(planes * (layers + GAP) + GAP),
+            scratch(planes * (layers + GAP) + GAP),
+            scratch(planes, layers),
+            scratch(planes, layers),
+            scratch(planes, layers),
         ],
         compiler_params=pltpu.CompilerParams(vmem_limit_bytes=KERNEL_VMEM),
         name="design",
@@ -539,7 +607,7 @@
     )
     sens = with_other_core(chip_gathered(scattered_sum(sens)))
     new_density = design_call(weights, sens, coef, whole)
-    return new_density, new_displacement[None]
+    return new_density, new_displacement.reshape(displacement.shape)
 
 
 def from_behind(block, axis, distance):

time: 48.9 us -> 48.7 us (level)
  no operation moved by 1% of the time
where the time goes in v14:
time: 48.7 us; the launch traced here: 48.2 us
  blocking collectives  33.4 us (69%)
  Pallas kernels  9.61 us (20%)
  waiting for transfers between devices  2.32 us (5%)
  starting transfers between devices  1.31 us (3%)
  local copies, waits for them, and re-layouts  0.83 us (2%)
  between operations  0.71 us (1%)
    all_to_all x3, blocking collectives, between_chips(): lax.all_to_all(pieces, 'space', 0, 0, axis_index_groups=chip_groups())  33.4 us
    pallas_call x1, Pallas kernels, sweep_call(): pl.pallas_call(sweep_kernel, out_shape=[floats(3, planes * layers, row_wi...  4.85 us
    pallas_call x1, Pallas kernels, design_call(): pl.pallas_call(design_kernel, out_shape=floats(own_planes, layers, row_wi...  3.36 us
    ppermute x3, waiting for transfers between devices, other_core(): return lax.ppermute(block, 'space', [(i, i ^ 1) for i in range(devices)])  2.32 us
    pallas_call x1, Pallas kernels, prepare_call(): pl.pallas_call(prepare_kernel, out_shape=[floats(len(ALL_SQUARES), layers...  1.4 us
    ppermute x3, starting transfers between devices, other_core(): return lax.ppermute(block, 'space', [(i, i ^ 1) for i in range(devices)])  1.31 us
  transfers between devices with their start and end apart: 3, of which 2 were waited for; matrix products, arithmetic and copies ran while one was open for 0% of the time, Pallas kernels for 3%

profile of v14, /device:TPU:0, one launch (start us, length us, event | category | flops | bytes accessed | tf_op | source)
XLA Modules:
  0.0 48.2 jit_solution(2795718986153723790)
XLA Ops:
  0.6 0.0 copy-start
  0.6 0.8 %broadcast_in_dim.4 = f32[8,2,16,128]{3,2,1,0:T(8,128)S(1)} broadcast(f32[2,16,128]{2,1,0:T(8,128)} %param.6), dimensions={1,2,3} | broadcast | bytes 147456 | tf_op jit(solution)/shard_map/broadcast_in_dim | solution.py:588
  1.4 13.5 %all_to_all.15 = f32[8,2,16,128]{3,2,1,0:T(8,128)S(1)} all-to-all(f32[8,2,16,128]{3,2,1,0:T(8,128)S(1)} %broadcast_in_dim.4), channel_id=1, replica_groups={{0,3,4,7,8,11,12,15},{1,2,5,6,9,10,13,14},{16,19,20,23,24,27,28,31},{17..., dimensions={0} | all-to-all | bytes 262144 | tf_op jit(solution)/shard_map/all_to_all | solution.py:583
  14.9 0.7 %collective-permute-start = (f32[8,2,16,128]{3,2,1,0:T(8,128)S(1)}, f32[8,2,16,128]{3,2,1,0:T(8,128)S(1)}, u32[]{:S(2)}, u32[]{:S(2)}) collective-permute-start(f32[8,2,16,128]{3,2,1,0:T(8,128)S(1)} %all_to_all.15), channel_id=1, source_target_pairs={{0,1},{1,0},{2,3},{3,2},{4,5},{5,4},{6,7},{7,6},{8,9},{9,8},{10,11... | collective-permute-start | bytes 393224 | tf_op jit(solution)/shard_map/ppermute | solution.py:574
  15.6 1.4 %prepare.1 = (f32[10,16,128]{2,1,0:T(8,128)S(1)}, f32[5,16,128]{2,1,0:T(8,128)S(1)}, f32[32,16,128]{2,1,0:T(8,128)S(1)}, f32[3,16,128]{2,1,0:T(8,128)S(1)}, s32[1]{0:T(128)}) custom-call(s32[16]{0:T(128)} %radius_hbm, s32[16]{0:T(128)} %index_hbm, f32[3,16]{1,0:T(4,128)} %bitcast.16, s32[32,128]{1,0:T(8,128)} %fixed_hbm), custom_call_target="tpu_custom_call" | custom-call | flops 2621440 | bytes 524288 | tf_op jit(solution)/shard_map/prepare/pallas_call | solution.py:472
  17.0 0.0 collective-permute-done
  17.0 0.0 copy-done
  17.0 4.9 %sweeps.1 = (f32[3,512,128]{2,1,0:T(8,128)}, f32[2,8,2,16,128]{4,3,2,1,0:T(8,128)S(1)}, f32[32,16,128]{2,1,0:T(8,128)S(1)}) custom-call(s32[1]{0:T(128)} %get-tuple-element.20.spot_ref, f32[3,16,128]{2,1,0:T(8,128)S(1)} %get-tuple-element.21.load_ref, f32[10,16,128]{2,1,0:T(8,128)S(1)} %get-tuple-element.19.weight_ref, ...), custom_call_target="tpu_custom_call" | custom-call | tf_op jit(solution)/shard_map/sweeps/pallas_call | solution.py:512
  21.9 0.1 collective-permute-start.1
  22.0 1.3 %collective-permute-done.1 = f32[8,2,16,128]{3,2,1,0:T(8,128)S(1)} collective-permute-done((f32[8,2,16,128]{3,2,1,0:T(8,128)S(1)}, f32[8,2,16,128]{3,2,1,0:T(8,128)S(1)}, u32[]{:S(2)}, u32[]{:S(2)}) %collective-permute-start.1) | collective-permute-done | bytes 131104 | tf_op jit(solution)/shard_map/ppermute | solution.py:574
  23.4 10.1 %all_to_all.16 = f32[8,2,16,128]{3,2,1,0:T(8,128)S(1)} all-to-all(f32[8,2,16,128]{3,2,1,0:T(8,128)S(1)} %bitcast_add_fusion), channel_id=1, replica_groups={{0,3,4,7,8,11,12,15},{1,2,5,6,9,10,13,14},{16,19,20,23,24,27,28,31},{17..., dimensions={0} | all-to-all | bytes 262144 | tf_op jit(solution)/shard_map/all_to_all | solution.py:583
  33.5 9.8 %all_to_all.17 = f32[8,2,16,128]{3,2,1,0:T(8,128)S(1)} all-to-all(f32[8,2,16,128]{3,2,1,0:T(8,128)S(1)} %broadcast_in_dim.5), channel_id=1, replica_groups={{0,3,4,7,8,11,12,15},{1,2,5,6,9,10,13,14},{16,19,20,23,24,27,28,31},{17..., dimensions={0} | all-to-all | bytes 262144 | tf_op jit(solution)/shard_map/all_to_all | solution.py:583
  43.3 0.6 %collective-permute-start.2 = (f32[8,2,16,128]{3,2,1,0:T(8,128)S(1)}, f32[8,2,16,128]{3,2,1,0:T(8,128)S(1)}, u32[]{:S(2)}, u32[]{:S(2)}) collective-permute-start(f32[8,2,16,128]{3,2,1,0:T(8,128)S(1)} %all_to_all.17), channel_id=1, source_target_pairs={{0,1},{1,0},{2,3},{3,2},{4,5},{5,4},{6,7},{7,6},{8,9},{9,8},{10,11... | collective-permute-start | bytes 393224 | tf_op jit(solution)/shard_map/ppermute | solution.py:574
  43.9 1.0 %collective-permute-done.2 = f32[8,2,16,128]{3,2,1,0:T(8,128)S(1)} collective-permute-done((f32[8,2,16,128]{3,2,1,0:T(8,128)S(1)}, f32[8,2,16,128]{3,2,1,0:T(8,128)S(1)}, u32[]{:S(2)}, u32[]{:S(2)}) %collective-permute-start.2) | collective-permute-done | bytes 131104 | tf_op jit(solution)/shard_map/ppermute | solution.py:574
  44.9 3.4 %design.1 = f32[2,16,128]{2,1,0:T(8,128)} custom-call(f32[10,16,128]{2,1,0:T(8,128)S(1)} %get-tuple-element.19.weight_ref, f32[2,8,2,16,128]{4,3,2,1,0:T(8,128)S(1)} %pad_maximum_fusion.1.sens_ref, f32[32,16,128]{2,1,0:T(8,128)S(1)} %get-tuple-element.26.coef_ref, f32[2,8,2,16,128]{4,3,2,1,0:T(8,128)S(1)} %pad_maximum_fusion.density_ref), custom_call_target="tpu_custom_call" | custom-call | tf_op jit(solution)/shard_map/design/pallas_call | solution.py:551
  (6 shorter events, 0.1 us)
Async XLA Ops:
  0.6 16.4 %copy-start = (f32[1,3,32,16,128]{4,3,2,1,0:T(8,128)S(1)}, f32[1,3,32,16,128]{4,3,2,1,0:T(8,128)}, u32[]{:S(2)}) copy-start(f32[1,3,32,16,128]{4,3,2,1,0:T(8,128)} %param.7) | copy-start | bytes 2359300
  14.9 2.1 %collective-permute-start = (f32[8,2,16,128]{3,2,1,0:T(8,128)S(1)}, f32[8,2,16,128]{3,2,1,0:T(8,128)S(1)}, u32[]{:S(2)}, u32[]{:S(2)}) collective-permute-start(f32[8,2,16,128]{3,2,1,0:T(8,128)S(1)} %all_to_all.15), channel_id=1, source_target_pairs={{0,1},{1,0},{2,3},{3,2},{4,5},{5,4},{6,7},{7,6},{8,9},{9,8},{10,11... | collective-permute-start | bytes 393224 | tf_op jit(solution)/shard_map/ppermute | solution.py:574
  21.9 1.4 %collective-permute-start.1 = (f32[8,2,16,128]{3,2,1,0:T(8,128)S(1)}, f32[8,2,16,128]{3,2,1,0:T(8,128)S(1)}, u32[]{:S(2)}, u32[]{:S(2)}) collective-permute-start(f32[8,2,16,128]{3,2,1,0:T(8,128)S(1)} %slice_bitcast_fusion), channel_id=1, source_target_pairs={{0,1},{1,0},{2,3},{3,2},{4,5},{5,4},{6,7},{7,6},{8,9},{9,8},{10,11... | collective-permute-start | bytes 393224 | tf_op jit(solution)/shard_map/ppermute | solution.py:574
  43.3 1.5 %collective-permute-start.2 = (f32[8,2,16,128]{3,2,1,0:T(8,128)S(1)}, f32[8,2,16,128]{3,2,1,0:T(8,128)S(1)}, u32[]{:S(2)}, u32[]{:S(2)}) collective-permute-start(f32[8,2,16,128]{3,2,1,0:T(8,128)S(1)} %all_to_all.17), channel_id=1, source_target_pairs={{0,1},{1,0},{2,3},{3,2},{4,5},{5,4},{6,7},{7,6},{8,9},{9,8},{10,11... | collective-permute-start | bytes 393224 | tf_op jit(solution)/shard_map/ppermute | solution.py:574

commit v15 on v14

--- a/solution.py
+++ b/solution.py
@@ -178,8 +178,7 @@
     free_ref,
     density_ref,
     start_ref,
-    disp_hbm,
-    sens_ref,
+    disp_ref,
     coef_ref,
     plane_ref,
     beside_ref,
@@ -195,12 +194,9 @@
     rate_ref,
     first_ref,
     second_ref,
-    disp_ref,
-    stored,
 ):
     planes, layers, row_width = coef_ref.shape
     own_planes = density_ref.shape[2]
-    load_cases = lax.axis_size("space")
     shape = (layers, row_width)
     z = spot_iota(shape, 0)
     y = spot_iota(shape, 1)
@@ -263,7 +259,7 @@
     across_ref[0] = zero
     across_ref[planes] = zero
     up_ref[rows(0, layers)] = zero
-    for ref in (first_ref, second_ref):
+    for ref in (first_ref, second_ref, disp_ref):
         for part in range(3):
             ref[part, rows(0, layers)] = zero
             ref[part, rows(planes + 1, layers)] = zero
@@ -302,7 +298,7 @@
 
     own_x = spot_ref[0]
 
-    def sweep(source, target, lead):
+    def sweep(source, target):
         def sweep_plane(x, carry):
             before, after = across_ref[x], across_ref[x + 1]
             up, down = up_ref[rows(x + 1, layers)], up_ref[rows(x + 1, layers, -1)]
@@ -317,42 +313,70 @@
                     right * pltpu.roll(here, row_width - 1, 1) + left * pltpu.roll(here, 1, 1),
                 ]
                 pull = pulls[0] + pulls[1] + pulls[2] + pulls[part]
-                target[part, rows(x + lead, layers)] = (
+                target[part, rows(x + 1, layers)] = (
                     1.0 - relax_factor
                 ) * here + rate_ref[part, x] * pull
             return carry
 
         lax.fori_loop(0, planes, sweep_plane, 0, unroll=16)
         for part in range(3):
-            target[part, rows(own_x + lead, layers)] += rate_ref[part, own_x] * load_ref[part]
+            target[part, rows(own_x + 1, layers)] += rate_ref[part, own_x] * load_ref[part]
 
     stages = (first_ref, second_ref)
     for turn in range(SWEEPS - 1):
-        sweep(stages[turn % 2], stages[(turn + 1) % 2], 1)
-    sweep(stages[(SWEEPS - 1) % 2], disp_ref, 0)
-    store = pltpu.make_async_copy(
-        disp_ref.at[:, pl.ds(0, planes * layers)], disp_hbm, stored
-    )
-    store.start()
-
-    def energy_plane(x, carry):
-        later = jnp.minimum(x + 1, planes - 1)
-        ahead, upward, right = zero, zero, zero
+        sweep(stages[turn % 2], stages[(turn + 1) % 2])
+    sweep(stages[(SWEEPS - 1) % 2], disp_ref)
+
+
+def energy_planes(group, disp_ref, sens_ref):
+    chips, own_planes, layers, row_width = sens_ref.shape
+    planes = disp_ref.shape[1] // layers - 2
+    load_cases = lax.axis_size("space")
+    shape = (layers, row_width)
+    z = spot_iota(shape, 0)
+    y = spot_iota(shape, 1)
+    zero = jnp.zeros(shape, jnp.float32)
+    mine = lax.axis_index("space")
+    core = mine ^ mine >> 1 ^ group
+
+    def between(x):
+        result = zero
         for part in range(3):
-            here = disp_ref[part, rows(x, layers)]
-            step = disp_ref[part, rows(later, layers)] - here
-            climb = disp_ref[part, rows(x, layers, 1)] - here
+            step = disp_ref[part, rows(x + 1, layers)] - disp_ref[part, rows(x, layers)]
+            result = result + (2.0 if part == 0 else 1.0) * (step * step)
+        return jnp.where((x > 0) & (x < planes), result, 0.0)
+
+    def inside(x):
+        upward, right = zero, zero
+        for part in range(3):
+            here = disp_ref[part, rows(x + 1, layers)]
+            climb = disp_ref[part, rows(x + 1, layers, 1)] - here
             slide = pltpu.roll(here, row_width - 1, 1) - here
-            ahead = ahead + (2.0 if part == 0 else 1.0) * (step * step)
             upward = upward + (2.0 if part == 1 else 1.0) * (climb * climb)
             right = right + (2.0 if part == 2 else 1.0) * (slide * slide)
         upward = jnp.where(z < layers - 1, upward, 0.0)
         right = jnp.where(y < row_width - 1, right, 0.0)
-        total = carry + ahead + upward + pltpu.roll(upward, 1, 0) + right + pltpu.roll(right, 1, 1)
-        sens_ref[pair_spot(x, own_planes)] = (0.5 / load_cases) * total
-        return ahead
-
-    lax.fori_loop(0, planes, energy_plane, zero, unroll=16)
+        return upward + pltpu.roll(upward, 1, 0) + right + pltpu.roll(right, 1, 1)
+
+    for chip in range(chips):
+        first = own_planes * (2 * chip + ((core ^ chip) & 1))
+        before = between(first)
+        for own in range(own_planes):
+            after = between(first + own + 1)
+            sens_ref[chip, own] = (0.5 / load_cases) * (before + after + inside(first + own))
+            before = after
+
+
+def sent_energy_kernel(disp_ref, sens_ref):
+    energy_planes(1, disp_ref, sens_ref)
+
+
+def kept_energy_kernel(disp_ref, disp_hbm, sens_ref, stored):
+    layers = sens_ref.shape[2]
+    inner = pl.ds(layers, disp_ref.shape[1] - 2 * layers)
+    store = pltpu.make_async_copy(disp_ref.at[:, inner], disp_hbm, stored)
+    store.start()
+    energy_planes(0, disp_ref, sens_ref)
     store.wait()
 
 
@@ -512,12 +536,11 @@
     return pl.pallas_call(
         sweep_kernel,
         out_shape=[
-            floats(3, planes * layers, row_width),
-            floats(*density.shape),
+            floats(3, (planes + 2) * layers, row_width),
             floats(planes, layers, row_width),
         ],
         in_specs=[in_smem()] + [in_vmem()] * 6,
-        out_specs=[pl.BlockSpec(memory_space=pltpu.HBM), in_vmem(), in_vmem()],
+        out_specs=[in_vmem()] * 2,
         scratch_shapes=[
             scratch(planes * (layers + GAP) + GAP),
             scratch(planes * (layers + GAP) + GAP),
@@ -533,12 +556,38 @@
             scratch(3, planes, layers),
             scratch(3, (planes + 2) * layers),
             scratch(3, (planes + 2) * layers),
-            scratch(3, (planes + 1) * layers),
-            pltpu.SemaphoreType.DMA(()),
         ],
         compiler_params=pltpu.CompilerParams(vmem_limit_bytes=KERNEL_VMEM),
         name="sweeps",
     )(spot, load, weights, inverses, free, density, displacement)
+
+
+def sent_energy_call(disp, group_shape):
+    return pl.pallas_call(
+        sent_energy_kernel,
+        out_shape=floats(*group_shape),
+        in_specs=[in_vmem()],
+        out_specs=in_vmem(),
+        compiler_params=pltpu.CompilerParams(vmem_limit_bytes=KERNEL_VMEM),
+        name="sent_energy",
+    )(disp)
+
+
+def kept_energy_call(disp, group_shape):
+    parts, disp_rows, row_width = disp.shape
+    layers = group_shape[2]
+    return pl.pallas_call(
+        kept_energy_kernel,
+        out_shape=[floats(parts, disp_rows - 2 * layers, row_width), floats(*group_shape)],
+        in_specs=[in_vmem()],
+        out_specs=[pl.BlockSpec(memory_space=pltpu.HBM), in_vmem()],
+        scratch_shapes=[pltpu.SemaphoreType.DMA(())],
+        compiler_params=pltpu.CompilerParams(vmem_limit_bytes=KERNEL_VMEM),
+        cost_estimate=pl.CostEstimate(
+            flops=20 * disp.size, bytes_accessed=8 * disp.size, transcendentals=0
+        ),
+        name="kept_energy",
+    )(disp)
 
 
 def design_call(weights, sens, coef, density):
@@ -592,8 +641,10 @@
     return jnp.stack([blocks, other_core(blocks)])
 
 
-def scattered_sum(pieces):
-    return jnp.sum(between_chips(pieces[0] + other_core(pieces[1])), axis=0)
+def scattered_sum(sent, make_kept):
+    received = other_core(sent)
+    *others, kept = make_kept()
+    return jnp.sum(between_chips(kept + received), axis=0), others
 
 
 def one_slab(density, displacement, fixed, load_index, load_force, radius):
@@ -602,10 +653,12 @@
     )
     whole = with_other_core(same_group)
     weights, inverses, free, load, spot = prepare_call(*small)
-    new_displacement, sens, coef = sweep_call(
-        spot, load, weights, inverses, free, whole, displacement[0]
+    disp, coef = sweep_call(spot, load, weights, inverses, free, whole, displacement[0])
+    sent, disp = lax.optimization_barrier((sent_energy_call(disp, same_group.shape), disp))
+    sens, (new_displacement,) = scattered_sum(
+        sent, lambda: kept_energy_call(disp, same_group.shape)
     )
-    sens = with_other_core(chip_gathered(scattered_sum(sens)))
+    sens = with_other_core(chip_gathered(sens))
     new_density = design_call(weights, sens, coef, whole)
     return new_density, new_displacement.reshape(displacement.shape)
 

time: 48.7 us -> 48.1 us (0.988)
  waiting for transfers between devices: 2.32 us -> 1.41 us
    ppermute x3, waiting for transfers between devices: 2.32 us -> 1.41 us  [other_core(): return lax.ppermute(block, 'space', [(i, i ^ 1) for i in range(devices)])]
    pallas_call x1 -> x3, Pallas kernels: 4.85 us -> 5.2 us  [the longest x1 3.98 us: sweep_call(): pl.pallas_call(sweep_kernel, out_shape=[floats(3, (planes + 2) * layers,...]
  transfers between devices with their start and end apart: 3 -> 3, of which waited for: 2 -> 2; matrix products, arithmetic and copies ran while one was open for 0% -> 0% of each run, Pallas kernels for 3% -> 5%
where the time goes in v15:
time: 48.1 us; the launch traced here: 47.6 us
  blocking collectives  33.4 us (69%)
  Pallas kernels  9.96 us (21%)
  waiting for transfers between devices  1.41 us (3%)
  starting transfers between devices  1.31 us (3%)
  local copies, waits for them, and re-layouts  0.82 us (2%)
  between operations  0.71 us (1%)
    all_to_all x3, blocking collectives, between_chips(): lax.all_to_all(pieces, 'space', 0, 0, axis_index_groups=chip_groups())  33.4 us
    pallas_call x1, Pallas kernels, sweep_call(): pl.pallas_call(sweep_kernel, out_shape=[floats(3, (planes + 2) * layers,...  3.98 us
    pallas_call x1, Pallas kernels, design_call(): pl.pallas_call(design_kernel, out_shape=floats(own_planes, layers, row_wi...  3.36 us
    ppermute x3, waiting for transfers between devices, other_core(): return lax.ppermute(block, 'space', [(i, i ^ 1) for i in range(devices)])  1.41 us
    pallas_call x1, Pallas kernels, prepare_call(): pl.pallas_call(prepare_kernel, out_shape=[floats(len(ALL_SQUARES), layers...  1.4 us
    ppermute x3, starting transfers between devices, other_core(): return lax.ppermute(block, 'space', [(i, i ^ 1) for i in range(devices)])  1.31 us
  transfers between devices with their start and end apart: 3, of which 2 were waited for; matrix products, arithmetic and copies ran while one was open for 0% of the time, Pallas kernels for 5%

profile of v15, /device:TPU:0, one launch (start us, length us, event | category | flops | bytes accessed | tf_op | source)
XLA Modules:
  0.0 47.6 jit_solution(14349983681739275498)
XLA Ops:
  0.6 0.0 copy-start
  0.6 0.8 %broadcast_in_dim.4 = f32[8,2,16,128]{3,2,1,0:T(8,128)S(1)} broadcast(f32[2,16,128]{2,1,0:T(8,128)} %param.6), dimensions={1,2,3} | broadcast | bytes 147456 | tf_op jit(solution)/shard_map/broadcast_in_dim | solution.py:637
  1.4 13.5 %all_to_all.15 = f32[8,2,16,128]{3,2,1,0:T(8,128)S(1)} all-to-all(f32[8,2,16,128]{3,2,1,0:T(8,128)S(1)} %broadcast_in_dim.4), channel_id=1, replica_groups={{0,3,4,7,8,11,12,15},{1,2,5,6,9,10,13,14},{16,19,20,23,24,27,28,31},{17..., dimensions={0} | all-to-all | bytes 262144 | tf_op jit(solution)/shard_map/all_to_all | solution.py:632
  14.9 0.7 %collective-permute-start = (f32[8,2,16,128]{3,2,1,0:T(8,128)S(1)}, f32[8,2,16,128]{3,2,1,0:T(8,128)S(1)}, u32[]{:S(2)}, u32[]{:S(2)}) collective-permute-start(f32[8,2,16,128]{3,2,1,0:T(8,128)S(1)} %all_to_all.15), channel_id=1, source_target_pairs={{0,1},{1,0},{2,3},{3,2},{4,5},{5,4},{6,7},{7,6},{8,9},{9,8},{10,11... | collective-permute-start | bytes 393224 | tf_op jit(solution)/shard_map/ppermute | solution.py:623
  15.6 1.4 %prepare.1 = (f32[10,16,128]{2,1,0:T(8,128)S(1)}, f32[5,16,128]{2,1,0:T(8,128)S(1)}, f32[32,16,128]{2,1,0:T(8,128)S(1)}, f32[3,16,128]{2,1,0:T(8,128)S(1)}, s32[1]{0:T(128)}) custom-call(s32[16]{0:T(128)} %radius_hbm, s32[16]{0:T(128)} %index_hbm, f32[3,16]{1,0:T(4,128)} %bitcast.12, s32[32,128]{1,0:T(8,128)} %fixed_hbm), custom_call_target="tpu_custom_call" | custom-call | flops 2621440 | bytes 524288 | tf_op jit(solution)/shard_map/prepare/pallas_call | solution.py:496
  17.0 0.0 collective-permute-done
  17.0 0.0 copy-done
  17.0 4.0 %sweeps.1 = (f32[3,544,128]{2,1,0:T(8,128)S(1)}, f32[32,16,128]{2,1,0:T(8,128)S(1)}) custom-call(s32[1]{0:T(128)} %get-tuple-element.23.spot_ref, f32[3,16,128]{2,1,0:T(8,128)S(1)} %get-tuple-element.24.load_ref, f32[10,16,128]{2,1,0:T(8,128)S(1)} %get-tuple-element.22.weight_ref, f32[5,16,128]{2,1,0:T(8,128)S(1)} %get-tuple-element.25.inverse_ref, ...), custom_call_target="tpu_custom_call" | custom-call | tf_op jit(solution)/shard_map/sweeps/pallas_call | solution.py:536
  21.0 0.3 sent_energy.1
  21.3 0.1 collective-permute-start.1
  21.4 0.9 %kept_energy.1 = (f32[3,512,128]{2,1,0:T(8,128)}, f32[8,2,16,128]{3,2,1,0:T(8,128)S(1)}) custom-call(f32[3,544,128]{2,1,0:T(8,128)S(1)} %get-tuple-element.29.disp_ref), custom_call_target="tpu_custom_call" | custom-call | flops 4177920 | bytes 1671168 | tf_op jit(solution)/shard_map/kept_energy/pallas_call | solution.py:579
  22.3 0.4 collective-permute-done.1
  22.8 10.1 %all_to_all.16 = f32[8,2,16,128]{3,2,1,0:T(8,128)S(1)} all-to-all(f32[8,2,16,128]{3,2,1,0:T(8,128)S(1)} %add.3), channel_id=1, replica_groups={{0,3,4,7,8,11,12,15},{1,2,5,6,9,10,13,14},{16,19,20,23,24,27,28,31},{17..., dimensions={0} | all-to-all | bytes 262144 | tf_op jit(solution)/shard_map/all_to_all | solution.py:632
  32.9 9.8 %all_to_all.17 = f32[8,2,16,128]{3,2,1,0:T(8,128)S(1)} all-to-all(f32[8,2,16,128]{3,2,1,0:T(8,128)S(1)} %broadcast_in_dim.5), channel_id=1, replica_groups={{0,3,4,7,8,11,12,15},{1,2,5,6,9,10,13,14},{16,19,20,23,24,27,28,31},{17..., dimensions={0} | all-to-all | bytes 262144 | tf_op jit(solution)/shard_map/all_to_all | solution.py:632
  42.7 0.6 %collective-permute-start.2 = (f32[8,2,16,128]{3,2,1,0:T(8,128)S(1)}, f32[8,2,16,128]{3,2,1,0:T(8,128)S(1)}, u32[]{:S(2)}, u32[]{:S(2)}) collective-permute-start(f32[8,2,16,128]{3,2,1,0:T(8,128)S(1)} %all_to_all.17), channel_id=1, source_target_pairs={{0,1},{1,0},{2,3},{3,2},{4,5},{5,4},{6,7},{7,6},{8,9},{9,8},{10,11... | collective-permute-start | bytes 393224 | tf_op jit(solution)/shard_map/ppermute | solution.py:623
  43.3 1.0 %collective-permute-done.2 = f32[8,2,16,128]{3,2,1,0:T(8,128)S(1)} collective-permute-done((f32[8,2,16,128]{3,2,1,0:T(8,128)S(1)}, f32[8,2,16,128]{3,2,1,0:T(8,128)S(1)}, u32[]{:S(2)}, u32[]{:S(2)}) %collective-permute-start.2) | collective-permute-done | bytes 131104 | tf_op jit(solution)/shard_map/ppermute | solution.py:623
  44.3 3.4 %design.1 = f32[2,16,128]{2,1,0:T(8,128)} custom-call(f32[10,16,128]{2,1,0:T(8,128)S(1)} %get-tuple-element.22.weight_ref, f32[2,8,2,16,128]{4,3,2,1,0:T(8,128)S(1)} %pad_maximum_fusion.1.sens_ref, f32[32,16,128]{2,1,0:T(8,128)S(1)} %get-tuple-element.32.coef_ref, f32[2,8,2,16,128]{4,3,2,1,0:T(8,128)S(1)} %pad_maximum_fusion.density_ref), custom_call_target="tpu_custom_call" | custom-call | tf_op jit(solution)/shard_map/design/pallas_call | solution.py:600
  (5 shorter events, 0.1 us)
Async XLA Ops:
  0.6 16.4 %copy-start = (f32[1,3,32,16,128]{4,3,2,1,0:T(8,128)S(1)}, f32[1,3,32,16,128]{4,3,2,1,0:T(8,128)}, u32[]{:S(2)}) copy-start(f32[1,3,32,16,128]{4,3,2,1,0:T(8,128)} %param.7) | copy-start | bytes 2359300
  14.9 2.1 %collective-permute-start = (f32[8,2,16,128]{3,2,1,0:T(8,128)S(1)}, f32[8,2,16,128]{3,2,1,0:T(8,128)S(1)}, u32[]{:S(2)}, u32[]{:S(2)}) collective-permute-start(f32[8,2,16,128]{3,2,1,0:T(8,128)S(1)} %all_to_all.15), channel_id=1, source_target_pairs={{0,1},{1,0},{2,3},{3,2},{4,5},{5,4},{6,7},{7,6},{8,9},{9,8},{10,11... | collective-permute-start | bytes 393224 | tf_op jit(solution)/shard_map/ppermute | solution.py:623
  21.3 1.4 %collective-permute-start.1 = (f32[8,2,16,128]{3,2,1,0:T(8,128)S(1)}, f32[8,2,16,128]{3,2,1,0:T(8,128)S(1)}, u32[]{:S(2)}, u32[]{:S(2)}) collective-permute-start(f32[8,2,16,128]{3,2,1,0:T(8,128)S(1)} %sent_energy.1), channel_id=1, source_target_pairs={{0,1},{1,0},{2,3},{3,2},{4,5},{5,4},{6,7},{7,6},{8,9},{9,8},{10,11... | collective-permute-start | bytes 393224 | tf_op jit(solution)/shard_map/ppermute | solution.py:623
  42.7 1.5 %collective-permute-start.2 = (f32[8,2,16,128]{3,2,1,0:T(8,128)S(1)}, f32[8,2,16,128]{3,2,1,0:T(8,128)S(1)}, u32[]{:S(2)}, u32[]{:S(2)}) collective-permute-start(f32[8,2,16,128]{3,2,1,0:T(8,128)S(1)} %all_to_all.17), channel_id=1, source_target_pairs={{0,1},{1,0},{2,3},{3,2},{4,5},{5,4},{6,7},{7,6},{8,9},{9,8},{10,11... | collective-permute-start | bytes 393224 | tf_op jit(solution)/shard_map/ppermute | solution.py:623

commit v16 on v15

--- a/solution.py
+++ b/solution.py
@@ -26,6 +26,12 @@
 
 def spot_iota(shape, dim):
     return lax.broadcasted_iota(jnp.int32, shape, dim)
+
+
+def each_plane(planes, body, carry):
+    for x in range(planes):
+        carry = body(x, carry)
+    return carry
 
 
 def layer_radius(radius_ref, layers, row_width):
@@ -99,7 +105,7 @@
 
 
 def edge_class(x, planes):
-    return jnp.minimum(x, 2) + jnp.maximum(x - (planes - 3), 0)
+    return min(x, 2) + max(x - (planes - 3), 0)
 
 
 def zero_edges(ref):
@@ -159,7 +165,7 @@
         )
         return carry
 
-    lax.fori_loop(0, planes, free_plane, 0, unroll=16)
+    each_plane(planes, free_plane, 0)
 
     own_index = index_ref[load_place]
     own_z = own_index // row_width % layers
@@ -216,7 +222,7 @@
             ref[gapped(x, layers)] = field
         return carry
 
-    lax.fori_loop(0, planes, spread_plane, 0, unroll=16)
+    each_plane(planes, spread_plane, 0)
 
     def filter_plane(x, carry):
         def around(ref, distance):
@@ -237,7 +243,7 @@
         far_ref[x + 2] = weigh(sums, weight_ref, 4)
         return carry
 
-    lax.fori_loop(0, planes, filter_plane, 0, unroll=16)
+    each_plane(planes, filter_plane, 0)
 
     def modulus_plane(x, carry):
         inverse = inverse_ref[edge_class(x, planes)]
@@ -253,7 +259,7 @@
         coef_ref[x] = 3.0 * (1.0 - floor_modulus) * (filtered * filtered) * inverse
         return carry
 
-    lax.fori_loop(0, planes, modulus_plane, 0, unroll=16)
+    each_plane(planes, modulus_plane, 0)
 
     modulus_ref[rows(planes, layers)] = zero
     across_ref[0] = zero
@@ -268,7 +274,7 @@
         before = carry
         modulus = modulus_ref[rows(x, layers)]
         later = modulus_ref[rows(x + 1, layers)]
-        ahead = jnp.where(x + 1 < planes, 0.5 * (modulus + later), 0.0)
+        ahead = 0.5 * (modulus + later) if x + 1 < planes else zero
         across_ref[x + 1] = ahead
         above = modulus_ref[rows(x, layers, 1)]
         up = jnp.where(z < layers - 1, 0.5 * (modulus + above), 0.0)
@@ -294,7 +300,7 @@
             first_ref[part, rows(x + 1, layers)] = start_ref[part, x] * free
         return ahead
 
-    lax.fori_loop(0, planes, face_plane, zero, unroll=16)
+    each_plane(planes, face_plane, zero)
 
     own_x = spot_ref[0]
 
@@ -318,7 +324,7 @@
                 ) * here + rate_ref[part, x] * pull
             return carry
 
-        lax.fori_loop(0, planes, sweep_plane, 0, unroll=16)
+        each_plane(planes, sweep_plane, 0)
         for part in range(3):
             target[part, rows(own_x + 1, layers)] += rate_ref[part, own_x] * load_ref[part]
 
@@ -414,7 +420,7 @@
         further_ref[x + 2] = shift_sum(plane, 1, 2)
         return carry
 
-    lax.fori_loop(0, planes, spread_plane, 0, unroll=16)
+    each_plane(planes, spread_plane, 0)
 
     def filter_plane(x, carry):
         def around(ref, distance):
@@ -434,7 +440,7 @@
             ref[gapped(x, layers)] = weigh(sums, weight_ref, square)
         return carry
 
-    lax.fori_loop(0, planes, filter_plane, 0, unroll=16)
+    each_plane(planes, filter_plane, 0)
 
     def root_plane(x, carry):
         root = jnp.sqrt(
@@ -450,7 +456,7 @@
         high_ref[x] = jnp.minimum(density + move_limit, 1.0)
         return carry
 
-    lax.fori_loop(0, planes, root_plane, 0, unroll=16)
+    each_plane(planes, root_plane, 0)
 
     target = volume_share * planes * layers * row_width
 
@@ -462,9 +468,7 @@
         half = span * 0.5
         middle = lower + half
         factor = jnp.exp(-0.5 * middle)
-        total = lax.fori_loop(
-            0, planes, lambda x, acc: acc + trial(x, factor), zero, unroll=16
-        )
+        total = each_plane(planes, lambda x, acc: acc + trial(x, factor), zero)
         volume = jnp.sum(jnp.sum(total, axis=0, keepdims=True), axis=1, keepdims=True)
         return jnp.where(volume > target, middle, lower), half
 

time: 48.1 us -> 48.6 us (1.010)
  Pallas kernels: 9.96 us -> 10.5 us
    pallas_call x1, Pallas kernels: 3.98 us -> 5.06 us  [sweep_call(): pl.pallas_call(sweep_kernel, out_shape=[floats(3, (planes + 2) * layers,...]
where the time goes in v16:
time: 48.6 us; the launch traced here: 48.2 us
  blocking collectives  33.4 us (69%)
  Pallas kernels  10.5 us (22%)
  waiting for transfers between devices  1.41 us (3%)
  starting transfers between devices  1.32 us (3%)
  local copies, waits for them, and re-layouts  0.82 us (2%)
  between operations  0.71 us (1%)
    all_to_all x3, blocking collectives, between_chips(): lax.all_to_all(pieces, 'space', 0, 0, axis_index_groups=chip_groups())  33.4 us
    pallas_call x1, Pallas kernels, sweep_call(): pl.pallas_call(sweep_kernel, out_shape=[floats(3, (planes + 2) * layers,...  5.06 us
    pallas_call x1, Pallas kernels, design_call(): pl.pallas_call(design_kernel, out_shape=floats(own_planes, layers, row_wi...  2.88 us
    ppermute x3, waiting for transfers between devices, other_core(): return lax.ppermute(block, 'space', [(i, i ^ 1) for i in range(devices)])  1.41 us
    ppermute x3, starting transfers between devices, other_core(): return lax.ppermute(block, 'space', [(i, i ^ 1) for i in range(devices)])  1.32 us
    pallas_call x1, Pallas kernels, prepare_call(): pl.pallas_call(prepare_kernel, out_shape=[floats(len(ALL_SQUARES), layers...  1.31 us
  transfers between devices with their start and end apart: 3, of which 2 were waited for; matrix products, arithmetic and copies ran while one was open for 0% of the time, Pallas kernels for 5%

profile of v16, /device:TPU:0, one launch (start us, length us, event | category | flops | bytes accessed | tf_op | source)
XLA Modules:
  0.0 48.2 jit_solution(8808875844175956796)
XLA Ops:
  0.6 0.0 copy-start
  0.6 0.8 %broadcast_in_dim.4 = f32[8,2,16,128]{3,2,1,0:T(8,128)S(1)} broadcast(f32[2,16,128]{2,1,0:T(8,128)} %param.6), dimensions={1,2,3} | broadcast | bytes 147456 | tf_op jit(solution)/shard_map/broadcast_in_dim | solution.py:641
  1.4 13.5 %all_to_all.15 = f32[8,2,16,128]{3,2,1,0:T(8,128)S(1)} all-to-all(f32[8,2,16,128]{3,2,1,0:T(8,128)S(1)} %broadcast_in_dim.4), channel_id=1, replica_groups={{0,3,4,7,8,11,12,15},{1,2,5,6,9,10,13,14},{16,19,20,23,24,27,28,31},{17..., dimensions={0} | all-to-all | bytes 262144 | tf_op jit(solution)/shard_map/all_to_all | solution.py:636
  14.9 0.7 %collective-permute-start = (f32[8,2,16,128]{3,2,1,0:T(8,128)S(1)}, f32[8,2,16,128]{3,2,1,0:T(8,128)S(1)}, u32[]{:S(2)}, u32[]{:S(2)}) collective-permute-start(f32[8,2,16,128]{3,2,1,0:T(8,128)S(1)} %all_to_all.15), channel_id=1, source_target_pairs={{0,1},{1,0},{2,3},{3,2},{4,5},{5,4},{6,7},{7,6},{8,9},{9,8},{10,11... | collective-permute-start | bytes 393224 | tf_op jit(solution)/shard_map/ppermute | solution.py:627
  15.6 1.3 %prepare.1 = (f32[10,16,128]{2,1,0:T(8,128)S(1)}, f32[5,16,128]{2,1,0:T(8,128)S(1)}, f32[32,16,128]{2,1,0:T(8,128)S(1)}, f32[3,16,128]{2,1,0:T(8,128)S(1)}, s32[1]{0:T(128)}) custom-call(s32[16]{0:T(128)} %radius_hbm, s32[16]{0:T(128)} %index_hbm, f32[3,16]{1,0:T(4,128)} %bitcast.12, s32[32,128]{1,0:T(8,128)} %fixed_hbm), custom_call_target="tpu_custom_call" | custom-call | flops 2621440 | bytes 524288 | tf_op jit(solution)/shard_map/prepare/pallas_call | solution.py:500
  16.9 0.0 collective-permute-done
  16.9 0.0 copy-done
  16.9 5.1 %sweeps.1 = (f32[3,544,128]{2,1,0:T(8,128)S(1)}, f32[32,16,128]{2,1,0:T(8,128)S(1)}) custom-call(s32[1]{0:T(128)} %get-tuple-element.23.spot_ref, f32[3,16,128]{2,1,0:T(8,128)S(1)} %get-tuple-element.24.load_ref, f32[10,16,128]{2,1,0:T(8,128)S(1)} %get-tuple-element.22.weight_ref, f32[5,16,128]{2,1,0:T(8,128)S(1)} %get-tuple-element.25.inverse_ref, ...), custom_call_target="tpu_custom_call" | custom-call | tf_op jit(solution)/shard_map/sweeps/pallas_call | solution.py:540
  22.0 0.3 sent_energy.1
  22.3 0.1 collective-permute-start.1
  22.4 0.9 %kept_energy.1 = (f32[3,512,128]{2,1,0:T(8,128)}, f32[8,2,16,128]{3,2,1,0:T(8,128)S(1)}) custom-call(f32[3,544,128]{2,1,0:T(8,128)S(1)} %get-tuple-element.29.disp_ref), custom_call_target="tpu_custom_call" | custom-call | flops 4177920 | bytes 1671168 | tf_op jit(solution)/shard_map/kept_energy/pallas_call | solution.py:583
  23.3 0.4 collective-permute-done.1
  23.8 10.1 %all_to_all.16 = f32[8,2,16,128]{3,2,1,0:T(8,128)S(1)} all-to-all(f32[8,2,16,128]{3,2,1,0:T(8,128)S(1)} %add.3), channel_id=1, replica_groups={{0,3,4,7,8,11,12,15},{1,2,5,6,9,10,13,14},{16,19,20,23,24,27,28,31},{17..., dimensions={0} | all-to-all | bytes 262144 | tf_op jit(solution)/shard_map/all_to_all | solution.py:636
  33.9 9.8 %all_to_all.17 = f32[8,2,16,128]{3,2,1,0:T(8,128)S(1)} all-to-all(f32[8,2,16,128]{3,2,1,0:T(8,128)S(1)} %broadcast_in_dim.5), channel_id=1, replica_groups={{0,3,4,7,8,11,12,15},{1,2,5,6,9,10,13,14},{16,19,20,23,24,27,28,31},{17..., dimensions={0} | all-to-all | bytes 262144 | tf_op jit(solution)/shard_map/all_to_all | solution.py:636
  43.7 0.6 %collective-permute-start.2 = (f32[8,2,16,128]{3,2,1,0:T(8,128)S(1)}, f32[8,2,16,128]{3,2,1,0:T(8,128)S(1)}, u32[]{:S(2)}, u32[]{:S(2)}) collective-permute-start(f32[8,2,16,128]{3,2,1,0:T(8,128)S(1)} %all_to_all.17), channel_id=1, source_target_pairs={{0,1},{1,0},{2,3},{3,2},{4,5},{5,4},{6,7},{7,6},{8,9},{9,8},{10,11... | collective-permute-start | bytes 393224 | tf_op jit(solution)/shard_map/ppermute | solution.py:627
  44.3 1.0 %collective-permute-done.2 = f32[8,2,16,128]{3,2,1,0:T(8,128)S(1)} collective-permute-done((f32[8,2,16,128]{3,2,1,0:T(8,128)S(1)}, f32[8,2,16,128]{3,2,1,0:T(8,128)S(1)}, u32[]{:S(2)}, u32[]{:S(2)}) %collective-permute-start.2) | collective-permute-done | bytes 131104 | tf_op jit(solution)/shard_map/ppermute | solution.py:627
  45.3 2.9 %design.1 = f32[2,16,128]{2,1,0:T(8,128)} custom-call(f32[10,16,128]{2,1,0:T(8,128)S(1)} %get-tuple-element.22.weight_ref, f32[2,8,2,16,128]{4,3,2,1,0:T(8,128)S(1)} %pad_maximum_fusion.1.sens_ref, f32[32,16,128]{2,1,0:T(8,128)S(1)} %get-tuple-element.32.coef_ref, f32[2,8,2,16,128]{4,3,2,1,0:T(8,128)S(1)} %pad_maximum_fusion.density_ref), custom_call_target="tpu_custom_call" | custom-call | tf_op jit(solution)/shard_map/design/pallas_call | solution.py:604
  (5 shorter events, 0.1 us)
Async XLA Ops:
  0.6 16.3 %copy-start = (f32[1,3,32,16,128]{4,3,2,1,0:T(8,128)S(1)}, f32[1,3,32,16,128]{4,3,2,1,0:T(8,128)}, u32[]{:S(2)}) copy-start(f32[1,3,32,16,128]{4,3,2,1,0:T(8,128)} %param.7) | copy-start | bytes 2359300
  14.9 2.0 %collective-permute-start = (f32[8,2,16,128]{3,2,1,0:T(8,128)S(1)}, f32[8,2,16,128]{3,2,1,0:T(8,128)S(1)}, u32[]{:S(2)}, u32[]{:S(2)}) collective-permute-start(f32[8,2,16,128]{3,2,1,0:T(8,128)S(1)} %all_to_all.15), channel_id=1, source_target_pairs={{0,1},{1,0},{2,3},{3,2},{4,5},{5,4},{6,7},{7,6},{8,9},{9,8},{10,11... | collective-permute-start | bytes 393224 | tf_op jit(solution)/shard_map/ppermute | solution.py:627
  22.3 1.4 %collective-permute-start.1 = (f32[8,2,16,128]{3,2,1,0:T(8,128)S(1)}, f32[8,2,16,128]{3,2,1,0:T(8,128)S(1)}, u32[]{:S(2)}, u32[]{:S(2)}) collective-permute-start(f32[8,2,16,128]{3,2,1,0:T(8,128)S(1)} %sent_energy.1), channel_id=1, source_target_pairs={{0,1},{1,0},{2,3},{3,2},{4,5},{5,4},{6,7},{7,6},{8,9},{9,8},{10,11... | collective-permute-start | bytes 393224 | tf_op jit(solution)/shard_map/ppermute | solution.py:627
  43.7 1.5 %collective-permute-start.2 = (f32[8,2,16,128]{3,2,1,0:T(8,128)S(1)}, f32[8,2,16,128]{3,2,1,0:T(8,128)S(1)}, u32[]{:S(2)}, u32[]{:S(2)}) collective-permute-start(f32[8,2,16,128]{3,2,1,0:T(8,128)S(1)} %all_to_all.17), channel_id=1, source_target_pairs={{0,1},{1,0},{2,3},{3,2},{4,5},{5,4},{6,7},{7,6},{8,9},{9,8},{10,11... | collective-permute-start | bytes 393224 | tf_op jit(solution)/shard_map/ppermute | solution.py:627

commit v17 on v16

--- a/solution.py
+++ b/solution.py
@@ -32,6 +32,11 @@
     for x in range(planes):
         carry = body(x, carry)
     return carry
+
+
+def each_half(planes, body, carry):
+    count = planes // 2
+    return lax.fori_loop(0, 2, lambda half, carry: body(half * count, count, carry), carry)
 
 
 def layer_radius(radius_ref, layers, row_width):
@@ -104,8 +109,22 @@
     return (apart ^ apart >> 1) & 1, device >> 1, x % own_planes
 
 
+def half_views(ref, first, count):
+    own_planes = ref.shape[2]
+    mine = lax.axis_index("space")
+    side = (mine ^ mine >> 1) & 1
+    chips = pl.ds(first // (2 * own_planes), count // (2 * own_planes))
+    views = (ref.at[side, chips], ref.at[1 - side, chips])
+
+    def plane(p):
+        device = p // own_planes
+        return views[(device ^ device >> 1) & 1], (device >> 1, p % own_planes)
+
+    return plane
+
+
 def edge_class(x, planes):
-    return min(x, 2) + max(x - (planes - 3), 0)
+    return jnp.minimum(x, 2) + jnp.maximum(x - (planes - 3), 0)
 
 
 def zero_edges(ref):
@@ -199,10 +218,8 @@
     left_ref,
     rate_ref,
     first_ref,
-    second_ref,
 ):
     planes, layers, row_width = coef_ref.shape
-    own_planes = density_ref.shape[2]
     shape = (layers, row_width)
     z = spot_iota(shape, 0)
     y = spot_iota(shape, 1)
@@ -211,127 +228,164 @@
 
     for ref in (side_ref, far_ref):
         zero_edges(ref)
-    for ref in (plane_ref, beside_ref, further_ref):
-        ref[gap(planes, layers)] = zero_gap
-
-    def spread_plane(x, carry):
-        plane = density_ref[pair_spot(x, own_planes)]
-        fields = (plane, shift_sum(plane, 1, 1), shift_sum(plane, 1, 2))
-        for ref, field in zip((plane_ref, beside_ref, further_ref), fields):
-            ref[gap(x, layers)] = zero_gap
-            ref[gapped(x, layers)] = field
+    def filter_half(first, count, carry):
+        density = half_views(density_ref, first, count)
+        spread = [
+            ref.at[pl.ds(first * (layers + GAP), count * (layers + GAP) + GAP)]
+            for ref in (plane_ref, beside_ref, further_ref)
+        ]
+        results = [ref.at[pl.ds(first + 2, count)] for ref in (near_ref, side_ref, far_ref)]
+        for ref in spread:
+            ref[gap(0, layers)] = zero_gap
+        for p in range(count):
+            view, spot = density(p)
+            plane = view[spot]
+            beside, further = shift_sum(plane, 1, 1), shift_sum(plane, 1, 2)
+            for ref, field in zip(spread, (plane, beside, further)):
+                ref[gapped(p, layers)] = field
+                ref[gap(p + 1, layers)] = zero_gap
+
+            def around(place, distance):
+                ref = spread[place]
+                return ref[gapped(p, layers, distance)] + ref[gapped(p, layers, -distance)]
+
+            sums = {
+                0: plane,
+                1: beside + around(0, 1),
+                2: around(1, 1),
+                4: further + around(0, 2),
+                5: around(2, 1) + around(1, 2),
+                8: around(2, 2),
+            }
+            for ref, square in zip(results, (0, 1, 4)):
+                ref[p] = weigh(sums, weight_ref, square)
         return carry
 
-    each_plane(planes, spread_plane, 0)
-
-    def filter_plane(x, carry):
-        def around(ref, distance):
-            return ref[gapped(x, layers, distance)] + ref[gapped(x, layers, -distance)]
-
-        beside = beside_ref[gapped(x, layers)]
-        further = further_ref[gapped(x, layers)]
-        sums = {
-            0: plane_ref[gapped(x, layers)],
-            1: beside + around(plane_ref, 1),
-            2: around(beside_ref, 1),
-            4: further + around(plane_ref, 2),
-            5: around(further_ref, 1) + around(beside_ref, 2),
-            8: around(further_ref, 2),
-        }
-        near_ref[x + 2] = weigh(sums, weight_ref, 0)
-        side_ref[x + 2] = weigh(sums, weight_ref, 1)
-        far_ref[x + 2] = weigh(sums, weight_ref, 4)
-        return carry
-
-    each_plane(planes, filter_plane, 0)
-
-    def modulus_plane(x, carry):
-        inverse = inverse_ref[edge_class(x, planes)]
-        filtered = (
-            near_ref[x + 2]
-            + side_ref[x + 1]
-            + side_ref[x + 3]
-            + far_ref[x]
-            + far_ref[x + 4]
-        ) * inverse
-        modulus = floor_modulus + (1.0 - floor_modulus) * (filtered * filtered * filtered)
-        modulus_ref[rows(x, layers)] = modulus
-        coef_ref[x] = 3.0 * (1.0 - floor_modulus) * (filtered * filtered) * inverse
-        return carry
-
-    each_plane(planes, modulus_plane, 0)
-
-    modulus_ref[rows(planes, layers)] = zero
-    across_ref[0] = zero
-    across_ref[planes] = zero
-    up_ref[rows(0, layers)] = zero
-    for ref in (first_ref, second_ref, disp_ref):
+    each_half(planes, filter_half, 0)
+
+    for ref in (first_ref, disp_ref):
         for part in range(3):
             ref[part, rows(0, layers)] = zero
             ref[part, rows(planes + 1, layers)] = zero
 
-    def face_plane(x, carry):
-        before = carry
-        modulus = modulus_ref[rows(x, layers)]
-        later = modulus_ref[rows(x + 1, layers)]
-        ahead = 0.5 * (modulus + later) if x + 1 < planes else zero
-        across_ref[x + 1] = ahead
-        above = modulus_ref[rows(x, layers, 1)]
+    def store_faces(slot, modulus, above, later, before, free, start, views):
+        across, up_view, right_view, left_view, rate, source = views
+        across[slot] = later
         up = jnp.where(z < layers - 1, 0.5 * (modulus + above), 0.0)
         right = jnp.where(
             y < row_width - 1, 0.5 * (modulus + pltpu.roll(modulus, row_width - 1, 1)), 0.0
         )
         left = pltpu.roll(right, 1, 1)
-        up_ref[rows(x + 1, layers)] = up
-        right_ref[x] = right
-        left_ref[x] = left
-        free = free_ref[x]
-        sums = (before + ahead, up + pltpu.roll(up, 1, 0), left + right)
+        up_view[rows(slot, layers)] = up
+        right_view[slot] = right
+        left_view[slot] = left
+        sums = (before + later, up + pltpu.roll(up, 1, 0), left + right)
         every = sums[0] + sums[1] + sums[2]
-        push = relax_factor * free
         diagonal = [every + part_sum for part_sum in sums]
         pair = diagonal[0] * diagonal[1]
-        push = push / (pair * diagonal[2])
+        push = relax_factor * free / (pair * diagonal[2])
         side = push * diagonal[2]
-        rate_ref[0, x] = side * diagonal[1]
-        rate_ref[1, x] = side * diagonal[0]
-        rate_ref[2, x] = push * pair
+        for part, factor in enumerate((side * diagonal[1], side * diagonal[0], push * pair)):
+            rate[part, slot] = factor
+            source[part, rows(slot, layers)] = start[part] * free
+
+    def modulus_half(first, count, carry):
+        near = near_ref.at[pl.ds(first + 2, count)]
+        side = side_ref.at[pl.ds(first + 1, count + 2)]
+        far = far_ref.at[pl.ds(first, count + 4)]
+        moduli = modulus_ref.at[pl.ds(first * layers, (count + 1) * layers)]
+        coef = coef_ref.at[pl.ds(first, count)]
+        free = free_ref.at[pl.ds(first, count)]
+        views = (
+            across_ref.at[pl.ds(first, count)],
+            up_ref.at[pl.ds(first * layers, count * layers)],
+            right_ref.at[pl.ds(first, count)],
+            left_ref.at[pl.ds(first, count)],
+            rate_ref.at[:, pl.ds(first, count)],
+            first_ref.at[:, pl.ds(first * layers, count * layers)],
+        )
+        modulus, before = carry
+        for p in range(count):
+            inverse = inverse_ref[edge_class(first + p, planes)]
+            filtered = near[p] + side[p] + side[p + 2] + far[p] + far[p + 4]
+            filtered = filtered * inverse
+            later = floor_modulus + (1.0 - floor_modulus) * (filtered * filtered * filtered)
+            coef[p] = 3.0 * (1.0 - floor_modulus) * (filtered * filtered) * inverse
+            moduli[rows(p + 1, layers)] = later
+            ahead = 0.5 * (modulus + later)
+            if p == 0:
+                ahead = jnp.where(first > 0, ahead, 0.0)
+            above = moduli[rows(p, layers, 1)] if p else pltpu.roll(modulus, layers - 1, 0)
+            previous = jnp.maximum(first + p - 1, 0)
+            store_faces(
+                p,
+                modulus,
+                above,
+                ahead,
+                before,
+                free_ref[previous],
+                [start_ref[part, previous] for part in range(3)],
+                views,
+            )
+            modulus, before = later, ahead
+        return modulus, before
+
+    modulus, before = each_half(planes, modulus_half, (jnp.ones(shape, jnp.float32), zero))
+    store_faces(
+        planes,
+        modulus,
+        pltpu.roll(modulus, layers - 1, 0),
+        zero,
+        before,
+        free_ref[planes - 1],
+        [start_ref[part, planes - 1] for part in range(3)],
+        (across_ref, up_ref, right_ref, left_ref, rate_ref, first_ref),
+    )
+
+    own_x = spot_ref[0]
+
+    def sweep(source, target):
+        def sweep_half(first, count, carry):
+            old = source.at[:, pl.ds(first * layers, (count + 2) * layers)]
+            new = target.at[:, pl.ds((first + 1) * layers, count * layers)]
+            across = across_ref.at[pl.ds(first, count + 1)]
+            up = up_ref.at[pl.ds(first * layers, (count + 1) * layers)]
+            right = right_ref.at[pl.ds(first + 1, count)]
+            left = left_ref.at[pl.ds(first + 1, count)]
+            rate = rate_ref.at[:, pl.ds(first + 1, count)]
+            behind = [old[part, rows(0, layers)] for part in range(3)]
+            here = [old[part, rows(1, layers)] for part in range(3)]
+            for p in range(count):
+                ahead = [old[part, rows(p + 2, layers)] for part in range(3)]
+                for part in range(3):
+                    pulls = [
+                        across[p] * behind[part] + across[p + 1] * ahead[part],
+                        up[rows(p + 1, layers)] * old[part, rows(p + 1, layers, 1)]
+                        + up[rows(p + 1, layers, -1)] * old[part, rows(p + 1, layers, -1)],
+                        right[p] * pltpu.roll(here[part], row_width - 1, 1)
+                        + left[p] * pltpu.roll(here[part], 1, 1),
+                    ]
+                    pull = pulls[0] + pulls[1] + pulls[2] + pulls[part]
+                    new[part, rows(p, layers)] = (
+                        1.0 - relax_factor
+                    ) * here[part] + rate[part, p] * pull
+                behind, here = here, ahead
+            return carry
+
+        each_half(planes, sweep_half, 0)
         for part in range(3):
-            first_ref[part, rows(x + 1, layers)] = start_ref[part, x] * free
-        return ahead
-
-    each_plane(planes, face_plane, zero)
-
-    own_x = spot_ref[0]
-
-    def sweep(source, target):
-        def sweep_plane(x, carry):
-            before, after = across_ref[x], across_ref[x + 1]
-            up, down = up_ref[rows(x + 1, layers)], up_ref[rows(x + 1, layers, -1)]
-            right, left = right_ref[x], left_ref[x]
-            for part in range(3):
-                here = source[part, rows(x + 1, layers)]
-                pulls = [
-                    before * source[part, rows(x, layers)]
-                    + after * source[part, rows(x + 2, layers)],
-                    up * source[part, rows(x + 1, layers, 1)]
-                    + down * source[part, rows(x + 1, layers, -1)],
-                    right * pltpu.roll(here, row_width - 1, 1) + left * pltpu.roll(here, 1, 1),
-                ]
-                pull = pulls[0] + pulls[1] + pulls[2] + pulls[part]
-                target[part, rows(x + 1, layers)] = (
-                    1.0 - relax_factor
-                ) * here + rate_ref[part, x] * pull
-            return carry
-
-        each_plane(planes, sweep_plane, 0)
-        for part in range(3):
-            target[part, rows(own_x + 1, layers)] += rate_ref[part, own_x] * load_ref[part]
-
-    stages = (first_ref, second_ref)
-    for turn in range(SWEEPS - 1):
-        sweep(stages[turn % 2], stages[(turn + 1) % 2])
-    sweep(stages[(SWEEPS - 1) % 2], disp_ref)
+            target[part, rows(own_x + 1, layers)] += rate_ref[part, own_x + 1] * load_ref[part]
+
+    def two_sweeps(turn, carry):
+        sweep(first_ref, disp_ref)
+
+        @pl.when(turn < SWEEPS // 2)
+        def _():
+            sweep(disp_ref, first_ref)
+
+        return carry
+
+    lax.fori_loop(0, SWEEPS // 2 + 1, two_sweeps, 0)
 
 
 def energy_planes(group, disp_ref, sens_ref):
@@ -395,7 +449,6 @@
     plane_ref,
     beside_ref,
     further_ref,
-    level_ref,
     near_ref,
     far_ref,
     pull_ref,
@@ -410,71 +463,101 @@
     zero_gap = jnp.zeros((GAP, row_width), jnp.float32)
     for ref in (plane_ref, beside_ref, further_ref):
         zero_edges(ref)
-    for ref in (near_ref, far_ref):
-        ref[gap(planes, layers)] = zero_gap
-
-    def spread_plane(x, carry):
-        plane = sens_ref[pair_spot(x, own_planes)] * coef_ref[x]
-        plane_ref[x + 2] = plane
-        beside_ref[x + 2] = shift_sum(plane, 1, 1)
-        further_ref[x + 2] = shift_sum(plane, 1, 2)
+
+    def spread_half(first, count, carry):
+        sens = half_views(sens_ref, first, count)
+        coef = coef_ref.at[pl.ds(first, count)]
+        plane_view, beside, further = (
+            ref.at[pl.ds(first + 2, count)] for ref in (plane_ref, beside_ref, further_ref)
+        )
+        for p in range(count):
+            view, spot = sens(p)
+            plane = view[spot] * coef[p]
+            plane_view[p] = plane
+            beside[p] = shift_sum(plane, 1, 1)
+            further[p] = shift_sum(plane, 1, 2)
         return carry
 
-    each_plane(planes, spread_plane, 0)
-
-    def filter_plane(x, carry):
-        def around(ref, distance):
-            return ref[x + 2 + distance] + ref[x + 2 - distance]
-
-        sums = {
-            0: plane_ref[x + 2],
-            1: beside_ref[x + 2] + around(plane_ref, 1),
-            2: around(beside_ref, 1),
-            4: further_ref[x + 2] + around(plane_ref, 2),
-            5: around(further_ref, 1) + around(beside_ref, 2),
-            8: around(further_ref, 2),
-        }
-        level_ref[x] = weigh(sums, weight_ref, 0)
-        for ref, square in ((near_ref, 1), (far_ref, 4)):
-            ref[gap(x, layers)] = zero_gap
-            ref[gapped(x, layers)] = weigh(sums, weight_ref, square)
+    each_half(planes, spread_half, 0)
+
+    def root_half(first, count, carry):
+        density_at = half_views(density_ref, first, count)
+        plane_view, beside, further = (
+            ref.at[pl.ds(first, count + 4)] for ref in (plane_ref, beside_ref, further_ref)
+        )
+        near, far = (
+            ref.at[pl.ds(first * (layers + GAP), count * (layers + GAP) + GAP)]
+            for ref in (near_ref, far_ref)
+        )
+        for ref in (near, far):
+            ref[gap(0, layers)] = zero_gap
+        pull, low, high = (
+            ref.at[pl.ds(first, count)] for ref in (pull_ref, low_ref, high_ref)
+        )
+        for p in range(count):
+
+            def around(ref, distance):
+                return ref[p + 2 + distance] + ref[p + 2 - distance]
+
+            sums = {
+                0: plane_view[p + 2],
+                1: beside[p + 2] + around(plane_view, 1),
+                2: around(beside, 1),
+                4: further[p + 2] + around(plane_view, 2),
+                5: around(further, 1) + around(beside, 2),
+                8: around(further, 2),
+            }
+            level = weigh(sums, weight_ref, 0)
+            for ref, square in ((near, 1), (far, 4)):
+                ref[gapped(p, layers)] = weigh(sums, weight_ref, square)
+                ref[gap(p + 1, layers)] = zero_gap
+            root = jnp.sqrt(
+                level
+                + near[gapped(p, layers, 1)]
+                + near[gapped(p, layers, -1)]
+                + far[gapped(p, layers, 2)]
+                + far[gapped(p, layers, -2)]
+            )
+            view, spot = density_at(p)
+            density = view[spot]
+            pull[p] = density * root
+            low[p] = jnp.maximum(density - move_limit, density_floor)
+            high[p] = jnp.minimum(density + move_limit, 1.0)
         return carry
 
-    each_plane(planes, filter_plane, 0)
-
-    def root_plane(x, carry):
-        root = jnp.sqrt(
-            level_ref[x]
-            + near_ref[gapped(x, layers, 1)]
-            + near_ref[gapped(x, layers, -1)]
-            + far_ref[gapped(x, layers, 2)]
-            + far_ref[gapped(x, layers, -2)]
-        )
-        density = density_ref[pair_spot(x, own_planes)]
-        pull_ref[x] = density * root
-        low_ref[x] = jnp.maximum(density - move_limit, density_floor)
-        high_ref[x] = jnp.minimum(density + move_limit, 1.0)
-        return carry
-
-    each_plane(planes, root_plane, 0)
+    each_half(planes, root_half, 0)
 
     target = volume_share * planes * layers * row_width
 
     def trial(x, factor):
         return jnp.minimum(jnp.maximum(pull_ref[x] * factor, low_ref[x]), high_ref[x])
 
-    def halve(step, state):
+    def factor_of(log_level):
+        return jnp.broadcast_to(jnp.exp(-0.5 * log_level), shape)
+
+    def exceeds(total):
+        return jnp.sum(jnp.sum(total, axis=0, keepdims=True), axis=1, keepdims=True) > target
+
+    def halve_twice(step, state):
         lower, span = state
-        half = span * 0.5
-        middle = lower + half
-        factor = jnp.exp(-0.5 * middle)
-        total = each_plane(planes, lambda x, acc: acc + trial(x, factor), zero)
-        volume = jnp.sum(jnp.sum(total, axis=0, keepdims=True), axis=1, keepdims=True)
-        return jnp.where(volume > target, middle, lower), half
+        half, quarter = span * 0.5, span * 0.25
+        middles = (lower + quarter, lower + half, lower + half + quarter)
+        factors = [factor_of(middle) for middle in middles]
+        totals = [zero, zero, zero]
+        for x in range(planes):
+            pull, low, high = pull_ref[x], low_ref[x], high_ref[x]
+            totals = [
+                total + jnp.minimum(jnp.maximum(pull * factor, low), high)
+                for total, factor in zip(totals, factors)
+            ]
+        first, second, third = (exceeds(total) for total in totals)
+        upper = jnp.where(third, middles[2], middles[1])
+        below = jnp.where(first, middles[0], lower)
+        return jnp.where(second, upper, below), quarter
 
     start = (jnp.full((1, 1), log_lower, jnp.float32), jnp.full((1, 1), log_span, jnp.float32))
-    lower, span = lax.fori_loop(0, SEARCH, halve, start)
-    factor = jnp.exp(-0.5 * (lower + 0.5 * span))
+    lower, span = lax.fori_loop(0, SEARCH // 2, halve_twice, start)
+    factor = factor_of(lower + 0.5 * span)
     for own in range(own_planes):
         new_ref[own] = trial(place * own_planes + own, factor)
 
@@ -555,10 +638,9 @@
             scratch((planes + 1) * layers),
             scratch(planes + 1, layers),
             scratch((planes + 1) * layers),
-            scratch(planes, layers),
-            scratch(planes, layers),
-            scratch(3, planes, layers),
-            scratch(3, (planes + 2) * layers),
+            scratch(planes + 1, layers),
+            scratch(planes + 1, layers),
+            scratch(3, planes + 1, layers),
             scratch(3, (planes + 2) * layers),
         ],
         compiler_params=pltpu.CompilerParams(vmem_limit_bytes=KERNEL_VMEM),
@@ -610,7 +692,6 @@
             scratch(planes + 4, layers),
             scratch(planes + 4, layers),
             scratch(planes + 4, layers),
-            scratch(planes, layers),
             scratch(planes * (layers + GAP) + GAP),
             scratch(planes * (layers + GAP) + GAP),
             scratch(planes, layers),

time: 48.6 us -> 47.5 us (0.977)
  Pallas kernels: 10.5 us -> 9.36 us
    pallas_call x1, Pallas kernels: 5.06 us -> 3.92 us  [sweep_call(): pl.pallas_call(sweep_kernel, out_shape=[floats(3, (planes + 2) * layers,...]
where the time goes in v17:
time: 47.5 us; the launch traced here: 47 us
  blocking collectives  33.4 us (70%)
  Pallas kernels  9.36 us (20%)
  waiting for transfers between devices  1.41 us (3%)
  starting transfers between devices  1.31 us (3%)
  local copies, waits for them, and re-layouts  0.82 us (2%)
  between operations  0.71 us (1%)
    all_to_all x3, blocking collectives, between_chips(): lax.all_to_all(pieces, 'space', 0, 0, axis_index_groups=chip_groups())  33.4 us
    pallas_call x1, Pallas kernels, sweep_call(): pl.pallas_call(sweep_kernel, out_shape=[floats(3, (planes + 2) * layers,...  3.92 us
    pallas_call x1, Pallas kernels, design_call(): pl.pallas_call(design_kernel, out_shape=floats(own_planes, layers, row_wi...  2.91 us
    ppermute x3, waiting for transfers between devices, other_core(): return lax.ppermute(block, 'space', [(i, i ^ 1) for i in range(devices)])  1.41 us
    ppermute x3, starting transfers between devices, other_core(): return lax.ppermute(block, 'space', [(i, i ^ 1) for i in range(devices)])  1.31 us
    pallas_call x1, Pallas kernels, prepare_call(): pl.pallas_call(prepare_kernel, out_shape=[floats(len(ALL_SQUARES), layers...  1.31 us
  transfers between devices with their start and end apart: 3, of which 2 were waited for; matrix products, arithmetic and copies ran while one was open for 0% of the time, Pallas kernels for 5%

profile of v17, /device:TPU:0, one launch (start us, length us, event | category | flops | bytes accessed | tf_op | source)
XLA Modules:
  0.0 47.0 jit_solution(1962287158472335271)
XLA Ops:
  0.6 0.0 copy-start
  0.6 0.8 %broadcast_in_dim.4 = f32[8,2,16,128]{3,2,1,0:T(8,128)S(1)} broadcast(f32[2,16,128]{2,1,0:T(8,128)} %param.6), dimensions={1,2,3} | broadcast | bytes 147456 | tf_op jit(solution)/shard_map/broadcast_in_dim | solution.py:722
  1.4 13.5 %all_to_all.15 = f32[8,2,16,128]{3,2,1,0:T(8,128)S(1)} all-to-all(f32[8,2,16,128]{3,2,1,0:T(8,128)S(1)} %broadcast_in_dim.4), channel_id=1, replica_groups={{0,3,4,7,8,11,12,15},{1,2,5,6,9,10,13,14},{16,19,20,23,24,27,28,31},{17..., dimensions={0} | all-to-all | bytes 262144 | tf_op jit(solution)/shard_map/all_to_all | solution.py:717
  14.9 0.7 %collective-permute-start = (f32[8,2,16,128]{3,2,1,0:T(8,128)S(1)}, f32[8,2,16,128]{3,2,1,0:T(8,128)S(1)}, u32[]{:S(2)}, u32[]{:S(2)}) collective-permute-start(f32[8,2,16,128]{3,2,1,0:T(8,128)S(1)} %all_to_all.15), channel_id=1, source_target_pairs={{0,1},{1,0},{2,3},{3,2},{4,5},{5,4},{6,7},{7,6},{8,9},{9,8},{10,11... | collective-permute-start | bytes 393224 | tf_op jit(solution)/shard_map/ppermute | solution.py:708
  15.6 1.3 %prepare.1 = (f32[10,16,128]{2,1,0:T(8,128)S(1)}, f32[5,16,128]{2,1,0:T(8,128)S(1)}, f32[32,16,128]{2,1,0:T(8,128)S(1)}, f32[3,16,128]{2,1,0:T(8,128)S(1)}, s32[1]{0:T(128)}) custom-call(s32[16]{0:T(128)} %radius_hbm, s32[16]{0:T(128)} %index_hbm, f32[3,16]{1,0:T(4,128)} %bitcast.12, s32[32,128]{1,0:T(8,128)} %fixed_hbm), custom_call_target="tpu_custom_call" | custom-call | flops 2621440 | bytes 524288 | tf_op jit(solution)/shard_map/prepare/pallas_call | solution.py:583
  16.9 0.0 collective-permute-done
  16.9 0.0 copy-done
  16.9 3.9 %sweeps.1 = (f32[3,544,128]{2,1,0:T(8,128)S(1)}, f32[32,16,128]{2,1,0:T(8,128)S(1)}) custom-call(s32[1]{0:T(128)} %get-tuple-element.23.spot_ref, f32[3,16,128]{2,1,0:T(8,128)S(1)} %get-tuple-element.24.load_ref, f32[10,16,128]{2,1,0:T(8,128)S(1)} %get-tuple-element.22.weight_ref, f32[5,16,128]{2,1,0:T(8,128)S(1)} %get-tuple-element.25.inverse_ref, ...), custom_call_target="tpu_custom_call" | custom-call | tf_op jit(solution)/shard_map/sweeps/pallas_call | solution.py:623
  20.9 0.3 sent_energy.1
  21.2 0.1 collective-permute-start.1
  21.3 0.9 %kept_energy.1 = (f32[3,512,128]{2,1,0:T(8,128)}, f32[8,2,16,128]{3,2,1,0:T(8,128)S(1)}) custom-call(f32[3,544,128]{2,1,0:T(8,128)S(1)} %get-tuple-element.29.disp_ref), custom_call_target="tpu_custom_call" | custom-call | flops 4177920 | bytes 1671168 | tf_op jit(solution)/shard_map/kept_energy/pallas_call | solution.py:665
  22.2 0.4 collective-permute-done.1
  22.6 10.1 %all_to_all.16 = f32[8,2,16,128]{3,2,1,0:T(8,128)S(1)} all-to-all(f32[8,2,16,128]{3,2,1,0:T(8,128)S(1)} %add.3), channel_id=1, replica_groups={{0,3,4,7,8,11,12,15},{1,2,5,6,9,10,13,14},{16,19,20,23,24,27,28,31},{17..., dimensions={0} | all-to-all | bytes 262144 | tf_op jit(solution)/shard_map/all_to_all | solution.py:717
  32.8 9.8 %all_to_all.17 = f32[8,2,16,128]{3,2,1,0:T(8,128)S(1)} all-to-all(f32[8,2,16,128]{3,2,1,0:T(8,128)S(1)} %broadcast_in_dim.5), channel_id=1, replica_groups={{0,3,4,7,8,11,12,15},{1,2,5,6,9,10,13,14},{16,19,20,23,24,27,28,31},{17..., dimensions={0} | all-to-all | bytes 262144 | tf_op jit(solution)/shard_map/all_to_all | solution.py:717
  42.6 0.6 %collective-permute-start.2 = (f32[8,2,16,128]{3,2,1,0:T(8,128)S(1)}, f32[8,2,16,128]{3,2,1,0:T(8,128)S(1)}, u32[]{:S(2)}, u32[]{:S(2)}) collective-permute-start(f32[8,2,16,128]{3,2,1,0:T(8,128)S(1)} %all_to_all.17), channel_id=1, source_target_pairs={{0,1},{1,0},{2,3},{3,2},{4,5},{5,4},{6,7},{7,6},{8,9},{9,8},{10,11... | collective-permute-start | bytes 393224 | tf_op jit(solution)/shard_map/ppermute | solution.py:708
  43.1 1.0 %collective-permute-done.2 = f32[8,2,16,128]{3,2,1,0:T(8,128)S(1)} collective-permute-done((f32[8,2,16,128]{3,2,1,0:T(8,128)S(1)}, f32[8,2,16,128]{3,2,1,0:T(8,128)S(1)}, u32[]{:S(2)}, u32[]{:S(2)}) %collective-permute-start.2) | collective-permute-done | bytes 131104 | tf_op jit(solution)/shard_map/ppermute | solution.py:708
  44.1 2.9 %design.1 = f32[2,16,128]{2,1,0:T(8,128)} custom-call(f32[10,16,128]{2,1,0:T(8,128)S(1)} %get-tuple-element.22.weight_ref, f32[2,8,2,16,128]{4,3,2,1,0:T(8,128)S(1)} %pad_maximum_fusion.1.sens_ref, f32[32,16,128]{2,1,0:T(8,128)S(1)} %get-tuple-element.32.coef_ref, f32[2,8,2,16,128]{4,3,2,1,0:T(8,128)S(1)} %pad_maximum_fusion.density_ref), custom_call_target="tpu_custom_call" | custom-call | tf_op jit(solution)/shard_map/design/pallas_call | solution.py:686
  (5 shorter events, 0.1 us)
Async XLA Ops:
  0.6 16.3 %copy-start = (f32[1,3,32,16,128]{4,3,2,1,0:T(8,128)S(1)}, f32[1,3,32,16,128]{4,3,2,1,0:T(8,128)}, u32[]{:S(2)}) copy-start(f32[1,3,32,16,128]{4,3,2,1,0:T(8,128)} %param.7) | copy-start | bytes 2359300
  14.9 2.0 %collective-permute-start = (f32[8,2,16,128]{3,2,1,0:T(8,128)S(1)}, f32[8,2,16,128]{3,2,1,0:T(8,128)S(1)}, u32[]{:S(2)}, u32[]{:S(2)}) collective-permute-start(f32[8,2,16,128]{3,2,1,0:T(8,128)S(1)} %all_to_all.15), channel_id=1, source_target_pairs={{0,1},{1,0},{2,3},{3,2},{4,5},{5,4},{6,7},{7,6},{8,9},{9,8},{10,11... | collective-permute-start | bytes 393224 | tf_op jit(solution)/shard_map/ppermute | solution.py:708
  21.2 1.4 %collective-permute-start.1 = (f32[8,2,16,128]{3,2,1,0:T(8,128)S(1)}, f32[8,2,16,128]{3,2,1,0:T(8,128)S(1)}, u32[]{:S(2)}, u32[]{:S(2)}) collective-permute-start(f32[8,2,16,128]{3,2,1,0:T(8,128)S(1)} %sent_energy.1), channel_id=1, source_target_pairs={{0,1},{1,0},{2,3},{3,2},{4,5},{5,4},{6,7},{7,6},{8,9},{9,8},{10,11... | collective-permute-start | bytes 393224 | tf_op jit(solution)/shard_map/ppermute | solution.py:708
  42.6 1.5 %collective-permute-start.2 = (f32[8,2,16,128]{3,2,1,0:T(8,128)S(1)}, f32[8,2,16,128]{3,2,1,0:T(8,128)S(1)}, u32[]{:S(2)}, u32[]{:S(2)}) collective-permute-start(f32[8,2,16,128]{3,2,1,0:T(8,128)S(1)} %all_to_all.17), channel_id=1, source_target_pairs={{0,1},{1,0},{2,3},{3,2},{4,5},{5,4},{6,7},{7,6},{8,9},{9,8},{10,11... | collective-permute-start | bytes 393224 | tf_op jit(solution)/shard_map/ppermute | solution.py:708

commit v18 on v17

--- a/solution.py
+++ b/solution.py
@@ -192,7 +192,8 @@
     hit = (z == own_z) & (y == own_y)
     for part in range(3):
         load_ref[part] = jnp.where(hit, force_ref[part, load_place], 0.0)
-    spot_ref[0] = own_index // (layers * row_width)
+    own_x = (own_index // (layers * row_width)).astype(jnp.float32)
+    spot_ref[...] = jnp.full(spot_ref.shape, own_x)
 
 
 def sweep_kernel(
@@ -342,7 +343,7 @@
         (across_ref, up_ref, right_ref, left_ref, rate_ref, first_ref),
     )
 
-    own_x = spot_ref[0]
+    own_x = jnp.max(spot_ref[...]).astype(jnp.int32)
 
     def sweep(source, target):
         def sweep_half(first, count, carry):
@@ -566,10 +567,6 @@
     return pl.BlockSpec(memory_space=pltpu.VMEM)
 
 
-def in_smem():
-    return pl.BlockSpec(memory_space=pltpu.SMEM)
-
-
 KERNEL_VMEM = 24 * 2**20
 
 
@@ -587,10 +584,10 @@
             floats(2 * window_reach + 1, layers, row_width),
             floats(planes, layers, row_width),
             floats(3, layers, row_width),
-            jax.ShapeDtypeStruct((1,), jnp.int32),
+            floats(8, row_width),
         ],
         in_specs=[pl.BlockSpec(memory_space=pltpu.HBM)] * 4,
-        out_specs=[in_vmem()] * 4 + [in_smem()],
+        out_specs=[in_vmem()] * 5,
         scratch_shapes=[
             pltpu.SMEM(radius.shape, radius.dtype),
             pltpu.SMEM(load_index.shape, load_index.dtype),
@@ -626,7 +623,7 @@
             floats(3, (planes + 2) * layers, row_width),
             floats(planes, layers, row_width),
         ],
-        in_specs=[in_smem()] + [in_vmem()] * 6,
+        in_specs=[in_vmem()] * 7,
         out_specs=[in_vmem()] * 2,
         scratch_shapes=[
             scratch(planes * (layers + GAP) + GAP),

time: 47.5 us -> 46.1 us (0.971)
  Pallas kernels: 9.36 us -> 8.25 us
  blocking collectives: 33.4 us -> 32.8 us
    pallas_call x1, Pallas kernels: 3.92 us -> 3.28 us  [sweep_call(): pl.pallas_call(sweep_kernel, out_shape=[floats(3, (planes + 2) * layers,...]
    all_to_all x3, blocking collectives: 33.4 us -> 32.8 us  [between_chips(): lax.all_to_all(pieces, 'space', 0, 0, axis_index_groups=chip_groups())]
  transfers between devices with their start and end apart: 3 -> 3, of which waited for: 2 -> 3; matrix products, arithmetic and copies ran while one was open for 0% -> 0% of each run, Pallas kernels for 5% -> 4%
where the time goes in v18:
time: 46.1 us; the launch traced here: 45.6 us
  blocking collectives  32.8 us (71%)
  Pallas kernels  8.25 us (18%)
  starting transfers between devices  1.78 us (4%)
  waiting for transfers between devices  1.19 us (3%)
  local copies, waits for them, and re-layouts  0.82 us (2%)
  between operations  0.7 us (2%)
    all_to_all x3, blocking collectives, between_chips(): lax.all_to_all(pieces, 'space', 0, 0, axis_index_groups=chip_groups())  32.8 us
    pallas_call x1, Pallas kernels, sweep_call(): pl.pallas_call(sweep_kernel, out_shape=[floats(3, (planes + 2) * layers,...  3.28 us
    pallas_call x1, Pallas kernels, design_call(): pl.pallas_call(design_kernel, out_shape=floats(own_planes, layers, row_wi...  2.91 us
    ppermute x3, starting transfers between devices, other_core(): return lax.ppermute(block, 'space', [(i, i ^ 1) for i in range(devices)])  1.78 us
    ppermute x3, waiting for transfers between devices, other_core(): return lax.ppermute(block, 'space', [(i, i ^ 1) for i in range(devices)])  1.19 us
  transfers between devices with their start and end apart: 3, of which 3 were waited for; matrix products, arithmetic and copies ran while one was open for 0% of the time, Pallas kernels for 4%

profile of v18, /device:TPU:0, one launch (start us, length us, event | category | flops | bytes accessed | tf_op | source)
XLA Modules:
  0.0 45.6 jit_solution(2085069543624088034)
XLA Ops:
  0.6 0.0 copy-start
  0.6 0.8 %broadcast_in_dim.4 = f32[8,2,16,128]{3,2,1,0:T(8,128)S(1)} broadcast(f32[2,16,128]{2,1,0:T(8,128)} %param.6), dimensions={1,2,3} | broadcast | bytes 147456 | tf_op jit(solution)/shard_map/broadcast_in_dim | solution.py:719
  1.4 13.5 %all_to_all.15 = f32[8,2,16,128]{3,2,1,0:T(8,128)S(1)} all-to-all(f32[8,2,16,128]{3,2,1,0:T(8,128)S(1)} %broadcast_in_dim.4), channel_id=1, replica_groups={{0,3,4,7,8,11,12,15},{1,2,5,6,9,10,13,14},{16,19,20,23,24,27,28,31},{17..., dimensions={0} | all-to-all | bytes 262144 | tf_op jit(solution)/shard_map/all_to_all | solution.py:714
  14.9 0.7 %collective-permute-start = (f32[8,2,16,128]{3,2,1,0:T(8,128)S(1)}, f32[8,2,16,128]{3,2,1,0:T(8,128)S(1)}, u32[]{:S(2)}, u32[]{:S(2)}) collective-permute-start(f32[8,2,16,128]{3,2,1,0:T(8,128)S(1)} %all_to_all.15), channel_id=1, source_target_pairs={{0,1},{1,0},{2,3},{3,2},{4,5},{5,4},{6,7},{7,6},{8,9},{9,8},{10,11... | collective-permute-start | bytes 393224 | tf_op jit(solution)/shard_map/ppermute | solution.py:705
  15.6 0.9 %prepare.1 = (f32[10,16,128]{2,1,0:T(8,128)S(1)}, f32[5,16,128]{2,1,0:T(8,128)S(1)}, f32[32,16,128]{2,1,0:T(8,128)S(1)}, f32[3,16,128]{2,1,0:T(8,128)S(1)}, f32[8,128]{1,0:T(8,128)S(1)}) custom-call(s32[16]{0:T(128)} %radius_hbm, s32[16]{0:T(128)} %index_hbm, f32[3,16]{1,0:T(4,128)} %bitcast.12, s32[32,128]{1,0:T(8,128)} %fixed_hbm), custom_call_target="tpu_custom_call" | custom-call | flops 2621440 | bytes 524288 | tf_op jit(solution)/shard_map/prepare/pallas_call | solution.py:580
  16.4 0.1 collective-permute-done
  16.6 0.0 copy-done
  16.6 3.3 %sweeps.1 = (f32[3,544,128]{2,1,0:T(8,128)S(1)}, f32[32,16,128]{2,1,0:T(8,128)S(1)}) custom-call(f32[8,128]{1,0:T(8,128)S(1)} %get-tuple-element.23.spot_ref, f32[3,16,128]{2,1,0:T(8,128)S(1)} %get-tuple-element.24.load_ref, f32[10,16,128]{2,1,0:T(8,128)S(1)} %get-tuple-element.22.weight_ref, f32[5,16,128]{2,1,0:T(8,128)S(1)} %get-tuple-element.25.inverse_ref, ...), custom_call_target="tpu_custom_call" | custom-call | tf_op jit(solution)/shard_map/sweeps/pallas_call | solution.py:620
  19.9 0.3 sent_energy.1
  20.2 0.4 collective-permute-start.1
  20.6 0.9 %kept_energy.1 = (f32[3,512,128]{2,1,0:T(8,128)}, f32[8,2,16,128]{3,2,1,0:T(8,128)S(1)}) custom-call(f32[3,544,128]{2,1,0:T(8,128)S(1)} %get-tuple-element.29.disp_ref), custom_call_target="tpu_custom_call" | custom-call | flops 4177920 | bytes 1671168 | tf_op jit(solution)/shard_map/kept_energy/pallas_call | solution.py:662
  21.5 0.1 collective-permute-done.1
  21.6 10.0 %all_to_all.16 = f32[8,2,16,128]{3,2,1,0:T(8,128)S(1)} all-to-all(f32[8,2,16,128]{3,2,1,0:T(8,128)S(1)} %add.3), channel_id=1, replica_groups={{0,3,4,7,8,11,12,15},{1,2,5,6,9,10,13,14},{16,19,20,23,24,27,28,31},{17..., dimensions={0} | all-to-all | bytes 262144 | tf_op jit(solution)/shard_map/all_to_all | solution.py:714
  31.7 9.4 %all_to_all.17 = f32[8,2,16,128]{3,2,1,0:T(8,128)S(1)} all-to-all(f32[8,2,16,128]{3,2,1,0:T(8,128)S(1)} %broadcast_in_dim.5), channel_id=1, replica_groups={{0,3,4,7,8,11,12,15},{1,2,5,6,9,10,13,14},{16,19,20,23,24,27,28,31},{17..., dimensions={0} | all-to-all | bytes 262144 | tf_op jit(solution)/shard_map/all_to_all | solution.py:714
  41.0 0.7 %collective-permute-start.2 = (f32[8,2,16,128]{3,2,1,0:T(8,128)S(1)}, f32[8,2,16,128]{3,2,1,0:T(8,128)S(1)}, u32[]{:S(2)}, u32[]{:S(2)}) collective-permute-start(f32[8,2,16,128]{3,2,1,0:T(8,128)S(1)} %all_to_all.17), channel_id=1, source_target_pairs={{0,1},{1,0},{2,3},{3,2},{4,5},{5,4},{6,7},{7,6},{8,9},{9,8},{10,11... | collective-permute-start | bytes 393224 | tf_op jit(solution)/shard_map/ppermute | solution.py:705
  41.7 1.0 %collective-permute-done.2 = f32[8,2,16,128]{3,2,1,0:T(8,128)S(1)} collective-permute-done((f32[8,2,16,128]{3,2,1,0:T(8,128)S(1)}, f32[8,2,16,128]{3,2,1,0:T(8,128)S(1)}, u32[]{:S(2)}, u32[]{:S(2)}) %collective-permute-start.2) | collective-permute-done | bytes 131104 | tf_op jit(solution)/shard_map/ppermute | solution.py:705
  42.7 2.9 %design.1 = f32[2,16,128]{2,1,0:T(8,128)} custom-call(f32[10,16,128]{2,1,0:T(8,128)S(1)} %get-tuple-element.22.weight_ref, f32[2,8,2,16,128]{4,3,2,1,0:T(8,128)S(1)} %pad_maximum_fusion.1.sens_ref, f32[32,16,128]{2,1,0:T(8,128)S(1)} %get-tuple-element.32.coef_ref, f32[2,8,2,16,128]{4,3,2,1,0:T(8,128)S(1)} %pad_maximum_fusion.density_ref), custom_call_target="tpu_custom_call" | custom-call | tf_op jit(solution)/shard_map/design/pallas_call | solution.py:683
  (5 shorter events, 0.1 us)
Async XLA Ops:
  0.6 16.0 %copy-start = (f32[1,3,32,16,128]{4,3,2,1,0:T(8,128)S(1)}, f32[1,3,32,16,128]{4,3,2,1,0:T(8,128)}, u32[]{:S(2)}) copy-start(f32[1,3,32,16,128]{4,3,2,1,0:T(8,128)} %param.7) | copy-start | bytes 2359300
  14.9 1.7 %collective-permute-start = (f32[8,2,16,128]{3,2,1,0:T(8,128)S(1)}, f32[8,2,16,128]{3,2,1,0:T(8,128)S(1)}, u32[]{:S(2)}, u32[]{:S(2)}) collective-permute-start(f32[8,2,16,128]{3,2,1,0:T(8,128)S(1)} %all_to_all.15), channel_id=1, source_target_pairs={{0,1},{1,0},{2,3},{3,2},{4,5},{5,4},{6,7},{7,6},{8,9},{9,8},{10,11... | collective-permute-start | bytes 393224 | tf_op jit(solution)/shard_map/ppermute | solution.py:705
  20.2 1.4 %collective-permute-start.1 = (f32[8,2,16,128]{3,2,1,0:T(8,128)S(1)}, f32[8,2,16,128]{3,2,1,0:T(8,128)S(1)}, u32[]{:S(2)}, u32[]{:S(2)}) collective-permute-start(f32[8,2,16,128]{3,2,1,0:T(8,128)S(1)} %sent_energy.1), channel_id=1, source_target_pairs={{0,1},{1,0},{2,3},{3,2},{4,5},{5,4},{6,7},{7,6},{8,9},{9,8},{10,11... | collective-permute-start | bytes 393224 | tf_op jit(solution)/shard_map/ppermute | solution.py:705
  41.0 1.7 %collective-permute-start.2 = (f32[8,2,16,128]{3,2,1,0:T(8,128)S(1)}, f32[8,2,16,128]{3,2,1,0:T(8,128)S(1)}, u32[]{:S(2)}, u32[]{:S(2)}) collective-permute-start(f32[8,2,16,128]{3,2,1,0:T(8,128)S(1)} %all_to_all.17), channel_id=1, source_target_pairs={{0,1},{1,0},{2,3},{3,2},{4,5},{5,4},{6,7},{7,6},{8,9},{9,8},{10,11... | collective-permute-start | bytes 393224 | tf_op jit(solution)/shard_map/ppermute | solution.py:705

commit v19 on v18

--- a/solution.py
+++ b/solution.py
@@ -133,20 +133,64 @@
         ref[place] = jnp.zeros(ref.shape[1:], ref.dtype)
 
 
+def group_spots(group, blocks):
+    chips, own_planes = blocks.shape[:2]
+    mine = lax.axis_index("space")
+    core = mine ^ mine >> 1 ^ group
+    return [
+        (own_planes * (2 * chip + ((core ^ chip) & 1)) + own, (chip, own))
+        for chip in range(chips)
+        for own in range(own_planes)
+    ]
+
+
+def spread_group(blocks, spread):
+    chips, own_planes, layers, row_width = blocks.shape
+    zero_gap = jnp.zeros((GAP, row_width), jnp.float32)
+    for ref in spread:
+        ref[gap(0, layers)] = zero_gap
+    for p in range(chips * own_planes):
+        plane = blocks[p // own_planes, p % own_planes]
+        for ref, field in zip(spread, (plane, shift_sum(plane, 1, 1), shift_sum(plane, 1, 2))):
+            ref[gapped(p, layers)] = field
+            ref[gap(p + 1, layers)] = zero_gap
+
+
+def filter_plane(p, layers, spread, weight_ref):
+    def around(place, distance):
+        ref = spread[place]
+        return ref[gapped(p, layers, distance)] + ref[gapped(p, layers, -distance)]
+
+    sums = {
+        0: spread[0][gapped(p, layers)],
+        1: spread[1][gapped(p, layers)] + around(0, 1),
+        2: around(1, 1),
+        4: spread[2][gapped(p, layers)] + around(0, 2),
+        5: around(2, 1) + around(1, 2),
+        8: around(2, 2),
+    }
+    return [weigh(sums, weight_ref, square) for square in (0, 1, 4)]
+
+
 def prepare_kernel(
     radius_hbm,
     index_hbm,
     force_hbm,
     fixed_hbm,
+    density_ref,
     weight_ref,
     inverse_ref,
     free_ref,
     load_ref,
     spot_ref,
+    filter_ref,
     radius_ref,
     index_ref,
     force_ref,
     fixed_ref,
+    plane_ref,
+    beside_ref,
+    further_ref,
     arrived,
 ):
     copies = [
@@ -162,6 +206,8 @@
     ]
     for copy in copies:
         copy.start()
+    spread = (plane_ref, beside_ref, further_ref)
+    spread_group(density_ref, spread)
     for copy in copies:
         copy.wait()
     planes, layers, row_width = free_ref.shape
@@ -171,6 +217,11 @@
     y = spot_iota(shape, 1)
 
     class_weights(radius_ref, weight_ref)
+    own_planes = density_ref.shape[1]
+    for p in range(density_ref.shape[0] * own_planes):
+        for place, field in enumerate(filter_plane(p, layers, spread, weight_ref)):
+            filter_ref[place, p // own_planes, p % own_planes] = field
+
     ones = forward_planes(jnp.ones(shape, jnp.float32), weight_ref)
     for place, (lower, upper) in enumerate(((0, 2), (1, 2), (2, 2), (2, 1), (2, 0))):
         inverse_ref[place] = 1.0 / (
@@ -202,6 +253,7 @@
     weight_ref,
     inverse_ref,
     free_ref,
+    filter_ref,
     density_ref,
     start_ref,
     disp_ref,
@@ -225,44 +277,18 @@
     z = spot_iota(shape, 0)
     y = spot_iota(shape, 1)
     zero = jnp.zeros(shape, jnp.float32)
-    zero_gap = jnp.zeros((GAP, row_width), jnp.float32)
 
     for ref in (side_ref, far_ref):
         zero_edges(ref)
-    def filter_half(first, count, carry):
-        density = half_views(density_ref, first, count)
-        spread = [
-            ref.at[pl.ds(first * (layers + GAP), count * (layers + GAP) + GAP)]
-            for ref in (plane_ref, beside_ref, further_ref)
-        ]
-        results = [ref.at[pl.ds(first + 2, count)] for ref in (near_ref, side_ref, far_ref)]
-        for ref in spread:
-            ref[gap(0, layers)] = zero_gap
-        for p in range(count):
-            view, spot = density(p)
-            plane = view[spot]
-            beside, further = shift_sum(plane, 1, 1), shift_sum(plane, 1, 2)
-            for ref, field in zip(spread, (plane, beside, further)):
-                ref[gapped(p, layers)] = field
-                ref[gap(p + 1, layers)] = zero_gap
-
-            def around(place, distance):
-                ref = spread[place]
-                return ref[gapped(p, layers, distance)] + ref[gapped(p, layers, -distance)]
-
-            sums = {
-                0: plane,
-                1: beside + around(0, 1),
-                2: around(1, 1),
-                4: further + around(0, 2),
-                5: around(2, 1) + around(1, 2),
-                8: around(2, 2),
-            }
-            for ref, square in zip(results, (0, 1, 4)):
-                ref[p] = weigh(sums, weight_ref, square)
-        return carry
-
-    each_half(planes, filter_half, 0)
+    results = (near_ref, side_ref, far_ref)
+    for x, spot in group_spots(0, density_ref):
+        for place, ref in enumerate(results):
+            ref[x + 2] = filter_ref[(place,) + spot]
+    spread = (plane_ref, beside_ref, further_ref)
+    spread_group(density_ref, spread)
+    for p, (x, spot) in enumerate(group_spots(1, density_ref)):
+        for ref, field in zip(results, filter_plane(p, layers, spread, weight_ref)):
+            ref[x + 2] = field
 
     for ref in (first_ref, disp_ref):
         for part in range(3):
@@ -574,9 +600,10 @@
     return jax.ShapeDtypeStruct(shape, jnp.float32)
 
 
-def prepare_call(radius, load_index, load_force, fixed):
-    planes, row_width = fixed.shape
-    layers = radius.shape[0]
+def prepare_call(density, radius, load_index, load_force, fixed):
+    chips, own_planes, layers, row_width = density.shape
+    planes = fixed.shape[0]
+    spread = pltpu.VMEM((chips * own_planes * (layers + GAP) + GAP, row_width), jnp.float32)
     return pl.pallas_call(
         prepare_kernel,
         out_shape=[
@@ -585,19 +612,23 @@
             floats(planes, layers, row_width),
             floats(3, layers, row_width),
             floats(8, row_width),
+            floats(3, *density.shape),
         ],
-        in_specs=[pl.BlockSpec(memory_space=pltpu.HBM)] * 4,
-        out_specs=[in_vmem()] * 5,
+        in_specs=[pl.BlockSpec(memory_space=pltpu.HBM)] * 4 + [in_vmem()],
+        out_specs=[in_vmem()] * 6,
         scratch_shapes=[
             pltpu.SMEM(radius.shape, radius.dtype),
             pltpu.SMEM(load_index.shape, load_index.dtype),
             pltpu.SMEM(load_force.shape, load_force.dtype),
             pltpu.VMEM(fixed.shape, fixed.dtype),
+            spread,
+            spread,
+            spread,
             pltpu.SemaphoreType.DMA((4,)),
         ],
         compiler_params=pltpu.CompilerParams(vmem_limit_bytes=KERNEL_VMEM),
         cost_estimate=pl.CostEstimate(
-            flops=40 * planes * layers * row_width,
+            flops=80 * planes * layers * row_width,
             bytes_accessed=8 * planes * layers * row_width,
             transcendentals=0,
         ),
@@ -606,13 +637,14 @@
         *(
             pltpu.with_memory_space_constraint(array, pltpu.HBM)
             for array in (radius, load_index, load_force, fixed)
-        )
-    )
-
-
-def sweep_call(spot, load, weights, inverses, free, density, displacement):
-    cores, chips, own_planes, layers, row_width = density.shape
-    planes = cores * chips * own_planes
+        ),
+        density,
+    )
+
+
+def sweep_call(spot, load, weights, inverses, free, filtered, density, displacement):
+    chips, own_planes, layers, row_width = density.shape
+    planes = 2 * chips * own_planes
 
     def scratch(*lead):
         return pltpu.VMEM(lead + (row_width,), jnp.float32)
@@ -623,12 +655,12 @@
             floats(3, (planes + 2) * layers, row_width),
             floats(planes, layers, row_width),
         ],
-        in_specs=[in_vmem()] * 7,
+        in_specs=[in_vmem()] * 8,
         out_specs=[in_vmem()] * 2,
         scratch_shapes=[
-            scratch(planes * (layers + GAP) + GAP),
-            scratch(planes * (layers + GAP) + GAP),
-            scratch(planes * (layers + GAP) + GAP),
+            scratch(planes // 2 * (layers + GAP) + GAP),
+            scratch(planes // 2 * (layers + GAP) + GAP),
+            scratch(planes // 2 * (layers + GAP) + GAP),
             scratch(planes + 4, layers),
             scratch(planes + 4, layers),
             scratch(planes + 4, layers),
@@ -642,7 +674,7 @@
         ],
         compiler_params=pltpu.CompilerParams(vmem_limit_bytes=KERNEL_VMEM),
         name="sweeps",
-    )(spot, load, weights, inverses, free, density, displacement)
+    )(spot, load, weights, inverses, free, filtered, density, displacement)
 
 
 def sent_energy_call(disp, group_shape):
@@ -733,9 +765,12 @@
     same_group, small = lax.optimization_barrier(
         (chip_gathered(density), (radius, load_index, load_force.T, fixed))
     )
-    whole = with_other_core(same_group)
-    weights, inverses, free, load, spot = prepare_call(*small)
-    disp, coef = sweep_call(spot, load, weights, inverses, free, whole, displacement[0])
+    other_group = other_core(same_group)
+    weights, inverses, free, load, spot, filtered = prepare_call(same_group, *small)
+    disp, coef = sweep_call(
+        spot, load, weights, inverses, free, filtered, other_group, displacement[0]
+    )
+    whole = jnp.stack([same_group, other_group])
     sent, disp = lax.optimization_barrier((sent_energy_call(disp, same_group.shape), disp))
     sens, (new_displacement,) = scattered_sum(
         sent, lambda: kept_energy_call(disp, same_group.shape)

time: 46.1 us -> 47 us (1.020)
  local copies, waits for them, and re-layouts: 0.82 us -> 1.87 us
    unnamed x2, local copies, waits for them, and re-layouts: 0.01 us -> 1.13 us
  transfers between devices with their start and end apart: 3 -> 3, of which waited for: 3 -> 2; matrix products, arithmetic and copies ran while one was open for 0% -> 0% of each run, Pallas kernels for 4% -> 4%
where the time goes in v19:
time: 47 us; the launch traced here: 46.6 us
  blocking collectives  33.1 us (70%)
  Pallas kernels  7.97 us (17%)
  local copies, waits for them, and re-layouts  1.87 us (4%)
  starting transfers between devices  1.76 us (4%)
  waiting for transfers between devices  1.08 us (2%)
  between operations  0.7 us (1%)
    all_to_all x3, blocking collectives, between_chips(): lax.all_to_all(pieces, 'space', 0, 0, axis_index_groups=chip_groups())  33.1 us
    pallas_call x1, Pallas kernels, design_call(): pl.pallas_call(design_kernel, out_shape=floats(own_planes, layers, row_wi...  2.91 us
    pallas_call x1, Pallas kernels, sweep_call(): pl.pallas_call(sweep_kernel, out_shape=[floats(3, (planes + 2) * layers,...  2.86 us
    ppermute x3, starting transfers between devices, other_core(): return lax.ppermute(block, 'space', [(i, i ^ 1) for i in range(devices)])  1.76 us
    unnamed x2, local copies, waits for them, and re-layouts  1.13 us
    ppermute x3, waiting for transfers between devices, other_core(): return lax.ppermute(block, 'space', [(i, i ^ 1) for i in range(devices)])  1.08 us
    pallas_call x1, Pallas kernels, prepare_call(): pl.pallas_call(prepare_kernel, out_shape=[floats(len(ALL_SQUARES), layers...  1 us
  transfers between devices with their start and end apart: 3, of which 2 were waited for; matrix products, arithmetic and copies ran while one was open for 0% of the time, Pallas kernels for 4%

profile of v19, /device:TPU:0, one launch (start us, length us, event | category | flops | bytes accessed | tf_op | source)
XLA Modules:
  0.0 46.6 jit_solution(9677066459954504461)
XLA Ops:
  0.6 0.7 %broadcast_in_dim.4 = f32[8,2,16,128]{3,2,1,0:T(8,128)S(1)} broadcast(f32[2,16,128]{2,1,0:T(8,128)} %param.6), dimensions={1,2,3} | broadcast | bytes 147456 | tf_op jit(solution)/shard_map/broadcast_in_dim | solution.py:751
  1.4 13.5 %all_to_all.15.density_ref = f32[8,2,16,128]{3,2,1,0:T(8,128)S(1)} all-to-all(f32[8,2,16,128]{3,2,1,0:T(8,128)S(1)} %broadcast_in_dim.4), channel_id=1, replica_groups={{0,3,4,7,8,11,12,15},{1,2,5,6,9,10,13,14},{16,19,20,23,24,27,28,31},{17..., dimensions={0} | all-to-all | bytes 262144 | tf_op jit(solution)/shard_map/all_to_all | solution.py:746
  14.8 0.7 %collective-permute-start = (f32[8,2,16,128]{3,2,1,0:T(8,128)S(1)}, f32[8,2,16,128]{3,2,1,0:T(8,128)S(1)}, u32[]{:S(2)}, u32[]{:S(2)}) collective-permute-start(f32[8,2,16,128]{3,2,1,0:T(8,128)S(1)} %all_to_all.15.density_ref), channel_id=1, source_target_pairs={{0,1},{1,0},{2,3},{3,2},{4,5},{5,4},{6,7},{7,6},{8,9},{9,8},{10,11... | collective-permute-start | bytes 393224 | tf_op jit(solution)/shard_map/ppermute | solution.py:737
  15.5 1.0 %prepare.1 = (f32[10,16,128]{2,1,0:T(8,128)S(1)}, f32[5,16,128]{2,1,0:T(8,128)S(1)}, f32[32,16,128]{2,1,0:T(8,128)S(1)}, f32[3,16,128]{2,1,0:T(8,128)S(1)}, f32[...) custom-call(s32[16]{0:T(128)} %radius_hbm, s32[16]{0:T(128)} %index_hbm, f32[3,16]{1,0:T(4,128)} %bitcast.12, ...), custom_call_target="tpu_custom_call" | custom-call | flops 5242880 | bytes 524288 | tf_op jit(solution)/shard_map/prepare/pallas_call | solution.py:607
  16.5 0.0 collective-permute-done.density_ref
  16.5 0.0 copy-start
  16.5 1.1 %copy-done = f32[1,3,32,16,128]{4,3,2,1,0:T(8,128)S(1)} copy-done((f32[1,3,32,16,128]{4,3,2,1,0:T(8,128)S(1)}, f32[1,3,32,16,128]{4,3,2,1,0:T(8,128)}, u32[]{:S(2)}) %copy-start) | copy-done | bytes 786456
  17.6 2.9 %sweeps.1 = (f32[3,544,128]{2,1,0:T(8,128)S(1)}, f32[32,16,128]{2,1,0:T(8,128)S(1)}) custom-call(f32[8,128]{1,0:T(8,128)S(1)} %get-tuple-element.25.spot_ref, f32[3,16,128]{2,1,0:T(8,128)S(1)} %get-tuple-element.26.load_ref, f32[10,16,128]{2,1,0:T(8,128)S(1)} %get-tuple-element.24.weight_ref, f32[5,16,128]{2,1,0:T(8,128)S(1)} %get-tuple-element.27.inverse_ref, ...), custom_call_target="tpu_custom_call" | custom-call | tf_op jit(solution)/shard_map/sweeps/pallas_call | solution.py:652
  20.5 0.3 sent_energy.1
  20.8 0.4 collective-permute-start.1
  21.2 0.9 %kept_energy.1 = (f32[3,512,128]{2,1,0:T(8,128)}, f32[8,2,16,128]{3,2,1,0:T(8,128)S(1)}) custom-call(f32[3,544,128]{2,1,0:T(8,128)S(1)} %get-tuple-element.31.disp_ref), custom_call_target="tpu_custom_call" | custom-call | flops 4177920 | bytes 1671168 | tf_op jit(solution)/shard_map/kept_energy/pallas_call | solution.py:694
  22.1 0.1 collective-permute-done.1
  22.3 10.0 %all_to_all.16 = f32[8,2,16,128]{3,2,1,0:T(8,128)S(1)} all-to-all(f32[8,2,16,128]{3,2,1,0:T(8,128)S(1)} %add.3), channel_id=1, replica_groups={{0,3,4,7,8,11,12,15},{1,2,5,6,9,10,13,14},{16,19,20,23,24,27,28,31},{17..., dimensions={0} | all-to-all | bytes 262144 | tf_op jit(solution)/shard_map/all_to_all | solution.py:746
  32.3 9.6 %all_to_all.17 = f32[8,2,16,128]{3,2,1,0:T(8,128)S(1)} all-to-all(f32[8,2,16,128]{3,2,1,0:T(8,128)S(1)} %broadcast_in_dim.5), channel_id=1, replica_groups={{0,3,4,7,8,11,12,15},{1,2,5,6,9,10,13,14},{16,19,20,23,24,27,28,31},{17..., dimensions={0} | all-to-all | bytes 262144 | tf_op jit(solution)/shard_map/all_to_all | solution.py:746
  42.0 0.7 %collective-permute-start.2 = (f32[8,2,16,128]{3,2,1,0:T(8,128)S(1)}, f32[8,2,16,128]{3,2,1,0:T(8,128)S(1)}, u32[]{:S(2)}, u32[]{:S(2)}) collective-permute-start(f32[8,2,16,128]{3,2,1,0:T(8,128)S(1)} %all_to_all.17), channel_id=1, source_target_pairs={{0,1},{1,0},{2,3},{3,2},{4,5},{5,4},{6,7},{7,6},{8,9},{9,8},{10,11... | collective-permute-start | bytes 393224 | tf_op jit(solution)/shard_map/ppermute | solution.py:737
  42.7 1.0 %collective-permute-done.2 = f32[8,2,16,128]{3,2,1,0:T(8,128)S(1)} collective-permute-done((f32[8,2,16,128]{3,2,1,0:T(8,128)S(1)}, f32[8,2,16,128]{3,2,1,0:T(8,128)S(1)}, u32[]{:S(2)}, u32[]{:S(2)}) %collective-permute-start.2) | collective-permute-done | bytes 131104 | tf_op jit(solution)/shard_map/ppermute | solution.py:737
  43.7 2.9 %design.1 = f32[2,16,128]{2,1,0:T(8,128)} custom-call(f32[10,16,128]{2,1,0:T(8,128)S(1)} %get-tuple-element.24.weight_ref, f32[2,8,2,16,128]{4,3,2,1,0:T(8,128)S(1)} %pad_maximum_fusion.sens_ref, f32[32,16,128]{2,1,0:T(8,128)S(1)} %get-tuple-element.34.coef_ref, f32[2,8,2,16,128]{4,3,2,1,0:T(8,128)S(1)} %pad_maximum_fusion.1.density_ref), custom_call_target="tpu_custom_call" | custom-call | tf_op jit(solution)/shard_map/design/pallas_call | solution.py:715
  (5 shorter events, 0.1 us)
Async XLA Ops:
  14.8 1.7 %collective-permute-start = (f32[8,2,16,128]{3,2,1,0:T(8,128)S(1)}, f32[8,2,16,128]{3,2,1,0:T(8,128)S(1)}, u32[]{:S(2)}, u32[]{:S(2)}) collective-permute-start(f32[8,2,16,128]{3,2,1,0:T(8,128)S(1)} %all_to_all.15.density_ref), channel_id=1, source_target_pairs={{0,1},{1,0},{2,3},{3,2},{4,5},{5,4},{6,7},{7,6},{8,9},{9,8},{10,11... | collective-permute-start | bytes 393224 | tf_op jit(solution)/shard_map/ppermute | solution.py:737
  16.5 1.1 %copy-start = (f32[1,3,32,16,128]{4,3,2,1,0:T(8,128)S(1)}, f32[1,3,32,16,128]{4,3,2,1,0:T(8,128)}, u32[]{:S(2)}) copy-start(f32[1,3,32,16,128]{4,3,2,1,0:T(8,128)} %param.7) | copy-start | bytes 2359300
  20.8 1.4 %collective-permute-start.1 = (f32[8,2,16,128]{3,2,1,0:T(8,128)S(1)}, f32[8,2,16,128]{3,2,1,0:T(8,128)S(1)}, u32[]{:S(2)}, u32[]{:S(2)}) collective-permute-start(f32[8,2,16,128]{3,2,1,0:T(8,128)S(1)} %sent_energy.1), channel_id=1, source_target_pairs={{0,1},{1,0},{2,3},{3,2},{4,5},{5,4},{6,7},{7,6},{8,9},{9,8},{10,11... | collective-permute-start | bytes 393224 | tf_op jit(solution)/shard_map/ppermute | solution.py:737
  42.0 1.7 %collective-permute-start.2 = (f32[8,2,16,128]{3,2,1,0:T(8,128)S(1)}, f32[8,2,16,128]{3,2,1,0:T(8,128)S(1)}, u32[]{:S(2)}, u32[]{:S(2)}) collective-permute-start(f32[8,2,16,128]{3,2,1,0:T(8,128)S(1)} %all_to_all.17), channel_id=1, source_target_pairs={{0,1},{1,0},{2,3},{3,2},{4,5},{5,4},{6,7},{7,6},{8,9},{9,8},{10,11... | collective-permute-start | bytes 393224 | tf_op jit(solution)/shard_map/ppermute | solution.py:737

commit v20 on v19

--- a/solution.py
+++ b/solution.py
@@ -255,7 +255,7 @@
     free_ref,
     filter_ref,
     density_ref,
-    start_ref,
+    start_hbm,
     disp_ref,
     coef_ref,
     plane_ref,
@@ -271,8 +271,13 @@
     left_ref,
     rate_ref,
     first_ref,
+    arrived,
 ):
     planes, layers, row_width = coef_ref.shape
+    fetch = pltpu.make_async_copy(
+        start_hbm, first_ref.at[:, pl.ds(layers, planes * layers)], arrived
+    )
+    fetch.start()
     shape = (layers, row_width)
     z = spot_iota(shape, 0)
     y = spot_iota(shape, 1)
@@ -295,8 +300,8 @@
             ref[part, rows(0, layers)] = zero
             ref[part, rows(planes + 1, layers)] = zero
 
-    def store_faces(slot, modulus, above, later, before, free, start, views):
-        across, up_view, right_view, left_view, rate, source = views
+    def store_faces(slot, modulus, above, later, before, free, views):
+        across, up_view, right_view, left_view, rate = views
         across[slot] = later
         up = jnp.where(z < layers - 1, 0.5 * (modulus + above), 0.0)
         right = jnp.where(
@@ -314,7 +319,6 @@
         side = push * diagonal[2]
         for part, factor in enumerate((side * diagonal[1], side * diagonal[0], push * pair)):
             rate[part, slot] = factor
-            source[part, rows(slot, layers)] = start[part] * free
 
     def modulus_half(first, count, carry):
         near = near_ref.at[pl.ds(first + 2, count)]
@@ -329,7 +333,6 @@
             right_ref.at[pl.ds(first, count)],
             left_ref.at[pl.ds(first, count)],
             rate_ref.at[:, pl.ds(first, count)],
-            first_ref.at[:, pl.ds(first * layers, count * layers)],
         )
         modulus, before = carry
         for p in range(count):
@@ -351,7 +354,6 @@
                 ahead,
                 before,
                 free_ref[previous],
-                [start_ref[part, previous] for part in range(3)],
                 views,
             )
             modulus, before = later, ahead
@@ -365,9 +367,15 @@
         zero,
         before,
         free_ref[planes - 1],
-        [start_ref[part, planes - 1] for part in range(3)],
-        (across_ref, up_ref, right_ref, left_ref, rate_ref, first_ref),
-    )
+        (across_ref, up_ref, right_ref, left_ref, rate_ref),
+    )
+
+    fetch.wait()
+    bottom = min(layers, 8)
+    for x in range(planes):
+        free = free_ref[x, pl.ds(0, bottom)]
+        for part in range(3):
+            first_ref[part, pl.ds((x + 1) * layers, bottom)] *= free
 
     own_x = jnp.max(spot_ref[...]).astype(jnp.int32)
 
@@ -655,7 +663,7 @@
             floats(3, (planes + 2) * layers, row_width),
             floats(planes, layers, row_width),
         ],
-        in_specs=[in_vmem()] * 8,
+        in_specs=[in_vmem()] * 7 + [pl.BlockSpec(memory_space=pltpu.HBM)],
         out_specs=[in_vmem()] * 2,
         scratch_shapes=[
             scratch(planes // 2 * (layers + GAP) + GAP),
@@ -671,10 +679,20 @@
             scratch(planes + 1, layers),
             scratch(3, planes + 1, layers),
             scratch(3, (planes + 2) * layers),
+            pltpu.SemaphoreType.DMA(()),
         ],
         compiler_params=pltpu.CompilerParams(vmem_limit_bytes=KERNEL_VMEM),
         name="sweeps",
-    )(spot, load, weights, inverses, free, filtered, density, displacement)
+    )(
+        spot,
+        load,
+        weights,
+        inverses,
+        free,
+        filtered,
+        density,
+        pltpu.with_memory_space_constraint(displacement, pltpu.HBM),
+    )
 
 
 def sent_energy_call(disp, group_shape):
@@ -767,8 +785,9 @@
     )
     other_group = other_core(same_group)
     weights, inverses, free, load, spot, filtered = prepare_call(same_group, *small)
+    start = displacement.reshape(3, -1, displacement.shape[-1])
     disp, coef = sweep_call(
-        spot, load, weights, inverses, free, filtered, other_group, displacement[0]
+        spot, load, weights, inverses, free, filtered, other_group, start
     )
     whole = jnp.stack([same_group, other_group])
     sent, disp = lax.optimization_barrier((sent_energy_call(disp, same_group.shape), disp))

time: 47 us -> 46.4 us (0.987)
  local copies, waits for them, and re-layouts: 1.87 us -> 0.74 us
  Pallas kernels: 7.97 us -> 8.54 us
    unnamed x2 -> x0, local copies, waits for them, and re-layouts: 1.13 us -> none
    pallas_call x1, Pallas kernels: 2.86 us -> 3.42 us  [sweep_call(): pl.pallas_call(sweep_kernel, out_shape=[floats(3, (planes + 2) * layers,...]
where the time goes in v20:
time: 46.4 us; the launch traced here: 46 us
  blocking collectives  33.1 us (71%)
  Pallas kernels  8.54 us (18%)
  starting transfers between devices  1.77 us (4%)
  waiting for transfers between devices  1.07 us (2%)
  local copies, waits for them, and re-layouts  0.74 us (2%)
  between operations  0.69 us (1%)
    all_to_all x3, blocking collectives, between_chips(): lax.all_to_all(pieces, 'space', 0, 0, axis_index_groups=chip_groups())  33.1 us
    pallas_call x1, Pallas kernels, sweep_call(): pl.pallas_call(sweep_kernel, out_shape=[floats(3, (planes + 2) * layers,...  3.42 us
    pallas_call x1, Pallas kernels, design_call(): pl.pallas_call(design_kernel, out_shape=floats(own_planes, layers, row_wi...  2.91 us
    ppermute x3, starting transfers between devices, other_core(): return lax.ppermute(block, 'space', [(i, i ^ 1) for i in range(devices)])  1.77 us
    ppermute x3, waiting for transfers between devices, other_core(): return lax.ppermute(block, 'space', [(i, i ^ 1) for i in range(devices)])  1.07 us
    pallas_call x1, Pallas kernels, prepare_call(): pl.pallas_call(prepare_kernel, out_shape=[floats(len(ALL_SQUARES), layers...  1 us
  transfers between devices with their start and end apart: 3, of which 2 were waited for; matrix products, arithmetic and copies ran while one was open for 0% of the time, Pallas kernels for 4%

profile of v20, /device:TPU:0, one launch (start us, length us, event | category | flops | bytes accessed | tf_op | source)
XLA Modules:
  0.0 46.0 jit_solution(17002701421505060070)
XLA Ops:
  0.6 0.7 %broadcast_in_dim.4 = f32[8,2,16,128]{3,2,1,0:T(8,128)S(1)} broadcast(f32[2,16,128]{2,1,0:T(8,128)} %param.6), dimensions={1,2,3} | broadcast | bytes 147456 | tf_op jit(solution)/shard_map/broadcast_in_dim | solution.py:769
  1.4 13.5 %all_to_all.15.density_ref = f32[8,2,16,128]{3,2,1,0:T(8,128)S(1)} all-to-all(f32[8,2,16,128]{3,2,1,0:T(8,128)S(1)} %broadcast_in_dim.4), channel_id=1, replica_groups={{0,3,4,7,8,11,12,15},{1,2,5,6,9,10,13,14},{16,19,20,23,24,27,28,31},{17..., dimensions={0} | all-to-all | bytes 262144 | tf_op jit(solution)/shard_map/all_to_all | solution.py:764
  14.8 0.7 %collective-permute-start = (f32[8,2,16,128]{3,2,1,0:T(8,128)S(1)}, f32[8,2,16,128]{3,2,1,0:T(8,128)S(1)}, u32[]{:S(2)}, u32[]{:S(2)}) collective-permute-start(f32[8,2,16,128]{3,2,1,0:T(8,128)S(1)} %all_to_all.15.density_ref), channel_id=1, source_target_pairs={{0,1},{1,0},{2,3},{3,2},{4,5},{5,4},{6,7},{7,6},{8,9},{9,8},{10,11... | collective-permute-start | bytes 393224 | tf_op jit(solution)/shard_map/ppermute | solution.py:755
  15.5 1.0 %prepare.1 = (f32[10,16,128]{2,1,0:T(8,128)S(1)}, f32[5,16,128]{2,1,0:T(8,128)S(1)}, f32[32,16,128]{2,1,0:T(8,128)S(1)}, f32[3,16,128]{2,1,0:T(8,128)S(1)}, f32[...) custom-call(s32[16]{0:T(128)} %radius_hbm, s32[16]{0:T(128)} %index_hbm, f32[3,16]{1,0:T(4,128)} %bitcast.12, ...), custom_call_target="tpu_custom_call" | custom-call | flops 5242880 | bytes 524288 | tf_op jit(solution)/shard_map/prepare/pallas_call | solution.py:615
  16.5 0.0 collective-permute-done.density_ref
  16.5 3.4 %sweeps.1 = (f32[3,544,128]{2,1,0:T(8,128)S(1)}, f32[32,16,128]{2,1,0:T(8,128)S(1)}) custom-call(f32[8,128]{1,0:T(8,128)S(1)} %get-tuple-element.25.spot_ref, f32[3,16,128]{2,1,0:T(8,128)S(1)} %get-tuple-element.26.load_ref, f32[10,16,128]{2,1,0:T(8,128)S(1)} %get-tuple-element.24.weight_ref, f32[5,16,128]{2,1,0:T(8,128)S(1)} %get-tuple-element.27.inverse_ref, ...), custom_call_target="tpu_custom_call" | custom-call | tf_op jit(solution)/shard_map/sweeps/pallas_call | solution.py:660
  19.9 0.3 sent_energy.1
  20.3 0.4 collective-permute-start.1
  20.7 0.9 %kept_energy.1 = (f32[3,512,128]{2,1,0:T(8,128)}, f32[8,2,16,128]{3,2,1,0:T(8,128)S(1)}) custom-call(f32[3,544,128]{2,1,0:T(8,128)S(1)} %get-tuple-element.31.disp_ref), custom_call_target="tpu_custom_call" | custom-call | flops 4177920 | bytes 1671168 | tf_op jit(solution)/shard_map/kept_energy/pallas_call | solution.py:712
  21.6 0.1 collective-permute-done.1
  21.7 10.0 %all_to_all.16 = f32[8,2,16,128]{3,2,1,0:T(8,128)S(1)} all-to-all(f32[8,2,16,128]{3,2,1,0:T(8,128)S(1)} %add.3), channel_id=1, replica_groups={{0,3,4,7,8,11,12,15},{1,2,5,6,9,10,13,14},{16,19,20,23,24,27,28,31},{17..., dimensions={0} | all-to-all | bytes 262144 | tf_op jit(solution)/shard_map/all_to_all | solution.py:764
  31.7 9.6 %all_to_all.17 = f32[8,2,16,128]{3,2,1,0:T(8,128)S(1)} all-to-all(f32[8,2,16,128]{3,2,1,0:T(8,128)S(1)} %broadcast_in_dim.5), channel_id=1, replica_groups={{0,3,4,7,8,11,12,15},{1,2,5,6,9,10,13,14},{16,19,20,23,24,27,28,31},{17..., dimensions={0} | all-to-all | bytes 262144 | tf_op jit(solution)/shard_map/all_to_all | solution.py:764
  41.4 0.7 %collective-permute-start.2 = (f32[8,2,16,128]{3,2,1,0:T(8,128)S(1)}, f32[8,2,16,128]{3,2,1,0:T(8,128)S(1)}, u32[]{:S(2)}, u32[]{:S(2)}) collective-permute-start(f32[8,2,16,128]{3,2,1,0:T(8,128)S(1)} %all_to_all.17), channel_id=1, source_target_pairs={{0,1},{1,0},{2,3},{3,2},{4,5},{5,4},{6,7},{7,6},{8,9},{9,8},{10,11... | collective-permute-start | bytes 393224 | tf_op jit(solution)/shard_map/ppermute | solution.py:755
  42.1 1.0 %collective-permute-done.2 = f32[8,2,16,128]{3,2,1,0:T(8,128)S(1)} collective-permute-done((f32[8,2,16,128]{3,2,1,0:T(8,128)S(1)}, f32[8,2,16,128]{3,2,1,0:T(8,128)S(1)}, u32[]{:S(2)}, u32[]{:S(2)}) %collective-permute-start.2) | collective-permute-done | bytes 131104 | tf_op jit(solution)/shard_map/ppermute | solution.py:755
  43.1 2.9 %design.1 = f32[2,16,128]{2,1,0:T(8,128)} custom-call(f32[10,16,128]{2,1,0:T(8,128)S(1)} %get-tuple-element.24.weight_ref, f32[2,8,2,16,128]{4,3,2,1,0:T(8,128)S(1)} %pad_maximum_fusion.sens_ref, f32[32,16,128]{2,1,0:T(8,128)S(1)} %get-tuple-element.34.coef_ref, f32[2,8,2,16,128]{4,3,2,1,0:T(8,128)S(1)} %pad_maximum_fusion.1.density_ref), custom_call_target="tpu_custom_call" | custom-call | tf_op jit(solution)/shard_map/design/pallas_call | solution.py:733
  (5 shorter events, 0.1 us)
Async XLA Ops:
  14.8 1.7 %collective-permute-start = (f32[8,2,16,128]{3,2,1,0:T(8,128)S(1)}, f32[8,2,16,128]{3,2,1,0:T(8,128)S(1)}, u32[]{:S(2)}, u32[]{:S(2)}) collective-permute-start(f32[8,2,16,128]{3,2,1,0:T(8,128)S(1)} %all_to_all.15.density_ref), channel_id=1, source_target_pairs={{0,1},{1,0},{2,3},{3,2},{4,5},{5,4},{6,7},{7,6},{8,9},{9,8},{10,11... | collective-permute-start | bytes 393224 | tf_op jit(solution)/shard_map/ppermute | solution.py:755
  20.3 1.4 %collective-permute-start.1 = (f32[8,2,16,128]{3,2,1,0:T(8,128)S(1)}, f32[8,2,16,128]{3,2,1,0:T(8,128)S(1)}, u32[]{:S(2)}, u32[]{:S(2)}) collective-permute-start(f32[8,2,16,128]{3,2,1,0:T(8,128)S(1)} %sent_energy.1), channel_id=1, source_target_pairs={{0,1},{1,0},{2,3},{3,2},{4,5},{5,4},{6,7},{7,6},{8,9},{9,8},{10,11... | collective-permute-start | bytes 393224 | tf_op jit(solution)/shard_map/ppermute | solution.py:755
  41.4 1.7 %collective-permute-start.2 = (f32[8,2,16,128]{3,2,1,0:T(8,128)S(1)}, f32[8,2,16,128]{3,2,1,0:T(8,128)S(1)}, u32[]{:S(2)}, u32[]{:S(2)}) collective-permute-start(f32[8,2,16,128]{3,2,1,0:T(8,128)S(1)} %all_to_all.17), channel_id=1, source_target_pairs={{0,1},{1,0},{2,3},{3,2},{4,5},{5,4},{6,7},{7,6},{8,9},{9,8},{10,11... | collective-permute-start | bytes 393224 | tf_op jit(solution)/shard_map/ppermute | solution.py:755

commit v21 on v19

--- a/solution.py
+++ b/solution.py
@@ -281,12 +281,13 @@
     for ref in (side_ref, far_ref):
         zero_edges(ref)
     results = (near_ref, side_ref, far_ref)
-    for x, spot in group_spots(0, density_ref):
+    other_ref = density_ref.at[1]
+    for x, spot in group_spots(0, other_ref):
         for place, ref in enumerate(results):
             ref[x + 2] = filter_ref[(place,) + spot]
     spread = (plane_ref, beside_ref, further_ref)
-    spread_group(density_ref, spread)
-    for p, (x, spot) in enumerate(group_spots(1, density_ref)):
+    spread_group(other_ref, spread)
+    for p, (x, spot) in enumerate(group_spots(1, other_ref)):
         for ref, field in zip(results, filter_plane(p, layers, spread, weight_ref)):
             ref[x + 2] = field
 
@@ -643,8 +644,8 @@
 
 
 def sweep_call(spot, load, weights, inverses, free, filtered, density, displacement):
-    chips, own_planes, layers, row_width = density.shape
-    planes = 2 * chips * own_planes
+    groups, chips, own_planes, layers, row_width = density.shape
+    planes = groups * chips * own_planes
 
     def scratch(*lead):
         return pltpu.VMEM(lead + (row_width,), jnp.float32)
@@ -767,10 +768,10 @@
     )
     other_group = other_core(same_group)
     weights, inverses, free, load, spot, filtered = prepare_call(same_group, *small)
+    whole = jnp.stack([same_group, other_group])
     disp, coef = sweep_call(
-        spot, load, weights, inverses, free, filtered, other_group, displacement[0]
-    )
-    whole = jnp.stack([same_group, other_group])
+        spot, load, weights, inverses, free, filtered, whole, displacement[0]
+    )
     sent, disp = lax.optimization_barrier((sent_energy_call(disp, same_group.shape), disp))
     sens, (new_displacement,) = scattered_sum(
         sent, lambda: kept_energy_call(disp, same_group.shape)

time: 47 us -> 46 us (0.979)
  local copies, waits for them, and re-layouts: 1.87 us -> 0.82 us
    unnamed x2, local copies, waits for them, and re-layouts: 1.13 us -> 0.01 us
where the time goes in v21:
time: 46 us; the launch traced here: 45.5 us
  blocking collectives  33.1 us (72%)
  Pallas kernels  7.98 us (17%)
  starting transfers between devices  1.76 us (4%)
  waiting for transfers between devices  1.11 us (2%)
  local copies, waits for them, and re-layouts  0.82 us (2%)
  between operations  0.71 us (2%)
    all_to_all x3, blocking collectives, between_chips(): lax.all_to_all(pieces, 'space', 0, 0, axis_index_groups=chip_groups())  33.1 us
    pallas_call x1, Pallas kernels, design_call(): pl.pallas_call(design_kernel, out_shape=floats(own_planes, layers, row_wi...  2.91 us
    pallas_call x1, Pallas kernels, sweep_call(): pl.pallas_call(sweep_kernel, out_shape=[floats(3, (planes + 2) * layers,...  2.86 us
    ppermute x3, starting transfers between devices, other_core(): return lax.ppermute(block, 'space', [(i, i ^ 1) for i in range(devices)])  1.76 us
    ppermute x3, waiting for transfers between devices, other_core(): return lax.ppermute(block, 'space', [(i, i ^ 1) for i in range(devices)])  1.11 us
    pallas_call x1, Pallas kernels, prepare_call(): pl.pallas_call(prepare_kernel, out_shape=[floats(len(ALL_SQUARES), layers...  1 us
  transfers between devices with their start and end apart: 3, of which 2 were waited for; matrix products, arithmetic and copies ran while one was open for 0% of the time, Pallas kernels for 4%

profile of v21, /device:TPU:0, one launch (start us, length us, event | category | flops | bytes accessed | tf_op | source)
XLA Modules:
  0.0 45.5 jit_solution(7215217130054795419)
XLA Ops:
  0.6 0.0 copy-start
  0.6 0.8 %broadcast_in_dim.4 = f32[8,2,16,128]{3,2,1,0:T(8,128)S(1)} broadcast(f32[2,16,128]{2,1,0:T(8,128)} %param.6), dimensions={1,2,3} | broadcast | bytes 147456 | tf_op jit(solution)/shard_map/broadcast_in_dim | solution.py:752
  1.4 13.5 %all_to_all.15.density_ref = f32[8,2,16,128]{3,2,1,0:T(8,128)S(1)} all-to-all(f32[8,2,16,128]{3,2,1,0:T(8,128)S(1)} %broadcast_in_dim.4), channel_id=1, replica_groups={{0,3,4,7,8,11,12,15},{1,2,5,6,9,10,13,14},{16,19,20,23,24,27,28,31},{17..., dimensions={0} | all-to-all | bytes 262144 | tf_op jit(solution)/shard_map/all_to_all | solution.py:747
  14.9 0.7 %collective-permute-start = (f32[8,2,16,128]{3,2,1,0:T(8,128)S(1)}, f32[8,2,16,128]{3,2,1,0:T(8,128)S(1)}, u32[]{:S(2)}, u32[]{:S(2)}) collective-permute-start(f32[8,2,16,128]{3,2,1,0:T(8,128)S(1)} %all_to_all.15.density_ref), channel_id=1, source_target_pairs={{0,1},{1,0},{2,3},{3,2},{4,5},{5,4},{6,7},{7,6},{8,9},{9,8},{10,11... | collective-permute-start | bytes 393224 | tf_op jit(solution)/shard_map/ppermute | solution.py:738
  15.6 1.0 %prepare.1 = (f32[10,16,128]{2,1,0:T(8,128)S(1)}, f32[5,16,128]{2,1,0:T(8,128)S(1)}, f32[32,16,128]{2,1,0:T(8,128)S(1)}, f32[3,16,128]{2,1,0:T(8,128)S(1)}, f32[...) custom-call(s32[16]{0:T(128)} %radius_hbm, s32[16]{0:T(128)} %index_hbm, f32[3,16]{1,0:T(4,128)} %bitcast.12, ...), custom_call_target="tpu_custom_call" | custom-call | flops 5242880 | bytes 524288 | tf_op jit(solution)/shard_map/prepare/pallas_call | solution.py:608
  16.6 0.0 collective-permute-done
  16.6 0.0 copy-done
  16.6 2.9 %sweeps.1 = (f32[3,544,128]{2,1,0:T(8,128)S(1)}, f32[32,16,128]{2,1,0:T(8,128)S(1)}) custom-call(f32[8,128]{1,0:T(8,128)S(1)} %get-tuple-element.25.spot_ref, f32[3,16,128]{2,1,0:T(8,128)S(1)} %get-tuple-element.26.load_ref, f32[10,16,128]{2,1,0:T(8,128)S(1)} %get-tuple-element.24.weight_ref, f32[5,16,128]{2,1,0:T(8,128)S(1)} %get-tuple-element.27.inverse_ref, ...), custom_call_target="tpu_custom_call" | custom-call | tf_op jit(solution)/shard_map/sweeps/pallas_call | solution.py:653
  19.5 0.3 sent_energy.1
  19.8 0.4 collective-permute-start.1
  20.2 0.9 %kept_energy.1 = (f32[3,512,128]{2,1,0:T(8,128)}, f32[8,2,16,128]{3,2,1,0:T(8,128)S(1)}) custom-call(f32[3,544,128]{2,1,0:T(8,128)S(1)} %get-tuple-element.31.disp_ref), custom_call_target="tpu_custom_call" | custom-call | flops 4177920 | bytes 1671168 | tf_op jit(solution)/shard_map/kept_energy/pallas_call | solution.py:695
  21.1 0.1 collective-permute-done.1
  21.3 10.0 %all_to_all.16 = f32[8,2,16,128]{3,2,1,0:T(8,128)S(1)} all-to-all(f32[8,2,16,128]{3,2,1,0:T(8,128)S(1)} %add.3), channel_id=1, replica_groups={{0,3,4,7,8,11,12,15},{1,2,5,6,9,10,13,14},{16,19,20,23,24,27,28,31},{17..., dimensions={0} | all-to-all | bytes 262144 | tf_op jit(solution)/shard_map/all_to_all | solution.py:747
  31.3 9.6 %all_to_all.17 = f32[8,2,16,128]{3,2,1,0:T(8,128)S(1)} all-to-all(f32[8,2,16,128]{3,2,1,0:T(8,128)S(1)} %broadcast_in_dim.5), channel_id=1, replica_groups={{0,3,4,7,8,11,12,15},{1,2,5,6,9,10,13,14},{16,19,20,23,24,27,28,31},{17..., dimensions={0} | all-to-all | bytes 262144 | tf_op jit(solution)/shard_map/all_to_all | solution.py:747
  40.9 0.7 %collective-permute-start.2 = (f32[8,2,16,128]{3,2,1,0:T(8,128)S(1)}, f32[8,2,16,128]{3,2,1,0:T(8,128)S(1)}, u32[]{:S(2)}, u32[]{:S(2)}) collective-permute-start(f32[8,2,16,128]{3,2,1,0:T(8,128)S(1)} %all_to_all.17), channel_id=1, source_target_pairs={{0,1},{1,0},{2,3},{3,2},{4,5},{5,4},{6,7},{7,6},{8,9},{9,8},{10,11... | collective-permute-start | bytes 393224 | tf_op jit(solution)/shard_map/ppermute | solution.py:738
  41.6 1.0 %collective-permute-done.2 = f32[8,2,16,128]{3,2,1,0:T(8,128)S(1)} collective-permute-done((f32[8,2,16,128]{3,2,1,0:T(8,128)S(1)}, f32[8,2,16,128]{3,2,1,0:T(8,128)S(1)}, u32[]{:S(2)}, u32[]{:S(2)}) %collective-permute-start.2) | collective-permute-done | bytes 131104 | tf_op jit(solution)/shard_map/ppermute | solution.py:738
  42.6 2.9 %design.1 = f32[2,16,128]{2,1,0:T(8,128)} custom-call(f32[10,16,128]{2,1,0:T(8,128)S(1)} %get-tuple-element.24.weight_ref, f32[2,8,2,16,128]{4,3,2,1,0:T(8,128)S(1)} %pad_maximum_fusion.1.sens_ref, f32[32,16,128]{2,1,0:T(8,128)S(1)} %get-tuple-element.34.coef_ref, f32[2,8,2,16,128]{4,3,2,1,0:T(8,128)S(1)} %pad_maximum_fusion.density_ref), custom_call_target="tpu_custom_call" | custom-call | tf_op jit(solution)/shard_map/design/pallas_call | solution.py:716
  (5 shorter events, 0.1 us)
Async XLA Ops:
  0.6 16.0 %copy-start = (f32[1,3,32,16,128]{4,3,2,1,0:T(8,128)S(1)}, f32[1,3,32,16,128]{4,3,2,1,0:T(8,128)}, u32[]{:S(2)}) copy-start(f32[1,3,32,16,128]{4,3,2,1,0:T(8,128)} %param.7) | copy-start | bytes 2359300
  14.9 1.7 %collective-permute-start = (f32[8,2,16,128]{3,2,1,0:T(8,128)S(1)}, f32[8,2,16,128]{3,2,1,0:T(8,128)S(1)}, u32[]{:S(2)}, u32[]{:S(2)}) collective-permute-start(f32[8,2,16,128]{3,2,1,0:T(8,128)S(1)} %all_to_all.15.density_ref), channel_id=1, source_target_pairs={{0,1},{1,0},{2,3},{3,2},{4,5},{5,4},{6,7},{7,6},{8,9},{9,8},{10,11... | collective-permute-start | bytes 393224 | tf_op jit(solution)/shard_map/ppermute | solution.py:738
  19.8 1.4 %collective-permute-start.1 = (f32[8,2,16,128]{3,2,1,0:T(8,128)S(1)}, f32[8,2,16,128]{3,2,1,0:T(8,128)S(1)}, u32[]{:S(2)}, u32[]{:S(2)}) collective-permute-start(f32[8,2,16,128]{3,2,1,0:T(8,128)S(1)} %sent_energy.1), channel_id=1, source_target_pairs={{0,1},{1,0},{2,3},{3,2},{4,5},{5,4},{6,7},{7,6},{8,9},{9,8},{10,11... | collective-permute-start | bytes 393224 | tf_op jit(solution)/shard_map/ppermute | solution.py:738
  40.9 1.7 %collective-permute-start.2 = (f32[8,2,16,128]{3,2,1,0:T(8,128)S(1)}, f32[8,2,16,128]{3,2,1,0:T(8,128)S(1)}, u32[]{:S(2)}, u32[]{:S(2)}) collective-permute-start(f32[8,2,16,128]{3,2,1,0:T(8,128)S(1)} %all_to_all.17), channel_id=1, source_target_pairs={{0,1},{1,0},{2,3},{3,2},{4,5},{5,4},{6,7},{7,6},{8,9},{9,8},{10,11... | collective-permute-start | bytes 393224 | tf_op jit(solution)/shard_map/ppermute | solution.py:738

commit v22 on v21

--- a/solution.py
+++ b/solution.py
@@ -101,26 +101,6 @@
 
 def gap(x, layers):
     return pl.ds(x * (layers + GAP), GAP)
-
-
-def pair_spot(x, own_planes):
-    device = x // own_planes
-    apart = device ^ lax.axis_index("space")
-    return (apart ^ apart >> 1) & 1, device >> 1, x % own_planes
-
-
-def half_views(ref, first, count):
-    own_planes = ref.shape[2]
-    mine = lax.axis_index("space")
-    side = (mine ^ mine >> 1) & 1
-    chips = pl.ds(first // (2 * own_planes), count // (2 * own_planes))
-    views = (ref.at[side, chips], ref.at[1 - side, chips])
-
-    def plane(p):
-        device = p // own_planes
-        return views[(device ^ device >> 1) & 1], (device >> 1, p % own_planes)
-
-    return plane
 
 
 def edge_class(x, planes):
@@ -416,149 +396,131 @@
     lax.fori_loop(0, SWEEPS // 2 + 1, two_sweeps, 0)
 
 
-def energy_planes(group, disp_ref, sens_ref):
-    chips, own_planes, layers, row_width = sens_ref.shape
-    planes = disp_ref.shape[1] // layers - 2
+def filter_group(group, shares, weight_ref, near_ref, far_ref, result_ref):
+    chips, own_planes, layers, row_width = result_ref.shape
+    zero_gap = jnp.zeros((GAP, row_width), jnp.float32)
+    mine = lax.axis_index("space")
+    core = (mine ^ mine >> 1 ^ group) & 1
+    count = shares[0].shape[0] - own_planes
+    views = [
+        [ref.at[pl.ds(own_planes * start, count)] for ref in shares] for start in (core, 1 - core)
+    ]
+    for ref in (near_ref, far_ref):
+        ref[gap(0, layers)] = zero_gap
+    for p in range(chips * own_planes):
+        chip, own = p // own_planes, p % own_planes
+        plane, beside, further = views[chip & 1]
+        x = 2 * own_planes * chip + own + 2
+
+        def around(ref, distance):
+            return ref[x + distance] + ref[x - distance]
+
+        sums = {
+            0: plane[x],
+            1: beside[x] + around(plane, 1),
+            2: around(beside, 1),
+            4: further[x] + around(plane, 2),
+            5: around(further, 1) + around(beside, 2),
+            8: around(further, 2),
+        }
+        level = weigh(sums, weight_ref, 0)
+        for ref, square in ((near_ref, 1), (far_ref, 4)):
+            ref[gapped(p, layers)] = weigh(sums, weight_ref, square)
+            ref[gap(p + 1, layers)] = zero_gap
+        result_ref[chip, own] = (
+            level
+            + near_ref[gapped(p, layers, 1)]
+            + near_ref[gapped(p, layers, -1)]
+            + far_ref[gapped(p, layers, 2)]
+            + far_ref[gapped(p, layers, -2)]
+        )
+
+
+def share_kernel(
+    disp_ref,
+    coef_ref,
+    weight_ref,
+    sent_ref,
+    plane_ref,
+    beside_ref,
+    further_ref,
+    near_ref,
+    far_ref,
+):
+    planes, layers, row_width = coef_ref.shape
     load_cases = lax.axis_size("space")
     shape = (layers, row_width)
     z = spot_iota(shape, 0)
     y = spot_iota(shape, 1)
     zero = jnp.zeros(shape, jnp.float32)
-    mine = lax.axis_index("space")
-    core = mine ^ mine >> 1 ^ group
-
-    def between(x):
-        result = zero
+    shares = (plane_ref, beside_ref, further_ref)
+    for ref in shares:
+        zero_edges(ref)
+
+    before = zero
+    here = [disp_ref[part, rows(1, layers)] for part in range(3)]
+    for x in range(planes):
+        ahead, upward, right = zero, zero, zero
+        later = here
+        if x + 1 < planes:
+            later = [disp_ref[part, rows(x + 2, layers)] for part in range(3)]
         for part in range(3):
-            step = disp_ref[part, rows(x + 1, layers)] - disp_ref[part, rows(x, layers)]
-            result = result + (2.0 if part == 0 else 1.0) * (step * step)
-        return jnp.where((x > 0) & (x < planes), result, 0.0)
-
-    def inside(x):
-        upward, right = zero, zero
-        for part in range(3):
-            here = disp_ref[part, rows(x + 1, layers)]
-            climb = disp_ref[part, rows(x + 1, layers, 1)] - here
-            slide = pltpu.roll(here, row_width - 1, 1) - here
+            step = later[part] - here[part]
+            climb = disp_ref[part, rows(x + 1, layers, 1)] - here[part]
+            slide = pltpu.roll(here[part], row_width - 1, 1) - here[part]
+            ahead = ahead + (2.0 if part == 0 else 1.0) * (step * step)
             upward = upward + (2.0 if part == 1 else 1.0) * (climb * climb)
             right = right + (2.0 if part == 2 else 1.0) * (slide * slide)
         upward = jnp.where(z < layers - 1, upward, 0.0)
         right = jnp.where(y < row_width - 1, right, 0.0)
-        return upward + pltpu.roll(upward, 1, 0) + right + pltpu.roll(right, 1, 1)
-
-    for chip in range(chips):
-        first = own_planes * (2 * chip + ((core ^ chip) & 1))
-        before = between(first)
-        for own in range(own_planes):
-            after = between(first + own + 1)
-            sens_ref[chip, own] = (0.5 / load_cases) * (before + after + inside(first + own))
-            before = after
-
-
-def sent_energy_kernel(disp_ref, sens_ref):
-    energy_planes(1, disp_ref, sens_ref)
-
-
-def kept_energy_kernel(disp_ref, disp_hbm, sens_ref, stored):
-    layers = sens_ref.shape[2]
+        total = before + ahead + upward + pltpu.roll(upward, 1, 0) + right + pltpu.roll(right, 1, 1)
+        share = (0.5 / load_cases) * total * coef_ref[x]
+        plane_ref[x + 2] = share
+        beside_ref[x + 2] = shift_sum(share, 1, 1)
+        further_ref[x + 2] = shift_sum(share, 1, 2)
+        before, here = ahead, later
+    filter_group(1, shares, weight_ref, near_ref, far_ref, sent_ref)
+
+
+def kept_kernel(
+    disp_ref,
+    weight_ref,
+    plane_ref,
+    beside_ref,
+    further_ref,
+    disp_hbm,
+    kept_ref,
+    near_ref,
+    far_ref,
+    stored,
+):
+    layers = kept_ref.shape[2]
     inner = pl.ds(layers, disp_ref.shape[1] - 2 * layers)
     store = pltpu.make_async_copy(disp_ref.at[:, inner], disp_hbm, stored)
     store.start()
-    energy_planes(0, disp_ref, sens_ref)
+    shares = (plane_ref, beside_ref, further_ref)
+    filter_group(0, shares, weight_ref, near_ref, far_ref, kept_ref)
     store.wait()
 
 
-def design_kernel(
-    weight_ref,
-    sens_ref,
-    coef_ref,
-    density_ref,
-    new_ref,
-    plane_ref,
-    beside_ref,
-    further_ref,
-    near_ref,
-    far_ref,
-    pull_ref,
-    low_ref,
-    high_ref,
-):
-    planes, layers, row_width = coef_ref.shape
-    own_planes = density_ref.shape[2]
-    place = lax.axis_index("space")
+def design_kernel(root_ref, density_ref, new_ref, pull_ref, low_ref, high_ref):
+    groups, chips, own_planes, layers, row_width = density_ref.shape
+    own_chip = lax.axis_index("space") >> 1
     shape = (layers, row_width)
     zero = jnp.zeros(shape, jnp.float32)
-    zero_gap = jnp.zeros((GAP, row_width), jnp.float32)
-    for ref in (plane_ref, beside_ref, further_ref):
-        zero_edges(ref)
-
-    def spread_half(first, count, carry):
-        sens = half_views(sens_ref, first, count)
-        coef = coef_ref.at[pl.ds(first, count)]
-        plane_view, beside, further = (
-            ref.at[pl.ds(first + 2, count)] for ref in (plane_ref, beside_ref, further_ref)
-        )
-        for p in range(count):
-            view, spot = sens(p)
-            plane = view[spot] * coef[p]
-            plane_view[p] = plane
-            beside[p] = shift_sum(plane, 1, 1)
-            further[p] = shift_sum(plane, 1, 2)
-        return carry
-
-    each_half(planes, spread_half, 0)
-
-    def root_half(first, count, carry):
-        density_at = half_views(density_ref, first, count)
-        plane_view, beside, further = (
-            ref.at[pl.ds(first, count + 4)] for ref in (plane_ref, beside_ref, further_ref)
-        )
-        near, far = (
-            ref.at[pl.ds(first * (layers + GAP), count * (layers + GAP) + GAP)]
-            for ref in (near_ref, far_ref)
-        )
-        for ref in (near, far):
-            ref[gap(0, layers)] = zero_gap
-        pull, low, high = (
-            ref.at[pl.ds(first, count)] for ref in (pull_ref, low_ref, high_ref)
-        )
-        for p in range(count):
-
-            def around(ref, distance):
-                return ref[p + 2 + distance] + ref[p + 2 - distance]
-
-            sums = {
-                0: plane_view[p + 2],
-                1: beside[p + 2] + around(plane_view, 1),
-                2: around(beside, 1),
-                4: further[p + 2] + around(plane_view, 2),
-                5: around(further, 1) + around(beside, 2),
-                8: around(further, 2),
-            }
-            level = weigh(sums, weight_ref, 0)
-            for ref, square in ((near, 1), (far, 4)):
-                ref[gapped(p, layers)] = weigh(sums, weight_ref, square)
-                ref[gap(p + 1, layers)] = zero_gap
-            root = jnp.sqrt(
-                level
-                + near[gapped(p, layers, 1)]
-                + near[gapped(p, layers, -1)]
-                + far[gapped(p, layers, 2)]
-                + far[gapped(p, layers, -2)]
-            )
-            view, spot = density_at(p)
-            density = view[spot]
-            pull[p] = density * root
-            low[p] = jnp.maximum(density - move_limit, density_floor)
-            high[p] = jnp.minimum(density + move_limit, 1.0)
-        return carry
-
-    each_half(planes, root_half, 0)
-
-    target = volume_share * planes * layers * row_width
-
-    def trial(x, factor):
-        return jnp.minimum(jnp.maximum(pull_ref[x] * factor, low_ref[x]), high_ref[x])
+    planes = [
+        (group, chip, own)
+        for group in range(groups)
+        for chip in range(chips)
+        for own in range(own_planes)
+    ]
+    for spot in planes:
+        density = density_ref[spot]
+        pull_ref[spot] = density * root_ref[spot]
+        low_ref[spot] = jnp.maximum(density - move_limit, density_floor)
+        high_ref[spot] = jnp.minimum(density + move_limit, 1.0)
+
+    target = volume_share * len(planes) * layers * row_width
 
     def factor_of(log_level):
         return jnp.broadcast_to(jnp.exp(-0.5 * log_level), shape)
@@ -572,8 +534,8 @@
         middles = (lower + quarter, lower + half, lower + half + quarter)
         factors = [factor_of(middle) for middle in middles]
         totals = [zero, zero, zero]
-        for x in range(planes):
-            pull, low, high = pull_ref[x], low_ref[x], high_ref[x]
+        for spot in planes:
+            pull, low, high = pull_ref[spot], low_ref[spot], high_ref[spot]
             totals = [
                 total + jnp.minimum(jnp.maximum(pull * factor, low), high)
                 for total, factor in zip(totals, factors)
@@ -587,7 +549,10 @@
     lower, span = lax.fori_loop(0, SEARCH // 2, halve_twice, start)
     factor = factor_of(lower + 0.5 * span)
     for own in range(own_planes):
-        new_ref[own] = trial(place * own_planes + own, factor)
+        spot = (0, own_chip, own)
+        new_ref[own] = jnp.minimum(
+            jnp.maximum(pull_ref[spot] * factor, low_ref[spot]), high_ref[spot]
+        )
 
 
 def in_vmem():
@@ -678,59 +643,48 @@
     )(spot, load, weights, inverses, free, filtered, density, displacement)
 
 
-def sent_energy_call(disp, group_shape):
+def share_call(disp, coef, weights, group_shape):
+    planes, layers, row_width = coef.shape
+    gaps = pltpu.VMEM((planes // 2 * (layers + GAP) + GAP, row_width), jnp.float32)
     return pl.pallas_call(
-        sent_energy_kernel,
-        out_shape=floats(*group_shape),
-        in_specs=[in_vmem()],
-        out_specs=in_vmem(),
+        share_kernel,
+        out_shape=[floats(*group_shape)] + [floats(planes + 4, layers, row_width)] * 3,
+        in_specs=[in_vmem()] * 3,
+        out_specs=[in_vmem()] * 4,
+        scratch_shapes=[gaps, gaps],
         compiler_params=pltpu.CompilerParams(vmem_limit_bytes=KERNEL_VMEM),
-        name="sent_energy",
-    )(disp)
-
-
-def kept_energy_call(disp, group_shape):
+        name="share",
+    )(disp, coef, weights)
+
+
+def kept_call(disp, weights, shares, group_shape):
     parts, disp_rows, row_width = disp.shape
-    layers = group_shape[2]
+    chips, own_planes, layers = group_shape[:3]
+    gaps = pltpu.VMEM((chips * own_planes * (layers + GAP) + GAP, row_width), jnp.float32)
     return pl.pallas_call(
-        kept_energy_kernel,
+        kept_kernel,
         out_shape=[floats(parts, disp_rows - 2 * layers, row_width), floats(*group_shape)],
-        in_specs=[in_vmem()],
+        in_specs=[in_vmem()] * 5,
         out_specs=[pl.BlockSpec(memory_space=pltpu.HBM), in_vmem()],
-        scratch_shapes=[pltpu.SemaphoreType.DMA(())],
+        scratch_shapes=[gaps, gaps, pltpu.SemaphoreType.DMA(())],
         compiler_params=pltpu.CompilerParams(vmem_limit_bytes=KERNEL_VMEM),
         cost_estimate=pl.CostEstimate(
             flops=20 * disp.size, bytes_accessed=8 * disp.size, transcendentals=0
         ),
-        name="kept_energy",
-    )(disp)
-
-
-def design_call(weights, sens, coef, density):
-    cores, chips, own_planes, layers, row_width = density.shape
-    planes = cores * chips * own_planes
-
-    def scratch(*lead):
-        return pltpu.VMEM(lead + (row_width,), jnp.float32)
-
+        name="kept",
+    )(disp, weights, *shares)
+
+
+def design_call(root, density):
     return pl.pallas_call(
         design_kernel,
-        out_shape=floats(own_planes, layers, row_width),
-        in_specs=[in_vmem()] * 4,
+        out_shape=floats(*density.shape[2:]),
+        in_specs=[in_vmem()] * 2,
         out_specs=in_vmem(),
-        scratch_shapes=[
-            scratch(planes + 4, layers),
-            scratch(planes + 4, layers),
-            scratch(planes + 4, layers),
-            scratch(planes * (layers + GAP) + GAP),
-            scratch(planes * (layers + GAP) + GAP),
-            scratch(planes, layers),
-            scratch(planes, layers),
-            scratch(planes, layers),
-        ],
+        scratch_shapes=[pltpu.VMEM(density.shape, jnp.float32)] * 3,
         compiler_params=pltpu.CompilerParams(vmem_limit_bytes=KERNEL_VMEM),
         name="design",
-    )(weights, sens, coef, density)
+    )(root, density)
 
 
 def other_core(block):
@@ -772,12 +726,13 @@
     disp, coef = sweep_call(
         spot, load, weights, inverses, free, filtered, whole, displacement[0]
     )
-    sent, disp = lax.optimization_barrier((sent_energy_call(disp, same_group.shape), disp))
-    sens, (new_displacement,) = scattered_sum(
-        sent, lambda: kept_energy_call(disp, same_group.shape)
-    )
-    sens = with_other_core(chip_gathered(sens))
-    new_density = design_call(weights, sens, coef, whole)
+    sent, *shares = share_call(disp, coef, weights, same_group.shape)
+    sent, disp, shares = lax.optimization_barrier((sent, disp, shares))
+    squares, (new_displacement,) = scattered_sum(
+        sent, lambda: kept_call(disp, weights, shares, same_group.shape)
+    )
+    root = with_other_core(chip_gathered(jnp.sqrt(squares)))
+    new_density = design_call(root, whole)
     return new_density, new_displacement.reshape(displacement.shape)
 
 

time: 46 us -> 47.6 us (1.035)
  Pallas kernels: 7.98 us -> 9.57 us
    pallas_call x3, Pallas kernels: 4.12 us -> 5.7 us  [the longest x1 2.94 us: share_call(): pl.pallas_call(share_kernel, out_shape=[floats(*group_shape)] + [floats(p...]
where the time goes in v22:
time: 47.6 us; the launch traced here: 47.2 us
  blocking collectives  33.1 us (70%)
  Pallas kernels  9.57 us (20%)
  starting transfers between devices  1.75 us (4%)
  waiting for transfers between devices  1.11 us (2%)
  local copies, waits for them, and re-layouts  0.82 us (2%)
  between operations  0.72 us (2%)
    all_to_all x3, blocking collectives, between_chips(): lax.all_to_all(pieces, 'space', 0, 0, axis_index_groups=chip_groups())  33.1 us
    pallas_call x1, Pallas kernels, share_call(): pl.pallas_call(share_kernel, out_shape=[floats(*group_shape)] + [floats(p...  2.94 us
    pallas_call x1, Pallas kernels, sweep_call(): pl.pallas_call(sweep_kernel, out_shape=[floats(3, (planes + 2) * layers,...  2.86 us
    pallas_call x1, Pallas kernels, design_call(): pl.pallas_call(design_kernel, out_shape=floats(*density.shape[2:]), in_sp...  1.88 us
    ppermute x3, starting transfers between devices, other_core(): return lax.ppermute(block, 'space', [(i, i ^ 1) for i in range(devices)])  1.75 us
    ppermute x3, waiting for transfers between devices, other_core(): return lax.ppermute(block, 'space', [(i, i ^ 1) for i in range(devices)])  1.11 us
    pallas_call x1, Pallas kernels, prepare_call(): pl.pallas_call(prepare_kernel, out_shape=[floats(len(ALL_SQUARES), layers...  1 us
  transfers between devices with their start and end apart: 3, of which 2 were waited for; matrix products, arithmetic and copies ran while one was open for 0% of the time, Pallas kernels for 4%

profile of v22, /device:TPU:0, one launch (start us, length us, event | category | flops | bytes accessed | tf_op | source)
XLA Modules:
  0.0 47.2 jit_solution(9745121999730663756)
XLA Ops:
  0.6 0.0 copy-start
  0.6 0.8 %broadcast_in_dim.4 = f32[8,2,16,128]{3,2,1,0:T(8,128)S(1)} broadcast(f32[2,16,128]{2,1,0:T(8,128)} %param.6), dimensions={1,2,3} | broadcast | bytes 147456 | tf_op jit(solution)/shard_map/broadcast_in_dim | solution.py:706
  1.4 13.5 %all_to_all.15.density_ref = f32[8,2,16,128]{3,2,1,0:T(8,128)S(1)} all-to-all(f32[8,2,16,128]{3,2,1,0:T(8,128)S(1)} %broadcast_in_dim.4), channel_id=1, replica_groups={{0,3,4,7,8,11,12,15},{1,2,5,6,9,10,13,14},{16,19,20,23,24,27,28,31},{17..., dimensions={0} | all-to-all | bytes 262144 | tf_op jit(solution)/shard_map/all_to_all | solution.py:701
  14.9 0.7 %collective-permute-start = (f32[8,2,16,128]{3,2,1,0:T(8,128)S(1)}, f32[8,2,16,128]{3,2,1,0:T(8,128)S(1)}, u32[]{:S(2)}, u32[]{:S(2)}) collective-permute-start(f32[8,2,16,128]{3,2,1,0:T(8,128)S(1)} %all_to_all.15.density_ref), channel_id=1, source_target_pairs={{0,1},{1,0},{2,3},{3,2},{4,5},{5,4},{6,7},{7,6},{8,9},{9,8},{10,11... | collective-permute-start | bytes 393224 | tf_op jit(solution)/shard_map/ppermute | solution.py:692
  15.6 1.0 %prepare.1 = (f32[10,16,128]{2,1,0:T(8,128)S(1)}, f32[5,16,128]{2,1,0:T(8,128)S(1)}, f32[32,16,128]{2,1,0:T(8,128)S(1)}, f32[3,16,128]{2,1,0:T(8,128)S(1)}, f32[...) custom-call(s32[16]{0:T(128)} %radius_hbm, s32[16]{0:T(128)} %index_hbm, f32[3,16]{1,0:T(4,128)} %bitcast.12, ...), custom_call_target="tpu_custom_call" | custom-call | flops 5242880 | bytes 524288 | tf_op jit(solution)/shard_map/prepare/pallas_call | solution.py:573
  16.6 0.0 collective-permute-done
  16.6 0.0 copy-done
  16.6 2.9 %sweeps.1 = (f32[3,544,128]{2,1,0:T(8,128)S(1)}, f32[32,16,128]{2,1,0:T(8,128)S(1)}) custom-call(f32[8,128]{1,0:T(8,128)S(1)} %get-tuple-element.31.spot_ref, f32[3,16,128]{2,1,0:T(8,128)S(1)} %get-tuple-element.32.load_ref, f32[10,16,128]{2,1,0:T(8,128)S(1)} %get-tuple-element.33.weight_ref, f32[5,16,128]{2,1,0:T(8,128)S(1)} %get-tuple-element.34.inverse_ref, ...), custom_call_target="tpu_custom_call" | custom-call | tf_op jit(solution)/shard_map/sweeps/pallas_call | solution.py:618
  19.5 2.9 %share.1 = (f32[8,2,16,128]{3,2,1,0:T(8,128)S(1)}, f32[36,16,128]{2,1,0:T(8,128)S(1)}, f32[36,16,128]{2,1,0:T(8,128)S(1)}, f32[36,16,128]{2,1,0:T(8,128)S(1)}) custom-call(f32[3,544,128]{2,1,0:T(8,128)S(1)} %get-tuple-element.43.disp_ref, f32[32,16,128]{2,1,0:T(8,128)S(1)} %get-tuple-element.38.coef_ref, f32[10,16,128]{2,1,0:T(8,128)S(1)} %get-tuple-element.33.weight_ref), custom_call_target="tpu_custom_call" | custom-call | tf_op jit(solution)/shard_map/share/pallas_call | solution.py:649
  22.4 0.4 collective-permute-start.1
  22.8 0.9 %kept.1 = (f32[3,512,128]{2,1,0:T(8,128)}, f32[8,2,16,128]{3,2,1,0:T(8,128)S(1)}) custom-call(f32[3,544,128]{2,1,0:T(8,128)S(1)} %get-tuple-element.43.disp_ref, f32[10,16,128]{2,1,0:T(8,128)S(1)} %get-tuple-element.33.weight_ref, f32[36,16,128]{2,1,0:T(8,128)S(1)} %get-tuple-element.44.plane_ref, f32[36,16,128]{2,1,0:T(8,128)S(1)} %get-tuple-element.45.beside_ref, ...), custom_call_target="tpu_custom_call" | custom-call | flops 4177920 | bytes 1671168 | tf_op jit(solution)/shard_map/kept/pallas_call | solution.py:664
  23.7 0.1 collective-permute-done.1
  23.9 10.0 %all_to_all.16 = f32[8,2,16,128]{3,2,1,0:T(8,128)S(1)} all-to-all(f32[8,2,16,128]{3,2,1,0:T(8,128)S(1)} %add.3), channel_id=1, replica_groups={{0,3,4,7,8,11,12,15},{1,2,5,6,9,10,13,14},{16,19,20,23,24,27,28,31},{17..., dimensions={0} | all-to-all | bytes 262144 | tf_op jit(solution)/shard_map/all_to_all | solution.py:701
  34.0 9.6 %all_to_all.17 = f32[8,2,16,128]{3,2,1,0:T(8,128)S(1)} all-to-all(f32[8,2,16,128]{3,2,1,0:T(8,128)S(1)} %broadcast_in_dim.5), channel_id=1, replica_groups={{0,3,4,7,8,11,12,15},{1,2,5,6,9,10,13,14},{16,19,20,23,24,27,28,31},{17..., dimensions={0} | all-to-all | bytes 262144 | tf_op jit(solution)/shard_map/all_to_all | solution.py:701
  43.6 0.7 %collective-permute-start.2 = (f32[8,2,16,128]{3,2,1,0:T(8,128)S(1)}, f32[8,2,16,128]{3,2,1,0:T(8,128)S(1)}, u32[]{:S(2)}, u32[]{:S(2)}) collective-permute-start(f32[8,2,16,128]{3,2,1,0:T(8,128)S(1)} %all_to_all.17), channel_id=1, source_target_pairs={{0,1},{1,0},{2,3},{3,2},{4,5},{5,4},{6,7},{7,6},{8,9},{9,8},{10,11... | collective-permute-start | bytes 393224 | tf_op jit(solution)/shard_map/ppermute | solution.py:692
  44.3 1.0 %collective-permute-done.2 = f32[8,2,16,128]{3,2,1,0:T(8,128)S(1)} collective-permute-done((f32[8,2,16,128]{3,2,1,0:T(8,128)S(1)}, f32[8,2,16,128]{3,2,1,0:T(8,128)S(1)}, u32[]{:S(2)}, u32[]{:S(2)}) %collective-permute-start.2) | collective-permute-done | bytes 131104 | tf_op jit(solution)/shard_map/ppermute | solution.py:692
  45.3 1.9 %design.1 = f32[2,16,128]{2,1,0:T(8,128)} custom-call(f32[2,8,2,16,128]{4,3,2,1,0:T(8,128)S(1)} %pad_maximum_fusion.1.root_ref, f32[2,8,2,16,128]{4,3,2,1,0:T(8,128)S(1)} %pad_maximum_fusion.density_ref), custom_call_target="tpu_custom_call" | custom-call | tf_op jit(solution)/shard_map/design/pallas_call | solution.py:679
  (6 shorter events, 0.1 us)
Async XLA Ops:
  0.6 16.0 %copy-start = (f32[1,3,32,16,128]{4,3,2,1,0:T(8,128)S(1)}, f32[1,3,32,16,128]{4,3,2,1,0:T(8,128)}, u32[]{:S(2)}) copy-start(f32[1,3,32,16,128]{4,3,2,1,0:T(8,128)} %param.7) | copy-start | bytes 2359300
  14.9 1.7 %collective-permute-start = (f32[8,2,16,128]{3,2,1,0:T(8,128)S(1)}, f32[8,2,16,128]{3,2,1,0:T(8,128)S(1)}, u32[]{:S(2)}, u32[]{:S(2)}) collective-permute-start(f32[8,2,16,128]{3,2,1,0:T(8,128)S(1)} %all_to_all.15.density_ref), channel_id=1, source_target_pairs={{0,1},{1,0},{2,3},{3,2},{4,5},{5,4},{6,7},{7,6},{8,9},{9,8},{10,11... | collective-permute-start | bytes 393224 | tf_op jit(solution)/shard_map/ppermute | solution.py:692
  22.4 1.4 %collective-permute-start.1 = (f32[8,2,16,128]{3,2,1,0:T(8,128)S(1)}, f32[8,2,16,128]{3,2,1,0:T(8,128)S(1)}, u32[]{:S(2)}, u32[]{:S(2)}) collective-permute-start(f32[8,2,16,128]{3,2,1,0:T(8,128)S(1)} %get-tuple-element.48), channel_id=1, source_target_pairs={{0,1},{1,0},{2,3},{3,2},{4,5},{5,4},{6,7},{7,6},{8,9},{9,8},{10,11... | collective-permute-start | bytes 393224 | tf_op jit(solution)/shard_map/ppermute | solution.py:692
  43.6 1.7 %collective-permute-start.2 = (f32[8,2,16,128]{3,2,1,0:T(8,128)S(1)}, f32[8,2,16,128]{3,2,1,0:T(8,128)S(1)}, u32[]{:S(2)}, u32[]{:S(2)}) collective-permute-start(f32[8,2,16,128]{3,2,1,0:T(8,128)S(1)} %all_to_all.17), channel_id=1, source_target_pairs={{0,1},{1,0},{2,3},{3,2},{4,5},{5,4},{6,7},{7,6},{8,9},{9,8},{10,11... | collective-permute-start | bytes 393224 | tf_op jit(solution)/shard_map/ppermute | solution.py:692

commit v23 on v22

--- a/solution.py
+++ b/solution.py
@@ -34,9 +34,8 @@
     return carry
 
 
-def each_half(planes, body, carry):
-    count = planes // 2
-    return lax.fori_loop(0, 2, lambda half, carry: body(half * count, count, carry), carry)
+def each_chunk(planes, count, body, carry):
+    return lax.fori_loop(0, planes // count, lambda i, carry: body(i * count, carry), carry)
 
 
 def layer_radius(radius_ref, layers, row_width):
@@ -297,7 +296,10 @@
             rate[part, slot] = factor
             source[part, rows(slot, layers)] = start[part] * free
 
-    def modulus_half(first, count, carry):
+    half = planes // 2
+
+    def modulus_half(first, carry):
+        count = half
         near = near_ref.at[pl.ds(first + 2, count)]
         side = side_ref.at[pl.ds(first + 1, count + 2)]
         far = far_ref.at[pl.ds(first, count + 4)]
@@ -338,7 +340,7 @@
             modulus, before = later, ahead
         return modulus, before
 
-    modulus, before = each_half(planes, modulus_half, (jnp.ones(shape, jnp.float32), zero))
+    modulus, before = each_chunk(planes, half, modulus_half, (jnp.ones(shape, jnp.float32), zero))
     store_faces(
         planes,
         modulus,
@@ -353,7 +355,8 @@
     own_x = jnp.max(spot_ref[...]).astype(jnp.int32)
 
     def sweep(source, target):
-        def sweep_half(first, count, carry):
+        def sweep_half(first, carry):
+            count = half
             old = source.at[:, pl.ds(first * layers, (count + 2) * layers)]
             new = target.at[:, pl.ds((first + 1) * layers, count * layers)]
             across = across_ref.at[pl.ds(first, count + 1)]
@@ -380,7 +383,7 @@
                 behind, here = here, ahead
             return carry
 
-        each_half(planes, sweep_half, 0)
+        each_chunk(planes, half, sweep_half, 0)
         for part in range(3):
             target[part, rows(own_x + 1, layers)] += rate_ref[part, own_x + 1] * load_ref[part]
 
@@ -457,28 +460,37 @@
     for ref in shares:
         zero_edges(ref)
 
-    before = zero
-    here = [disp_ref[part, rows(1, layers)] for part in range(3)]
-    for x in range(planes):
-        ahead, upward, right = zero, zero, zero
-        later = here
-        if x + 1 < planes:
-            later = [disp_ref[part, rows(x + 2, layers)] for part in range(3)]
-        for part in range(3):
-            step = later[part] - here[part]
-            climb = disp_ref[part, rows(x + 1, layers, 1)] - here[part]
-            slide = pltpu.roll(here[part], row_width - 1, 1) - here[part]
-            ahead = ahead + (2.0 if part == 0 else 1.0) * (step * step)
-            upward = upward + (2.0 if part == 1 else 1.0) * (climb * climb)
-            right = right + (2.0 if part == 2 else 1.0) * (slide * slide)
-        upward = jnp.where(z < layers - 1, upward, 0.0)
-        right = jnp.where(y < row_width - 1, right, 0.0)
-        total = before + ahead + upward + pltpu.roll(upward, 1, 0) + right + pltpu.roll(right, 1, 1)
-        share = (0.5 / load_cases) * total * coef_ref[x]
-        plane_ref[x + 2] = share
-        beside_ref[x + 2] = shift_sum(share, 1, 1)
-        further_ref[x + 2] = shift_sum(share, 1, 2)
-        before, here = ahead, later
+    count = planes // 4
+
+    def share_chunk(first, before):
+        disp = disp_ref.at[:, pl.ds((first + 1) * layers, (count + 1) * layers)]
+        coef = coef_ref.at[pl.ds(first, count)]
+        plane, beside, further = (ref.at[pl.ds(first + 2, count)] for ref in shares)
+        here = [disp[part, rows(0, layers)] for part in range(3)]
+        for p in range(count):
+            later = [disp[part, rows(p + 1, layers)] for part in range(3)]
+            ahead, upward, right = zero, zero, zero
+            for part in range(3):
+                step = later[part] - here[part]
+                climb = disp[part, rows(p, layers, 1)] - here[part]
+                slide = pltpu.roll(here[part], row_width - 1, 1) - here[part]
+                ahead = ahead + (2.0 if part == 0 else 1.0) * (step * step)
+                upward = upward + (2.0 if part == 1 else 1.0) * (climb * climb)
+                right = right + (2.0 if part == 2 else 1.0) * (slide * slide)
+            if p == count - 1:
+                ahead = jnp.where(first + count < planes, ahead, 0.0)
+            upward = jnp.where(z < layers - 1, upward, 0.0)
+            right = jnp.where(y < row_width - 1, right, 0.0)
+            total = before + ahead + upward + pltpu.roll(upward, 1, 0)
+            total = total + right + pltpu.roll(right, 1, 1)
+            share = (0.5 / load_cases) * total * coef[p]
+            plane[p] = share
+            beside[p] = shift_sum(share, 1, 1)
+            further[p] = shift_sum(share, 1, 2)
+            before, here = ahead, later
+        return before
+
+    each_chunk(planes, count, share_chunk, zero)
     filter_group(1, shares, weight_ref, near_ref, far_ref, sent_ref)
 
 

time: 47.6 us -> 46.1 us (0.968)
  Pallas kernels: 9.57 us -> 8.05 us
    pallas_call x1, Pallas kernels: 2.94 us -> 1.41 us  [share_call(): pl.pallas_call(share_kernel, out_shape=[floats(*group_shape)] + [floats(p...]
where the time goes in v23:
time: 46.1 us; the launch traced here: 45.6 us
  blocking collectives  33.1 us (72%)
  Pallas kernels  8.05 us (17%)
  starting transfers between devices  1.74 us (4%)
  waiting for transfers between devices  1.12 us (2%)
  local copies, waits for them, and re-layouts  0.82 us (2%)
  between operations  0.72 us (2%)
    all_to_all x3, blocking collectives, between_chips(): lax.all_to_all(pieces, 'space', 0, 0, axis_index_groups=chip_groups())  33.1 us
    pallas_call x1, Pallas kernels, sweep_call(): pl.pallas_call(sweep_kernel, out_shape=[floats(3, (planes + 2) * layers,...  2.87 us
    pallas_call x1, Pallas kernels, design_call(): pl.pallas_call(design_kernel, out_shape=floats(*density.shape[2:]), in_sp...  1.88 us
    ppermute x3, starting transfers between devices, other_core(): return lax.ppermute(block, 'space', [(i, i ^ 1) for i in range(devices)])  1.74 us
    pallas_call x1, Pallas kernels, share_call(): pl.pallas_call(share_kernel, out_shape=[floats(*group_shape)] + [floats(p...  1.41 us
    ppermute x3, waiting for transfers between devices, other_core(): return lax.ppermute(block, 'space', [(i, i ^ 1) for i in range(devices)])  1.12 us
    pallas_call x1, Pallas kernels, prepare_call(): pl.pallas_call(prepare_kernel, out_shape=[floats(len(ALL_SQUARES), layers...  1 us
  transfers between devices with their start and end apart: 3, of which 2 were waited for; matrix products, arithmetic and copies ran while one was open for 0% of the time, Pallas kernels for 4%

profile of v23, /device:TPU:0, one launch (start us, length us, event | category | flops | bytes accessed | tf_op | source)
XLA Modules:
  0.0 45.6 jit_solution(4748506645287173917)
XLA Ops:
  0.6 0.0 copy-start
  0.6 0.8 %broadcast_in_dim.4 = f32[8,2,16,128]{3,2,1,0:T(8,128)S(1)} broadcast(f32[2,16,128]{2,1,0:T(8,128)} %param.6), dimensions={1,2,3} | broadcast | bytes 147456 | tf_op jit(solution)/shard_map/broadcast_in_dim | solution.py:718
  1.4 13.5 %all_to_all.15.density_ref = f32[8,2,16,128]{3,2,1,0:T(8,128)S(1)} all-to-all(f32[8,2,16,128]{3,2,1,0:T(8,128)S(1)} %broadcast_in_dim.4), channel_id=1, replica_groups={{0,3,4,7,8,11,12,15},{1,2,5,6,9,10,13,14},{16,19,20,23,24,27,28,31},{17..., dimensions={0} | all-to-all | bytes 262144 | tf_op jit(solution)/shard_map/all_to_all | solution.py:713
  14.9 0.7 %collective-permute-start = (f32[8,2,16,128]{3,2,1,0:T(8,128)S(1)}, f32[8,2,16,128]{3,2,1,0:T(8,128)S(1)}, u32[]{:S(2)}, u32[]{:S(2)}) collective-permute-start(f32[8,2,16,128]{3,2,1,0:T(8,128)S(1)} %all_to_all.15.density_ref), channel_id=1, source_target_pairs={{0,1},{1,0},{2,3},{3,2},{4,5},{5,4},{6,7},{7,6},{8,9},{9,8},{10,11... | collective-permute-start | bytes 393224 | tf_op jit(solution)/shard_map/ppermute | solution.py:704
  15.6 1.0 %prepare.1 = (f32[10,16,128]{2,1,0:T(8,128)S(1)}, f32[5,16,128]{2,1,0:T(8,128)S(1)}, f32[32,16,128]{2,1,0:T(8,128)S(1)}, f32[3,16,128]{2,1,0:T(8,128)S(1)}, f32[...) custom-call(s32[16]{0:T(128)} %radius_hbm, s32[16]{0:T(128)} %index_hbm, f32[3,16]{1,0:T(4,128)} %bitcast.12, ...), custom_call_target="tpu_custom_call" | custom-call | flops 5242880 | bytes 524288 | tf_op jit(solution)/shard_map/prepare/pallas_call | solution.py:585
  16.6 0.0 collective-permute-done
  16.6 0.0 copy-done
  16.6 2.9 %sweeps.1 = (f32[3,544,128]{2,1,0:T(8,128)S(1)}, f32[32,16,128]{2,1,0:T(8,128)S(1)}) custom-call(f32[8,128]{1,0:T(8,128)S(1)} %get-tuple-element.31.spot_ref, f32[3,16,128]{2,1,0:T(8,128)S(1)} %get-tuple-element.32.load_ref, f32[10,16,128]{2,1,0:T(8,128)S(1)} %get-tuple-element.33.weight_ref, f32[5,16,128]{2,1,0:T(8,128)S(1)} %get-tuple-element.34.inverse_ref, ...), custom_call_target="tpu_custom_call" | custom-call | tf_op jit(solution)/shard_map/sweeps/pallas_call | solution.py:630
  19.5 1.4 %share.1 = (f32[8,2,16,128]{3,2,1,0:T(8,128)S(1)}, f32[36,16,128]{2,1,0:T(8,128)S(1)}, f32[36,16,128]{2,1,0:T(8,128)S(1)}, f32[36,16,128]{2,1,0:T(8,128)S(1)}) custom-call(f32[3,544,128]{2,1,0:T(8,128)S(1)} %get-tuple-element.43.disp_ref, f32[32,16,128]{2,1,0:T(8,128)S(1)} %get-tuple-element.38.coef_ref, f32[10,16,128]{2,1,0:T(8,128)S(1)} %get-tuple-element.33.weight_ref), custom_call_target="tpu_custom_call" | custom-call | tf_op jit(solution)/shard_map/share/pallas_call | solution.py:661
  20.9 0.4 collective-permute-start.1
  21.3 0.9 %kept.1 = (f32[3,512,128]{2,1,0:T(8,128)}, f32[8,2,16,128]{3,2,1,0:T(8,128)S(1)}) custom-call(f32[3,544,128]{2,1,0:T(8,128)S(1)} %get-tuple-element.43.disp_ref, f32[10,16,128]{2,1,0:T(8,128)S(1)} %get-tuple-element.33.weight_ref, f32[36,16,128]{2,1,0:T(8,128)S(1)} %get-tuple-element.44.plane_ref, f32[36,16,128]{2,1,0:T(8,128)S(1)} %get-tuple-element.45.beside_ref, ...), custom_call_target="tpu_custom_call" | custom-call | flops 4177920 | bytes 1671168 | tf_op jit(solution)/shard_map/kept/pallas_call | solution.py:676
  22.2 0.1 collective-permute-done.1
  22.4 10.0 %all_to_all.16 = f32[8,2,16,128]{3,2,1,0:T(8,128)S(1)} all-to-all(f32[8,2,16,128]{3,2,1,0:T(8,128)S(1)} %add.3), channel_id=1, replica_groups={{0,3,4,7,8,11,12,15},{1,2,5,6,9,10,13,14},{16,19,20,23,24,27,28,31},{17..., dimensions={0} | all-to-all | bytes 262144 | tf_op jit(solution)/shard_map/all_to_all | solution.py:713
  32.4 9.6 %all_to_all.17 = f32[8,2,16,128]{3,2,1,0:T(8,128)S(1)} all-to-all(f32[8,2,16,128]{3,2,1,0:T(8,128)S(1)} %broadcast_in_dim.5), channel_id=1, replica_groups={{0,3,4,7,8,11,12,15},{1,2,5,6,9,10,13,14},{16,19,20,23,24,27,28,31},{17..., dimensions={0} | all-to-all | bytes 262144 | tf_op jit(solution)/shard_map/all_to_all | solution.py:713
  42.1 0.7 %collective-permute-start.2 = (f32[8,2,16,128]{3,2,1,0:T(8,128)S(1)}, f32[8,2,16,128]{3,2,1,0:T(8,128)S(1)}, u32[]{:S(2)}, u32[]{:S(2)}) collective-permute-start(f32[8,2,16,128]{3,2,1,0:T(8,128)S(1)} %all_to_all.17), channel_id=1, source_target_pairs={{0,1},{1,0},{2,3},{3,2},{4,5},{5,4},{6,7},{7,6},{8,9},{9,8},{10,11... | collective-permute-start | bytes 393224 | tf_op jit(solution)/shard_map/ppermute | solution.py:704
  42.7 1.0 %collective-permute-done.2 = f32[8,2,16,128]{3,2,1,0:T(8,128)S(1)} collective-permute-done((f32[8,2,16,128]{3,2,1,0:T(8,128)S(1)}, f32[8,2,16,128]{3,2,1,0:T(8,128)S(1)}, u32[]{:S(2)}, u32[]{:S(2)}) %collective-permute-start.2) | collective-permute-done | bytes 131104 | tf_op jit(solution)/shard_map/ppermute | solution.py:704
  43.8 1.9 %design.1 = f32[2,16,128]{2,1,0:T(8,128)} custom-call(f32[2,8,2,16,128]{4,3,2,1,0:T(8,128)S(1)} %pad_maximum_fusion.1.root_ref, f32[2,8,2,16,128]{4,3,2,1,0:T(8,128)S(1)} %pad_maximum_fusion.density_ref), custom_call_target="tpu_custom_call" | custom-call | tf_op jit(solution)/shard_map/design/pallas_call | solution.py:691
  (6 shorter events, 0.1 us)
Async XLA Ops:
  0.6 16.0 %copy-start = (f32[1,3,32,16,128]{4,3,2,1,0:T(8,128)S(1)}, f32[1,3,32,16,128]{4,3,2,1,0:T(8,128)}, u32[]{:S(2)}) copy-start(f32[1,3,32,16,128]{4,3,2,1,0:T(8,128)} %param.7) | copy-start | bytes 2359300
  14.9 1.7 %collective-permute-start = (f32[8,2,16,128]{3,2,1,0:T(8,128)S(1)}, f32[8,2,16,128]{3,2,1,0:T(8,128)S(1)}, u32[]{:S(2)}, u32[]{:S(2)}) collective-permute-start(f32[8,2,16,128]{3,2,1,0:T(8,128)S(1)} %all_to_all.15.density_ref), channel_id=1, source_target_pairs={{0,1},{1,0},{2,3},{3,2},{4,5},{5,4},{6,7},{7,6},{8,9},{9,8},{10,11... | collective-permute-start | bytes 393224 | tf_op jit(solution)/shard_map/ppermute | solution.py:704
  20.9 1.4 %collective-permute-start.1 = (f32[8,2,16,128]{3,2,1,0:T(8,128)S(1)}, f32[8,2,16,128]{3,2,1,0:T(8,128)S(1)}, u32[]{:S(2)}, u32[]{:S(2)}) collective-permute-start(f32[8,2,16,128]{3,2,1,0:T(8,128)S(1)} %get-tuple-element.48), channel_id=1, source_target_pairs={{0,1},{1,0},{2,3},{3,2},{4,5},{5,4},{6,7},{7,6},{8,9},{9,8},{10,11... | collective-permute-start | bytes 393224 | tf_op jit(solution)/shard_map/ppermute | solution.py:704
  42.1 1.7 %collective-permute-start.2 = (f32[8,2,16,128]{3,2,1,0:T(8,128)S(1)}, f32[8,2,16,128]{3,2,1,0:T(8,128)S(1)}, u32[]{:S(2)}, u32[]{:S(2)}) collective-permute-start(f32[8,2,16,128]{3,2,1,0:T(8,128)S(1)} %all_to_all.17), channel_id=1, source_target_pairs={{0,1},{1,0},{2,3},{3,2},{4,5},{5,4},{6,7},{7,6},{8,9},{9,8},{10,11... | collective-permute-start | bytes 393224 | tf_op jit(solution)/shard_map/ppermute | solution.py:704

commit v24 on v23

--- a/solution.py
+++ b/solution.py
@@ -296,10 +296,10 @@
             rate[part, slot] = factor
             source[part, rows(slot, layers)] = start[part] * free
 
-    half = planes // 2
-
-    def modulus_half(first, carry):
-        count = half
+    piece = planes // 4
+
+    def modulus_piece(first, carry):
+        count = piece
         near = near_ref.at[pl.ds(first + 2, count)]
         side = side_ref.at[pl.ds(first + 1, count + 2)]
         far = far_ref.at[pl.ds(first, count + 4)]
@@ -340,7 +340,7 @@
             modulus, before = later, ahead
         return modulus, before
 
-    modulus, before = each_chunk(planes, half, modulus_half, (jnp.ones(shape, jnp.float32), zero))
+    modulus, before = each_chunk(planes, piece, modulus_piece, (jnp.ones(shape, jnp.float32), zero))
     store_faces(
         planes,
         modulus,
@@ -355,8 +355,8 @@
     own_x = jnp.max(spot_ref[...]).astype(jnp.int32)
 
     def sweep(source, target):
-        def sweep_half(first, carry):
-            count = half
+        def sweep_piece(first, carry):
+            count = piece
             old = source.at[:, pl.ds(first * layers, (count + 2) * layers)]
             new = target.at[:, pl.ds((first + 1) * layers, count * layers)]
             across = across_ref.at[pl.ds(first, count + 1)]
@@ -383,7 +383,7 @@
                 behind, here = here, ahead
             return carry
 
-        each_chunk(planes, half, sweep_half, 0)
+        each_chunk(planes, piece, sweep_piece, 0)
         for part in range(3):
             target[part, rows(own_x + 1, layers)] += rate_ref[part, own_x + 1] * load_ref[part]
 
@@ -460,7 +460,7 @@
     for ref in shares:
         zero_edges(ref)
 
-    count = planes // 4
+    count = planes // 8
 
     def share_chunk(first, before):
         disp = disp_ref.at[:, pl.ds((first + 1) * layers, (count + 1) * layers)]

time: 46.1 us -> 47.7 us (1.035)
  Pallas kernels: 8.05 us -> 9.62 us
    pallas_call x1, Pallas kernels: 1.41 us -> 2.27 us  [share_call(): pl.pallas_call(share_kernel, out_shape=[floats(*group_shape)] + [floats(p...]
    pallas_call x1, Pallas kernels: 2.87 us -> 3.58 us  [sweep_call(): pl.pallas_call(sweep_kernel, out_shape=[floats(3, (planes + 2) * layers,...]
where the time goes in v24:
time: 47.7 us; the launch traced here: 47.2 us
  blocking collectives  33.1 us (69%)
  Pallas kernels  9.62 us (20%)
  starting transfers between devices  1.75 us (4%)
  waiting for transfers between devices  1.11 us (2%)
  local copies, waits for them, and re-layouts  0.82 us (2%)
  between operations  0.72 us (2%)
    all_to_all x3, blocking collectives, between_chips(): lax.all_to_all(pieces, 'space', 0, 0, axis_index_groups=chip_groups())  33.1 us
    pallas_call x1, Pallas kernels, sweep_call(): pl.pallas_call(sweep_kernel, out_shape=[floats(3, (planes + 2) * layers,...  3.58 us
    pallas_call x1, Pallas kernels, share_call(): pl.pallas_call(share_kernel, out_shape=[floats(*group_shape)] + [floats(p...  2.27 us
    pallas_call x1, Pallas kernels, design_call(): pl.pallas_call(design_kernel, out_shape=floats(*density.shape[2:]), in_sp...  1.88 us
    ppermute x3, starting transfers between devices, other_core(): return lax.ppermute(block, 'space', [(i, i ^ 1) for i in range(devices)])  1.75 us
    ppermute x3, waiting for transfers between devices, other_core(): return lax.ppermute(block, 'space', [(i, i ^ 1) for i in range(devices)])  1.11 us
    pallas_call x1, Pallas kernels, prepare_call(): pl.pallas_call(prepare_kernel, out_shape=[floats(len(ALL_SQUARES), layers...  1 us
  transfers between devices with their start and end apart: 3, of which 2 were waited for; matrix products, arithmetic and copies ran while one was open for 0% of the time, Pallas kernels for 4%

profile of v24, /device:TPU:0, one launch (start us, length us, event | category | flops | bytes accessed | tf_op | source)
XLA Modules:
  0.0 47.2 jit_solution(13431153470752649361)
XLA Ops:
  0.6 0.0 copy-start
  0.6 0.8 %broadcast_in_dim.4 = f32[8,2,16,128]{3,2,1,0:T(8,128)S(1)} broadcast(f32[2,16,128]{2,1,0:T(8,128)} %param.6), dimensions={1,2,3} | broadcast | bytes 147456 | tf_op jit(solution)/shard_map/broadcast_in_dim | solution.py:718
  1.4 13.5 %all_to_all.15.density_ref = f32[8,2,16,128]{3,2,1,0:T(8,128)S(1)} all-to-all(f32[8,2,16,128]{3,2,1,0:T(8,128)S(1)} %broadcast_in_dim.4), channel_id=1, replica_groups={{0,3,4,7,8,11,12,15},{1,2,5,6,9,10,13,14},{16,19,20,23,24,27,28,31},{17..., dimensions={0} | all-to-all | bytes 262144 | tf_op jit(solution)/shard_map/all_to_all | solution.py:713
  14.9 0.7 %collective-permute-start = (f32[8,2,16,128]{3,2,1,0:T(8,128)S(1)}, f32[8,2,16,128]{3,2,1,0:T(8,128)S(1)}, u32[]{:S(2)}, u32[]{:S(2)}) collective-permute-start(f32[8,2,16,128]{3,2,1,0:T(8,128)S(1)} %all_to_all.15.density_ref), channel_id=1, source_target_pairs={{0,1},{1,0},{2,3},{3,2},{4,5},{5,4},{6,7},{7,6},{8,9},{9,8},{10,11... | collective-permute-start | bytes 393224 | tf_op jit(solution)/shard_map/ppermute | solution.py:704
  15.6 1.0 %prepare.1 = (f32[10,16,128]{2,1,0:T(8,128)S(1)}, f32[5,16,128]{2,1,0:T(8,128)S(1)}, f32[32,16,128]{2,1,0:T(8,128)S(1)}, f32[3,16,128]{2,1,0:T(8,128)S(1)}, f32[...) custom-call(s32[16]{0:T(128)} %radius_hbm, s32[16]{0:T(128)} %index_hbm, f32[3,16]{1,0:T(4,128)} %bitcast.12, ...), custom_call_target="tpu_custom_call" | custom-call | flops 5242880 | bytes 524288 | tf_op jit(solution)/shard_map/prepare/pallas_call | solution.py:585
  16.6 0.0 collective-permute-done
  16.6 0.0 copy-done
  16.6 3.6 %sweeps.1 = (f32[3,544,128]{2,1,0:T(8,128)S(1)}, f32[32,16,128]{2,1,0:T(8,128)S(1)}) custom-call(f32[8,128]{1,0:T(8,128)S(1)} %get-tuple-element.31.spot_ref, f32[3,16,128]{2,1,0:T(8,128)S(1)} %get-tuple-element.32.load_ref, f32[10,16,128]{2,1,0:T(8,128)S(1)} %get-tuple-element.33.weight_ref, f32[5,16,128]{2,1,0:T(8,128)S(1)} %get-tuple-element.34.inverse_ref, ...), custom_call_target="tpu_custom_call" | custom-call | tf_op jit(solution)/shard_map/sweeps/pallas_call | solution.py:630
  20.2 2.3 %share.1 = (f32[8,2,16,128]{3,2,1,0:T(8,128)S(1)}, f32[36,16,128]{2,1,0:T(8,128)S(1)}, f32[36,16,128]{2,1,0:T(8,128)S(1)}, f32[36,16,128]{2,1,0:T(8,128)S(1)}) custom-call(f32[3,544,128]{2,1,0:T(8,128)S(1)} %get-tuple-element.43.disp_ref, f32[32,16,128]{2,1,0:T(8,128)S(1)} %get-tuple-element.38.coef_ref, f32[10,16,128]{2,1,0:T(8,128)S(1)} %get-tuple-element.33.weight_ref), custom_call_target="tpu_custom_call" | custom-call | tf_op jit(solution)/shard_map/share/pallas_call | solution.py:661
  22.5 0.4 collective-permute-start.1
  22.9 0.9 %kept.1 = (f32[3,512,128]{2,1,0:T(8,128)}, f32[8,2,16,128]{3,2,1,0:T(8,128)S(1)}) custom-call(f32[3,544,128]{2,1,0:T(8,128)S(1)} %get-tuple-element.43.disp_ref, f32[10,16,128]{2,1,0:T(8,128)S(1)} %get-tuple-element.33.weight_ref, f32[36,16,128]{2,1,0:T(8,128)S(1)} %get-tuple-element.44.plane_ref, f32[36,16,128]{2,1,0:T(8,128)S(1)} %get-tuple-element.45.beside_ref, ...), custom_call_target="tpu_custom_call" | custom-call | flops 4177920 | bytes 1671168 | tf_op jit(solution)/shard_map/kept/pallas_call | solution.py:676
  23.8 0.1 collective-permute-done.1
  23.9 10.0 %all_to_all.16 = f32[8,2,16,128]{3,2,1,0:T(8,128)S(1)} all-to-all(f32[8,2,16,128]{3,2,1,0:T(8,128)S(1)} %add.3), channel_id=1, replica_groups={{0,3,4,7,8,11,12,15},{1,2,5,6,9,10,13,14},{16,19,20,23,24,27,28,31},{17..., dimensions={0} | all-to-all | bytes 262144 | tf_op jit(solution)/shard_map/all_to_all | solution.py:713
  34.0 9.6 %all_to_all.17 = f32[8,2,16,128]{3,2,1,0:T(8,128)S(1)} all-to-all(f32[8,2,16,128]{3,2,1,0:T(8,128)S(1)} %broadcast_in_dim.5), channel_id=1, replica_groups={{0,3,4,7,8,11,12,15},{1,2,5,6,9,10,13,14},{16,19,20,23,24,27,28,31},{17..., dimensions={0} | all-to-all | bytes 262144 | tf_op jit(solution)/shard_map/all_to_all | solution.py:713
  43.6 0.7 %collective-permute-start.2 = (f32[8,2,16,128]{3,2,1,0:T(8,128)S(1)}, f32[8,2,16,128]{3,2,1,0:T(8,128)S(1)}, u32[]{:S(2)}, u32[]{:S(2)}) collective-permute-start(f32[8,2,16,128]{3,2,1,0:T(8,128)S(1)} %all_to_all.17), channel_id=1, source_target_pairs={{0,1},{1,0},{2,3},{3,2},{4,5},{5,4},{6,7},{7,6},{8,9},{9,8},{10,11... | collective-permute-start | bytes 393224 | tf_op jit(solution)/shard_map/ppermute | solution.py:704
  44.3 1.0 %collective-permute-done.2 = f32[8,2,16,128]{3,2,1,0:T(8,128)S(1)} collective-permute-done((f32[8,2,16,128]{3,2,1,0:T(8,128)S(1)}, f32[8,2,16,128]{3,2,1,0:T(8,128)S(1)}, u32[]{:S(2)}, u32[]{:S(2)}) %collective-permute-start.2) | collective-permute-done | bytes 131104 | tf_op jit(solution)/shard_map/ppermute | solution.py:704
  45.3 1.9 %design.1 = f32[2,16,128]{2,1,0:T(8,128)} custom-call(f32[2,8,2,16,128]{4,3,2,1,0:T(8,128)S(1)} %pad_maximum_fusion.1.root_ref, f32[2,8,2,16,128]{4,3,2,1,0:T(8,128)S(1)} %pad_maximum_fusion.density_ref), custom_call_target="tpu_custom_call" | custom-call | tf_op jit(solution)/shard_map/design/pallas_call | solution.py:691
  (6 shorter events, 0.1 us)
Async XLA Ops:
  0.6 16.0 %copy-start = (f32[1,3,32,16,128]{4,3,2,1,0:T(8,128)S(1)}, f32[1,3,32,16,128]{4,3,2,1,0:T(8,128)}, u32[]{:S(2)}) copy-start(f32[1,3,32,16,128]{4,3,2,1,0:T(8,128)} %param.7) | copy-start | bytes 2359300
  14.9 1.7 %collective-permute-start = (f32[8,2,16,128]{3,2,1,0:T(8,128)S(1)}, f32[8,2,16,128]{3,2,1,0:T(8,128)S(1)}, u32[]{:S(2)}, u32[]{:S(2)}) collective-permute-start(f32[8,2,16,128]{3,2,1,0:T(8,128)S(1)} %all_to_all.15.density_ref), channel_id=1, source_target_pairs={{0,1},{1,0},{2,3},{3,2},{4,5},{5,4},{6,7},{7,6},{8,9},{9,8},{10,11... | collective-permute-start | bytes 393224 | tf_op jit(solution)/shard_map/ppermute | solution.py:704
  22.5 1.4 %collective-permute-start.1 = (f32[8,2,16,128]{3,2,1,0:T(8,128)S(1)}, f32[8,2,16,128]{3,2,1,0:T(8,128)S(1)}, u32[]{:S(2)}, u32[]{:S(2)}) collective-permute-start(f32[8,2,16,128]{3,2,1,0:T(8,128)S(1)} %get-tuple-element.48), channel_id=1, source_target_pairs={{0,1},{1,0},{2,3},{3,2},{4,5},{5,4},{6,7},{7,6},{8,9},{9,8},{10,11... | collective-permute-start | bytes 393224 | tf_op jit(solution)/shard_map/ppermute | solution.py:704
  43.6 1.7 %collective-permute-start.2 = (f32[8,2,16,128]{3,2,1,0:T(8,128)S(1)}, f32[8,2,16,128]{3,2,1,0:T(8,128)S(1)}, u32[]{:S(2)}, u32[]{:S(2)}) collective-permute-start(f32[8,2,16,128]{3,2,1,0:T(8,128)S(1)} %all_to_all.17), channel_id=1, source_target_pairs={{0,1},{1,0},{2,3},{3,2},{4,5},{5,4},{6,7},{7,6},{8,9},{9,8},{10,11... | collective-permute-start | bytes 393224 | tf_op jit(solution)/shard_map/ppermute | solution.py:704

commit v25 on v24

--- a/solution.py
+++ b/solution.py
@@ -296,7 +296,7 @@
             rate[part, slot] = factor
             source[part, rows(slot, layers)] = start[part] * free
 
-    piece = planes // 4
+    piece = planes // 2
 
     def modulus_piece(first, carry):
         count = piece
@@ -460,7 +460,7 @@
     for ref in shares:
         zero_edges(ref)
 
-    count = planes // 8
+    count = planes // 2
 
     def share_chunk(first, before):
         disp = disp_ref.at[:, pl.ds((first + 1) * layers, (count + 1) * layers)]

time: 47.7 us -> 45.9 us (0.962)
  Pallas kernels: 9.62 us -> 7.91 us
    pallas_call x1, Pallas kernels: 2.27 us -> 1.28 us  [share_call(): pl.pallas_call(share_kernel, out_shape=[floats(*group_shape)] + [floats(p...]
    pallas_call x1, Pallas kernels: 3.58 us -> 2.86 us  [sweep_call(): pl.pallas_call(sweep_kernel, out_shape=[floats(3, (planes + 2) * layers,...]
where the time goes in v25:
time: 45.9 us; the launch traced here: 45.5 us
  blocking collectives  33.1 us (72%)
  Pallas kernels  7.91 us (17%)
  starting transfers between devices  1.75 us (4%)
  waiting for transfers between devices  1.12 us (2%)
  local copies, waits for them, and re-layouts  0.82 us (2%)
  between operations  0.72 us (2%)
    all_to_all x3, blocking collectives, between_chips(): lax.all_to_all(pieces, 'space', 0, 0, axis_index_groups=chip_groups())  33.1 us
    pallas_call x1, Pallas kernels, sweep_call(): pl.pallas_call(sweep_kernel, out_shape=[floats(3, (planes + 2) * layers,...  2.86 us
    pallas_call x1, Pallas kernels, design_call(): pl.pallas_call(design_kernel, out_shape=floats(*density.shape[2:]), in_sp...  1.88 us
    ppermute x3, starting transfers between devices, other_core(): return lax.ppermute(block, 'space', [(i, i ^ 1) for i in range(devices)])  1.75 us
    pallas_call x1, Pallas kernels, share_call(): pl.pallas_call(share_kernel, out_shape=[floats(*group_shape)] + [floats(p...  1.28 us
    ppermute x3, waiting for transfers between devices, other_core(): return lax.ppermute(block, 'space', [(i, i ^ 1) for i in range(devices)])  1.12 us
    pallas_call x1, Pallas kernels, prepare_call(): pl.pallas_call(prepare_kernel, out_shape=[floats(len(ALL_SQUARES), layers...  1 us
  transfers between devices with their start and end apart: 3, of which 2 were waited for; matrix products, arithmetic and copies ran while one was open for 0% of the time, Pallas kernels for 4%

profile of v25, /device:TPU:0, one launch (start us, length us, event | category | flops | bytes accessed | tf_op | source)
XLA Modules:
  0.0 45.5 jit_solution(7781790166622076711)
XLA Ops:
  0.6 0.0 copy-start
  0.6 0.8 %broadcast_in_dim.4 = f32[8,2,16,128]{3,2,1,0:T(8,128)S(1)} broadcast(f32[2,16,128]{2,1,0:T(8,128)} %param.6), dimensions={1,2,3} | broadcast | bytes 147456 | tf_op jit(solution)/shard_map/broadcast_in_dim | solution.py:718
  1.4 13.5 %all_to_all.15.density_ref = f32[8,2,16,128]{3,2,1,0:T(8,128)S(1)} all-to-all(f32[8,2,16,128]{3,2,1,0:T(8,128)S(1)} %broadcast_in_dim.4), channel_id=1, replica_groups={{0,3,4,7,8,11,12,15},{1,2,5,6,9,10,13,14},{16,19,20,23,24,27,28,31},{17..., dimensions={0} | all-to-all | bytes 262144 | tf_op jit(solution)/shard_map/all_to_all | solution.py:713
  14.9 0.7 %collective-permute-start = (f32[8,2,16,128]{3,2,1,0:T(8,128)S(1)}, f32[8,2,16,128]{3,2,1,0:T(8,128)S(1)}, u32[]{:S(2)}, u32[]{:S(2)}) collective-permute-start(f32[8,2,16,128]{3,2,1,0:T(8,128)S(1)} %all_to_all.15.density_ref), channel_id=1, source_target_pairs={{0,1},{1,0},{2,3},{3,2},{4,5},{5,4},{6,7},{7,6},{8,9},{9,8},{10,11... | collective-permute-start | bytes 393224 | tf_op jit(solution)/shard_map/ppermute | solution.py:704
  15.6 1.0 %prepare.1 = (f32[10,16,128]{2,1,0:T(8,128)S(1)}, f32[5,16,128]{2,1,0:T(8,128)S(1)}, f32[32,16,128]{2,1,0:T(8,128)S(1)}, f32[3,16,128]{2,1,0:T(8,128)S(1)}, f32[...) custom-call(s32[16]{0:T(128)} %radius_hbm, s32[16]{0:T(128)} %index_hbm, f32[3,16]{1,0:T(4,128)} %bitcast.12, ...), custom_call_target="tpu_custom_call" | custom-call | flops 5242880 | bytes 524288 | tf_op jit(solution)/shard_map/prepare/pallas_call | solution.py:585
  16.6 0.0 collective-permute-done
  16.6 0.0 copy-done
  16.6 2.9 %sweeps.1 = (f32[3,544,128]{2,1,0:T(8,128)S(1)}, f32[32,16,128]{2,1,0:T(8,128)S(1)}) custom-call(f32[8,128]{1,0:T(8,128)S(1)} %get-tuple-element.31.spot_ref, f32[3,16,128]{2,1,0:T(8,128)S(1)} %get-tuple-element.32.load_ref, f32[10,16,128]{2,1,0:T(8,128)S(1)} %get-tuple-element.33.weight_ref, f32[5,16,128]{2,1,0:T(8,128)S(1)} %get-tuple-element.34.inverse_ref, ...), custom_call_target="tpu_custom_call" | custom-call | tf_op jit(solution)/shard_map/sweeps/pallas_call | solution.py:630
  19.5 1.3 %share.1 = (f32[8,2,16,128]{3,2,1,0:T(8,128)S(1)}, f32[36,16,128]{2,1,0:T(8,128)S(1)}, f32[36,16,128]{2,1,0:T(8,128)S(1)}, f32[36,16,128]{2,1,0:T(8,128)S(1)}) custom-call(f32[3,544,128]{2,1,0:T(8,128)S(1)} %get-tuple-element.43.disp_ref, f32[32,16,128]{2,1,0:T(8,128)S(1)} %get-tuple-element.38.coef_ref, f32[10,16,128]{2,1,0:T(8,128)S(1)} %get-tuple-element.33.weight_ref), custom_call_target="tpu_custom_call" | custom-call | tf_op jit(solution)/shard_map/share/pallas_call | solution.py:661
  20.8 0.4 collective-permute-start.1
  21.2 0.9 %kept.1 = (f32[3,512,128]{2,1,0:T(8,128)}, f32[8,2,16,128]{3,2,1,0:T(8,128)S(1)}) custom-call(f32[3,544,128]{2,1,0:T(8,128)S(1)} %get-tuple-element.43.disp_ref, f32[10,16,128]{2,1,0:T(8,128)S(1)} %get-tuple-element.33.weight_ref, f32[36,16,128]{2,1,0:T(8,128)S(1)} %get-tuple-element.44.plane_ref, f32[36,16,128]{2,1,0:T(8,128)S(1)} %get-tuple-element.45.beside_ref, ...), custom_call_target="tpu_custom_call" | custom-call | flops 4177920 | bytes 1671168 | tf_op jit(solution)/shard_map/kept/pallas_call | solution.py:676
  22.1 0.1 collective-permute-done.1
  22.2 10.0 %all_to_all.16 = f32[8,2,16,128]{3,2,1,0:T(8,128)S(1)} all-to-all(f32[8,2,16,128]{3,2,1,0:T(8,128)S(1)} %add.3), channel_id=1, replica_groups={{0,3,4,7,8,11,12,15},{1,2,5,6,9,10,13,14},{16,19,20,23,24,27,28,31},{17..., dimensions={0} | all-to-all | bytes 262144 | tf_op jit(solution)/shard_map/all_to_all | solution.py:713
  32.3 9.6 %all_to_all.17 = f32[8,2,16,128]{3,2,1,0:T(8,128)S(1)} all-to-all(f32[8,2,16,128]{3,2,1,0:T(8,128)S(1)} %broadcast_in_dim.5), channel_id=1, replica_groups={{0,3,4,7,8,11,12,15},{1,2,5,6,9,10,13,14},{16,19,20,23,24,27,28,31},{17..., dimensions={0} | all-to-all | bytes 262144 | tf_op jit(solution)/shard_map/all_to_all | solution.py:713
  41.9 0.7 %collective-permute-start.2 = (f32[8,2,16,128]{3,2,1,0:T(8,128)S(1)}, f32[8,2,16,128]{3,2,1,0:T(8,128)S(1)}, u32[]{:S(2)}, u32[]{:S(2)}) collective-permute-start(f32[8,2,16,128]{3,2,1,0:T(8,128)S(1)} %all_to_all.17), channel_id=1, source_target_pairs={{0,1},{1,0},{2,3},{3,2},{4,5},{5,4},{6,7},{7,6},{8,9},{9,8},{10,11... | collective-permute-start | bytes 393224 | tf_op jit(solution)/shard_map/ppermute | solution.py:704
  42.6 1.0 %collective-permute-done.2 = f32[8,2,16,128]{3,2,1,0:T(8,128)S(1)} collective-permute-done((f32[8,2,16,128]{3,2,1,0:T(8,128)S(1)}, f32[8,2,16,128]{3,2,1,0:T(8,128)S(1)}, u32[]{:S(2)}, u32[]{:S(2)}) %collective-permute-start.2) | collective-permute-done | bytes 131104 | tf_op jit(solution)/shard_map/ppermute | solution.py:704
  43.6 1.9 %design.1 = f32[2,16,128]{2,1,0:T(8,128)} custom-call(f32[2,8,2,16,128]{4,3,2,1,0:T(8,128)S(1)} %pad_maximum_fusion.1.root_ref, f32[2,8,2,16,128]{4,3,2,1,0:T(8,128)S(1)} %pad_maximum_fusion.density_ref), custom_call_target="tpu_custom_call" | custom-call | tf_op jit(solution)/shard_map/design/pallas_call | solution.py:691
  (6 shorter events, 0.1 us)
Async XLA Ops:
  0.6 16.0 %copy-start = (f32[1,3,32,16,128]{4,3,2,1,0:T(8,128)S(1)}, f32[1,3,32,16,128]{4,3,2,1,0:T(8,128)}, u32[]{:S(2)}) copy-start(f32[1,3,32,16,128]{4,3,2,1,0:T(8,128)} %param.7) | copy-start | bytes 2359300
  14.9 1.7 %collective-permute-start = (f32[8,2,16,128]{3,2,1,0:T(8,128)S(1)}, f32[8,2,16,128]{3,2,1,0:T(8,128)S(1)}, u32[]{:S(2)}, u32[]{:S(2)}) collective-permute-start(f32[8,2,16,128]{3,2,1,0:T(8,128)S(1)} %all_to_all.15.density_ref), channel_id=1, source_target_pairs={{0,1},{1,0},{2,3},{3,2},{4,5},{5,4},{6,7},{7,6},{8,9},{9,8},{10,11... | collective-permute-start | bytes 393224 | tf_op jit(solution)/shard_map/ppermute | solution.py:704
  20.8 1.4 %collective-permute-start.1 = (f32[8,2,16,128]{3,2,1,0:T(8,128)S(1)}, f32[8,2,16,128]{3,2,1,0:T(8,128)S(1)}, u32[]{:S(2)}, u32[]{:S(2)}) collective-permute-start(f32[8,2,16,128]{3,2,1,0:T(8,128)S(1)} %get-tuple-element.48), channel_id=1, source_target_pairs={{0,1},{1,0},{2,3},{3,2},{4,5},{5,4},{6,7},{7,6},{8,9},{9,8},{10,11... | collective-permute-start | bytes 393224 | tf_op jit(solution)/shard_map/ppermute | solution.py:704
  41.9 1.7 %collective-permute-start.2 = (f32[8,2,16,128]{3,2,1,0:T(8,128)S(1)}, f32[8,2,16,128]{3,2,1,0:T(8,128)S(1)}, u32[]{:S(2)}, u32[]{:S(2)}) collective-permute-start(f32[8,2,16,128]{3,2,1,0:T(8,128)S(1)} %all_to_all.17), channel_id=1, source_target_pairs={{0,1},{1,0},{2,3},{3,2},{4,5},{5,4},{6,7},{7,6},{8,9},{9,8},{10,11... | collective-permute-start | bytes 393224 | tf_op jit(solution)/shard_map/ppermute | solution.py:704

commit v26 on v25

--- a/solution.py
+++ b/solution.py
@@ -356,7 +356,7 @@
 
     def sweep(source, target):
         def sweep_piece(first, carry):
-            count = piece
+            count = planes
             old = source.at[:, pl.ds(first * layers, (count + 2) * layers)]
             new = target.at[:, pl.ds((first + 1) * layers, count * layers)]
             across = across_ref.at[pl.ds(first, count + 1)]
@@ -383,7 +383,7 @@
                 behind, here = here, ahead
             return carry
 
-        each_chunk(planes, piece, sweep_piece, 0)
+        sweep_piece(0, 0)
         for part in range(3):
             target[part, rows(own_x + 1, layers)] += rate_ref[part, own_x + 1] * load_ref[part]
 
@@ -576,6 +576,27 @@
 
 def floats(*shape):
     return jax.ShapeDtypeStruct(shape, jnp.float32)
+
+
+def spread_call(block, count):
+    def kernel(block_hbm, copies_ref, arrived):
+        copies = [
+            pltpu.make_async_copy(block_hbm, copies_ref.at[place], arrived.at[place])
+            for place in range(count)
+        ]
+        for copy in copies:
+            copy.start()
+        for copy in copies:
+            copy.wait()
+
+    return pl.pallas_call(
+        kernel,
+        out_shape=floats(count, *block.shape),
+        in_specs=[pl.BlockSpec(memory_space=pltpu.HBM)],
+        out_specs=in_vmem(),
+        scratch_shapes=[pltpu.SemaphoreType.DMA((count,))],
+        name="copies",
+    )(pltpu.with_memory_space_constraint(block, pltpu.HBM))
 
 
 def prepare_call(density, radius, load_index, load_force, fixed):
@@ -729,8 +750,9 @@
 
 
 def one_slab(density, displacement, fixed, load_index, load_force, radius):
+    chips = lax.axis_size("space") // 2
     same_group, small = lax.optimization_barrier(
-        (chip_gathered(density), (radius, load_index, load_force.T, fixed))
+        (between_chips(spread_call(density, chips)), (radius, load_index, load_force.T, fixed))
     )
     other_group = other_core(same_group)
     weights, inverses, free, load, spot, filtered = prepare_call(same_group, *small)

time: 45.9 us -> 46.9 us (1.022)
  Pallas kernels: 7.91 us -> 9.35 us
  local copies, waits for them, and re-layouts: 0.82 us -> 0.02 us
    pallas_call x0 -> x1, Pallas kernels: none -> 1.73 us  [spread_call(): pl.pallas_call(kernel, out_shape=floats(count, *block.shape), in_specs=[p...]
    broadcast_in_dim x2 -> x1, local copies, waits for them, and re-layouts: 0.81 us -> 0.01 us  [chip_gathered(): return between_chips(jnp.broadcast_to(block[None], (chips,) + block.shape))]
where the time goes in v26:
time: 46.9 us; the launch traced here: 46.4 us
  blocking collectives  33.3 us (71%)
  Pallas kernels  9.35 us (20%)
  starting transfers between devices  1.75 us (4%)
  waiting for transfers between devices  1.12 us (2%)
  between operations  0.72 us (2%)
    all_to_all x3, blocking collectives, between_chips(): lax.all_to_all(pieces, 'space', 0, 0, axis_index_groups=chip_groups())  33.3 us
    pallas_call x1, Pallas kernels, sweep_call(): pl.pallas_call(sweep_kernel, out_shape=[floats(3, (planes + 2) * layers,...  2.56 us
    pallas_call x1, Pallas kernels, design_call(): pl.pallas_call(design_kernel, out_shape=floats(*density.shape[2:]), in_sp...  1.88 us
    ppermute x3, starting transfers between devices, other_core(): return lax.ppermute(block, 'space', [(i, i ^ 1) for i in range(devices)])  1.75 us
    pallas_call x1, Pallas kernels, spread_call(): pl.pallas_call(kernel, out_shape=floats(count, *block.shape), in_specs=[p...  1.73 us
    pallas_call x1, Pallas kernels, share_call(): pl.pallas_call(share_kernel, out_shape=[floats(*group_shape)] + [floats(p...  1.29 us
    ppermute x3, waiting for transfers between devices, other_core(): return lax.ppermute(block, 'space', [(i, i ^ 1) for i in range(devices)])  1.12 us
    pallas_call x1, Pallas kernels, prepare_call(): pl.pallas_call(prepare_kernel, out_shape=[floats(len(ALL_SQUARES), layers...  1 us
  transfers between devices with their start and end apart: 3, of which 2 were waited for; matrix products, arithmetic and copies ran while one was open for 0% of the time, Pallas kernels for 4%

profile of v26, /device:TPU:0, one launch (start us, length us, event | category | flops | bytes accessed | tf_op | source)
XLA Modules:
  0.0 46.4 jit_solution(16015821514134045158)
XLA Ops:
  0.6 0.0 copy-start
  0.6 1.7 %copies.1 = f32[8,2,16,128]{3,2,1,0:T(8,128)} custom-call(f32[2,16,128]{2,1,0:T(8,128)} %block_hbm.1), custom_call_target="tpu_custom_call" | custom-call | tf_op jit(solution)/shard_map/copies/pallas_call | solution.py:592
  2.4 13.7 %all_to_all.15.density_ref = f32[8,2,16,128]{3,2,1,0:T(8,128)S(1)} all-to-all(f32[8,2,16,128]{3,2,1,0:T(8,128)} %copies.1), channel_id=1, replica_groups={{0,3,4,7,8,11,12,15},{1,2,5,6,9,10,13,14},{16,19,20,23,24,27,28,31},{17..., dimensions={0} | all-to-all | bytes 262144 | tf_op jit(solution)/shard_map/all_to_all | solution.py:734
  16.0 0.7 %collective-permute-start = (f32[8,2,16,128]{3,2,1,0:T(8,128)S(1)}, f32[8,2,16,128]{3,2,1,0:T(8,128)S(1)}, u32[]{:S(2)}, u32[]{:S(2)}) collective-permute-start(f32[8,2,16,128]{3,2,1,0:T(8,128)S(1)} %all_to_all.15.density_ref), channel_id=1, source_target_pairs={{0,1},{1,0},{2,3},{3,2},{4,5},{5,4},{6,7},{7,6},{8,9},{9,8},{10,11... | collective-permute-start | bytes 393224 | tf_op jit(solution)/shard_map/ppermute | solution.py:725
  16.7 1.0 %prepare.1 = (f32[10,16,128]{2,1,0:T(8,128)S(1)}, f32[5,16,128]{2,1,0:T(8,128)S(1)}, f32[32,16,128]{2,1,0:T(8,128)S(1)}, f32[3,16,128]{2,1,0:T(8,128)S(1)}, f32[...) custom-call(s32[16]{0:T(128)} %radius_hbm, s32[16]{0:T(128)} %index_hbm, f32[3,16]{1,0:T(4,128)} %bitcast.12, ...), custom_call_target="tpu_custom_call" | custom-call | flops 5242880 | bytes 524288 | tf_op jit(solution)/shard_map/prepare/pallas_call | solution.py:606
  17.7 0.0 collective-permute-done
  17.8 0.0 copy-done
  17.8 2.6 %sweeps.1 = (f32[3,544,128]{2,1,0:T(8,128)S(1)}, f32[32,16,128]{2,1,0:T(8,128)S(1)}) custom-call(f32[8,128]{1,0:T(8,128)S(1)} %get-tuple-element.31.spot_ref, f32[3,16,128]{2,1,0:T(8,128)S(1)} %get-tuple-element.32.load_ref, f32[10,16,128]{2,1,0:T(8,128)S(1)} %get-tuple-element.33.weight_ref, f32[5,16,128]{2,1,0:T(8,128)S(1)} %get-tuple-element.34.inverse_ref, ...), custom_call_target="tpu_custom_call" | custom-call | tf_op jit(solution)/shard_map/sweeps/pallas_call | solution.py:651
  20.3 1.3 %share.1 = (f32[8,2,16,128]{3,2,1,0:T(8,128)S(1)}, f32[36,16,128]{2,1,0:T(8,128)S(1)}, f32[36,16,128]{2,1,0:T(8,128)S(1)}, f32[36,16,128]{2,1,0:T(8,128)S(1)}) custom-call(f32[3,544,128]{2,1,0:T(8,128)S(1)} %get-tuple-element.43.disp_ref, f32[32,16,128]{2,1,0:T(8,128)S(1)} %get-tuple-element.38.coef_ref, f32[10,16,128]{2,1,0:T(8,128)S(1)} %get-tuple-element.33.weight_ref), custom_call_target="tpu_custom_call" | custom-call | tf_op jit(solution)/shard_map/share/pallas_call | solution.py:682
  21.6 0.4 collective-permute-start.1
  22.0 0.9 %kept.1 = (f32[3,512,128]{2,1,0:T(8,128)}, f32[8,2,16,128]{3,2,1,0:T(8,128)S(1)}) custom-call(f32[3,544,128]{2,1,0:T(8,128)S(1)} %get-tuple-element.43.disp_ref, f32[10,16,128]{2,1,0:T(8,128)S(1)} %get-tuple-element.33.weight_ref, f32[36,16,128]{2,1,0:T(8,128)S(1)} %get-tuple-element.44.plane_ref, f32[36,16,128]{2,1,0:T(8,128)S(1)} %get-tuple-element.45.beside_ref, ...), custom_call_target="tpu_custom_call" | custom-call | flops 4177920 | bytes 1671168 | tf_op jit(solution)/shard_map/kept/pallas_call | solution.py:697
  22.9 0.1 collective-permute-done.1
  23.1 10.0 %all_to_all.16 = f32[8,2,16,128]{3,2,1,0:T(8,128)S(1)} all-to-all(f32[8,2,16,128]{3,2,1,0:T(8,128)S(1)} %add.3), channel_id=1, replica_groups={{0,3,4,7,8,11,12,15},{1,2,5,6,9,10,13,14},{16,19,20,23,24,27,28,31},{17..., dimensions={0} | all-to-all | bytes 262144 | tf_op jit(solution)/shard_map/all_to_all | solution.py:734
  33.1 9.6 %all_to_all.17 = f32[8,2,16,128]{3,2,1,0:T(8,128)S(1)} all-to-all(f32[8,2,16,128]{3,2,1,0:T(8,128)S(1)} %broadcast_in_dim.2), channel_id=1, replica_groups={{0,3,4,7,8,11,12,15},{1,2,5,6,9,10,13,14},{16,19,20,23,24,27,28,31},{17..., dimensions={0} | all-to-all | bytes 262144 | tf_op jit(solution)/shard_map/all_to_all | solution.py:734
  42.8 0.7 %collective-permute-start.2 = (f32[8,2,16,128]{3,2,1,0:T(8,128)S(1)}, f32[8,2,16,128]{3,2,1,0:T(8,128)S(1)}, u32[]{:S(2)}, u32[]{:S(2)}) collective-permute-start(f32[8,2,16,128]{3,2,1,0:T(8,128)S(1)} %all_to_all.17), channel_id=1, source_target_pairs={{0,1},{1,0},{2,3},{3,2},{4,5},{5,4},{6,7},{7,6},{8,9},{9,8},{10,11... | collective-permute-start | bytes 393224 | tf_op jit(solution)/shard_map/ppermute | solution.py:725
  43.5 1.0 %collective-permute-done.2 = f32[8,2,16,128]{3,2,1,0:T(8,128)S(1)} collective-permute-done((f32[8,2,16,128]{3,2,1,0:T(8,128)S(1)}, f32[8,2,16,128]{3,2,1,0:T(8,128)S(1)}, u32[]{:S(2)}, u32[]{:S(2)}) %collective-permute-start.2) | collective-permute-done | bytes 131104 | tf_op jit(solution)/shard_map/ppermute | solution.py:725
  44.5 1.9 %design.1 = f32[2,16,128]{2,1,0:T(8,128)} custom-call(f32[2,8,2,16,128]{4,3,2,1,0:T(8,128)S(1)} %pad_maximum_fusion.1.root_ref, f32[2,8,2,16,128]{4,3,2,1,0:T(8,128)S(1)} %pad_maximum_fusion.density_ref), custom_call_target="tpu_custom_call" | custom-call | tf_op jit(solution)/shard_map/design/pallas_call | solution.py:712
  (6 shorter events, 0.1 us)
Async XLA Ops:
  0.6 17.1 %copy-start = (f32[1,3,32,16,128]{4,3,2,1,0:T(8,128)S(1)}, f32[1,3,32,16,128]{4,3,2,1,0:T(8,128)}, u32[]{:S(2)}) copy-start(f32[1,3,32,16,128]{4,3,2,1,0:T(8,128)} %param.7) | copy-start | bytes 2359300
  16.0 1.7 %collective-permute-start = (f32[8,2,16,128]{3,2,1,0:T(8,128)S(1)}, f32[8,2,16,128]{3,2,1,0:T(8,128)S(1)}, u32[]{:S(2)}, u32[]{:S(2)}) collective-permute-start(f32[8,2,16,128]{3,2,1,0:T(8,128)S(1)} %all_to_all.15.density_ref), channel_id=1, source_target_pairs={{0,1},{1,0},{2,3},{3,2},{4,5},{5,4},{6,7},{7,6},{8,9},{9,8},{10,11... | collective-permute-start | bytes 393224 | tf_op jit(solution)/shard_map/ppermute | solution.py:725
  21.6 1.4 %collective-permute-start.1 = (f32[8,2,16,128]{3,2,1,0:T(8,128)S(1)}, f32[8,2,16,128]{3,2,1,0:T(8,128)S(1)}, u32[]{:S(2)}, u32[]{:S(2)}) collective-permute-start(f32[8,2,16,128]{3,2,1,0:T(8,128)S(1)} %get-tuple-element.48), channel_id=1, source_target_pairs={{0,1},{1,0},{2,3},{3,2},{4,5},{5,4},{6,7},{7,6},{8,9},{9,8},{10,11... | collective-permute-start | bytes 393224 | tf_op jit(solution)/shard_map/ppermute | solution.py:725
  42.8 1.7 %collective-permute-start.2 = (f32[8,2,16,128]{3,2,1,0:T(8,128)S(1)}, f32[8,2,16,128]{3,2,1,0:T(8,128)S(1)}, u32[]{:S(2)}, u32[]{:S(2)}) collective-permute-start(f32[8,2,16,128]{3,2,1,0:T(8,128)S(1)} %all_to_all.17), channel_id=1, source_target_pairs={{0,1},{1,0},{2,3},{3,2},{4,5},{5,4},{6,7},{7,6},{8,9},{9,8},{10,11... | collective-permute-start | bytes 393224 | tf_op jit(solution)/shard_map/ppermute | solution.py:725

commit v27 on v25

--- a/solution.py
+++ b/solution.py
@@ -296,10 +296,8 @@
             rate[part, slot] = factor
             source[part, rows(slot, layers)] = start[part] * free
 
-    piece = planes // 2
-
     def modulus_piece(first, carry):
-        count = piece
+        count = planes
         near = near_ref.at[pl.ds(first + 2, count)]
         side = side_ref.at[pl.ds(first + 1, count + 2)]
         far = far_ref.at[pl.ds(first, count + 4)]
@@ -340,7 +338,7 @@
             modulus, before = later, ahead
         return modulus, before
 
-    modulus, before = each_chunk(planes, piece, modulus_piece, (jnp.ones(shape, jnp.float32), zero))
+    modulus, before = each_chunk(planes, planes, modulus_piece, (jnp.ones(shape, jnp.float32), zero))
     store_faces(
         planes,
         modulus,
@@ -356,7 +354,7 @@
 
     def sweep(source, target):
         def sweep_piece(first, carry):
-            count = piece
+            count = planes
             old = source.at[:, pl.ds(first * layers, (count + 2) * layers)]
             new = target.at[:, pl.ds((first + 1) * layers, count * layers)]
             across = across_ref.at[pl.ds(first, count + 1)]
@@ -383,7 +381,7 @@
                 behind, here = here, ahead
             return carry
 
-        each_chunk(planes, piece, sweep_piece, 0)
+        sweep_piece(0, 0)
         for part in range(3):
             target[part, rows(own_x + 1, layers)] += rate_ref[part, own_x + 1] * load_ref[part]
 

time: 45.9 us -> 45.8 us (level)
  no operation moved by 1% of the time
where the time goes in v27:
time: 45.8 us; the launch traced here: 45.4 us
  blocking collectives  33.1 us (72%)
  Pallas kernels  7.78 us (17%)
  starting transfers between devices  1.76 us (4%)
  waiting for transfers between devices  1.11 us (2%)
  local copies, waits for them, and re-layouts  0.82 us (2%)
  between operations  0.72 us (2%)
    all_to_all x3, blocking collectives, between_chips(): lax.all_to_all(pieces, 'space', 0, 0, axis_index_groups=chip_groups())  33.1 us
    pallas_call x1, Pallas kernels, sweep_call(): pl.pallas_call(sweep_kernel, out_shape=[floats(3, (planes + 2) * layers,...  2.73 us
    pallas_call x1, Pallas kernels, design_call(): pl.pallas_call(design_kernel, out_shape=floats(*density.shape[2:]), in_sp...  1.88 us
    ppermute x3, starting transfers between devices, other_core(): return lax.ppermute(block, 'space', [(i, i ^ 1) for i in range(devices)])  1.76 us
    pallas_call x1, Pallas kernels, share_call(): pl.pallas_call(share_kernel, out_shape=[floats(*group_shape)] + [floats(p...  1.28 us
    ppermute x3, waiting for transfers between devices, other_core(): return lax.ppermute(block, 'space', [(i, i ^ 1) for i in range(devices)])  1.11 us
    pallas_call x1, Pallas kernels, prepare_call(): pl.pallas_call(prepare_kernel, out_shape=[floats(len(ALL_SQUARES), layers...  1 us
  transfers between devices with their start and end apart: 3, of which 2 were waited for; matrix products, arithmetic and copies ran while one was open for 0% of the time, Pallas kernels for 4%

profile of v27, /device:TPU:0, one launch (start us, length us, event | category | flops | bytes accessed | tf_op | source)
XLA Modules:
  0.0 45.4 jit_solution(9114910302877851142)
XLA Ops:
  0.6 0.0 copy-start
  0.6 0.8 %broadcast_in_dim.4 = f32[8,2,16,128]{3,2,1,0:T(8,128)S(1)} broadcast(f32[2,16,128]{2,1,0:T(8,128)} %param.6), dimensions={1,2,3} | broadcast | bytes 147456 | tf_op jit(solution)/shard_map/broadcast_in_dim | solution.py:716
  1.4 13.5 %all_to_all.15.density_ref = f32[8,2,16,128]{3,2,1,0:T(8,128)S(1)} all-to-all(f32[8,2,16,128]{3,2,1,0:T(8,128)S(1)} %broadcast_in_dim.4), channel_id=1, replica_groups={{0,3,4,7,8,11,12,15},{1,2,5,6,9,10,13,14},{16,19,20,23,24,27,28,31},{17..., dimensions={0} | all-to-all | bytes 262144 | tf_op jit(solution)/shard_map/all_to_all | solution.py:711
  14.9 0.7 %collective-permute-start = (f32[8,2,16,128]{3,2,1,0:T(8,128)S(1)}, f32[8,2,16,128]{3,2,1,0:T(8,128)S(1)}, u32[]{:S(2)}, u32[]{:S(2)}) collective-permute-start(f32[8,2,16,128]{3,2,1,0:T(8,128)S(1)} %all_to_all.15.density_ref), channel_id=1, source_target_pairs={{0,1},{1,0},{2,3},{3,2},{4,5},{5,4},{6,7},{7,6},{8,9},{9,8},{10,11... | collective-permute-start | bytes 393224 | tf_op jit(solution)/shard_map/ppermute | solution.py:702
  15.6 1.0 %prepare.1 = (f32[10,16,128]{2,1,0:T(8,128)S(1)}, f32[5,16,128]{2,1,0:T(8,128)S(1)}, f32[32,16,128]{2,1,0:T(8,128)S(1)}, f32[3,16,128]{2,1,0:T(8,128)S(1)}, f32[...) custom-call(s32[16]{0:T(128)} %radius_hbm, s32[16]{0:T(128)} %index_hbm, f32[3,16]{1,0:T(4,128)} %bitcast.12, ...), custom_call_target="tpu_custom_call" | custom-call | flops 5242880 | bytes 524288 | tf_op jit(solution)/shard_map/prepare/pallas_call | solution.py:583
  16.6 0.0 collective-permute-done
  16.6 0.0 copy-done
  16.6 2.7 %sweeps.1 = (f32[3,544,128]{2,1,0:T(8,128)S(1)}, f32[32,16,128]{2,1,0:T(8,128)S(1)}) custom-call(f32[8,128]{1,0:T(8,128)S(1)} %get-tuple-element.31.spot_ref, f32[3,16,128]{2,1,0:T(8,128)S(1)} %get-tuple-element.32.load_ref, f32[10,16,128]{2,1,0:T(8,128)S(1)} %get-tuple-element.33.weight_ref, f32[5,16,128]{2,1,0:T(8,128)S(1)} %get-tuple-element.34.inverse_ref, ...), custom_call_target="tpu_custom_call" | custom-call | tf_op jit(solution)/shard_map/sweeps/pallas_call | solution.py:628
  19.4 1.3 %share.1 = (f32[8,2,16,128]{3,2,1,0:T(8,128)S(1)}, f32[36,16,128]{2,1,0:T(8,128)S(1)}, f32[36,16,128]{2,1,0:T(8,128)S(1)}, f32[36,16,128]{2,1,0:T(8,128)S(1)}) custom-call(f32[3,544,128]{2,1,0:T(8,128)S(1)} %get-tuple-element.43.disp_ref, f32[32,16,128]{2,1,0:T(8,128)S(1)} %get-tuple-element.38.coef_ref, f32[10,16,128]{2,1,0:T(8,128)S(1)} %get-tuple-element.33.weight_ref), custom_call_target="tpu_custom_call" | custom-call | tf_op jit(solution)/shard_map/share/pallas_call | solution.py:659
  20.6 0.4 collective-permute-start.1
  21.0 0.9 %kept.1 = (f32[3,512,128]{2,1,0:T(8,128)}, f32[8,2,16,128]{3,2,1,0:T(8,128)S(1)}) custom-call(f32[3,544,128]{2,1,0:T(8,128)S(1)} %get-tuple-element.43.disp_ref, f32[10,16,128]{2,1,0:T(8,128)S(1)} %get-tuple-element.33.weight_ref, f32[36,16,128]{2,1,0:T(8,128)S(1)} %get-tuple-element.44.plane_ref, f32[36,16,128]{2,1,0:T(8,128)S(1)} %get-tuple-element.45.beside_ref, ...), custom_call_target="tpu_custom_call" | custom-call | flops 4177920 | bytes 1671168 | tf_op jit(solution)/shard_map/kept/pallas_call | solution.py:674
  21.9 0.1 collective-permute-done.1
  22.1 10.0 %all_to_all.16 = f32[8,2,16,128]{3,2,1,0:T(8,128)S(1)} all-to-all(f32[8,2,16,128]{3,2,1,0:T(8,128)S(1)} %add.3), channel_id=1, replica_groups={{0,3,4,7,8,11,12,15},{1,2,5,6,9,10,13,14},{16,19,20,23,24,27,28,31},{17..., dimensions={0} | all-to-all | bytes 262144 | tf_op jit(solution)/shard_map/all_to_all | solution.py:711
  32.1 9.6 %all_to_all.17 = f32[8,2,16,128]{3,2,1,0:T(8,128)S(1)} all-to-all(f32[8,2,16,128]{3,2,1,0:T(8,128)S(1)} %broadcast_in_dim.5), channel_id=1, replica_groups={{0,3,4,7,8,11,12,15},{1,2,5,6,9,10,13,14},{16,19,20,23,24,27,28,31},{17..., dimensions={0} | all-to-all | bytes 262144 | tf_op jit(solution)/shard_map/all_to_all | solution.py:711
  41.8 0.7 %collective-permute-start.2 = (f32[8,2,16,128]{3,2,1,0:T(8,128)S(1)}, f32[8,2,16,128]{3,2,1,0:T(8,128)S(1)}, u32[]{:S(2)}, u32[]{:S(2)}) collective-permute-start(f32[8,2,16,128]{3,2,1,0:T(8,128)S(1)} %all_to_all.17), channel_id=1, source_target_pairs={{0,1},{1,0},{2,3},{3,2},{4,5},{5,4},{6,7},{7,6},{8,9},{9,8},{10,11... | collective-permute-start | bytes 393224 | tf_op jit(solution)/shard_map/ppermute | solution.py:702
  42.5 1.0 %collective-permute-done.2 = f32[8,2,16,128]{3,2,1,0:T(8,128)S(1)} collective-permute-done((f32[8,2,16,128]{3,2,1,0:T(8,128)S(1)}, f32[8,2,16,128]{3,2,1,0:T(8,128)S(1)}, u32[]{:S(2)}, u32[]{:S(2)}) %collective-permute-start.2) | collective-permute-done | bytes 131104 | tf_op jit(solution)/shard_map/ppermute | solution.py:702
  43.5 1.9 %design.1 = f32[2,16,128]{2,1,0:T(8,128)} custom-call(f32[2,8,2,16,128]{4,3,2,1,0:T(8,128)S(1)} %pad_maximum_fusion.1.root_ref, f32[2,8,2,16,128]{4,3,2,1,0:T(8,128)S(1)} %pad_maximum_fusion.density_ref), custom_call_target="tpu_custom_call" | custom-call | tf_op jit(solution)/shard_map/design/pallas_call | solution.py:689
  (6 shorter events, 0.1 us)
Async XLA Ops:
  0.6 16.0 %copy-start = (f32[1,3,32,16,128]{4,3,2,1,0:T(8,128)S(1)}, f32[1,3,32,16,128]{4,3,2,1,0:T(8,128)}, u32[]{:S(2)}) copy-start(f32[1,3,32,16,128]{4,3,2,1,0:T(8,128)} %param.7) | copy-start | bytes 2359300
  14.9 1.7 %collective-permute-start = (f32[8,2,16,128]{3,2,1,0:T(8,128)S(1)}, f32[8,2,16,128]{3,2,1,0:T(8,128)S(1)}, u32[]{:S(2)}, u32[]{:S(2)}) collective-permute-start(f32[8,2,16,128]{3,2,1,0:T(8,128)S(1)} %all_to_all.15.density_ref), channel_id=1, source_target_pairs={{0,1},{1,0},{2,3},{3,2},{4,5},{5,4},{6,7},{7,6},{8,9},{9,8},{10,11... | collective-permute-start | bytes 393224 | tf_op jit(solution)/shard_map/ppermute | solution.py:702
  20.6 1.4 %collective-permute-start.1 = (f32[8,2,16,128]{3,2,1,0:T(8,128)S(1)}, f32[8,2,16,128]{3,2,1,0:T(8,128)S(1)}, u32[]{:S(2)}, u32[]{:S(2)}) collective-permute-start(f32[8,2,16,128]{3,2,1,0:T(8,128)S(1)} %get-tuple-element.48), channel_id=1, source_target_pairs={{0,1},{1,0},{2,3},{3,2},{4,5},{5,4},{6,7},{7,6},{8,9},{9,8},{10,11... | collective-permute-start | bytes 393224 | tf_op jit(solution)/shard_map/ppermute | solution.py:702
  41.8 1.7 %collective-permute-start.2 = (f32[8,2,16,128]{3,2,1,0:T(8,128)S(1)}, f32[8,2,16,128]{3,2,1,0:T(8,128)S(1)}, u32[]{:S(2)}, u32[]{:S(2)}) collective-permute-start(f32[8,2,16,128]{3,2,1,0:T(8,128)S(1)} %all_to_all.17), channel_id=1, source_target_pairs={{0,1},{1,0},{2,3},{3,2},{4,5},{5,4},{6,7},{7,6},{8,9},{9,8},{10,11... | collective-permute-start | bytes 393224 | tf_op jit(solution)/shard_map/ppermute | solution.py:702

commit v28 on v27

--- a/solution.py
+++ b/solution.py
@@ -275,18 +275,19 @@
             ref[part, rows(0, layers)] = zero
             ref[part, rows(planes + 1, layers)] = zero
 
-    def store_faces(slot, modulus, above, later, before, free, start, views):
+    def store_faces(slot, modulus, above, below, later, before, free, start, views):
         across, up_view, right_view, left_view, rate, source = views
         across[slot] = later
         up = jnp.where(z < layers - 1, 0.5 * (modulus + above), 0.0)
         right = jnp.where(
             y < row_width - 1, 0.5 * (modulus + pltpu.roll(modulus, row_width - 1, 1)), 0.0
         )
-        left = pltpu.roll(right, 1, 1)
+        left = jnp.where(y > 0, 0.5 * (modulus + pltpu.roll(modulus, 1, 1)), 0.0)
+        down = jnp.where(z > 0, 0.5 * (modulus + below), 0.0)
         up_view[rows(slot, layers)] = up
         right_view[slot] = right
         left_view[slot] = left
-        sums = (before + later, up + pltpu.roll(up, 1, 0), left + right)
+        sums = (before + later, up + down, left + right)
         every = sums[0] + sums[1] + sums[2]
         diagonal = [every + part_sum for part_sum in sums]
         pair = diagonal[0] * diagonal[1]
@@ -296,8 +297,10 @@
             rate[part, slot] = factor
             source[part, rows(slot, layers)] = start[part] * free
 
+    piece = planes // 2
+
     def modulus_piece(first, carry):
-        count = planes
+        count = piece
         near = near_ref.at[pl.ds(first + 2, count)]
         side = side_ref.at[pl.ds(first + 1, count + 2)]
         far = far_ref.at[pl.ds(first, count + 4)]
@@ -324,11 +327,13 @@
             if p == 0:
                 ahead = jnp.where(first > 0, ahead, 0.0)
             above = moduli[rows(p, layers, 1)] if p else pltpu.roll(modulus, layers - 1, 0)
+            below = moduli[rows(p, layers, -1)] if p else pltpu.roll(modulus, 1, 0)
             previous = jnp.maximum(first + p - 1, 0)
             store_faces(
                 p,
                 modulus,
                 above,
+                below,
                 ahead,
                 before,
                 free_ref[previous],
@@ -338,11 +343,14 @@
             modulus, before = later, ahead
         return modulus, before
 
-    modulus, before = each_chunk(planes, planes, modulus_piece, (jnp.ones(shape, jnp.float32), zero))
+    modulus, before = each_chunk(
+        planes, piece, modulus_piece, (jnp.ones(shape, jnp.float32), zero)
+    )
     store_faces(
         planes,
         modulus,
         pltpu.roll(modulus, layers - 1, 0),
+        pltpu.roll(modulus, 1, 0),
         zero,
         before,
         free_ref[planes - 1],

time: 45.8 us -> 45.6 us (level)
  no operation moved by 1% of the time
where the time goes in v28:
time: 45.6 us; the launch traced here: 45.2 us
  blocking collectives  33.1 us (73%)
  Pallas kernels  7.57 us (17%)
  starting transfers between devices  1.75 us (4%)
  waiting for transfers between devices  1.12 us (2%)
  local copies, waits for them, and re-layouts  0.82 us (2%)
  between operations  0.72 us (2%)
    all_to_all x3, blocking collectives, between_chips(): lax.all_to_all(pieces, 'space', 0, 0, axis_index_groups=chip_groups())  33.1 us
    pallas_call x1, Pallas kernels, sweep_call(): pl.pallas_call(sweep_kernel, out_shape=[floats(3, (planes + 2) * layers,...  2.52 us
    pallas_call x1, Pallas kernels, design_call(): pl.pallas_call(design_kernel, out_shape=floats(*density.shape[2:]), in_sp...  1.88 us
    ppermute x3, starting transfers between devices, other_core(): return lax.ppermute(block, 'space', [(i, i ^ 1) for i in range(devices)])  1.75 us
    pallas_call x1, Pallas kernels, share_call(): pl.pallas_call(share_kernel, out_shape=[floats(*group_shape)] + [floats(p...  1.28 us
    ppermute x3, waiting for transfers between devices, other_core(): return lax.ppermute(block, 'space', [(i, i ^ 1) for i in range(devices)])  1.12 us
    pallas_call x1, Pallas kernels, prepare_call(): pl.pallas_call(prepare_kernel, out_shape=[floats(len(ALL_SQUARES), layers...  1 us
  transfers between devices with their start and end apart: 3, of which 2 were waited for; matrix products, arithmetic and copies ran while one was open for 0% of the time, Pallas kernels for 4%

profile of v28, /device:TPU:0, one launch (start us, length us, event | category | flops | bytes accessed | tf_op | source)
XLA Modules:
  0.0 45.2 jit_solution(10942849568503513348)
XLA Ops:
  0.6 0.0 copy-start
  0.6 0.8 %broadcast_in_dim.4 = f32[8,2,16,128]{3,2,1,0:T(8,128)S(1)} broadcast(f32[2,16,128]{2,1,0:T(8,128)} %param.6), dimensions={1,2,3} | broadcast | bytes 147456 | tf_op jit(solution)/shard_map/broadcast_in_dim | solution.py:724
  1.4 13.5 %all_to_all.15.density_ref = f32[8,2,16,128]{3,2,1,0:T(8,128)S(1)} all-to-all(f32[8,2,16,128]{3,2,1,0:T(8,128)S(1)} %broadcast_in_dim.4), channel_id=1, replica_groups={{0,3,4,7,8,11,12,15},{1,2,5,6,9,10,13,14},{16,19,20,23,24,27,28,31},{17..., dimensions={0} | all-to-all | bytes 262144 | tf_op jit(solution)/shard_map/all_to_all | solution.py:719
  14.9 0.7 %collective-permute-start = (f32[8,2,16,128]{3,2,1,0:T(8,128)S(1)}, f32[8,2,16,128]{3,2,1,0:T(8,128)S(1)}, u32[]{:S(2)}, u32[]{:S(2)}) collective-permute-start(f32[8,2,16,128]{3,2,1,0:T(8,128)S(1)} %all_to_all.15.density_ref), channel_id=1, source_target_pairs={{0,1},{1,0},{2,3},{3,2},{4,5},{5,4},{6,7},{7,6},{8,9},{9,8},{10,11... | collective-permute-start | bytes 393224 | tf_op jit(solution)/shard_map/ppermute | solution.py:710
  15.6 1.0 %prepare.1 = (f32[10,16,128]{2,1,0:T(8,128)S(1)}, f32[5,16,128]{2,1,0:T(8,128)S(1)}, f32[32,16,128]{2,1,0:T(8,128)S(1)}, f32[3,16,128]{2,1,0:T(8,128)S(1)}, f32[...) custom-call(s32[16]{0:T(128)} %radius_hbm, s32[16]{0:T(128)} %index_hbm, f32[3,16]{1,0:T(4,128)} %bitcast.12, ...), custom_call_target="tpu_custom_call" | custom-call | flops 5242880 | bytes 524288 | tf_op jit(solution)/shard_map/prepare/pallas_call | solution.py:591
  16.6 0.0 collective-permute-done
  16.6 0.0 copy-done
  16.6 2.5 %sweeps.1 = (f32[3,544,128]{2,1,0:T(8,128)S(1)}, f32[32,16,128]{2,1,0:T(8,128)S(1)}) custom-call(f32[8,128]{1,0:T(8,128)S(1)} %get-tuple-element.31.spot_ref, f32[3,16,128]{2,1,0:T(8,128)S(1)} %get-tuple-element.32.load_ref, f32[10,16,128]{2,1,0:T(8,128)S(1)} %get-tuple-element.33.weight_ref, f32[5,16,128]{2,1,0:T(8,128)S(1)} %get-tuple-element.34.inverse_ref, ...), custom_call_target="tpu_custom_call" | custom-call | tf_op jit(solution)/shard_map/sweeps/pallas_call | solution.py:636
  19.2 1.3 %share.1 = (f32[8,2,16,128]{3,2,1,0:T(8,128)S(1)}, f32[36,16,128]{2,1,0:T(8,128)S(1)}, f32[36,16,128]{2,1,0:T(8,128)S(1)}, f32[36,16,128]{2,1,0:T(8,128)S(1)}) custom-call(f32[3,544,128]{2,1,0:T(8,128)S(1)} %get-tuple-element.43.disp_ref, f32[32,16,128]{2,1,0:T(8,128)S(1)} %get-tuple-element.38.coef_ref, f32[10,16,128]{2,1,0:T(8,128)S(1)} %get-tuple-element.33.weight_ref), custom_call_target="tpu_custom_call" | custom-call | tf_op jit(solution)/shard_map/share/pallas_call | solution.py:667
  20.4 0.4 collective-permute-start.1
  20.8 0.9 %kept.1 = (f32[3,512,128]{2,1,0:T(8,128)}, f32[8,2,16,128]{3,2,1,0:T(8,128)S(1)}) custom-call(f32[3,544,128]{2,1,0:T(8,128)S(1)} %get-tuple-element.43.disp_ref, f32[10,16,128]{2,1,0:T(8,128)S(1)} %get-tuple-element.33.weight_ref, f32[36,16,128]{2,1,0:T(8,128)S(1)} %get-tuple-element.44.plane_ref, f32[36,16,128]{2,1,0:T(8,128)S(1)} %get-tuple-element.45.beside_ref, ...), custom_call_target="tpu_custom_call" | custom-call | flops 4177920 | bytes 1671168 | tf_op jit(solution)/shard_map/kept/pallas_call | solution.py:682
  21.7 0.1 collective-permute-done.1
  21.9 10.0 %all_to_all.16 = f32[8,2,16,128]{3,2,1,0:T(8,128)S(1)} all-to-all(f32[8,2,16,128]{3,2,1,0:T(8,128)S(1)} %add.3), channel_id=1, replica_groups={{0,3,4,7,8,11,12,15},{1,2,5,6,9,10,13,14},{16,19,20,23,24,27,28,31},{17..., dimensions={0} | all-to-all | bytes 262144 | tf_op jit(solution)/shard_map/all_to_all | solution.py:719
  32.0 9.6 %all_to_all.17 = f32[8,2,16,128]{3,2,1,0:T(8,128)S(1)} all-to-all(f32[8,2,16,128]{3,2,1,0:T(8,128)S(1)} %broadcast_in_dim.5), channel_id=1, replica_groups={{0,3,4,7,8,11,12,15},{1,2,5,6,9,10,13,14},{16,19,20,23,24,27,28,31},{17..., dimensions={0} | all-to-all | bytes 262144 | tf_op jit(solution)/shard_map/all_to_all | solution.py:719
  41.6 0.7 %collective-permute-start.2 = (f32[8,2,16,128]{3,2,1,0:T(8,128)S(1)}, f32[8,2,16,128]{3,2,1,0:T(8,128)S(1)}, u32[]{:S(2)}, u32[]{:S(2)}) collective-permute-start(f32[8,2,16,128]{3,2,1,0:T(8,128)S(1)} %all_to_all.17), channel_id=1, source_target_pairs={{0,1},{1,0},{2,3},{3,2},{4,5},{5,4},{6,7},{7,6},{8,9},{9,8},{10,11... | collective-permute-start | bytes 393224 | tf_op jit(solution)/shard_map/ppermute | solution.py:710
  42.3 1.0 %collective-permute-done.2 = f32[8,2,16,128]{3,2,1,0:T(8,128)S(1)} collective-permute-done((f32[8,2,16,128]{3,2,1,0:T(8,128)S(1)}, f32[8,2,16,128]{3,2,1,0:T(8,128)S(1)}, u32[]{:S(2)}, u32[]{:S(2)}) %collective-permute-start.2) | collective-permute-done | bytes 131104 | tf_op jit(solution)/shard_map/ppermute | solution.py:710
  43.3 1.9 %design.1 = f32[2,16,128]{2,1,0:T(8,128)} custom-call(f32[2,8,2,16,128]{4,3,2,1,0:T(8,128)S(1)} %pad_maximum_fusion.1.root_ref, f32[2,8,2,16,128]{4,3,2,1,0:T(8,128)S(1)} %pad_maximum_fusion.density_ref), custom_call_target="tpu_custom_call" | custom-call | tf_op jit(solution)/shard_map/design/pallas_call | solution.py:697
  (6 shorter events, 0.1 us)
Async XLA Ops:
  0.6 16.0 %copy-start = (f32[1,3,32,16,128]{4,3,2,1,0:T(8,128)S(1)}, f32[1,3,32,16,128]{4,3,2,1,0:T(8,128)}, u32[]{:S(2)}) copy-start(f32[1,3,32,16,128]{4,3,2,1,0:T(8,128)} %param.7) | copy-start | bytes 2359300
  14.9 1.7 %collective-permute-start = (f32[8,2,16,128]{3,2,1,0:T(8,128)S(1)}, f32[8,2,16,128]{3,2,1,0:T(8,128)S(1)}, u32[]{:S(2)}, u32[]{:S(2)}) collective-permute-start(f32[8,2,16,128]{3,2,1,0:T(8,128)S(1)} %all_to_all.15.density_ref), channel_id=1, source_target_pairs={{0,1},{1,0},{2,3},{3,2},{4,5},{5,4},{6,7},{7,6},{8,9},{9,8},{10,11... | collective-permute-start | bytes 393224 | tf_op jit(solution)/shard_map/ppermute | solution.py:710
  20.4 1.4 %collective-permute-start.1 = (f32[8,2,16,128]{3,2,1,0:T(8,128)S(1)}, f32[8,2,16,128]{3,2,1,0:T(8,128)S(1)}, u32[]{:S(2)}, u32[]{:S(2)}) collective-permute-start(f32[8,2,16,128]{3,2,1,0:T(8,128)S(1)} %get-tuple-element.48), channel_id=1, source_target_pairs={{0,1},{1,0},{2,3},{3,2},{4,5},{5,4},{6,7},{7,6},{8,9},{9,8},{10,11... | collective-permute-start | bytes 393224 | tf_op jit(solution)/shard_map/ppermute | solution.py:710
  41.6 1.7 %collective-permute-start.2 = (f32[8,2,16,128]{3,2,1,0:T(8,128)S(1)}, f32[8,2,16,128]{3,2,1,0:T(8,128)S(1)}, u32[]{:S(2)}, u32[]{:S(2)}) collective-permute-start(f32[8,2,16,128]{3,2,1,0:T(8,128)S(1)} %all_to_all.17), channel_id=1, source_target_pairs={{0,1},{1,0},{2,3},{3,2},{4,5},{5,4},{6,7},{7,6},{8,9},{9,8},{10,11... | collective-permute-start | bytes 393224 | tf_op jit(solution)/shard_map/ppermute | solution.py:710

commit v29 on v28

--- a/solution.py
+++ b/solution.py
@@ -112,12 +112,20 @@
         ref[place] = jnp.zeros(ref.shape[1:], ref.dtype)
 
 
+def far_half(chip):
+    return chip * 4 // lax.axis_size("space")
+
+
+def own_core(group):
+    mine = lax.axis_index("space")
+    return (mine ^ far_half(mine >> 1) ^ group) & 1
+
+
 def group_spots(group, blocks):
     chips, own_planes = blocks.shape[:2]
-    mine = lax.axis_index("space")
-    core = mine ^ mine >> 1 ^ group
+    core = own_core(group)
     return [
-        (own_planes * (2 * chip + ((core ^ chip) & 1)) + own, (chip, own))
+        (own_planes * (2 * chip + (core ^ far_half(chip))) + own, (chip, own))
         for chip in range(chips)
         for own in range(own_planes)
     ]
@@ -408,8 +416,7 @@
 def filter_group(group, shares, weight_ref, near_ref, far_ref, result_ref):
     chips, own_planes, layers, row_width = result_ref.shape
     zero_gap = jnp.zeros((GAP, row_width), jnp.float32)
-    mine = lax.axis_index("space")
-    core = (mine ^ mine >> 1 ^ group) & 1
+    core = own_core(group)
     count = shares[0].shape[0] - own_planes
     views = [
         [ref.at[pl.ds(own_planes * start, count)] for ref in shares] for start in (core, 1 - core)
@@ -418,7 +425,7 @@
         ref[gap(0, layers)] = zero_gap
     for p in range(chips * own_planes):
         chip, own = p // own_planes, p % own_planes
-        plane, beside, further = views[chip & 1]
+        plane, beside, further = views[far_half(chip)]
         x = 2 * own_planes * chip + own + 2
 
         def around(ref, distance):
@@ -712,7 +719,7 @@
 
 def chip_groups():
     chips = lax.axis_size("space") // 2
-    return [[2 * chip + (chip ^ group) % 2 for chip in range(chips)] for group in range(2)]
+    return [[2 * chip + (far_half(chip) ^ group) for chip in range(chips)] for group in range(2)]
 
 
 def between_chips(pieces):

time: 45.6 us -> 45.7 us (level)
  no operation moved by 1% of the time
where the time goes in v29:
time: 45.7 us; the launch traced here: 45.3 us
  blocking collectives  33.3 us (73%)
  Pallas kernels  7.56 us (17%)
  starting transfers between devices  1.76 us (4%)
  waiting for transfers between devices  1.11 us (2%)
  local copies, waits for them, and re-layouts  0.82 us (2%)
  between operations  0.72 us (2%)
    all_to_all x3, blocking collectives, between_chips(): lax.all_to_all(pieces, 'space', 0, 0, axis_index_groups=chip_groups())  33.3 us
    pallas_call x1, Pallas kernels, sweep_call(): pl.pallas_call(sweep_kernel, out_shape=[floats(3, (planes + 2) * layers,...  2.51 us
    pallas_call x1, Pallas kernels, design_call(): pl.pallas_call(design_kernel, out_shape=floats(*density.shape[2:]), in_sp...  1.88 us
    ppermute x3, starting transfers between devices, other_core(): return lax.ppermute(block, 'space', [(i, i ^ 1) for i in range(devices)])  1.76 us
    pallas_call x1, Pallas kernels, share_call(): pl.pallas_call(share_kernel, out_shape=[floats(*group_shape)] + [floats(p...  1.28 us
    ppermute x3, waiting for transfers between devices, other_core(): return lax.ppermute(block, 'space', [(i, i ^ 1) for i in range(devices)])  1.11 us
    pallas_call x1, Pallas kernels, prepare_call(): pl.pallas_call(prepare_kernel, out_shape=[floats(len(ALL_SQUARES), layers...  1 us
  transfers between devices with their start and end apart: 3, of which 2 were waited for; matrix products, arithmetic and copies ran while one was open for 0% of the time, Pallas kernels for 4%

profile of v29, /device:TPU:0, one launch (start us, length us, event | category | flops | bytes accessed | tf_op | source)
XLA Modules:
  0.0 45.3 jit_solution(17393697507300380408)
XLA Ops:
  0.6 0.0 copy-start
  0.6 0.8 %broadcast_in_dim.4 = f32[8,2,16,128]{3,2,1,0:T(8,128)S(1)} broadcast(f32[2,16,128]{2,1,0:T(8,128)} %param.6), dimensions={1,2,3} | broadcast | bytes 147456 | tf_op jit(solution)/shard_map/broadcast_in_dim | solution.py:731
  1.4 13.3 %all_to_all.15.density_ref = f32[8,2,16,128]{3,2,1,0:T(8,128)S(1)} all-to-all(f32[8,2,16,128]{3,2,1,0:T(8,128)S(1)} %broadcast_in_dim.4), channel_id=1, replica_groups={{0,2,4,6,9,11,13,15},{1,3,5,7,8,10,12,14},{16,18,20,22,25,27,29,31},{17..., dimensions={0} | all-to-all | bytes 262144 | tf_op jit(solution)/shard_map/all_to_all | solution.py:726
  14.7 0.8 %collective-permute-start = (f32[8,2,16,128]{3,2,1,0:T(8,128)S(1)}, f32[8,2,16,128]{3,2,1,0:T(8,128)S(1)}, u32[]{:S(2)}, u32[]{:S(2)}) collective-permute-start(f32[8,2,16,128]{3,2,1,0:T(8,128)S(1)} %all_to_all.15.density_ref), channel_id=1, source_target_pairs={{0,1},{1,0},{2,3},{3,2},{4,5},{5,4},{6,7},{7,6},{8,9},{9,8},{10,11... | collective-permute-start | bytes 393224 | tf_op jit(solution)/shard_map/ppermute | solution.py:717
  15.6 1.0 %prepare.1 = (f32[10,16,128]{2,1,0:T(8,128)S(1)}, f32[5,16,128]{2,1,0:T(8,128)S(1)}, f32[32,16,128]{2,1,0:T(8,128)S(1)}, f32[3,16,128]{2,1,0:T(8,128)S(1)}, f32[...) custom-call(s32[16]{0:T(128)} %radius_hbm, s32[16]{0:T(128)} %index_hbm, f32[3,16]{1,0:T(4,128)} %bitcast.12, ...), custom_call_target="tpu_custom_call" | custom-call | flops 5242880 | bytes 524288 | tf_op jit(solution)/shard_map/prepare/pallas_call | solution.py:598
  16.6 0.0 collective-permute-done
  16.6 0.0 copy-done
  16.6 2.5 %sweeps.1 = (f32[3,544,128]{2,1,0:T(8,128)S(1)}, f32[32,16,128]{2,1,0:T(8,128)S(1)}) custom-call(f32[8,128]{1,0:T(8,128)S(1)} %get-tuple-element.31.spot_ref, f32[3,16,128]{2,1,0:T(8,128)S(1)} %get-tuple-element.32.load_ref, f32[10,16,128]{2,1,0:T(8,128)S(1)} %get-tuple-element.33.weight_ref, f32[5,16,128]{2,1,0:T(8,128)S(1)} %get-tuple-element.34.inverse_ref, ...), custom_call_target="tpu_custom_call" | custom-call | tf_op jit(solution)/shard_map/sweeps/pallas_call | solution.py:643
  19.2 1.3 %share.1 = (f32[8,2,16,128]{3,2,1,0:T(8,128)S(1)}, f32[36,16,128]{2,1,0:T(8,128)S(1)}, f32[36,16,128]{2,1,0:T(8,128)S(1)}, f32[36,16,128]{2,1,0:T(8,128)S(1)}) custom-call(f32[3,544,128]{2,1,0:T(8,128)S(1)} %get-tuple-element.43.disp_ref, f32[32,16,128]{2,1,0:T(8,128)S(1)} %get-tuple-element.38.coef_ref, f32[10,16,128]{2,1,0:T(8,128)S(1)} %get-tuple-element.33.weight_ref), custom_call_target="tpu_custom_call" | custom-call | tf_op jit(solution)/shard_map/share/pallas_call | solution.py:674
  20.4 0.4 collective-permute-start.1
  20.8 0.9 %kept.1 = (f32[3,512,128]{2,1,0:T(8,128)}, f32[8,2,16,128]{3,2,1,0:T(8,128)S(1)}) custom-call(f32[3,544,128]{2,1,0:T(8,128)S(1)} %get-tuple-element.43.disp_ref, f32[10,16,128]{2,1,0:T(8,128)S(1)} %get-tuple-element.33.weight_ref, f32[36,16,128]{2,1,0:T(8,128)S(1)} %get-tuple-element.44.plane_ref, f32[36,16,128]{2,1,0:T(8,128)S(1)} %get-tuple-element.45.beside_ref, ...), custom_call_target="tpu_custom_call" | custom-call | flops 4177920 | bytes 1671168 | tf_op jit(solution)/shard_map/kept/pallas_call | solution.py:689
  21.7 0.1 collective-permute-done.1
  21.9 10.3 %all_to_all.16 = f32[8,2,16,128]{3,2,1,0:T(8,128)S(1)} all-to-all(f32[8,2,16,128]{3,2,1,0:T(8,128)S(1)} %add.3), channel_id=1, replica_groups={{0,2,4,6,9,11,13,15},{1,3,5,7,8,10,12,14},{16,18,20,22,25,27,29,31},{17..., dimensions={0} | all-to-all | bytes 262144 | tf_op jit(solution)/shard_map/all_to_all | solution.py:726
  32.2 9.7 %all_to_all.17 = f32[8,2,16,128]{3,2,1,0:T(8,128)S(1)} all-to-all(f32[8,2,16,128]{3,2,1,0:T(8,128)S(1)} %broadcast_in_dim.5), channel_id=1, replica_groups={{0,2,4,6,9,11,13,15},{1,3,5,7,8,10,12,14},{16,18,20,22,25,27,29,31},{17..., dimensions={0} | all-to-all | bytes 262144 | tf_op jit(solution)/shard_map/all_to_all | solution.py:726
  41.9 0.5 %collective-permute-start.2 = (f32[8,2,16,128]{3,2,1,0:T(8,128)S(1)}, f32[8,2,16,128]{3,2,1,0:T(8,128)S(1)}, u32[]{:S(2)}, u32[]{:S(2)}) collective-permute-start(f32[8,2,16,128]{3,2,1,0:T(8,128)S(1)} %all_to_all.17), channel_id=1, source_target_pairs={{0,1},{1,0},{2,3},{3,2},{4,5},{5,4},{6,7},{7,6},{8,9},{9,8},{10,11... | collective-permute-start | bytes 393224 | tf_op jit(solution)/shard_map/ppermute | solution.py:717
  42.4 1.0 %collective-permute-done.2 = f32[8,2,16,128]{3,2,1,0:T(8,128)S(1)} collective-permute-done((f32[8,2,16,128]{3,2,1,0:T(8,128)S(1)}, f32[8,2,16,128]{3,2,1,0:T(8,128)S(1)}, u32[]{:S(2)}, u32[]{:S(2)}) %collective-permute-start.2) | collective-permute-done | bytes 131104 | tf_op jit(solution)/shard_map/ppermute | solution.py:717
  43.4 1.9 %design.1 = f32[2,16,128]{2,1,0:T(8,128)} custom-call(f32[2,8,2,16,128]{4,3,2,1,0:T(8,128)S(1)} %pad_maximum_fusion.1.root_ref, f32[2,8,2,16,128]{4,3,2,1,0:T(8,128)S(1)} %pad_maximum_fusion.density_ref), custom_call_target="tpu_custom_call" | custom-call | tf_op jit(solution)/shard_map/design/pallas_call | solution.py:704
  (6 shorter events, 0.1 us)
Async XLA Ops:
  0.6 16.0 %copy-start = (f32[1,3,32,16,128]{4,3,2,1,0:T(8,128)S(1)}, f32[1,3,32,16,128]{4,3,2,1,0:T(8,128)}, u32[]{:S(2)}) copy-start(f32[1,3,32,16,128]{4,3,2,1,0:T(8,128)} %param.7) | copy-start | bytes 2359300
  14.7 1.8 %collective-permute-start = (f32[8,2,16,128]{3,2,1,0:T(8,128)S(1)}, f32[8,2,16,128]{3,2,1,0:T(8,128)S(1)}, u32[]{:S(2)}, u32[]{:S(2)}) collective-permute-start(f32[8,2,16,128]{3,2,1,0:T(8,128)S(1)} %all_to_all.15.density_ref), channel_id=1, source_target_pairs={{0,1},{1,0},{2,3},{3,2},{4,5},{5,4},{6,7},{7,6},{8,9},{9,8},{10,11... | collective-permute-start | bytes 393224 | tf_op jit(solution)/shard_map/ppermute | solution.py:717
  20.4 1.4 %collective-permute-start.1 = (f32[8,2,16,128]{3,2,1,0:T(8,128)S(1)}, f32[8,2,16,128]{3,2,1,0:T(8,128)S(1)}, u32[]{:S(2)}, u32[]{:S(2)}) collective-permute-start(f32[8,2,16,128]{3,2,1,0:T(8,128)S(1)} %get-tuple-element.48), channel_id=1, source_target_pairs={{0,1},{1,0},{2,3},{3,2},{4,5},{5,4},{6,7},{7,6},{8,9},{9,8},{10,11... | collective-permute-start | bytes 393224 | tf_op jit(solution)/shard_map/ppermute | solution.py:717
  41.9 1.5 %collective-permute-start.2 = (f32[8,2,16,128]{3,2,1,0:T(8,128)S(1)}, f32[8,2,16,128]{3,2,1,0:T(8,128)S(1)}, u32[]{:S(2)}, u32[]{:S(2)}) collective-permute-start(f32[8,2,16,128]{3,2,1,0:T(8,128)S(1)} %all_to_all.17), channel_id=1, source_target_pairs={{0,1},{1,0},{2,3},{3,2},{4,5},{5,4},{6,7},{7,6},{8,9},{9,8},{10,11... | collective-permute-start | bytes 393224 | tf_op jit(solution)/shard_map/ppermute | solution.py:717

commit v30 on v28

--- a/solution.py
+++ b/solution.py
@@ -466,37 +466,38 @@
     for ref in shares:
         zero_edges(ref)
 
+    before = zero
+    here = [disp_ref[part, rows(1, layers)] for part in range(3)]
+    for x in range(planes):
+        later = [disp_ref[part, rows(x + 2, layers)] for part in range(3)]
+        ahead, upward, right = zero, zero, zero
+        for part in range(3):
+            step = later[part] - here[part]
+            climb = disp_ref[part, rows(x + 1, layers, 1)] - here[part]
+            slide = pltpu.roll(here[part], row_width - 1, 1) - here[part]
+            ahead = ahead + (2.0 if part == 0 else 1.0) * (step * step)
+            upward = upward + (2.0 if part == 1 else 1.0) * (climb * climb)
+            right = right + (2.0 if part == 2 else 1.0) * (slide * slide)
+        if x + 1 == planes:
+            ahead = zero
+        upward = jnp.where(z < layers - 1, upward, 0.0)
+        right = jnp.where(y < row_width - 1, right, 0.0)
+        total = before + ahead + upward + pltpu.roll(upward, 1, 0)
+        total = total + right + pltpu.roll(right, 1, 1)
+        plane_ref[x + 2] = (0.5 / load_cases) * total * coef_ref[x]
+        before, here = ahead, later
+
     count = planes // 2
 
-    def share_chunk(first, before):
-        disp = disp_ref.at[:, pl.ds((first + 1) * layers, (count + 1) * layers)]
-        coef = coef_ref.at[pl.ds(first, count)]
+    def spread_piece(first, carry):
         plane, beside, further = (ref.at[pl.ds(first + 2, count)] for ref in shares)
-        here = [disp[part, rows(0, layers)] for part in range(3)]
         for p in range(count):
-            later = [disp[part, rows(p + 1, layers)] for part in range(3)]
-            ahead, upward, right = zero, zero, zero
-            for part in range(3):
-                step = later[part] - here[part]
-                climb = disp[part, rows(p, layers, 1)] - here[part]
-                slide = pltpu.roll(here[part], row_width - 1, 1) - here[part]
-                ahead = ahead + (2.0 if part == 0 else 1.0) * (step * step)
-                upward = upward + (2.0 if part == 1 else 1.0) * (climb * climb)
-                right = right + (2.0 if part == 2 else 1.0) * (slide * slide)
-            if p == count - 1:
-                ahead = jnp.where(first + count < planes, ahead, 0.0)
-            upward = jnp.where(z < layers - 1, upward, 0.0)
-            right = jnp.where(y < row_width - 1, right, 0.0)
-            total = before + ahead + upward + pltpu.roll(upward, 1, 0)
-            total = total + right + pltpu.roll(right, 1, 1)
-            share = (0.5 / load_cases) * total * coef[p]
-            plane[p] = share
+            share = plane[p]
             beside[p] = shift_sum(share, 1, 1)
             further[p] = shift_sum(share, 1, 2)
-            before, here = ahead, later
-        return before
-
-    each_chunk(planes, count, share_chunk, zero)
+        return carry
+
+    each_chunk(planes, count, spread_piece, 0)
     filter_group(1, shares, weight_ref, near_ref, far_ref, sent_ref)
 
 

time: 45.6 us -> 46.4 us (1.018)
  Pallas kernels: 7.57 us -> 8.38 us
    pallas_call x1, Pallas kernels: 1.28 us -> 2.1 us  [share_call(): pl.pallas_call(share_kernel, out_shape=[floats(*group_shape)] + [floats(p...]
where the time goes in v30:
time: 46.4 us; the launch traced here: 46 us
  blocking collectives  33.1 us (71%)
  Pallas kernels  8.38 us (18%)
  starting transfers between devices  1.75 us (4%)
  waiting for transfers between devices  1.12 us (2%)
  local copies, waits for them, and re-layouts  0.82 us (2%)
  between operations  0.72 us (2%)
    all_to_all x3, blocking collectives, between_chips(): lax.all_to_all(pieces, 'space', 0, 0, axis_index_groups=chip_groups())  33.1 us
    pallas_call x1, Pallas kernels, sweep_call(): pl.pallas_call(sweep_kernel, out_shape=[floats(3, (planes + 2) * layers,...  2.52 us
    pallas_call x1, Pallas kernels, share_call(): pl.pallas_call(share_kernel, out_shape=[floats(*group_shape)] + [floats(p...  2.1 us
    pallas_call x1, Pallas kernels, design_call(): pl.pallas_call(design_kernel, out_shape=floats(*density.shape[2:]), in_sp...  1.88 us
    ppermute x3, starting transfers between devices, other_core(): return lax.ppermute(block, 'space', [(i, i ^ 1) for i in range(devices)])  1.75 us
    ppermute x3, waiting for transfers between devices, other_core(): return lax.ppermute(block, 'space', [(i, i ^ 1) for i in range(devices)])  1.12 us
    pallas_call x1, Pallas kernels, prepare_call(): pl.pallas_call(prepare_kernel, out_shape=[floats(len(ALL_SQUARES), layers...  1 us
  transfers between devices with their start and end apart: 3, of which 2 were waited for; matrix products, arithmetic and copies ran while one was open for 0% of the time, Pallas kernels for 4%

profile of v30, /device:TPU:0, one launch (start us, length us, event | category | flops | bytes accessed | tf_op | source)
XLA Modules:
  0.0 46.0 jit_solution(17965492439401721192)
XLA Ops:
  0.6 0.0 copy-start
  0.6 0.8 %broadcast_in_dim.4 = f32[8,2,16,128]{3,2,1,0:T(8,128)S(1)} broadcast(f32[2,16,128]{2,1,0:T(8,128)} %param.6), dimensions={1,2,3} | broadcast | bytes 147456 | tf_op jit(solution)/shard_map/broadcast_in_dim | solution.py:725
  1.4 13.5 %all_to_all.15.density_ref = f32[8,2,16,128]{3,2,1,0:T(8,128)S(1)} all-to-all(f32[8,2,16,128]{3,2,1,0:T(8,128)S(1)} %broadcast_in_dim.4), channel_id=1, replica_groups={{0,3,4,7,8,11,12,15},{1,2,5,6,9,10,13,14},{16,19,20,23,24,27,28,31},{17..., dimensions={0} | all-to-all | bytes 262144 | tf_op jit(solution)/shard_map/all_to_all | solution.py:720
  14.9 0.7 %collective-permute-start = (f32[8,2,16,128]{3,2,1,0:T(8,128)S(1)}, f32[8,2,16,128]{3,2,1,0:T(8,128)S(1)}, u32[]{:S(2)}, u32[]{:S(2)}) collective-permute-start(f32[8,2,16,128]{3,2,1,0:T(8,128)S(1)} %all_to_all.15.density_ref), channel_id=1, source_target_pairs={{0,1},{1,0},{2,3},{3,2},{4,5},{5,4},{6,7},{7,6},{8,9},{9,8},{10,11... | collective-permute-start | bytes 393224 | tf_op jit(solution)/shard_map/ppermute | solution.py:711
  15.6 1.0 %prepare.1 = (f32[10,16,128]{2,1,0:T(8,128)S(1)}, f32[5,16,128]{2,1,0:T(8,128)S(1)}, f32[32,16,128]{2,1,0:T(8,128)S(1)}, f32[3,16,128]{2,1,0:T(8,128)S(1)}, f32[...) custom-call(s32[16]{0:T(128)} %radius_hbm, s32[16]{0:T(128)} %index_hbm, f32[3,16]{1,0:T(4,128)} %bitcast.12, ...), custom_call_target="tpu_custom_call" | custom-call | flops 5242880 | bytes 524288 | tf_op jit(solution)/shard_map/prepare/pallas_call | solution.py:592
  16.6 0.0 collective-permute-done
  16.6 0.0 copy-done
  16.6 2.5 %sweeps.1 = (f32[3,544,128]{2,1,0:T(8,128)S(1)}, f32[32,16,128]{2,1,0:T(8,128)S(1)}) custom-call(f32[8,128]{1,0:T(8,128)S(1)} %get-tuple-element.31.spot_ref, f32[3,16,128]{2,1,0:T(8,128)S(1)} %get-tuple-element.32.load_ref, f32[10,16,128]{2,1,0:T(8,128)S(1)} %get-tuple-element.33.weight_ref, f32[5,16,128]{2,1,0:T(8,128)S(1)} %get-tuple-element.34.inverse_ref, ...), custom_call_target="tpu_custom_call" | custom-call | tf_op jit(solution)/shard_map/sweeps/pallas_call | solution.py:637
  19.2 2.1 %share.1 = (f32[8,2,16,128]{3,2,1,0:T(8,128)S(1)}, f32[36,16,128]{2,1,0:T(8,128)S(1)}, f32[36,16,128]{2,1,0:T(8,128)S(1)}, f32[36,16,128]{2,1,0:T(8,128)S(1)}) custom-call(f32[3,544,128]{2,1,0:T(8,128)S(1)} %get-tuple-element.43.disp_ref, f32[32,16,128]{2,1,0:T(8,128)S(1)} %get-tuple-element.38.coef_ref, f32[10,16,128]{2,1,0:T(8,128)S(1)} %get-tuple-element.33.weight_ref), custom_call_target="tpu_custom_call" | custom-call | tf_op jit(solution)/shard_map/share/pallas_call | solution.py:668
  21.3 0.4 collective-permute-start.1
  21.6 0.9 %kept.1 = (f32[3,512,128]{2,1,0:T(8,128)}, f32[8,2,16,128]{3,2,1,0:T(8,128)S(1)}) custom-call(f32[3,544,128]{2,1,0:T(8,128)S(1)} %get-tuple-element.43.disp_ref, f32[10,16,128]{2,1,0:T(8,128)S(1)} %get-tuple-element.33.weight_ref, f32[36,16,128]{2,1,0:T(8,128)S(1)} %get-tuple-element.44.plane_ref, f32[36,16,128]{2,1,0:T(8,128)S(1)} %get-tuple-element.45.beside_ref, ...), custom_call_target="tpu_custom_call" | custom-call | flops 4177920 | bytes 1671168 | tf_op jit(solution)/shard_map/kept/pallas_call | solution.py:683
  22.5 0.1 collective-permute-done.1
  22.7 10.0 %all_to_all.16 = f32[8,2,16,128]{3,2,1,0:T(8,128)S(1)} all-to-all(f32[8,2,16,128]{3,2,1,0:T(8,128)S(1)} %add.3), channel_id=1, replica_groups={{0,3,4,7,8,11,12,15},{1,2,5,6,9,10,13,14},{16,19,20,23,24,27,28,31},{17..., dimensions={0} | all-to-all | bytes 262144 | tf_op jit(solution)/shard_map/all_to_all | solution.py:720
  32.8 9.6 %all_to_all.17 = f32[8,2,16,128]{3,2,1,0:T(8,128)S(1)} all-to-all(f32[8,2,16,128]{3,2,1,0:T(8,128)S(1)} %broadcast_in_dim.5), channel_id=1, replica_groups={{0,3,4,7,8,11,12,15},{1,2,5,6,9,10,13,14},{16,19,20,23,24,27,28,31},{17..., dimensions={0} | all-to-all | bytes 262144 | tf_op jit(solution)/shard_map/all_to_all | solution.py:720
  42.4 0.7 %collective-permute-start.2 = (f32[8,2,16,128]{3,2,1,0:T(8,128)S(1)}, f32[8,2,16,128]{3,2,1,0:T(8,128)S(1)}, u32[]{:S(2)}, u32[]{:S(2)}) collective-permute-start(f32[8,2,16,128]{3,2,1,0:T(8,128)S(1)} %all_to_all.17), channel_id=1, source_target_pairs={{0,1},{1,0},{2,3},{3,2},{4,5},{5,4},{6,7},{7,6},{8,9},{9,8},{10,11... | collective-permute-start | bytes 393224 | tf_op jit(solution)/shard_map/ppermute | solution.py:711
  43.1 1.0 %collective-permute-done.2 = f32[8,2,16,128]{3,2,1,0:T(8,128)S(1)} collective-permute-done((f32[8,2,16,128]{3,2,1,0:T(8,128)S(1)}, f32[8,2,16,128]{3,2,1,0:T(8,128)S(1)}, u32[]{:S(2)}, u32[]{:S(2)}) %collective-permute-start.2) | collective-permute-done | bytes 131104 | tf_op jit(solution)/shard_map/ppermute | solution.py:711
  44.1 1.9 %design.1 = f32[2,16,128]{2,1,0:T(8,128)} custom-call(f32[2,8,2,16,128]{4,3,2,1,0:T(8,128)S(1)} %pad_maximum_fusion.1.root_ref, f32[2,8,2,16,128]{4,3,2,1,0:T(8,128)S(1)} %pad_maximum_fusion.density_ref), custom_call_target="tpu_custom_call" | custom-call | tf_op jit(solution)/shard_map/design/pallas_call | solution.py:698
  (6 shorter events, 0.1 us)
Async XLA Ops:
  0.6 16.0 %copy-start = (f32[1,3,32,16,128]{4,3,2,1,0:T(8,128)S(1)}, f32[1,3,32,16,128]{4,3,2,1,0:T(8,128)}, u32[]{:S(2)}) copy-start(f32[1,3,32,16,128]{4,3,2,1,0:T(8,128)} %param.7) | copy-start | bytes 2359300
  14.9 1.7 %collective-permute-start = (f32[8,2,16,128]{3,2,1,0:T(8,128)S(1)}, f32[8,2,16,128]{3,2,1,0:T(8,128)S(1)}, u32[]{:S(2)}, u32[]{:S(2)}) collective-permute-start(f32[8,2,16,128]{3,2,1,0:T(8,128)S(1)} %all_to_all.15.density_ref), channel_id=1, source_target_pairs={{0,1},{1,0},{2,3},{3,2},{4,5},{5,4},{6,7},{7,6},{8,9},{9,8},{10,11... | collective-permute-start | bytes 393224 | tf_op jit(solution)/shard_map/ppermute | solution.py:711
  21.3 1.4 %collective-permute-start.1 = (f32[8,2,16,128]{3,2,1,0:T(8,128)S(1)}, f32[8,2,16,128]{3,2,1,0:T(8,128)S(1)}, u32[]{:S(2)}, u32[]{:S(2)}) collective-permute-start(f32[8,2,16,128]{3,2,1,0:T(8,128)S(1)} %get-tuple-element.48), channel_id=1, source_target_pairs={{0,1},{1,0},{2,3},{3,2},{4,5},{5,4},{6,7},{7,6},{8,9},{9,8},{10,11... | collective-permute-start | bytes 393224 | tf_op jit(solution)/shard_map/ppermute | solution.py:711
  42.4 1.7 %collective-permute-start.2 = (f32[8,2,16,128]{3,2,1,0:T(8,128)S(1)}, f32[8,2,16,128]{3,2,1,0:T(8,128)S(1)}, u32[]{:S(2)}, u32[]{:S(2)}) collective-permute-start(f32[8,2,16,128]{3,2,1,0:T(8,128)S(1)} %all_to_all.17), channel_id=1, source_target_pairs={{0,1},{1,0},{2,3},{3,2},{4,5},{5,4},{6,7},{7,6},{8,9},{9,8},{10,11... | collective-permute-start | bytes 393224 | tf_op jit(solution)/shard_map/ppermute | solution.py:711

commit v31 on v28

--- a/solution.py
+++ b/solution.py
@@ -523,54 +523,66 @@
 
 def design_kernel(root_ref, density_ref, new_ref, pull_ref, low_ref, high_ref):
     groups, chips, own_planes, layers, row_width = density_ref.shape
-    own_chip = lax.axis_index("space") >> 1
-    shape = (layers, row_width)
+    tile_rows = pull_ref.shape[1]
+    steps = layers // tile_rows
+    shape = (tile_rows, row_width)
     zero = jnp.zeros(shape, jnp.float32)
-    planes = [
-        (group, chip, own)
+    tiles = [
+        (group, chip, own, pl.ds(step * tile_rows, tile_rows))
         for group in range(groups)
         for chip in range(chips)
         for own in range(own_planes)
+        for step in range(steps)
     ]
-    for spot in planes:
+    for place, spot in enumerate(tiles):
         density = density_ref[spot]
-        pull_ref[spot] = density * root_ref[spot]
-        low_ref[spot] = jnp.maximum(density - move_limit, density_floor)
-        high_ref[spot] = jnp.minimum(density + move_limit, 1.0)
-
-    target = volume_share * len(planes) * layers * row_width
-
-    def factor_of(log_level):
-        return jnp.broadcast_to(jnp.exp(-0.5 * log_level), shape)
+        pull_ref[place] = density * root_ref[spot]
+        low_ref[place] = jnp.maximum(density - move_limit, density_floor)
+        high_ref[place] = jnp.minimum(density + move_limit, 1.0)
+
+    target = volume_share * len(tiles) * tile_rows * row_width
 
     def exceeds(total):
-        return jnp.sum(jnp.sum(total, axis=0, keepdims=True), axis=1, keepdims=True) > target
+        volume = jnp.sum(jnp.sum(total, axis=0, keepdims=True), axis=1, keepdims=True)
+        return jnp.broadcast_to(volume, shape) > target
+
+    def middles_of(lower, span):
+        half, quarter = span * 0.5, span * 0.25
+        return lower + quarter, lower + half, lower + half + quarter
+
+    def factors_of(lower, span):
+        return [jnp.exp(-0.5 * middle) for middle in middles_of(lower, span)]
 
     def halve_twice(step, state):
-        lower, span = state
-        half, quarter = span * 0.5, span * 0.25
-        middles = (lower + quarter, lower + half, lower + half + quarter)
-        factors = [factor_of(middle) for middle in middles]
-        totals = [zero, zero, zero]
-        for spot in planes:
-            pull, low, high = pull_ref[spot], low_ref[spot], high_ref[spot]
-            totals = [
-                total + jnp.minimum(jnp.maximum(pull * factor, low), high)
-                for total, factor in zip(totals, factors)
-            ]
-        first, second, third = (exceeds(total) for total in totals)
-        upper = jnp.where(third, middles[2], middles[1])
-        below = jnp.where(first, middles[0], lower)
-        return jnp.where(second, upper, below), quarter
-
-    start = (jnp.full((1, 1), log_lower, jnp.float32), jnp.full((1, 1), log_span, jnp.float32))
-    lower, span = lax.fori_loop(0, SEARCH // 2, halve_twice, start)
-    factor = factor_of(lower + 0.5 * span)
+        lower, span, *factors = state
+        places = (lower,) + middles_of(lower, span)
+        quarter = span * 0.25
+        ahead = [factors_of(place, quarter) for place in places]
+        totals = [[zero, zero] for _ in factors]
+        for place in range(len(tiles)):
+            pull, low, high = pull_ref[place], low_ref[place], high_ref[place]
+            for total, factor in zip(totals, factors):
+                trial = jnp.minimum(jnp.maximum(pull * factor, low), high)
+                total[place % 2] = total[place % 2] + trial
+        first, second, third = (exceeds(even + odd) for even, odd in totals)
+
+        def pick(options):
+            upper = jnp.where(third, options[3], options[2])
+            return jnp.where(second, upper, jnp.where(first, options[1], options[0]))
+
+        return (pick(places), quarter, *(pick(options) for options in zip(*ahead)))
+
+    lower, span = jnp.full(shape, log_lower), jnp.full(shape, log_span)
+    state = (lower, span, *factors_of(lower, span))
+    lower, span, *_ = lax.fori_loop(0, SEARCH // 2, halve_twice, state)
+    factor = jnp.exp(-0.5 * (lower + 0.5 * span))
+    own_chip = lax.axis_index("space") >> 1
     for own in range(own_planes):
-        spot = (0, own_chip, own)
-        new_ref[own] = jnp.minimum(
-            jnp.maximum(pull_ref[spot] * factor, low_ref[spot]), high_ref[spot]
-        )
+        for step in range(steps):
+            place = (own_chip * own_planes + own) * steps + step
+            new_ref[own, pl.ds(step * tile_rows, tile_rows)] = jnp.minimum(
+                jnp.maximum(pull_ref[place] * factor, low_ref[place]), high_ref[place]
+            )
 
 
 def in_vmem():
@@ -694,12 +706,15 @@
 
 
 def design_call(root, density):
+    tile_rows = min(8, density.shape[-2])
+    row_width = density.shape[-1]
+    tiles = pltpu.VMEM((density.size // (tile_rows * row_width), tile_rows, row_width), jnp.float32)
     return pl.pallas_call(
         design_kernel,
         out_shape=floats(*density.shape[2:]),
         in_specs=[in_vmem()] * 2,
         out_specs=in_vmem(),
-        scratch_shapes=[pltpu.VMEM(density.shape, jnp.float32)] * 3,
+        scratch_shapes=[tiles] * 3,
         compiler_params=pltpu.CompilerParams(vmem_limit_bytes=KERNEL_VMEM),
         name="design",
     )(root, density)

time: 45.6 us -> 45.5 us (level)
  no operation moved by 1% of the time
where the time goes in v31:
time: 45.5 us; the launch traced here: 45.1 us
  blocking collectives  33.1 us (73%)
  Pallas kernels  7.51 us (17%)
  starting transfers between devices  1.75 us (4%)
  waiting for transfers between devices  1.11 us (2%)
  local copies, waits for them, and re-layouts  0.82 us (2%)
  between operations  0.72 us (2%)
    all_to_all x3, blocking collectives, between_chips(): lax.all_to_all(pieces, 'space', 0, 0, axis_index_groups=chip_groups())  33.1 us
    pallas_call x1, Pallas kernels, sweep_call(): pl.pallas_call(sweep_kernel, out_shape=[floats(3, (planes + 2) * layers,...  2.52 us
    pallas_call x1, Pallas kernels, design_call(): pl.pallas_call(design_kernel, out_shape=floats(*density.shape[2:]), in_sp...  1.82 us
    ppermute x3, starting transfers between devices, other_core(): return lax.ppermute(block, 'space', [(i, i ^ 1) for i in range(devices)])  1.75 us
    pallas_call x1, Pallas kernels, share_call(): pl.pallas_call(share_kernel, out_shape=[floats(*group_shape)] + [floats(p...  1.28 us
    ppermute x3, waiting for transfers between devices, other_core(): return lax.ppermute(block, 'space', [(i, i ^ 1) for i in range(devices)])  1.11 us
    pallas_call x1, Pallas kernels, prepare_call(): pl.pallas_call(prepare_kernel, out_shape=[floats(len(ALL_SQUARES), layers...  1 us
  transfers between devices with their start and end apart: 3, of which 2 were waited for; matrix products, arithmetic and copies ran while one was open for 0% of the time, Pallas kernels for 4%

profile of v31, /device:TPU:0, one launch (start us, length us, event | category | flops | bytes accessed | tf_op | source)
XLA Modules:
  0.0 45.1 jit_solution(17328687071999632305)
XLA Ops:
  0.6 0.0 copy-start
  0.6 0.8 %broadcast_in_dim.4 = f32[8,2,16,128]{3,2,1,0:T(8,128)S(1)} broadcast(f32[2,16,128]{2,1,0:T(8,128)} %param.6), dimensions={1,2,3} | broadcast | bytes 147456 | tf_op jit(solution)/shard_map/broadcast_in_dim | solution.py:739
  1.4 13.5 %all_to_all.15.density_ref = f32[8,2,16,128]{3,2,1,0:T(8,128)S(1)} all-to-all(f32[8,2,16,128]{3,2,1,0:T(8,128)S(1)} %broadcast_in_dim.4), channel_id=1, replica_groups={{0,3,4,7,8,11,12,15},{1,2,5,6,9,10,13,14},{16,19,20,23,24,27,28,31},{17..., dimensions={0} | all-to-all | bytes 262144 | tf_op jit(solution)/shard_map/all_to_all | solution.py:734
  14.9 0.7 %collective-permute-start = (f32[8,2,16,128]{3,2,1,0:T(8,128)S(1)}, f32[8,2,16,128]{3,2,1,0:T(8,128)S(1)}, u32[]{:S(2)}, u32[]{:S(2)}) collective-permute-start(f32[8,2,16,128]{3,2,1,0:T(8,128)S(1)} %all_to_all.15.density_ref), channel_id=1, source_target_pairs={{0,1},{1,0},{2,3},{3,2},{4,5},{5,4},{6,7},{7,6},{8,9},{9,8},{10,11... | collective-permute-start | bytes 393224 | tf_op jit(solution)/shard_map/ppermute | solution.py:725
  15.6 1.0 %prepare.1 = (f32[10,16,128]{2,1,0:T(8,128)S(1)}, f32[5,16,128]{2,1,0:T(8,128)S(1)}, f32[32,16,128]{2,1,0:T(8,128)S(1)}, f32[3,16,128]{2,1,0:T(8,128)S(1)}, f32[...) custom-call(s32[16]{0:T(128)} %radius_hbm, s32[16]{0:T(128)} %index_hbm, f32[3,16]{1,0:T(4,128)} %bitcast.12, ...), custom_call_target="tpu_custom_call" | custom-call | flops 5242880 | bytes 524288 | tf_op jit(solution)/shard_map/prepare/pallas_call | solution.py:603
  16.6 0.0 collective-permute-done
  16.6 0.0 copy-done
  16.6 2.5 %sweeps.1 = (f32[3,544,128]{2,1,0:T(8,128)S(1)}, f32[32,16,128]{2,1,0:T(8,128)S(1)}) custom-call(f32[8,128]{1,0:T(8,128)S(1)} %get-tuple-element.31.spot_ref, f32[3,16,128]{2,1,0:T(8,128)S(1)} %get-tuple-element.32.load_ref, f32[10,16,128]{2,1,0:T(8,128)S(1)} %get-tuple-element.33.weight_ref, f32[5,16,128]{2,1,0:T(8,128)S(1)} %get-tuple-element.34.inverse_ref, ...), custom_call_target="tpu_custom_call" | custom-call | tf_op jit(solution)/shard_map/sweeps/pallas_call | solution.py:648
  19.2 1.3 %share.1 = (f32[8,2,16,128]{3,2,1,0:T(8,128)S(1)}, f32[36,16,128]{2,1,0:T(8,128)S(1)}, f32[36,16,128]{2,1,0:T(8,128)S(1)}, f32[36,16,128]{2,1,0:T(8,128)S(1)}) custom-call(f32[3,544,128]{2,1,0:T(8,128)S(1)} %get-tuple-element.43.disp_ref, f32[32,16,128]{2,1,0:T(8,128)S(1)} %get-tuple-element.38.coef_ref, f32[10,16,128]{2,1,0:T(8,128)S(1)} %get-tuple-element.33.weight_ref), custom_call_target="tpu_custom_call" | custom-call | tf_op jit(solution)/shard_map/share/pallas_call | solution.py:679
  20.4 0.4 collective-permute-start.1
  20.8 0.9 %kept.1 = (f32[3,512,128]{2,1,0:T(8,128)}, f32[8,2,16,128]{3,2,1,0:T(8,128)S(1)}) custom-call(f32[3,544,128]{2,1,0:T(8,128)S(1)} %get-tuple-element.43.disp_ref, f32[10,16,128]{2,1,0:T(8,128)S(1)} %get-tuple-element.33.weight_ref, f32[36,16,128]{2,1,0:T(8,128)S(1)} %get-tuple-element.44.plane_ref, f32[36,16,128]{2,1,0:T(8,128)S(1)} %get-tuple-element.45.beside_ref, ...), custom_call_target="tpu_custom_call" | custom-call | flops 4177920 | bytes 1671168 | tf_op jit(solution)/shard_map/kept/pallas_call | solution.py:694
  21.7 0.1 collective-permute-done.1
  21.9 10.0 %all_to_all.16 = f32[8,2,16,128]{3,2,1,0:T(8,128)S(1)} all-to-all(f32[8,2,16,128]{3,2,1,0:T(8,128)S(1)} %add.3), channel_id=1, replica_groups={{0,3,4,7,8,11,12,15},{1,2,5,6,9,10,13,14},{16,19,20,23,24,27,28,31},{17..., dimensions={0} | all-to-all | bytes 262144 | tf_op jit(solution)/shard_map/all_to_all | solution.py:734
  31.9 9.6 %all_to_all.17 = f32[8,2,16,128]{3,2,1,0:T(8,128)S(1)} all-to-all(f32[8,2,16,128]{3,2,1,0:T(8,128)S(1)} %broadcast_in_dim.5), channel_id=1, replica_groups={{0,3,4,7,8,11,12,15},{1,2,5,6,9,10,13,14},{16,19,20,23,24,27,28,31},{17..., dimensions={0} | all-to-all | bytes 262144 | tf_op jit(solution)/shard_map/all_to_all | solution.py:734
  41.6 0.7 %collective-permute-start.2 = (f32[8,2,16,128]{3,2,1,0:T(8,128)S(1)}, f32[8,2,16,128]{3,2,1,0:T(8,128)S(1)}, u32[]{:S(2)}, u32[]{:S(2)}) collective-permute-start(f32[8,2,16,128]{3,2,1,0:T(8,128)S(1)} %all_to_all.17), channel_id=1, source_target_pairs={{0,1},{1,0},{2,3},{3,2},{4,5},{5,4},{6,7},{7,6},{8,9},{9,8},{10,11... | collective-permute-start | bytes 393224 | tf_op jit(solution)/shard_map/ppermute | solution.py:725
  42.3 1.0 %collective-permute-done.2 = f32[8,2,16,128]{3,2,1,0:T(8,128)S(1)} collective-permute-done((f32[8,2,16,128]{3,2,1,0:T(8,128)S(1)}, f32[8,2,16,128]{3,2,1,0:T(8,128)S(1)}, u32[]{:S(2)}, u32[]{:S(2)}) %collective-permute-start.2) | collective-permute-done | bytes 131104 | tf_op jit(solution)/shard_map/ppermute | solution.py:725
  43.3 1.8 %design.1 = f32[2,16,128]{2,1,0:T(8,128)} custom-call(f32[2,8,2,16,128]{4,3,2,1,0:T(8,128)S(1)} %pad_maximum_fusion.1.root_ref, f32[2,8,2,16,128]{4,3,2,1,0:T(8,128)S(1)} %pad_maximum_fusion.density_ref), custom_call_target="tpu_custom_call" | custom-call | tf_op jit(solution)/shard_map/design/pallas_call | solution.py:712
  (6 shorter events, 0.1 us)
Async XLA Ops:
  0.6 16.0 %copy-start = (f32[1,3,32,16,128]{4,3,2,1,0:T(8,128)S(1)}, f32[1,3,32,16,128]{4,3,2,1,0:T(8,128)}, u32[]{:S(2)}) copy-start(f32[1,3,32,16,128]{4,3,2,1,0:T(8,128)} %param.7) | copy-start | bytes 2359300
  14.9 1.7 %collective-permute-start = (f32[8,2,16,128]{3,2,1,0:T(8,128)S(1)}, f32[8,2,16,128]{3,2,1,0:T(8,128)S(1)}, u32[]{:S(2)}, u32[]{:S(2)}) collective-permute-start(f32[8,2,16,128]{3,2,1,0:T(8,128)S(1)} %all_to_all.15.density_ref), channel_id=1, source_target_pairs={{0,1},{1,0},{2,3},{3,2},{4,5},{5,4},{6,7},{7,6},{8,9},{9,8},{10,11... | collective-permute-start | bytes 393224 | tf_op jit(solution)/shard_map/ppermute | solution.py:725
  20.4 1.4 %collective-permute-start.1 = (f32[8,2,16,128]{3,2,1,0:T(8,128)S(1)}, f32[8,2,16,128]{3,2,1,0:T(8,128)S(1)}, u32[]{:S(2)}, u32[]{:S(2)}) collective-permute-start(f32[8,2,16,128]{3,2,1,0:T(8,128)S(1)} %get-tuple-element.48), channel_id=1, source_target_pairs={{0,1},{1,0},{2,3},{3,2},{4,5},{5,4},{6,7},{7,6},{8,9},{9,8},{10,11... | collective-permute-start | bytes 393224 | tf_op jit(solution)/shard_map/ppermute | solution.py:725
  41.6 1.7 %collective-permute-start.2 = (f32[8,2,16,128]{3,2,1,0:T(8,128)S(1)}, f32[8,2,16,128]{3,2,1,0:T(8,128)S(1)}, u32[]{:S(2)}, u32[]{:S(2)}) collective-permute-start(f32[8,2,16,128]{3,2,1,0:T(8,128)S(1)} %all_to_all.17), channel_id=1, source_target_pairs={{0,1},{1,0},{2,3},{3,2},{4,5},{5,4},{6,7},{7,6},{8,9},{9,8},{10,11... | collective-permute-start | bytes 393224 | tf_op jit(solution)/shard_map/ppermute | solution.py:725

commit v32 on v31

--- a/solution.py
+++ b/solution.py
@@ -471,7 +471,7 @@
     def share_chunk(first, before):
         disp = disp_ref.at[:, pl.ds((first + 1) * layers, (count + 1) * layers)]
         coef = coef_ref.at[pl.ds(first, count)]
-        plane, beside, further = (ref.at[pl.ds(first + 2, count)] for ref in shares)
+        plane = plane_ref.at[pl.ds(first + 2, count)]
         here = [disp[part, rows(0, layers)] for part in range(3)]
         for p in range(count):
             later = [disp[part, rows(p + 1, layers)] for part in range(3)]
@@ -489,14 +489,21 @@
             right = jnp.where(y < row_width - 1, right, 0.0)
             total = before + ahead + upward + pltpu.roll(upward, 1, 0)
             total = total + right + pltpu.roll(right, 1, 1)
-            share = (0.5 / load_cases) * total * coef[p]
-            plane[p] = share
+            plane[p] = (0.5 / load_cases) * total * coef[p]
+            before, here = ahead, later
+        return before
+
+    each_chunk(planes, count, share_chunk, zero)
+
+    def spread_chunk(first, carry):
+        plane, beside, further = (ref.at[pl.ds(first + 2, count)] for ref in shares)
+        for p in range(count):
+            share = plane[p]
             beside[p] = shift_sum(share, 1, 1)
             further[p] = shift_sum(share, 1, 2)
-            before, here = ahead, later
-        return before
-
-    each_chunk(planes, count, share_chunk, zero)
+        return carry
+
+    each_chunk(planes, count, spread_chunk, 0)
     filter_group(1, shares, weight_ref, near_ref, far_ref, sent_ref)
 
 

time: 45.5 us -> 45.5 us (level)
  no operation moved by 1% of the time
where the time goes in v32:
time: 45.5 us; the launch traced here: 45.1 us
  blocking collectives  33.1 us (73%)
  Pallas kernels  7.52 us (17%)
  starting transfers between devices  1.75 us (4%)
  waiting for transfers between devices  1.11 us (2%)
  local copies, waits for them, and re-layouts  0.82 us (2%)
  between operations  0.72 us (2%)
    all_to_all x3, blocking collectives, between_chips(): lax.all_to_all(pieces, 'space', 0, 0, axis_index_groups=chip_groups())  33.1 us
    pallas_call x1, Pallas kernels, sweep_call(): pl.pallas_call(sweep_kernel, out_shape=[floats(3, (planes + 2) * layers,...  2.52 us
    pallas_call x1, Pallas kernels, design_call(): pl.pallas_call(design_kernel, out_shape=floats(*density.shape[2:]), in_sp...  1.82 us
    ppermute x3, starting transfers between devices, other_core(): return lax.ppermute(block, 'space', [(i, i ^ 1) for i in range(devices)])  1.75 us
    pallas_call x1, Pallas kernels, share_call(): pl.pallas_call(share_kernel, out_shape=[floats(*group_shape)] + [floats(p...  1.29 us
    ppermute x3, waiting for transfers between devices, other_core(): return lax.ppermute(block, 'space', [(i, i ^ 1) for i in range(devices)])  1.11 us
    pallas_call x1, Pallas kernels, prepare_call(): pl.pallas_call(prepare_kernel, out_shape=[floats(len(ALL_SQUARES), layers...  1 us
  transfers between devices with their start and end apart: 3, of which 2 were waited for; matrix products, arithmetic and copies ran while one was open for 0% of the time, Pallas kernels for 4%

profile of v32, /device:TPU:0, one launch (start us, length us, event | category | flops | bytes accessed | tf_op | source)
XLA Modules:
  0.0 45.1 jit_solution(9800154542172345731)
XLA Ops:
  0.6 0.0 copy-start
  0.6 0.8 %broadcast_in_dim.4 = f32[8,2,16,128]{3,2,1,0:T(8,128)S(1)} broadcast(f32[2,16,128]{2,1,0:T(8,128)} %param.6), dimensions={1,2,3} | broadcast | bytes 147456 | tf_op jit(solution)/shard_map/broadcast_in_dim | solution.py:746
  1.4 13.5 %all_to_all.15.density_ref = f32[8,2,16,128]{3,2,1,0:T(8,128)S(1)} all-to-all(f32[8,2,16,128]{3,2,1,0:T(8,128)S(1)} %broadcast_in_dim.4), channel_id=1, replica_groups={{0,3,4,7,8,11,12,15},{1,2,5,6,9,10,13,14},{16,19,20,23,24,27,28,31},{17..., dimensions={0} | all-to-all | bytes 262144 | tf_op jit(solution)/shard_map/all_to_all | solution.py:741
  14.9 0.7 %collective-permute-start = (f32[8,2,16,128]{3,2,1,0:T(8,128)S(1)}, f32[8,2,16,128]{3,2,1,0:T(8,128)S(1)}, u32[]{:S(2)}, u32[]{:S(2)}) collective-permute-start(f32[8,2,16,128]{3,2,1,0:T(8,128)S(1)} %all_to_all.15.density_ref), channel_id=1, source_target_pairs={{0,1},{1,0},{2,3},{3,2},{4,5},{5,4},{6,7},{7,6},{8,9},{9,8},{10,11... | collective-permute-start | bytes 393224 | tf_op jit(solution)/shard_map/ppermute | solution.py:732
  15.6 1.0 %prepare.1 = (f32[10,16,128]{2,1,0:T(8,128)S(1)}, f32[5,16,128]{2,1,0:T(8,128)S(1)}, f32[32,16,128]{2,1,0:T(8,128)S(1)}, f32[3,16,128]{2,1,0:T(8,128)S(1)}, f32[...) custom-call(s32[16]{0:T(128)} %radius_hbm, s32[16]{0:T(128)} %index_hbm, f32[3,16]{1,0:T(4,128)} %bitcast.12, ...), custom_call_target="tpu_custom_call" | custom-call | flops 5242880 | bytes 524288 | tf_op jit(solution)/shard_map/prepare/pallas_call | solution.py:610
  16.6 0.0 collective-permute-done
  16.6 0.0 copy-done
  16.6 2.5 %sweeps.1 = (f32[3,544,128]{2,1,0:T(8,128)S(1)}, f32[32,16,128]{2,1,0:T(8,128)S(1)}) custom-call(f32[8,128]{1,0:T(8,128)S(1)} %get-tuple-element.31.spot_ref, f32[3,16,128]{2,1,0:T(8,128)S(1)} %get-tuple-element.32.load_ref, f32[10,16,128]{2,1,0:T(8,128)S(1)} %get-tuple-element.33.weight_ref, f32[5,16,128]{2,1,0:T(8,128)S(1)} %get-tuple-element.34.inverse_ref, ...), custom_call_target="tpu_custom_call" | custom-call | tf_op jit(solution)/shard_map/sweeps/pallas_call | solution.py:655
  19.2 1.3 %share.1 = (f32[8,2,16,128]{3,2,1,0:T(8,128)S(1)}, f32[36,16,128]{2,1,0:T(8,128)S(1)}, f32[36,16,128]{2,1,0:T(8,128)S(1)}, f32[36,16,128]{2,1,0:T(8,128)S(1)}) custom-call(f32[3,544,128]{2,1,0:T(8,128)S(1)} %get-tuple-element.43.disp_ref, f32[32,16,128]{2,1,0:T(8,128)S(1)} %get-tuple-element.38.coef_ref, f32[10,16,128]{2,1,0:T(8,128)S(1)} %get-tuple-element.33.weight_ref), custom_call_target="tpu_custom_call" | custom-call | tf_op jit(solution)/shard_map/share/pallas_call | solution.py:686
  20.5 0.4 collective-permute-start.1
  20.8 0.9 %kept.1 = (f32[3,512,128]{2,1,0:T(8,128)}, f32[8,2,16,128]{3,2,1,0:T(8,128)S(1)}) custom-call(f32[3,544,128]{2,1,0:T(8,128)S(1)} %get-tuple-element.43.disp_ref, f32[10,16,128]{2,1,0:T(8,128)S(1)} %get-tuple-element.33.weight_ref, f32[36,16,128]{2,1,0:T(8,128)S(1)} %get-tuple-element.44.plane_ref, f32[36,16,128]{2,1,0:T(8,128)S(1)} %get-tuple-element.45.beside_ref, ...), custom_call_target="tpu_custom_call" | custom-call | flops 4177920 | bytes 1671168 | tf_op jit(solution)/shard_map/kept/pallas_call | solution.py:701
  21.7 0.1 collective-permute-done.1
  21.9 10.0 %all_to_all.16 = f32[8,2,16,128]{3,2,1,0:T(8,128)S(1)} all-to-all(f32[8,2,16,128]{3,2,1,0:T(8,128)S(1)} %add.3), channel_id=1, replica_groups={{0,3,4,7,8,11,12,15},{1,2,5,6,9,10,13,14},{16,19,20,23,24,27,28,31},{17..., dimensions={0} | all-to-all | bytes 262144 | tf_op jit(solution)/shard_map/all_to_all | solution.py:741
  32.0 9.6 %all_to_all.17 = f32[8,2,16,128]{3,2,1,0:T(8,128)S(1)} all-to-all(f32[8,2,16,128]{3,2,1,0:T(8,128)S(1)} %broadcast_in_dim.5), channel_id=1, replica_groups={{0,3,4,7,8,11,12,15},{1,2,5,6,9,10,13,14},{16,19,20,23,24,27,28,31},{17..., dimensions={0} | all-to-all | bytes 262144 | tf_op jit(solution)/shard_map/all_to_all | solution.py:741
  41.6 0.7 %collective-permute-start.2 = (f32[8,2,16,128]{3,2,1,0:T(8,128)S(1)}, f32[8,2,16,128]{3,2,1,0:T(8,128)S(1)}, u32[]{:S(2)}, u32[]{:S(2)}) collective-permute-start(f32[8,2,16,128]{3,2,1,0:T(8,128)S(1)} %all_to_all.17), channel_id=1, source_target_pairs={{0,1},{1,0},{2,3},{3,2},{4,5},{5,4},{6,7},{7,6},{8,9},{9,8},{10,11... | collective-permute-start | bytes 393224 | tf_op jit(solution)/shard_map/ppermute | solution.py:732
  42.3 1.0 %collective-permute-done.2 = f32[8,2,16,128]{3,2,1,0:T(8,128)S(1)} collective-permute-done((f32[8,2,16,128]{3,2,1,0:T(8,128)S(1)}, f32[8,2,16,128]{3,2,1,0:T(8,128)S(1)}, u32[]{:S(2)}, u32[]{:S(2)}) %collective-permute-start.2) | collective-permute-done | bytes 131104 | tf_op jit(solution)/shard_map/ppermute | solution.py:732
  43.3 1.8 %design.1 = f32[2,16,128]{2,1,0:T(8,128)} custom-call(f32[2,8,2,16,128]{4,3,2,1,0:T(8,128)S(1)} %pad_maximum_fusion.1.root_ref, f32[2,8,2,16,128]{4,3,2,1,0:T(8,128)S(1)} %pad_maximum_fusion.density_ref), custom_call_target="tpu_custom_call" | custom-call | tf_op jit(solution)/shard_map/design/pallas_call | solution.py:719
  (6 shorter events, 0.1 us)
Async XLA Ops:
  0.6 16.0 %copy-start = (f32[1,3,32,16,128]{4,3,2,1,0:T(8,128)S(1)}, f32[1,3,32,16,128]{4,3,2,1,0:T(8,128)}, u32[]{:S(2)}) copy-start(f32[1,3,32,16,128]{4,3,2,1,0:T(8,128)} %param.7) | copy-start | bytes 2359300
  14.9 1.7 %collective-permute-start = (f32[8,2,16,128]{3,2,1,0:T(8,128)S(1)}, f32[8,2,16,128]{3,2,1,0:T(8,128)S(1)}, u32[]{:S(2)}, u32[]{:S(2)}) collective-permute-start(f32[8,2,16,128]{3,2,1,0:T(8,128)S(1)} %all_to_all.15.density_ref), channel_id=1, source_target_pairs={{0,1},{1,0},{2,3},{3,2},{4,5},{5,4},{6,7},{7,6},{8,9},{9,8},{10,11... | collective-permute-start | bytes 393224 | tf_op jit(solution)/shard_map/ppermute | solution.py:732
  20.5 1.4 %collective-permute-start.1 = (f32[8,2,16,128]{3,2,1,0:T(8,128)S(1)}, f32[8,2,16,128]{3,2,1,0:T(8,128)S(1)}, u32[]{:S(2)}, u32[]{:S(2)}) collective-permute-start(f32[8,2,16,128]{3,2,1,0:T(8,128)S(1)} %get-tuple-element.48), channel_id=1, source_target_pairs={{0,1},{1,0},{2,3},{3,2},{4,5},{5,4},{6,7},{7,6},{8,9},{9,8},{10,11... | collective-permute-start | bytes 393224 | tf_op jit(solution)/shard_map/ppermute | solution.py:732
  41.6 1.7 %collective-permute-start.2 = (f32[8,2,16,128]{3,2,1,0:T(8,128)S(1)}, f32[8,2,16,128]{3,2,1,0:T(8,128)S(1)}, u32[]{:S(2)}, u32[]{:S(2)}) collective-permute-start(f32[8,2,16,128]{3,2,1,0:T(8,128)S(1)} %all_to_all.17), channel_id=1, source_target_pairs={{0,1},{1,0},{2,3},{3,2},{4,5},{5,4},{6,7},{7,6},{8,9},{9,8},{10,11... | collective-permute-start | bytes 393224 | tf_op jit(solution)/shard_map/ppermute | solution.py:732

commit v33 on v31

--- a/solution.py
+++ b/solution.py
@@ -471,7 +471,7 @@
     def share_chunk(first, before):
         disp = disp_ref.at[:, pl.ds((first + 1) * layers, (count + 1) * layers)]
         coef = coef_ref.at[pl.ds(first, count)]
-        plane, beside, further = (ref.at[pl.ds(first + 2, count)] for ref in shares)
+        plane = plane_ref.at[pl.ds(first + 2, count)]
         here = [disp[part, rows(0, layers)] for part in range(3)]
         for p in range(count):
             later = [disp[part, rows(p + 1, layers)] for part in range(3)]
@@ -489,14 +489,16 @@
             right = jnp.where(y < row_width - 1, right, 0.0)
             total = before + ahead + upward + pltpu.roll(upward, 1, 0)
             total = total + right + pltpu.roll(right, 1, 1)
-            share = (0.5 / load_cases) * total * coef[p]
-            plane[p] = share
-            beside[p] = shift_sum(share, 1, 1)
-            further[p] = shift_sum(share, 1, 2)
+            plane[p] = (0.5 / load_cases) * total * coef[p]
             before, here = ahead, later
         return before
 
     each_chunk(planes, count, share_chunk, zero)
+
+    for x in range(planes):
+        share = plane_ref[x + 2]
+        beside_ref[x + 2] = shift_sum(share, 1, 1)
+        further_ref[x + 2] = shift_sum(share, 1, 2)
     filter_group(1, shares, weight_ref, near_ref, far_ref, sent_ref)
 
 

time: 45.5 us -> 45.3 us (level)
  no operation moved by 1% of the time
where the time goes in v33:
time: 45.3 us; the launch traced here: 44.9 us
  blocking collectives  33.1 us (73%)
  Pallas kernels  7.3 us (16%)
  starting transfers between devices  1.75 us (4%)
  waiting for transfers between devices  1.12 us (2%)
  local copies, waits for them, and re-layouts  0.82 us (2%)
  between operations  0.72 us (2%)
    all_to_all x3, blocking collectives, between_chips(): lax.all_to_all(pieces, 'space', 0, 0, axis_index_groups=chip_groups())  33.1 us
    pallas_call x1, Pallas kernels, sweep_call(): pl.pallas_call(sweep_kernel, out_shape=[floats(3, (planes + 2) * layers,...  2.52 us
    pallas_call x1, Pallas kernels, design_call(): pl.pallas_call(design_kernel, out_shape=floats(*density.shape[2:]), in_sp...  1.82 us
    ppermute x3, starting transfers between devices, other_core(): return lax.ppermute(block, 'space', [(i, i ^ 1) for i in range(devices)])  1.75 us
    ppermute x3, waiting for transfers between devices, other_core(): return lax.ppermute(block, 'space', [(i, i ^ 1) for i in range(devices)])  1.12 us
    pallas_call x1, Pallas kernels, share_call(): pl.pallas_call(share_kernel, out_shape=[floats(*group_shape)] + [floats(p...  1.07 us
    pallas_call x1, Pallas kernels, prepare_call(): pl.pallas_call(prepare_kernel, out_shape=[floats(len(ALL_SQUARES), layers...  1 us
  transfers between devices with their start and end apart: 3, of which 2 were waited for; matrix products, arithmetic and copies ran while one was open for 0% of the time, Pallas kernels for 4%

profile of v33, /device:TPU:0, one launch (start us, length us, event | category | flops | bytes accessed | tf_op | source)
XLA Modules:
  0.0 44.9 jit_solution(9259484847879845491)
XLA Ops:
  0.6 0.0 copy-start
  0.6 0.8 %broadcast_in_dim.4 = f32[8,2,16,128]{3,2,1,0:T(8,128)S(1)} broadcast(f32[2,16,128]{2,1,0:T(8,128)} %param.6), dimensions={1,2,3} | broadcast | bytes 147456 | tf_op jit(solution)/shard_map/broadcast_in_dim | solution.py:741
  1.4 13.5 %all_to_all.15.density_ref = f32[8,2,16,128]{3,2,1,0:T(8,128)S(1)} all-to-all(f32[8,2,16,128]{3,2,1,0:T(8,128)S(1)} %broadcast_in_dim.4), channel_id=1, replica_groups={{0,3,4,7,8,11,12,15},{1,2,5,6,9,10,13,14},{16,19,20,23,24,27,28,31},{17..., dimensions={0} | all-to-all | bytes 262144 | tf_op jit(solution)/shard_map/all_to_all | solution.py:736
  14.9 0.7 %collective-permute-start = (f32[8,2,16,128]{3,2,1,0:T(8,128)S(1)}, f32[8,2,16,128]{3,2,1,0:T(8,128)S(1)}, u32[]{:S(2)}, u32[]{:S(2)}) collective-permute-start(f32[8,2,16,128]{3,2,1,0:T(8,128)S(1)} %all_to_all.15.density_ref), channel_id=1, source_target_pairs={{0,1},{1,0},{2,3},{3,2},{4,5},{5,4},{6,7},{7,6},{8,9},{9,8},{10,11... | collective-permute-start | bytes 393224 | tf_op jit(solution)/shard_map/ppermute | solution.py:727
  15.6 1.0 %prepare.1 = (f32[10,16,128]{2,1,0:T(8,128)S(1)}, f32[5,16,128]{2,1,0:T(8,128)S(1)}, f32[32,16,128]{2,1,0:T(8,128)S(1)}, f32[3,16,128]{2,1,0:T(8,128)S(1)}, f32[...) custom-call(s32[16]{0:T(128)} %radius_hbm, s32[16]{0:T(128)} %index_hbm, f32[3,16]{1,0:T(4,128)} %bitcast.12, ...), custom_call_target="tpu_custom_call" | custom-call | flops 5242880 | bytes 524288 | tf_op jit(solution)/shard_map/prepare/pallas_call | solution.py:605
  16.6 0.0 collective-permute-done
  16.6 0.0 copy-done
  16.6 2.5 %sweeps.1 = (f32[3,544,128]{2,1,0:T(8,128)S(1)}, f32[32,16,128]{2,1,0:T(8,128)S(1)}) custom-call(f32[8,128]{1,0:T(8,128)S(1)} %get-tuple-element.31.spot_ref, f32[3,16,128]{2,1,0:T(8,128)S(1)} %get-tuple-element.32.load_ref, f32[10,16,128]{2,1,0:T(8,128)S(1)} %get-tuple-element.33.weight_ref, f32[5,16,128]{2,1,0:T(8,128)S(1)} %get-tuple-element.34.inverse_ref, ...), custom_call_target="tpu_custom_call" | custom-call | tf_op jit(solution)/shard_map/sweeps/pallas_call | solution.py:650
  19.2 1.1 %share.1 = (f32[8,2,16,128]{3,2,1,0:T(8,128)S(1)}, f32[36,16,128]{2,1,0:T(8,128)S(1)}, f32[36,16,128]{2,1,0:T(8,128)S(1)}, f32[36,16,128]{2,1,0:T(8,128)S(1)}) custom-call(f32[3,544,128]{2,1,0:T(8,128)S(1)} %get-tuple-element.43.disp_ref, f32[32,16,128]{2,1,0:T(8,128)S(1)} %get-tuple-element.38.coef_ref, f32[10,16,128]{2,1,0:T(8,128)S(1)} %get-tuple-element.33.weight_ref), custom_call_target="tpu_custom_call" | custom-call | tf_op jit(solution)/shard_map/share/pallas_call | solution.py:681
  20.2 0.4 collective-permute-start.1
  20.6 0.9 %kept.1 = (f32[3,512,128]{2,1,0:T(8,128)}, f32[8,2,16,128]{3,2,1,0:T(8,128)S(1)}) custom-call(f32[3,544,128]{2,1,0:T(8,128)S(1)} %get-tuple-element.43.disp_ref, f32[10,16,128]{2,1,0:T(8,128)S(1)} %get-tuple-element.33.weight_ref, f32[36,16,128]{2,1,0:T(8,128)S(1)} %get-tuple-element.44.plane_ref, f32[36,16,128]{2,1,0:T(8,128)S(1)} %get-tuple-element.45.beside_ref, ...), custom_call_target="tpu_custom_call" | custom-call | flops 4177920 | bytes 1671168 | tf_op jit(solution)/shard_map/kept/pallas_call | solution.py:696
  21.5 0.1 collective-permute-done.1
  21.7 10.0 %all_to_all.16 = f32[8,2,16,128]{3,2,1,0:T(8,128)S(1)} all-to-all(f32[8,2,16,128]{3,2,1,0:T(8,128)S(1)} %add.3), channel_id=1, replica_groups={{0,3,4,7,8,11,12,15},{1,2,5,6,9,10,13,14},{16,19,20,23,24,27,28,31},{17..., dimensions={0} | all-to-all | bytes 262144 | tf_op jit(solution)/shard_map/all_to_all | solution.py:736
  31.7 9.6 %all_to_all.17 = f32[8,2,16,128]{3,2,1,0:T(8,128)S(1)} all-to-all(f32[8,2,16,128]{3,2,1,0:T(8,128)S(1)} %broadcast_in_dim.5), channel_id=1, replica_groups={{0,3,4,7,8,11,12,15},{1,2,5,6,9,10,13,14},{16,19,20,23,24,27,28,31},{17..., dimensions={0} | all-to-all | bytes 262144 | tf_op jit(solution)/shard_map/all_to_all | solution.py:736
  41.4 0.7 %collective-permute-start.2 = (f32[8,2,16,128]{3,2,1,0:T(8,128)S(1)}, f32[8,2,16,128]{3,2,1,0:T(8,128)S(1)}, u32[]{:S(2)}, u32[]{:S(2)}) collective-permute-start(f32[8,2,16,128]{3,2,1,0:T(8,128)S(1)} %all_to_all.17), channel_id=1, source_target_pairs={{0,1},{1,0},{2,3},{3,2},{4,5},{5,4},{6,7},{7,6},{8,9},{9,8},{10,11... | collective-permute-start | bytes 393224 | tf_op jit(solution)/shard_map/ppermute | solution.py:727
  42.1 1.0 %collective-permute-done.2 = f32[8,2,16,128]{3,2,1,0:T(8,128)S(1)} collective-permute-done((f32[8,2,16,128]{3,2,1,0:T(8,128)S(1)}, f32[8,2,16,128]{3,2,1,0:T(8,128)S(1)}, u32[]{:S(2)}, u32[]{:S(2)}) %collective-permute-start.2) | collective-permute-done | bytes 131104 | tf_op jit(solution)/shard_map/ppermute | solution.py:727
  43.1 1.8 %design.1 = f32[2,16,128]{2,1,0:T(8,128)} custom-call(f32[2,8,2,16,128]{4,3,2,1,0:T(8,128)S(1)} %pad_maximum_fusion.1.root_ref, f32[2,8,2,16,128]{4,3,2,1,0:T(8,128)S(1)} %pad_maximum_fusion.density_ref), custom_call_target="tpu_custom_call" | custom-call | tf_op jit(solution)/shard_map/design/pallas_call | solution.py:714
  (6 shorter events, 0.1 us)
Async XLA Ops:
  0.6 16.0 %copy-start = (f32[1,3,32,16,128]{4,3,2,1,0:T(8,128)S(1)}, f32[1,3,32,16,128]{4,3,2,1,0:T(8,128)}, u32[]{:S(2)}) copy-start(f32[1,3,32,16,128]{4,3,2,1,0:T(8,128)} %param.7) | copy-start | bytes 2359300
  14.9 1.7 %collective-permute-start = (f32[8,2,16,128]{3,2,1,0:T(8,128)S(1)}, f32[8,2,16,128]{3,2,1,0:T(8,128)S(1)}, u32[]{:S(2)}, u32[]{:S(2)}) collective-permute-start(f32[8,2,16,128]{3,2,1,0:T(8,128)S(1)} %all_to_all.15.density_ref), channel_id=1, source_target_pairs={{0,1},{1,0},{2,3},{3,2},{4,5},{5,4},{6,7},{7,6},{8,9},{9,8},{10,11... | collective-permute-start | bytes 393224 | tf_op jit(solution)/shard_map/ppermute | solution.py:727
  20.2 1.4 %collective-permute-start.1 = (f32[8,2,16,128]{3,2,1,0:T(8,128)S(1)}, f32[8,2,16,128]{3,2,1,0:T(8,128)S(1)}, u32[]{:S(2)}, u32[]{:S(2)}) collective-permute-start(f32[8,2,16,128]{3,2,1,0:T(8,128)S(1)} %get-tuple-element.48), channel_id=1, source_target_pairs={{0,1},{1,0},{2,3},{3,2},{4,5},{5,4},{6,7},{7,6},{8,9},{9,8},{10,11... | collective-permute-start | bytes 393224 | tf_op jit(solution)/shard_map/ppermute | solution.py:727
  41.4 1.7 %collective-permute-start.2 = (f32[8,2,16,128]{3,2,1,0:T(8,128)S(1)}, f32[8,2,16,128]{3,2,1,0:T(8,128)S(1)}, u32[]{:S(2)}, u32[]{:S(2)}) collective-permute-start(f32[8,2,16,128]{3,2,1,0:T(8,128)S(1)} %all_to_all.17), channel_id=1, source_target_pairs={{0,1},{1,0},{2,3},{3,2},{4,5},{5,4},{6,7},{7,6},{8,9},{9,8},{10,11... | collective-permute-start | bytes 393224 | tf_op jit(solution)/shard_map/ppermute | solution.py:727

commit v34 on v33

--- a/solution.py
+++ b/solution.py
@@ -103,7 +103,7 @@
 
 
 def edge_class(x, planes):
-    return jnp.minimum(x, 2) + jnp.maximum(x - (planes - 3), 0)
+    return min(x, 2) + max(x - (planes - 3), 0)
 
 
 def zero_edges(ref):
@@ -297,66 +297,52 @@
             rate[part, slot] = factor
             source[part, rows(slot, layers)] = start[part] * free
 
-    piece = planes // 2
-
-    def modulus_piece(first, carry):
-        count = piece
-        near = near_ref.at[pl.ds(first + 2, count)]
-        side = side_ref.at[pl.ds(first + 1, count + 2)]
-        far = far_ref.at[pl.ds(first, count + 4)]
-        moduli = modulus_ref.at[pl.ds(first * layers, (count + 1) * layers)]
-        coef = coef_ref.at[pl.ds(first, count)]
+    for x in range(planes):
+        inverse = inverse_ref[edge_class(x, planes)]
+        filtered = near_ref[x + 2] + side_ref[x + 1] + side_ref[x + 3] + far_ref[x] + far_ref[x + 4]
+        filtered = filtered * inverse
+        modulus_ref[rows(x + 1, layers)] = floor_modulus + (1.0 - floor_modulus) * (
+            filtered * filtered * filtered
+        )
+        coef_ref[x] = 3.0 * (1.0 - floor_modulus) * (filtered * filtered) * inverse
+
+    modulus_ref[rows(planes + 1, layers)] = zero
+    across_ref[0] = zero
+    up_ref[rows(0, layers)] = zero
+    count = planes // 2
+
+    def face_piece(first, before):
+        moduli = modulus_ref.at[pl.ds(first * layers, (count + 2) * layers)]
         free = free_ref.at[pl.ds(first, count)]
+        start = start_ref.at[:, pl.ds(first, count)]
         views = (
-            across_ref.at[pl.ds(first, count)],
-            up_ref.at[pl.ds(first * layers, count * layers)],
-            right_ref.at[pl.ds(first, count)],
-            left_ref.at[pl.ds(first, count)],
-            rate_ref.at[:, pl.ds(first, count)],
-            first_ref.at[:, pl.ds(first * layers, count * layers)],
+            across_ref.at[pl.ds(first + 1, count)],
+            up_ref.at[pl.ds((first + 1) * layers, count * layers)],
+            right_ref.at[pl.ds(first + 1, count)],
+            left_ref.at[pl.ds(first + 1, count)],
+            rate_ref.at[:, pl.ds(first + 1, count)],
+            first_ref.at[:, pl.ds((first + 1) * layers, count * layers)],
         )
-        modulus, before = carry
         for p in range(count):
-            inverse = inverse_ref[edge_class(first + p, planes)]
-            filtered = near[p] + side[p] + side[p + 2] + far[p] + far[p + 4]
-            filtered = filtered * inverse
-            later = floor_modulus + (1.0 - floor_modulus) * (filtered * filtered * filtered)
-            coef[p] = 3.0 * (1.0 - floor_modulus) * (filtered * filtered) * inverse
-            moduli[rows(p + 1, layers)] = later
-            ahead = 0.5 * (modulus + later)
-            if p == 0:
-                ahead = jnp.where(first > 0, ahead, 0.0)
-            above = moduli[rows(p, layers, 1)] if p else pltpu.roll(modulus, layers - 1, 0)
-            below = moduli[rows(p, layers, -1)] if p else pltpu.roll(modulus, 1, 0)
-            previous = jnp.maximum(first + p - 1, 0)
+            modulus = moduli[rows(p + 1, layers)]
+            ahead = 0.5 * (modulus + moduli[rows(p + 2, layers)])
+            if p == count - 1:
+                ahead = jnp.where(first + count < planes, ahead, 0.0)
             store_faces(
                 p,
                 modulus,
-                above,
-                below,
+                moduli[rows(p + 1, layers, 1)],
+                moduli[rows(p + 1, layers, -1)],
                 ahead,
                 before,
-                free_ref[previous],
-                [start_ref[part, previous] for part in range(3)],
+                free[p],
+                [start[part, p] for part in range(3)],
                 views,
             )
-            modulus, before = later, ahead
-        return modulus, before
-
-    modulus, before = each_chunk(
-        planes, piece, modulus_piece, (jnp.ones(shape, jnp.float32), zero)
-    )
-    store_faces(
-        planes,
-        modulus,
-        pltpu.roll(modulus, layers - 1, 0),
-        pltpu.roll(modulus, 1, 0),
-        zero,
-        before,
-        free_ref[planes - 1],
-        [start_ref[part, planes - 1] for part in range(3)],
-        (across_ref, up_ref, right_ref, left_ref, rate_ref, first_ref),
-    )
+            before = ahead
+        return before
+
+    each_chunk(planes, count, face_piece, zero)
 
     own_x = jnp.max(spot_ref[...]).astype(jnp.int32)
 
@@ -662,7 +648,7 @@
             scratch(planes + 4, layers),
             scratch(planes + 4, layers),
             scratch(planes + 4, layers),
-            scratch((planes + 1) * layers),
+            scratch((planes + 2) * layers),
             scratch(planes + 1, layers),
             scratch((planes + 1) * layers),
             scratch(planes + 1, layers),

time: 45.3 us -> 45.3 us (level)
  no operation moved by 1% of the time
where the time goes in v34:
time: 45.3 us; the launch traced here: 44.9 us
  blocking collectives  33.1 us (73%)
  Pallas kernels  7.31 us (16%)
  starting transfers between devices  1.75 us (4%)
  waiting for transfers between devices  1.12 us (2%)
  local copies, waits for them, and re-layouts  0.82 us (2%)
  between operations  0.72 us (2%)
    all_to_all x3, blocking collectives, between_chips(): lax.all_to_all(pieces, 'space', 0, 0, axis_index_groups=chip_groups())  33.1 us
    pallas_call x1, Pallas kernels, sweep_call(): pl.pallas_call(sweep_kernel, out_shape=[floats(3, (planes + 2) * layers,...  2.53 us
    pallas_call x1, Pallas kernels, design_call(): pl.pallas_call(design_kernel, out_shape=floats(*density.shape[2:]), in_sp...  1.82 us
    ppermute x3, starting transfers between devices, other_core(): return lax.ppermute(block, 'space', [(i, i ^ 1) for i in range(devices)])  1.75 us
    ppermute x3, waiting for transfers between devices, other_core(): return lax.ppermute(block, 'space', [(i, i ^ 1) for i in range(devices)])  1.12 us
    pallas_call x1, Pallas kernels, share_call(): pl.pallas_call(share_kernel, out_shape=[floats(*group_shape)] + [floats(p...  1.07 us
    pallas_call x1, Pallas kernels, prepare_call(): pl.pallas_call(prepare_kernel, out_shape=[floats(len(ALL_SQUARES), layers...  1 us
  transfers between devices with their start and end apart: 3, of which 2 were waited for; matrix products, arithmetic and copies ran while one was open for 0% of the time, Pallas kernels for 4%

profile of v34, /device:TPU:0, one launch (start us, length us, event | category | flops | bytes accessed | tf_op | source)
XLA Modules:
  0.0 44.9 jit_solution(9127753358740493214)
XLA Ops:
  0.6 0.0 copy-start
  0.6 0.8 %broadcast_in_dim.4 = f32[8,2,16,128]{3,2,1,0:T(8,128)S(1)} broadcast(f32[2,16,128]{2,1,0:T(8,128)} %param.6), dimensions={1,2,3} | broadcast | bytes 147456 | tf_op jit(solution)/shard_map/broadcast_in_dim | solution.py:727
  1.4 13.5 %all_to_all.15.density_ref = f32[8,2,16,128]{3,2,1,0:T(8,128)S(1)} all-to-all(f32[8,2,16,128]{3,2,1,0:T(8,128)S(1)} %broadcast_in_dim.4), channel_id=1, replica_groups={{0,3,4,7,8,11,12,15},{1,2,5,6,9,10,13,14},{16,19,20,23,24,27,28,31},{17..., dimensions={0} | all-to-all | bytes 262144 | tf_op jit(solution)/shard_map/all_to_all | solution.py:722
  14.9 0.7 %collective-permute-start = (f32[8,2,16,128]{3,2,1,0:T(8,128)S(1)}, f32[8,2,16,128]{3,2,1,0:T(8,128)S(1)}, u32[]{:S(2)}, u32[]{:S(2)}) collective-permute-start(f32[8,2,16,128]{3,2,1,0:T(8,128)S(1)} %all_to_all.15.density_ref), channel_id=1, source_target_pairs={{0,1},{1,0},{2,3},{3,2},{4,5},{5,4},{6,7},{7,6},{8,9},{9,8},{10,11... | collective-permute-start | bytes 393224 | tf_op jit(solution)/shard_map/ppermute | solution.py:713
  15.6 1.0 %prepare.1 = (f32[10,16,128]{2,1,0:T(8,128)S(1)}, f32[5,16,128]{2,1,0:T(8,128)S(1)}, f32[32,16,128]{2,1,0:T(8,128)S(1)}, f32[3,16,128]{2,1,0:T(8,128)S(1)}, f32[...) custom-call(s32[16]{0:T(128)} %radius_hbm, s32[16]{0:T(128)} %index_hbm, f32[3,16]{1,0:T(4,128)} %bitcast.12, ...), custom_call_target="tpu_custom_call" | custom-call | flops 5242880 | bytes 524288 | tf_op jit(solution)/shard_map/prepare/pallas_call | solution.py:591
  16.6 0.0 collective-permute-done
  16.6 0.0 copy-done
  16.6 2.5 %sweeps.1 = (f32[3,544,128]{2,1,0:T(8,128)S(1)}, f32[32,16,128]{2,1,0:T(8,128)S(1)}) custom-call(f32[8,128]{1,0:T(8,128)S(1)} %get-tuple-element.31.spot_ref, f32[3,16,128]{2,1,0:T(8,128)S(1)} %get-tuple-element.32.load_ref, f32[10,16,128]{2,1,0:T(8,128)S(1)} %get-tuple-element.33.weight_ref, f32[5,16,128]{2,1,0:T(8,128)S(1)} %get-tuple-element.34.inverse_ref, ...), custom_call_target="tpu_custom_call" | custom-call | tf_op jit(solution)/shard_map/sweeps/pallas_call | solution.py:636
  19.2 1.1 %share.1 = (f32[8,2,16,128]{3,2,1,0:T(8,128)S(1)}, f32[36,16,128]{2,1,0:T(8,128)S(1)}, f32[36,16,128]{2,1,0:T(8,128)S(1)}, f32[36,16,128]{2,1,0:T(8,128)S(1)}) custom-call(f32[3,544,128]{2,1,0:T(8,128)S(1)} %get-tuple-element.43.disp_ref, f32[32,16,128]{2,1,0:T(8,128)S(1)} %get-tuple-element.38.coef_ref, f32[10,16,128]{2,1,0:T(8,128)S(1)} %get-tuple-element.33.weight_ref), custom_call_target="tpu_custom_call" | custom-call | tf_op jit(solution)/shard_map/share/pallas_call | solution.py:667
  20.2 0.4 collective-permute-start.1
  20.6 0.9 %kept.1 = (f32[3,512,128]{2,1,0:T(8,128)}, f32[8,2,16,128]{3,2,1,0:T(8,128)S(1)}) custom-call(f32[3,544,128]{2,1,0:T(8,128)S(1)} %get-tuple-element.43.disp_ref, f32[10,16,128]{2,1,0:T(8,128)S(1)} %get-tuple-element.33.weight_ref, f32[36,16,128]{2,1,0:T(8,128)S(1)} %get-tuple-element.44.plane_ref, f32[36,16,128]{2,1,0:T(8,128)S(1)} %get-tuple-element.45.beside_ref, ...), custom_call_target="tpu_custom_call" | custom-call | flops 4177920 | bytes 1671168 | tf_op jit(solution)/shard_map/kept/pallas_call | solution.py:682
  21.5 0.1 collective-permute-done.1
  21.7 10.0 %all_to_all.16 = f32[8,2,16,128]{3,2,1,0:T(8,128)S(1)} all-to-all(f32[8,2,16,128]{3,2,1,0:T(8,128)S(1)} %add.3), channel_id=1, replica_groups={{0,3,4,7,8,11,12,15},{1,2,5,6,9,10,13,14},{16,19,20,23,24,27,28,31},{17..., dimensions={0} | all-to-all | bytes 262144 | tf_op jit(solution)/shard_map/all_to_all | solution.py:722
  31.7 9.6 %all_to_all.17 = f32[8,2,16,128]{3,2,1,0:T(8,128)S(1)} all-to-all(f32[8,2,16,128]{3,2,1,0:T(8,128)S(1)} %broadcast_in_dim.5), channel_id=1, replica_groups={{0,3,4,7,8,11,12,15},{1,2,5,6,9,10,13,14},{16,19,20,23,24,27,28,31},{17..., dimensions={0} | all-to-all | bytes 262144 | tf_op jit(solution)/shard_map/all_to_all | solution.py:722
  41.4 0.7 %collective-permute-start.2 = (f32[8,2,16,128]{3,2,1,0:T(8,128)S(1)}, f32[8,2,16,128]{3,2,1,0:T(8,128)S(1)}, u32[]{:S(2)}, u32[]{:S(2)}) collective-permute-start(f32[8,2,16,128]{3,2,1,0:T(8,128)S(1)} %all_to_all.17), channel_id=1, source_target_pairs={{0,1},{1,0},{2,3},{3,2},{4,5},{5,4},{6,7},{7,6},{8,9},{9,8},{10,11... | collective-permute-start | bytes 393224 | tf_op jit(solution)/shard_map/ppermute | solution.py:713
  42.1 1.0 %collective-permute-done.2 = f32[8,2,16,128]{3,2,1,0:T(8,128)S(1)} collective-permute-done((f32[8,2,16,128]{3,2,1,0:T(8,128)S(1)}, f32[8,2,16,128]{3,2,1,0:T(8,128)S(1)}, u32[]{:S(2)}, u32[]{:S(2)}) %collective-permute-start.2) | collective-permute-done | bytes 131104 | tf_op jit(solution)/shard_map/ppermute | solution.py:713
  43.1 1.8 %design.1 = f32[2,16,128]{2,1,0:T(8,128)} custom-call(f32[2,8,2,16,128]{4,3,2,1,0:T(8,128)S(1)} %pad_maximum_fusion.1.root_ref, f32[2,8,2,16,128]{4,3,2,1,0:T(8,128)S(1)} %pad_maximum_fusion.density_ref), custom_call_target="tpu_custom_call" | custom-call | tf_op jit(solution)/shard_map/design/pallas_call | solution.py:700
  (6 shorter events, 0.1 us)
Async XLA Ops:
  0.6 16.0 %copy-start = (f32[1,3,32,16,128]{4,3,2,1,0:T(8,128)S(1)}, f32[1,3,32,16,128]{4,3,2,1,0:T(8,128)}, u32[]{:S(2)}) copy-start(f32[1,3,32,16,128]{4,3,2,1,0:T(8,128)} %param.7) | copy-start | bytes 2359300
  14.9 1.7 %collective-permute-start = (f32[8,2,16,128]{3,2,1,0:T(8,128)S(1)}, f32[8,2,16,128]{3,2,1,0:T(8,128)S(1)}, u32[]{:S(2)}, u32[]{:S(2)}) collective-permute-start(f32[8,2,16,128]{3,2,1,0:T(8,128)S(1)} %all_to_all.15.density_ref), channel_id=1, source_target_pairs={{0,1},{1,0},{2,3},{3,2},{4,5},{5,4},{6,7},{7,6},{8,9},{9,8},{10,11... | collective-permute-start | bytes 393224 | tf_op jit(solution)/shard_map/ppermute | solution.py:713
  20.2 1.4 %collective-permute-start.1 = (f32[8,2,16,128]{3,2,1,0:T(8,128)S(1)}, f32[8,2,16,128]{3,2,1,0:T(8,128)S(1)}, u32[]{:S(2)}, u32[]{:S(2)}) collective-permute-start(f32[8,2,16,128]{3,2,1,0:T(8,128)S(1)} %get-tuple-element.48), channel_id=1, source_target_pairs={{0,1},{1,0},{2,3},{3,2},{4,5},{5,4},{6,7},{7,6},{8,9},{9,8},{10,11... | collective-permute-start | bytes 393224 | tf_op jit(solution)/shard_map/ppermute | solution.py:713
  41.4 1.7 %collective-permute-start.2 = (f32[8,2,16,128]{3,2,1,0:T(8,128)S(1)}, f32[8,2,16,128]{3,2,1,0:T(8,128)S(1)}, u32[]{:S(2)}, u32[]{:S(2)}) collective-permute-start(f32[8,2,16,128]{3,2,1,0:T(8,128)S(1)} %all_to_all.17), channel_id=1, source_target_pairs={{0,1},{1,0},{2,3},{3,2},{4,5},{5,4},{6,7},{7,6},{8,9},{9,8},{10,11... | collective-permute-start | bytes 393224 | tf_op jit(solution)/shard_map/ppermute | solution.py:713

commit v35 on v34

--- a/solution.py
+++ b/solution.py
@@ -494,8 +494,11 @@
     plane_ref,
     beside_ref,
     further_ref,
+    density_ref,
     disp_hbm,
     kept_ref,
+    low_ref,
+    high_ref,
     near_ref,
     far_ref,
     stored,
@@ -506,10 +509,17 @@
     store.start()
     shares = (plane_ref, beside_ref, further_ref)
     filter_group(0, shares, weight_ref, near_ref, far_ref, kept_ref)
+    groups, chips, own_planes = density_ref.shape[:3]
+    for group in range(groups):
+        for chip in range(chips):
+            for own in range(own_planes):
+                density = density_ref[group, chip, own]
+                low_ref[group, chip, own] = jnp.maximum(density - move_limit, density_floor)
+                high_ref[group, chip, own] = jnp.minimum(density + move_limit, 1.0)
     store.wait()
 
 
-def design_kernel(root_ref, density_ref, new_ref, pull_ref, low_ref, high_ref):
+def design_kernel(root_ref, density_ref, low_ref, high_ref, new_ref, pull_ref):
     groups, chips, own_planes, layers, row_width = density_ref.shape
     tile_rows = pull_ref.shape[1]
     steps = layers // tile_rows
@@ -523,10 +533,7 @@
         for step in range(steps)
     ]
     for place, spot in enumerate(tiles):
-        density = density_ref[spot]
-        pull_ref[place] = density * root_ref[spot]
-        low_ref[place] = jnp.maximum(density - move_limit, density_floor)
-        high_ref[place] = jnp.minimum(density + move_limit, 1.0)
+        pull_ref[place] = density_ref[spot] * root_ref[spot]
 
     target = volume_share * len(tiles) * tile_rows * row_width
 
@@ -547,8 +554,8 @@
         quarter = span * 0.25
         ahead = [factors_of(place, quarter) for place in places]
         totals = [[zero, zero] for _ in factors]
-        for place in range(len(tiles)):
-            pull, low, high = pull_ref[place], low_ref[place], high_ref[place]
+        for place, spot in enumerate(tiles):
+            pull, low, high = pull_ref[place], low_ref[spot], high_ref[spot]
             for total, factor in zip(totals, factors):
                 trial = jnp.minimum(jnp.maximum(pull * factor, low), high)
                 total[place % 2] = total[place % 2] + trial
@@ -568,8 +575,10 @@
     for own in range(own_planes):
         for step in range(steps):
             place = (own_chip * own_planes + own) * steps + step
-            new_ref[own, pl.ds(step * tile_rows, tile_rows)] = jnp.minimum(
-                jnp.maximum(pull_ref[place] * factor, low_ref[place]), high_ref[place]
+            part = pl.ds(step * tile_rows, tile_rows)
+            spot = (0, own_chip, own, part)
+            new_ref[own, part] = jnp.minimum(
+                jnp.maximum(pull_ref[place] * factor, low_ref[spot]), high_ref[spot]
             )
 
 
@@ -675,37 +684,42 @@
     )(disp, coef, weights)
 
 
-def kept_call(disp, weights, shares, group_shape):
+def kept_call(disp, weights, shares, density, group_shape):
     parts, disp_rows, row_width = disp.shape
     chips, own_planes, layers = group_shape[:3]
     gaps = pltpu.VMEM((chips * own_planes * (layers + GAP) + GAP, row_width), jnp.float32)
     return pl.pallas_call(
         kept_kernel,
-        out_shape=[floats(parts, disp_rows - 2 * layers, row_width), floats(*group_shape)],
-        in_specs=[in_vmem()] * 5,
-        out_specs=[pl.BlockSpec(memory_space=pltpu.HBM), in_vmem()],
+        out_shape=[
+            floats(parts, disp_rows - 2 * layers, row_width),
+            floats(*group_shape),
+            floats(*density.shape),
+            floats(*density.shape),
+        ],
+        in_specs=[in_vmem()] * 6,
+        out_specs=[pl.BlockSpec(memory_space=pltpu.HBM)] + [in_vmem()] * 3,
         scratch_shapes=[gaps, gaps, pltpu.SemaphoreType.DMA(())],
         compiler_params=pltpu.CompilerParams(vmem_limit_bytes=KERNEL_VMEM),
         cost_estimate=pl.CostEstimate(
             flops=20 * disp.size, bytes_accessed=8 * disp.size, transcendentals=0
         ),
         name="kept",
-    )(disp, weights, *shares)
-
-
-def design_call(root, density):
+    )(disp, weights, *shares, density)
+
+
+def design_call(root, density, low, high):
     tile_rows = min(8, density.shape[-2])
     row_width = density.shape[-1]
     tiles = pltpu.VMEM((density.size // (tile_rows * row_width), tile_rows, row_width), jnp.float32)
     return pl.pallas_call(
         design_kernel,
         out_shape=floats(*density.shape[2:]),
-        in_specs=[in_vmem()] * 2,
+        in_specs=[in_vmem()] * 4,
         out_specs=in_vmem(),
-        scratch_shapes=[tiles] * 3,
+        scratch_shapes=[tiles],
         compiler_params=pltpu.CompilerParams(vmem_limit_bytes=KERNEL_VMEM),
         name="design",
-    )(root, density)
+    )(root, density, low, high)
 
 
 def other_core(block):
@@ -733,7 +747,7 @@
 
 def scattered_sum(sent, make_kept):
     received = other_core(sent)
-    *others, kept = make_kept()
+    kept, *others = make_kept()
     return jnp.sum(between_chips(kept + received), axis=0), others
 
 
@@ -749,11 +763,13 @@
     )
     sent, *shares = share_call(disp, coef, weights, same_group.shape)
     sent, disp, shares = lax.optimization_barrier((sent, disp, shares))
-    squares, (new_displacement,) = scattered_sum(
-        sent, lambda: kept_call(disp, weights, shares, same_group.shape)
-    )
+    def make_kept():
+        stored, kept, *limits = kept_call(disp, weights, shares, whole, same_group.shape)
+        return kept, stored, *limits
+
+    squares, (new_displacement, low, high) = scattered_sum(sent, make_kept)
     root = with_other_core(chip_gathered(jnp.sqrt(squares)))
-    new_density = design_call(root, whole)
+    new_density = design_call(root, whole, low, high)
     return new_density, new_displacement.reshape(displacement.shape)
 
 

time: 45.3 us -> 45.4 us (level)
  no operation moved by 1% of the time
where the time goes in v35:
time: 45.4 us; the launch traced here: 44.9 us
  blocking collectives  33.2 us (73%)
  Pallas kernels  7.33 us (16%)
  starting transfers between devices  1.73 us (4%)
  waiting for transfers between devices  1.12 us (2%)
  local copies, waits for them, and re-layouts  0.82 us (2%)
  between operations  0.72 us (2%)
    all_to_all x3, blocking collectives, between_chips(): lax.all_to_all(pieces, 'space', 0, 0, axis_index_groups=chip_groups())  33.2 us
    pallas_call x1, Pallas kernels, sweep_call(): pl.pallas_call(sweep_kernel, out_shape=[floats(3, (planes + 2) * layers,...  2.55 us
    pallas_call x1, Pallas kernels, design_call(): pl.pallas_call(design_kernel, out_shape=floats(*density.shape[2:]), in_sp...  1.81 us
    ppermute x3, starting transfers between devices, other_core(): return lax.ppermute(block, 'space', [(i, i ^ 1) for i in range(devices)])  1.73 us
    ppermute x3, waiting for transfers between devices, other_core(): return lax.ppermute(block, 'space', [(i, i ^ 1) for i in range(devices)])  1.12 us
    pallas_call x1, Pallas kernels, share_call(): pl.pallas_call(share_kernel, out_shape=[floats(*group_shape)] + [floats(p...  1.08 us
    pallas_call x1, Pallas kernels, prepare_call(): pl.pallas_call(prepare_kernel, out_shape=[floats(len(ALL_SQUARES), layers...  1.01 us
  transfers between devices with their start and end apart: 3, of which 2 were waited for; matrix products, arithmetic and copies ran while one was open for 0% of the time, Pallas kernels for 4%

profile of v35, /device:TPU:0, one launch (start us, length us, event | category | flops | bytes accessed | tf_op | source)
XLA Modules:
  0.0 44.9 jit_solution(18235178771733665396)
XLA Ops:
  0.6 0.0 copy-start
  0.6 0.8 %broadcast_in_dim.4 = f32[8,2,16,128]{3,2,1,0:T(8,128)S(1)} broadcast(f32[2,16,128]{2,1,0:T(8,128)} %param.6), dimensions={1,2,3} | broadcast | bytes 147456 | tf_op jit(solution)/shard_map/broadcast_in_dim | solution.py:741
  1.4 13.5 %all_to_all.15.density_ref = f32[8,2,16,128]{3,2,1,0:T(8,128)S(1)} all-to-all(f32[8,2,16,128]{3,2,1,0:T(8,128)S(1)} %broadcast_in_dim.4), channel_id=1, replica_groups={{0,3,4,7,8,11,12,15},{1,2,5,6,9,10,13,14},{16,19,20,23,24,27,28,31},{17..., dimensions={0} | all-to-all | bytes 262144 | tf_op jit(solution)/shard_map/all_to_all | solution.py:736
  14.9 0.7 %collective-permute-start = (f32[8,2,16,128]{3,2,1,0:T(8,128)S(1)}, f32[8,2,16,128]{3,2,1,0:T(8,128)S(1)}, u32[]{:S(2)}, u32[]{:S(2)}) collective-permute-start(f32[8,2,16,128]{3,2,1,0:T(8,128)S(1)} %all_to_all.15.density_ref), channel_id=1, source_target_pairs={{0,1},{1,0},{2,3},{3,2},{4,5},{5,4},{6,7},{7,6},{8,9},{9,8},{10,11... | collective-permute-start | bytes 393224 | tf_op jit(solution)/shard_map/ppermute | solution.py:727
  15.6 1.0 %prepare.1 = (f32[10,16,128]{2,1,0:T(8,128)S(1)}, f32[5,16,128]{2,1,0:T(8,128)S(1)}, f32[32,16,128]{2,1,0:T(8,128)S(1)}, f32[3,16,128]{2,1,0:T(8,128)S(1)}, f32[...) custom-call(s32[16]{0:T(128)} %radius_hbm, s32[16]{0:T(128)} %index_hbm, f32[3,16]{1,0:T(4,128)} %bitcast.12, ...), custom_call_target="tpu_custom_call" | custom-call | flops 5242880 | bytes 524288 | tf_op jit(solution)/shard_map/prepare/pallas_call | solution.py:600
  16.6 0.0 collective-permute-done
  16.6 0.0 copy-done
  16.6 2.5 %sweeps.1 = (f32[3,544,128]{2,1,0:T(8,128)S(1)}, f32[32,16,128]{2,1,0:T(8,128)S(1)}) custom-call(f32[8,128]{1,0:T(8,128)S(1)} %get-tuple-element.33.spot_ref, f32[3,16,128]{2,1,0:T(8,128)S(1)} %get-tuple-element.34.load_ref, f32[10,16,128]{2,1,0:T(8,128)S(1)} %get-tuple-element.35.weight_ref, f32[5,16,128]{2,1,0:T(8,128)S(1)} %get-tuple-element.36.inverse_ref, ...), custom_call_target="tpu_custom_call" | custom-call | tf_op jit(solution)/shard_map/sweeps/pallas_call | solution.py:645
  19.2 1.1 %share.1 = (f32[8,2,16,128]{3,2,1,0:T(8,128)S(1)}, f32[36,16,128]{2,1,0:T(8,128)S(1)}, f32[36,16,128]{2,1,0:T(8,128)S(1)}, f32[36,16,128]{2,1,0:T(8,128)S(1)}) custom-call(f32[3,544,128]{2,1,0:T(8,128)S(1)} %get-tuple-element.45.disp_ref, f32[32,16,128]{2,1,0:T(8,128)S(1)} %get-tuple-element.40.coef_ref, f32[10,16,128]{2,1,0:T(8,128)S(1)} %get-tuple-element.35.weight_ref), custom_call_target="tpu_custom_call" | custom-call | tf_op jit(solution)/shard_map/share/pallas_call | solution.py:676
  20.3 0.4 collective-permute-start.1
  20.7 0.9 %kept.1 = (f32[3,512,128]{2,1,0:T(8,128)}, f32[8,2,16,128]{3,2,1,0:T(8,128)S(1)}, f32[2,8,2,16,128]{4,3,2,1,0:T(8,128)S(1)}, f32[2,8,2,16,128]{4,3,2,1,0:T(8,128)S(1)}) custom-call(f32[3,544,128]{2,1,0:T(8,128)S(1)} %get-tuple-element.45.disp_ref, f32[10,16,128]{2,1,0:T(8,128)S(1)} %get-tuple-element.35.weight_ref, ...), custom_call_target="tpu_custom_call" | custom-call | flops 4177920 | bytes 1671168 | tf_op jit(solution)/shard_map/kept/pallas_call | solution.py:691
  21.6 0.1 collective-permute-done.1
  21.7 10.0 %all_to_all.16 = f32[8,2,16,128]{3,2,1,0:T(8,128)S(1)} all-to-all(f32[8,2,16,128]{3,2,1,0:T(8,128)S(1)} %add.3), channel_id=1, replica_groups={{0,3,4,7,8,11,12,15},{1,2,5,6,9,10,13,14},{16,19,20,23,24,27,28,31},{17..., dimensions={0} | all-to-all | bytes 262144 | tf_op jit(solution)/shard_map/all_to_all | solution.py:736
  31.8 9.7 %all_to_all.17 = f32[8,2,16,128]{3,2,1,0:T(8,128)S(1)} all-to-all(f32[8,2,16,128]{3,2,1,0:T(8,128)S(1)} %broadcast_in_dim.5), channel_id=1, replica_groups={{0,3,4,7,8,11,12,15},{1,2,5,6,9,10,13,14},{16,19,20,23,24,27,28,31},{17..., dimensions={0} | all-to-all | bytes 262144 | tf_op jit(solution)/shard_map/all_to_all | solution.py:736
  41.5 0.7 %collective-permute-start.2 = (f32[8,2,16,128]{3,2,1,0:T(8,128)S(1)}, f32[8,2,16,128]{3,2,1,0:T(8,128)S(1)}, u32[]{:S(2)}, u32[]{:S(2)}) collective-permute-start(f32[8,2,16,128]{3,2,1,0:T(8,128)S(1)} %all_to_all.17), channel_id=1, source_target_pairs={{0,1},{1,0},{2,3},{3,2},{4,5},{5,4},{6,7},{7,6},{8,9},{9,8},{10,11... | collective-permute-start | bytes 393224 | tf_op jit(solution)/shard_map/ppermute | solution.py:727
  42.1 1.0 %collective-permute-done.2 = f32[8,2,16,128]{3,2,1,0:T(8,128)S(1)} collective-permute-done((f32[8,2,16,128]{3,2,1,0:T(8,128)S(1)}, f32[8,2,16,128]{3,2,1,0:T(8,128)S(1)}, u32[]{:S(2)}, u32[]{:S(2)}) %collective-permute-start.2) | collective-permute-done | bytes 131104 | tf_op jit(solution)/shard_map/ppermute | solution.py:727
  43.1 1.8 %design.1 = f32[2,16,128]{2,1,0:T(8,128)} custom-call(f32[2,8,2,16,128]{4,3,2,1,0:T(8,128)S(1)} %pad_maximum_fusion.1.root_ref, f32[2,8,2,16,128]{4,3,2,1,0:T(8,128)S(1)} %pad_maximum_fusion.density_ref, f32[2,8,2,16,128]{4,3,2,1,0:T(8,128)S(1)} %get-tuple-element.51.low_ref, f32[2,8,2,16,128]{4,3,2,1,0:T(8,128)S(1)} %get-tuple-element.52.high_ref), custom_call_target="tpu_custom_call" | custom-call | tf_op jit(solution)/shard_map/design/pallas_call | solution.py:714
  (6 shorter events, 0.1 us)
Async XLA Ops:
  0.6 16.0 %copy-start = (f32[1,3,32,16,128]{4,3,2,1,0:T(8,128)S(1)}, f32[1,3,32,16,128]{4,3,2,1,0:T(8,128)}, u32[]{:S(2)}) copy-start(f32[1,3,32,16,128]{4,3,2,1,0:T(8,128)} %param.7) | copy-start | bytes 2359300
  14.9 1.7 %collective-permute-start = (f32[8,2,16,128]{3,2,1,0:T(8,128)S(1)}, f32[8,2,16,128]{3,2,1,0:T(8,128)S(1)}, u32[]{:S(2)}, u32[]{:S(2)}) collective-permute-start(f32[8,2,16,128]{3,2,1,0:T(8,128)S(1)} %all_to_all.15.density_ref), channel_id=1, source_target_pairs={{0,1},{1,0},{2,3},{3,2},{4,5},{5,4},{6,7},{7,6},{8,9},{9,8},{10,11... | collective-permute-start | bytes 393224 | tf_op jit(solution)/shard_map/ppermute | solution.py:727
  20.3 1.4 %collective-permute-start.1 = (f32[8,2,16,128]{3,2,1,0:T(8,128)S(1)}, f32[8,2,16,128]{3,2,1,0:T(8,128)S(1)}, u32[]{:S(2)}, u32[]{:S(2)}) collective-permute-start(f32[8,2,16,128]{3,2,1,0:T(8,128)S(1)} %get-tuple-element.50), channel_id=1, source_target_pairs={{0,1},{1,0},{2,3},{3,2},{4,5},{5,4},{6,7},{7,6},{8,9},{9,8},{10,11... | collective-permute-start | bytes 393224 | tf_op jit(solution)/shard_map/ppermute | solution.py:727
  41.5 1.7 %collective-permute-start.2 = (f32[8,2,16,128]{3,2,1,0:T(8,128)S(1)}, f32[8,2,16,128]{3,2,1,0:T(8,128)S(1)}, u32[]{:S(2)}, u32[]{:S(2)}) collective-permute-start(f32[8,2,16,128]{3,2,1,0:T(8,128)S(1)} %all_to_all.17), channel_id=1, source_target_pairs={{0,1},{1,0},{2,3},{3,2},{4,5},{5,4},{6,7},{7,6},{8,9},{9,8},{10,11... | collective-permute-start | bytes 393224 | tf_op jit(solution)/shard_map/ppermute | solution.py:727
